TPU v7x, 32 devices: a whole 2x2x4 slice. The times are simulated.
32 devices in a mesh: dp: 8 (over y, x, core), tensor: 4 (over z).
Axes of the slice: x: 2, y: 2, z: 4, core: 2. Of those that a mesh axis runs over, the one named last changes fastest.
Arguments:
- inputs: bfloat16 [2048, 768], P('dp'), may hold values from -6 to 6
- segments: int32 [8, 256], P('dp'), may hold values from 0 to 3, never falling along the last dimension, each value on 1 to 128 neighbouring positions
- buckets: int32 [511], replicated, may hold values from 0 to 31
- routes: int32 [2048], P('dp'), may hold values from 0 to 1, as said below
- capacity_slots: int32 [2048], P('dp'), may hold values from 0 to 143, as said below
- gain_attn: float32 [768], replicated, may hold values from 0.25 to 1.75
- bias_table: float32 [32, 12], P(None, 'tensor'), may hold values from -4 to 4
- query_weight: bfloat16 [768, 768], P(None, 'tensor'), may hold values from -0.0546875 to 0.0546875
- key_weight: bfloat16 [768, 768], P(None, 'tensor'), may hold values from -0.21875 to 0.21875
- value_weight: bfloat16 [768, 768], P(None, 'tensor'), may hold values from -0.21875 to 0.21875
- out_weight: bfloat16 [768, 768], P('tensor'), may hold values from -0.875 to 0.875
- gain_expert: float32 [768], replicated, may hold values from 0.25 to 1.75
- router_weight: bfloat16 [768, 2], replicated, may hold values from -0.15625 to 0.15625
- expert_up: bfloat16 [2, 768, 3072], P(None, None, 'tensor'), may hold values from -0.21875 to 0.21875
- expert_down: bfloat16 [2, 3072, 768], P(None, 'tensor'), may hold values from -0.21875 to 0.21875
- cotangent: bfloat16 [2048, 768], P('dp'), may hold values from -6 to 6
Outputs:
- output: bfloat16 [2048, 768], P('dp')
- grad_inputs: bfloat16 [2048, 768], P('dp')
- grad_gain_attn: float32 [768], P(('dp', 'tensor'))
- grad_table: float32 [32, 12], P(None, 'tensor')
- grad_query_weight: float32 [768, 768], P('dp', 'tensor')
- grad_key_weight: float32 [768, 768], P('dp', 'tensor')
- grad_value_weight: float32 [768, 768], P('dp', 'tensor')
- grad_out_weight: float32 [768, 768], P('tensor', 'dp')
- grad_gain_expert: float32 [768], P(('dp', 'tensor'))
- grad_router: float32 [768, 2], P(('dp', 'tensor'))
- grad_expert_up: float32 [2, 768, 3072], P(None, 'dp', 'tensor')
- grad_expert_down: float32 [2, 3072, 768], P(None, 'tensor', 'dp')
Inputs may be any that keep to these rules, and one draw needn't show every extreme that they name: `routes`: in each sequence one expert receives exactly 144 tokens and every other fewer. `capacity_slots`: within one sequence, tokens of the same expert have distinct slots. `buckets`: the bucket of the offset j - i stands at index j - i + 255.
All inputs are finite; a program needn't handle non-finite values.
Results may differ from a plain program's by a relative error of at most 0.018.
Values may be sent and summed in bfloat16 or wider, within the bound.
No kernel may reach another device: no remote copies, remote signals or barrier semaphores. Data moves between devices by JAX's collectives and lax.ppermute only.
A program may use at most 128 MiB of HBM per device.

v0:
```python
import jax
import jax.numpy as jnp
from jax import lax
from jax.sharding import PartitionSpec as P

HEAD_DIM = 64
EXPERTS = 2
CAP = 144


def norm_rows(values, gains):
    return values * lax.rsqrt(jnp.mean(values * values, axis=-1, keepdims=True) + 1e-06) * gains


def offset_totals(grad_scores):
    head_count, row_count, length = grad_scores.shape
    reversed_cols = grad_scores[:, :, ::-1]
    padded = jnp.pad(reversed_cols, ((0, 0), (0, 0), (0, row_count)))
    sheared = padded.reshape(head_count, row_count * (length + row_count))[
        :, : row_count * (length + row_count - 1)
    ]
    sheared = sheared.reshape(head_count, row_count, length + row_count - 1)
    return jnp.sum(sheared, axis=1, dtype=jnp.float32)[:, ::-1]


def shards(
    inputs,
    segments,
    buckets,
    routes,
    capacity_slots,
    gain_attn,
    bias_table,
    query_weight,
    key_weight,
    value_weight,
    out_weight,
    gain_expert,
    router_weight,
    expert_up,
    expert_down,
    cotangent,
):
    length, model_width = inputs.shape
    members = lax.axis_size("tensor")
    share_rows = length // members
    first_row = lax.axis_index("tensor") * share_rows
    heads_here = query_weight.shape[1] // HEAD_DIM
    bucket_count = bias_table.shape[0]
    block_rows = min(512, length)
    blocks = length // block_rows
    segment = segments[0]
    inputs_wide = inputs.astype(jnp.float32)
    inputs_share = lax.dynamic_slice_in_dim(inputs_wide, first_row, share_rows)
    normed = norm_rows(inputs_wide, gain_attn).astype(jnp.bfloat16)

    def project(weight):
        projected = jnp.dot(normed, weight, preferred_element_type=jnp.float32)
        return projected.astype(jnp.bfloat16).reshape(length, heads_here, HEAD_DIM)

    queries, key_rows, value_rows = (
        project(query_weight),
        project(key_weight),
        project(value_weight),
    )
    bucket_hot = (buckets[:, None] == jnp.arange(bucket_count, dtype=jnp.int32)[None, :]).astype(
        jnp.float32
    )
    offset_bias = jnp.einsum("ob,bh->ho", bucket_hot, bias_table, precision=lax.Precision.HIGHEST)

    def block_scores(block_id):
        start_row = block_id * block_rows
        scores = jnp.einsum("qhd,khd->hqk", queries, key_rows, preferred_element_type=jnp.float32)
        offset_index = (
            jnp.arange(length, dtype=jnp.int32)[None, :]
            - jnp.arange(block_rows, dtype=jnp.int32)[:, None]
            - start_row
            + length
            - 1
        )
        scores = scores + jnp.take(offset_bias, offset_index, axis=1)
        same_doc = segment[:, None] == segment[None, :]
        return (jnp.where(same_doc[None], scores, -1e30), queries)

    def forward_block(block_id):
        scores, _ = block_scores(block_id)
        row_max = jnp.max(scores, axis=-1, keepdims=True)
        shifted = jnp.exp(scores - row_max)
        totals = jnp.sum(shifted, axis=-1, keepdims=True)
        weights = (shifted / totals).astype(jnp.bfloat16)
        mixed_block = jnp.einsum(
            "hqk,khd->qhd", weights, value_rows, preferred_element_type=jnp.float32
        )
        return (
            mixed_block.reshape(block_rows, heads_here * HEAD_DIM),
            (row_max + jnp.log(totals))[..., 0],
        )

    mixed_blocks, log_totals = lax.map(forward_block, jnp.arange(blocks, dtype=jnp.int32))
    mixed_rows = mixed_blocks.reshape(length, heads_here * HEAD_DIM).astype(jnp.bfloat16)
    attended = lax.psum_scatter(
        jnp.dot(mixed_rows, out_weight, preferred_element_type=jnp.float32),
        "tensor",
        scatter_dimension=0,
        tiled=True,
    )
    hidden_share = inputs_share + attended
    normed_two = lax.all_gather(
        norm_rows(hidden_share, gain_expert).astype(jnp.bfloat16), "tensor", axis=0, tiled=True
    )
    logits = jnp.dot(normed_two, router_weight, preferred_element_type=jnp.float32)
    router_probs = jax.nn.softmax(logits, axis=-1)
    chosen = (routes[:, None] == jnp.arange(EXPERTS, dtype=jnp.int32)[None, :]).astype(jnp.float32)
    gate_value = jnp.sum(router_probs * chosen, axis=-1)
    where_to = routes * CAP + capacity_slots
    buffer = jnp.zeros((EXPERTS * CAP, model_width), jnp.bfloat16).at[where_to].set(normed_two)
    buffer = buffer.reshape(EXPERTS, CAP, model_width)
    before = jnp.einsum("ecd,edf->ecf", buffer, expert_up, preferred_element_type=jnp.float32)
    active = jax.nn.gelu(before).astype(jnp.bfloat16)
    result = jnp.einsum(
        "ecf,efd->ecd", active, expert_down, preferred_element_type=jnp.float32
    ).reshape(EXPERTS * CAP, model_width)
    expert_share = lax.psum_scatter(
        result[where_to].astype(jnp.bfloat16), "tensor", scatter_dimension=0, tiled=True
    ).astype(jnp.float32)
    gate_share = lax.dynamic_slice_in_dim(gate_value, first_row, share_rows)
    output_share = (hidden_share + gate_share[:, None] * expert_share).astype(jnp.bfloat16)
    output = lax.all_gather(output_share, "tensor", axis=0, tiled=True)
    grad_rows = cotangent.astype(jnp.float32)
    grad_expert = (grad_rows * gate_value[:, None]).astype(jnp.bfloat16)
    grad_buffer = (
        jnp.zeros((EXPERTS * CAP, model_width), jnp.bfloat16).at[where_to].set(grad_expert)
    )
    grad_buffer = grad_buffer.reshape(EXPERTS, CAP, model_width)
    grad_expert_down = jnp.einsum(
        "ecf,ecd->efd", active, grad_buffer, preferred_element_type=jnp.float32
    )
    grad_active = jnp.einsum(
        "ecd,efd->ecf", grad_buffer, expert_down, preferred_element_type=jnp.float32
    )
    _, gelu_pull = jax.vjp(jax.nn.gelu, before)
    grad_before = gelu_pull(grad_active)[0].astype(jnp.bfloat16)
    grad_expert_up = jnp.einsum(
        "ecd,ecf->edf", buffer, grad_before, preferred_element_type=jnp.float32
    )
    back_rows = jnp.einsum(
        "ecf,edf->ecd", grad_before, expert_up, preferred_element_type=jnp.float32
    ).reshape(EXPERTS * CAP, model_width)
    grad_normed_share = lax.psum_scatter(
        back_rows[where_to].astype(jnp.bfloat16), "tensor", scatter_dimension=0, tiled=True
    ).astype(jnp.float32)
    grad_share_rows = lax.dynamic_slice_in_dim(grad_rows, first_row, share_rows)
    grad_gate = jnp.sum(grad_share_rows * expert_share, axis=-1)
    probs_share = lax.dynamic_slice_in_dim(router_probs, first_row, share_rows)
    chosen_share = lax.dynamic_slice_in_dim(chosen, first_row, share_rows)
    grad_logits = (grad_gate * gate_share)[:, None] * (chosen_share - probs_share)
    normed_share = lax.dynamic_slice_in_dim(normed_two, first_row, share_rows).astype(jnp.float32)
    grad_router = jnp.dot(normed_share.T, grad_logits, precision=lax.Precision.HIGHEST)
    grad_normed_share = grad_normed_share + jnp.dot(
        grad_logits, router_weight.astype(jnp.float32).T, precision=lax.Precision.HIGHEST
    )
    _, second_pull = jax.vjp(norm_rows, hidden_share, gain_expert)
    grad_hidden_norm, grad_gain_expert = second_pull(grad_normed_share)
    grad_hidden = grad_share_rows + grad_hidden_norm
    grad_attended = lax.all_gather(grad_hidden.astype(jnp.bfloat16), "tensor", axis=0, tiled=True)
    grad_out_weight = jnp.einsum(
        "tk,td->kd", mixed_rows, grad_attended, preferred_element_type=jnp.float32
    )
    grad_mixed = jnp.einsum(
        "td,kd->tk", grad_attended, out_weight, preferred_element_type=jnp.float32
    )
    grad_mixed = grad_mixed.astype(jnp.bfloat16).reshape(length, heads_here, HEAD_DIM)

    def backward_block(running, block_id):
        grad_keys, grad_values, offset_sums = running
        scores, block_queries = block_scores(block_id)
        probs_block = jnp.exp(scores - log_totals[block_id][..., None])
        grad_probs = jnp.einsum(
            "qhd,khd->hqk", grad_mixed, value_rows, preferred_element_type=jnp.float32
        )
        grad_scores = probs_block * (
            grad_probs - jnp.sum(probs_block * grad_probs, axis=-1, keepdims=True)
        )
        grad_scores = grad_scores.astype(jnp.bfloat16)
        grad_queries = jnp.einsum(
            "hqk,khd->qhd", grad_scores, key_rows, preferred_element_type=jnp.float32
        )
        grad_keys = grad_keys + jnp.einsum(
            "hqk,qhd->khd", grad_scores, block_queries, preferred_element_type=jnp.float32
        )
        grad_values = grad_values + jnp.einsum(
            "hqk,qhd->khd",
            probs_block.astype(jnp.bfloat16),
            grad_mixed,
            preferred_element_type=jnp.float32,
        )
        current = offset_sums
        offset_sums = current + offset_totals(grad_scores)
        return ((grad_keys, grad_values, offset_sums), grad_queries)

    zero_heads = jnp.zeros((length, heads_here, HEAD_DIM), jnp.float32)
    zero_offsets = jnp.zeros((heads_here, 2 * length - 1), jnp.float32)
    (grad_keys, grad_values, offset_sums), grad_queries = lax.scan(
        backward_block, (zero_heads, zero_heads, zero_offsets), jnp.arange(blocks, dtype=jnp.int32)
    )
    table_term = jnp.einsum("ho,ob->bh", offset_sums, bucket_hot, precision=lax.Precision.HIGHEST)
    grad_queries = grad_queries.reshape(length, heads_here * HEAD_DIM).astype(jnp.bfloat16)
    grad_keys = grad_keys.reshape(length, heads_here * HEAD_DIM).astype(jnp.bfloat16)
    grad_values = grad_values.reshape(length, heads_here * HEAD_DIM).astype(jnp.bfloat16)
    grad_query_weight = jnp.einsum(
        "td,tk->dk", normed, grad_queries, preferred_element_type=jnp.float32
    )
    grad_key_weight = jnp.einsum("td,tk->dk", normed, grad_keys, preferred_element_type=jnp.float32)
    grad_value_weight = jnp.einsum(
        "td,tk->dk", normed, grad_values, preferred_element_type=jnp.float32
    )
    total = jnp.einsum("tk,dk->td", grad_queries, query_weight, preferred_element_type=jnp.float32)
    total = total + jnp.einsum(
        "tk,dk->td", grad_keys, key_weight, preferred_element_type=jnp.float32
    )
    grad_normed_first = lax.psum_scatter(
        (
            total
            + jnp.einsum("tk,dk->td", grad_values, value_weight, preferred_element_type=jnp.float32)
        ).astype(jnp.bfloat16),
        "tensor",
        scatter_dimension=0,
        tiled=True,
    ).astype(jnp.float32)
    _, first_pull = jax.vjp(norm_rows, inputs_share, gain_attn)
    grad_input_norm, grad_gain_attn = first_pull(grad_normed_first)
    grad_inputs = lax.all_gather(
        (grad_hidden + grad_input_norm).astype(jnp.bfloat16), "tensor", axis=0, tiled=True
    )
    grad_table = lax.psum(table_term, "dp")
    grad_gain_attn, grad_gain_expert, grad_router = (
        lax.psum_scatter(grad_gain_attn, ("dp", "tensor"), scatter_dimension=0, tiled=True),
        lax.psum_scatter(grad_gain_expert, ("dp", "tensor"), scatter_dimension=0, tiled=True),
        lax.psum_scatter(grad_router, ("dp", "tensor"), scatter_dimension=0, tiled=True),
    )
    (
        grad_query_weight,
        grad_key_weight,
        grad_value_weight,
        grad_out_weight,
        grad_expert_up,
        grad_expert_down,
    ) = (
        lax.psum_scatter(grad_query_weight, "dp", scatter_dimension=0, tiled=True),
        lax.psum_scatter(grad_key_weight, "dp", scatter_dimension=0, tiled=True),
        lax.psum_scatter(grad_value_weight, "dp", scatter_dimension=0, tiled=True),
        lax.psum_scatter(grad_out_weight, "dp", scatter_dimension=1, tiled=True),
        lax.psum_scatter(grad_expert_up, "dp", scatter_dimension=1, tiled=True),
        lax.psum_scatter(grad_expert_down, "dp", scatter_dimension=2, tiled=True),
    )
    return (
        output,
        grad_inputs,
        grad_gain_attn,
        grad_table,
        grad_query_weight,
        grad_key_weight,
        grad_value_weight,
        grad_out_weight,
        grad_gain_expert,
        grad_router,
        grad_expert_up,
        grad_expert_down,
    )


def solution(mesh):
    return jax.shard_map(
        shards,
        mesh=mesh,
        in_specs=(
            P("dp", None),
            P("dp", None),
            P(),
            P("dp"),
            P("dp"),
            P(),
            P(None, "tensor"),
            P(None, "tensor"),
            P(None, "tensor"),
            P(None, "tensor"),
            P("tensor", None),
            P(),
            P(),
            P(None, None, "tensor"),
            P(None, "tensor", None),
            P("dp", None),
        ),
        out_specs=(
            P("dp", None),
            P("dp", None),
            P(("dp", "tensor")),
            P(None, "tensor"),
            P("dp", "tensor"),
            P("dp", "tensor"),
            P("dp", "tensor"),
            P("tensor", "dp"),
            P(("dp", "tensor")),
            P(("dp", "tensor"), None),
            P(None, "dp", "tensor"),
            P(None, "tensor", "dp"),
        ),
        check_vma=False,
    )
```

profile of v0, /device:TPU:0, one launch (start us, length us, event | category | flops | bytes accessed | tf_op | source)
XLA Modules:
  0.0 671.1 jit_solution(18064135713207698312)
XLA Ops:
  7.3 0.6 fusion.19
  7.9 1.2 multiply_reduce_fusion.1
  9.1 1.0 convolution_bitcast_fusion.1
  10.5 215.5 %gather_fusion.2 = f32[65536,3]{1,0:T(8,128)} fusion(f32[3,511]{0,1:T(8,128)S(1)} %copy.43, s32[65536]{0:T(1024)S(1)} %broadcast_clamp_fusion), kind=kCustom, calls=%fused_computation.clone | custom fusion | bytes 1835008 | tf_op jit(solution)/shard_map/while/body/eval_jaxpr/jit(_take)/gather | solution.py:81
  226.0 19.0 %copy.45 = f32[256,256,3]{0,1,2:T(8,128)S(1)} copy(f32[256,256,3]{2,1,0:T(8,128)} %bitcast.80) | data formatting | bytes 1572864 | tf_op jit(solution)/shard_map/while/body/eval_jaxpr/jit(_take)/gather | solution.py:81
  245.0 1.6 copy.42
  246.6 1.4 convolution_convert_fusion.7
  248.0 1.4 convolution_convert_fusion.6
  249.4 1.4 convolution_convert_fusion.5
  250.9 0.5 copy-done.20
  252.0 0.7 copy-done.2
  253.0 1.2 fusion.59
  254.3 1.0 convert_element_type.124
  255.3 25.1 %reduce-scatter.14.cloned.1.call-done = f32[64,768]{1,0:T(8,128)} async-done(((f32[256,768]{1,0:T(8,128)}), f32[64,768]{1,0:T(8,128)}) %reduce-scatter.14.cloned.1.call-update) | async-done | bytes 196624 | tf_op jit(solution)/shard_map/reduce_scatter | solution.py:101
  280.3 1.7 multiply_reduce_fusion.5
  282.5 15.0 %all_gather.12 = bf16[256,768]{1,0:T(8,128)(2,1)S(1)} all-gather(bf16[64,768]{1,0:T(8,128)(2,1)S(1)} %multiply_convert_fusion.5), channel_id=1, replica_groups=mesh['dp'=8,'tensor'=4] {'tensor'}, dimensions={0}, use_global_device_ids=true | all-gather | bytes 491520 | tf_op jit(solution)/shard_map/all_gather | solution.py:108
  297.8 2.4 scatter_custom_fusion
  300.2 2.3 scatter_custom_fusion.1
  302.5 2.7 fusion.60
  305.3 1.7 fusion.8
  307.0 0.6 fusion.48
  307.9 1.9 gather_fusion
  309.9 2.0 convert_element_type.138
  311.9 1.9 fusion.61
  313.8 1.9 gather_fusion.1
  315.9 14.2 %reduce-scatter.16.cloned.1.call-done = bf16[64,768]{1,0:T(8,128)(2,1)} async-done(((bf16[256,768]{1,0:T(8,128)(2,1)}), bf16[64,768]{1,0:T(8,128)(2,1)}) %reduce-scatter.16.cloned.1.call-update) | async-done | bytes 98320 | tf_op jit(solution)/shard_map/reduce_scatter | solution.py:123
  330.1 1.0 fusion.28
  331.2 20.8 %reduce-scatter.18.cloned.1.call-done = bf16[64,768]{1,0:T(8,128)(2,1)} async-done(((bf16[256,768]{1,0:T(8,128)(2,1)}), bf16[64,768]{1,0:T(8,128)(2,1)}) %reduce-scatter.18.cloned.1.call-update) | async-done | bytes 98320 | tf_op jit(solution)/shard_map/reduce_scatter | solution.py:149
  351.9 1.4 multiply_reduce_fusion.2
  353.4 1.7 fusion.52
  355.0 15.0 %all_gather.14 = bf16[256,768]{1,0:T(8,128)(2,1)S(1)} all-gather(bf16[64,768]{1,0:T(8,128)(2,1)S(1)} %get-tuple-element.80), channel_id=1, replica_groups=mesh['dp'=8,'tensor'=4] {'tensor'}, dimensions={0}, use_global_device_ids=true | all-gather | bytes 491520 | tf_op jit(solution)/shard_map/all_gather | solution.py:165
  372.4 1.0 fusion.1
  373.5 1.2 convolution_bitcast_fusion
  374.8 1.3 fusion.51
  376.2 1.3 fusion.50
  377.6 1.3 fusion.49
  379.0 3.0 fusion.63
  382.1 0.6 copy-done.37
  382.6 0.5 fusion.44
  383.3 3.1 fusion.47
  387.1 0.7 copy.63
  387.8 1.5 slice_convert_fusion
  389.4 14.5 %all_gather.13 = bf16[256,768]{1,0:T(8,128)(2,1)S(1)} all-gather(bf16[64,768]{1,0:T(8,128)(2,1)S(1)} %get-tuple-element.89), channel_id=1, replica_groups=mesh['dp'=8,'tensor'=4] {'tensor'}, dimensions={0}, use_global_device_ids=true | all-gather | bytes 491520 | tf_op jit(solution)/shard_map/all_gather | solution.py:128
  403.8 4.7 reshape.183
  408.6 1.5 reduce_sum.151
  410.1 1.4 reverse
  411.5 1.0 fusion.18
  412.5 12.5 %psum.7 = f32[32,3]{0,1:T(4,128)} all-reduce(f32[32,3]{0,1:T(4,128)S(1)} %fusion.18), channel_id=1, replica_groups=mesh['dp'=8,'tensor'=4] {'dp'}, use_global_device_ids=true, to_apply=%region_21.23 | all-reduce | flops 96 | bytes 768 | tf_op jit(solution)/shard_map/psum | solution.py:235
  425.0 1.1 fusion.36
  426.2 1.6 fusion.29
  427.8 0.7 multiply_multiply_fusion.2
  428.4 1.1 fusion.32
  429.5 15.0 %all_gather.15 = bf16[256,768]{1,0:T(8,128)(2,1)S(1)} all-gather(bf16[64,768]{1,0:T(8,128)(2,1)S(1)} %fusion.32), channel_id=1, replica_groups=mesh['dp'=8,'tensor'=4] {'tensor'}, dimensions={0}, use_global_device_ids=true | all-gather | bytes 491520 | tf_op jit(solution)/shard_map/all_gather | solution.py:232
  444.5 37.9 %all-reduce.4 = (f32[768]{0:T(1024)S(1)}, f32[768]{0:T(1024)S(1)}, f32[768,2]{0,1:T(2,128)S(1)}) all-reduce(f32[768]{0:T(1024)} %get-tuple-element.61, f32[768]{0:T(1024)S(1)} %get-tuple-element.63, f32[768,2]{0,1:T(2,128)S(1)} %fusion.36), channel_id=6, replica_groups=mesh['dp'=8,'tensor'=4] {'dp','tensor'}, use_global_device_ids=true, to_apply=%region_19.21.clone | all-reduce | flops 3072 | bytes 24576
  482.4 0.6 dynamic-slice
  483.0 0.6 dynamic-slice.1
  483.6 0.6 constant_dynamic-slice_fusion.1
  484.2 1.6 copy.58
  485.9 21.7 %reduce-scatter.24.cloned.1.call-done = f32[96,192]{1,0:T(8,128)} async-done(((f32[768,192]{1,0:T(8,128)}), f32[96,192]{1,0:T(8,128)}) %reduce-scatter.24.cloned.1.call-update) | async-done | bytes 73744 | tf_op jit(solution)/shard_map/reduce_scatter | solution.py:250
  507.6 39.0 %reduce-scatter.26.cloned.1.call-done = f32[96,192]{1,0:T(8,128)} async-done(((f32[768,192]{1,0:T(8,128)}), f32[96,192]{1,0:T(8,128)}) %reduce-scatter.26.cloned.1.call-update) | async-done | bytes 73744 | tf_op jit(solution)/shard_map/reduce_scatter | solution.py:251
  546.6 58.3 %reduce-scatter.28.cloned.1.call-done = f32[2,96,768]{2,1,0:T(8,128)} async-done(((f32[2,768,768]{2,1,0:T(8,128)}), f32[2,96,768]{2,1,0:T(8,128)}) %reduce-scatter.28.cloned.1.call-update) | async-done | bytes 589840 | tf_op jit(solution)/shard_map/reduce_scatter | solution.py:253
  604.9 57.8 %reduce-scatter.30.cloned.1.call-done = f32[2,768,96]{1,2,0:T(8,128)} async-done(((f32[2,768,768]{1,2,0:T(8,128)}), f32[2,768,96]{1,2,0:T(8,128)}) %reduce-scatter.30.cloned.1.call-update) | async-done | bytes 589840 | tf_op jit(solution)/shard_map/reduce_scatter | solution.py:254
  662.7 0.7 copy.66
  663.5 0.7 copy.67
  (131 shorter events, 6.4 us)
Async XLA Ops:
  7.2 298.1 %copy-start = (bf16[2,768,768]{2,1,0:T(8,128)(2,1)S(1)}, bf16[2,768,768]{2,1,0:T(8,128)(2,1)}, u32[]{:S(2)}) copy-start(bf16[2,768,768]{2,1,0:T(8,128)(2,1)} %param.31) | copy-start | bytes 7077892
  7.2 273.2 %reduce-scatter.14.cloned.1.call-start = ((), (), s32[]{:S(2)}) async-start(), calls=%async_computation.10 | async-start | bytes 983040 | tf_op jit(solution)/shard_map/reduce_scatter | solution.py:101
  226.0 20.7 %copy-start.4 = (bf16[256,768]{1,0:T(8,128)(2,1)S(1)}, bf16[256,768]{1,0:T(8,128)(2,1)}, u32[]{:S(2)}) copy-start(bf16[256,768]{1,0:T(8,128)(2,1)} %param.18) | copy-start | bytes 1179652
  226.0 20.7 %copy-start.26 = (f32[768]{0:T(1024)S(1)}, f32[768]{0:T(1024)}, u32[]{:S(2)}) copy-start(f32[768]{0:T(1024)} %param.23) | copy-start | bytes 9220
  245.0 5.8 copy-start.35
  246.6 4.8 copy-start.25
  248.0 4.0 copy-start.27
  249.4 1.5 copy-start.18
  250.7 0.6 copy-start.20
  251.8 0.9 copy-start.2
  251.8 1.2 copy-start.14
  252.9 2.3 copy-start.31
  252.9 2.3 copy-start.36
  252.9 29.1 %copy-start.29 = (f32[768]{0:T(1024)S(1)}, f32[768]{0:T(1024)}, u32[]{:S(2)}) copy-start(f32[768]{0:T(1024)} %param.29) | copy-start | bytes 9220
  252.9 44.6 %copy-start.30 = (bf16[768,2]{0,1:T(2,128)(2,1)S(1)}, bf16[768,2]{0,1:T(2,128)(2,1)}, u32[]{:S(2)}) copy-start(bf16[768,2]{0,1:T(2,128)(2,1)} %param.30) | copy-start | bytes 9220
  254.2 75.9 %reduce-scatter.16.cloned.1.call-start = ((), (), s32[]{:S(2)}) async-start(), calls=%async_computation.11 | async-start | bytes 491520 | tf_op jit(solution)/shard_map/reduce_scatter | solution.py:123
  282.0 0.5 copy-start.38
  297.5 2.7 copy-start.9
  297.8 54.1 %copy-start.32 = (f32[256,2]{0,1:T(2,128)}, f32[256,2]{0,1:T(2,128)S(1)}, u32[]{:S(2)}) copy-start(f32[256,2]{0,1:T(2,128)S(1)} %get-tuple-element.85) | copy-start | bytes 6148
  302.5 4.5 copy-start.5
  302.5 2.8 copy-start.12
  305.3 1.7 copy-start.8
  307.0 0.9 copy-start.16
  309.9 42.1 %reduce-scatter.18.cloned.1.call-start = ((), (), s32[]{:S(2)}) async-start(), calls=%async_computation.12 | async-start | bytes 491520 | tf_op jit(solution)/shard_map/reduce_scatter | solution.py:149
  313.8 16.3 %copy-start.10 = (f32[256,768]{1,0:T(8,128)S(1)}, f32[256,768]{1,0:T(8,128)}, u32[]{:S(2)}) copy-start(f32[256,768]{1,0:T(8,128)} %convert_element_type.138) | copy-start | bytes 2359300
  313.8 39.5 %copy-start.39 = (f32[64]{0:T(128)S(1)}, f32[64]{0:T(128)}, u32[]{:S(2)}) copy-start(f32[64]{0:T(128)} %copy-done.38) | copy-start | bytes 772
  313.8 56.2 %copy-start.15 = (bf16[192,768]{1,0:T(8,128)(2,1)S(1)}, bf16[192,768]{1,0:T(8,128)(2,1)}, u32[]{:S(2)}) copy-start(bf16[192,768]{1,0:T(8,128)(2,1)} %param.28) | copy-start | bytes 884740
  315.7 54.6 %copy-start.3 = (f32[3,256,256]{1,2,0:T(8,128)S(1)}, f32[3,256,256]{1,2,0:T(8,128)}, u32[]{:S(2)}) copy-start(f32[3,256,256]{1,2,0:T(8,128)} %copy-done.2) | copy-start | bytes 2359300
  315.7 54.6 %copy-start.28 = (bf16[256,192]{0,1:T(8,128)(2,1)S(1)}, bf16[256,192]{0,1:T(8,128)(2,1)}, u32[]{:S(2)}) copy-start(bf16[256,192]{0,1:T(8,128)(2,1)} %copy-done.27) | copy-start | bytes 294916
  315.8 110.4 %reduce-scatter.20.cloned.1.call-start = ((), (), s32[]{:S(2)}) async-start(), calls=%async_computation.13 | async-start | bytes 491520 | tf_op jit(solution)/shard_map/reduce_scatter | solution.py:221
  315.8 54.8 %copy-start.34 = (pred[256,2]{0,1:T(4,128)(4,1)}, pred[256,2]{0,1:T(4,128)(4,1)S(1)}, u32[]{:S(2)}) copy-start(pred[256,2]{0,1:T(4,128)(4,1)S(1)} %iota_compare_fusion.3) | copy-start | bytes 1540
  331.2 39.7 %copy-start.33 = (f32[64]{0:T(128)}, f32[64]{0:T(128)S(1)}, u32[]{:S(2)}) copy-start(f32[64]{0:T(128)S(1)} %get-tuple-element.82) | copy-start | bytes 772
  370.0 0.9 copy-start.21
  370.3 0.9 copy-start.19
  370.7 1.1 copy-start.22
  370.7 1.4 copy-start.23
  371.2 1.2 copy-start.24
  373.5 110.7 %reduce-scatter.32.cloned.1.call-start = ((), (), s32[]{:S(2)}) async-start(), calls=%async_computation.19 | async-start | bytes 884736
  374.8 111.1 %reduce-scatter.22.cloned.1.call-start = ((), (), s32[]{:S(2)}) async-start(), calls=%async_computation.14 | async-start | bytes 884736 | tf_op jit(solution)/shard_map/reduce_scatter | solution.py:249
  376.1 2.8 copy-start.11
  376.1 2.8 copy-start.13
  376.1 131.4 %reduce-scatter.24.cloned.1.call-start = ((), (), s32[]{:S(2)}) async-start(), calls=%async_computation.15 | async-start | bytes 884736 | tf_op jit(solution)/shard_map/reduce_scatter | solution.py:250
  377.5 169.1 %reduce-scatter.26.cloned.1.call-start = ((), (), s32[]{:S(2)}) async-start(), calls=%async_computation.16 | async-start | bytes 884736 | tf_op jit(solution)/shard_map/reduce_scatter | solution.py:251
  378.9 226.0 %reduce-scatter.28.cloned.1.call-start = ((), (), s32[]{:S(2)}) async-start(), calls=%async_computation.17 | async-start | bytes 5308416 | tf_op jit(solution)/shard_map/reduce_scatter | solution.py:253
  382.0 0.7 copy-start.37
  382.0 1.2 copy-start.6
  382.0 1.3 copy-start.17
  382.0 280.7 %reduce-scatter.30.cloned.1.call-start = ((), (), s32[]{:S(2)}) async-start(), calls=%async_computation.18 | async-start | bytes 5308416 | tf_op jit(solution)/shard_map/reduce_scatter | solution.py:254
  403.8 22.3 %copy-start.7 = (f32[256,768]{1,0:T(8,128)S(1)}, f32[256,768]{1,0:T(8,128)}, u32[]{:S(2)}) copy-start(f32[256,768]{1,0:T(8,128)} %convert_element_type.124) | copy-start | bytes 2359300
  403.8 260.4 %copy-start.1 = (bf16[2,768,768]{2,1,0:T(8,128)(2,1)S(1)}, bf16[2,768,768]{2,1,0:T(8,128)(2,1)}, u32[]{:S(2)}) copy-start(bf16[2,768,768]{2,1,0:T(8,128)(2,1)} %param.31) | copy-start | bytes 7077892
Sparse Core Ops, SparseCore 0:
  254.3 25.9 reduce-scatter.13
  310.0 20.0 reduce-scatter.15
  333.0 18.8 reduce-scatter.17
  373.6 19.0 reduce-scatter.19
  396.0 33.4 reduce-scatter.31
  433.4 35.0 reduce-scatter.21
  472.5 34.9 reduce-scatter.23
  511.6 34.9 reduce-scatter.25
  551.0 53.8 reduce-scatter.27
  608.8 53.8 reduce-scatter.29
where the time goes:
time: 672 us; the launch traced here: 671 us
  local copies, waits for them, and re-layouts  258 us (38%)
  waiting for transfers between devices  237 us (35%)
  blocking collectives  110 us (16%)
  matrix products  31.8 us (5%)
  other arithmetic  19.1 us (3%)
  between operations  14.7 us (2%)
    gather x2, local copies, waits for them, and re-layouts, block_scores(): scores = scores + jnp.take(offset_bias, offset_index, axis=1)  235 us
    reduce_scatter x1, waiting for transfers between devices, shards(): lax.psum_scatter(grad_expert_up, 'dp', scatter_dimension=1, tiled=True)  58.3 us
    reduce_scatter x1, waiting for transfers between devices, shards(): lax.psum_scatter(grad_expert_down, 'dp', scatter_dimension=2, tiled=True)  57.8 us
    reduce_scatter x1, waiting for transfers between devices, shards(): lax.psum_scatter(grad_value_weight, 'dp', scatter_dimension=0, tiled=True)  39 us
    unnamed x1, blocking collectives  37.9 us
    reduce_scatter x1, waiting for transfers between devices, shards(): lax.psum_scatter(jnp.dot(mixed_rows, out_weight, preferred_element_type=j...  25.1 us
    reduce_scatter x1, waiting for transfers between devices, shards(): lax.psum_scatter(grad_key_weight, 'dp', scatter_dimension=0, tiled=True)  21.7 us
    reduce_scatter x1, waiting for transfers between devices, shards(): lax.psum_scatter(back_rows[where_to].astype(jnp.bfloat16), 'tensor', scat...  20.8 us
  transfers between devices with their start and end apart: 10, of which 7 were waited for; matrix products, arithmetic and copies ran while one was open for 6% of the time, Pallas kernels for 0%

commit v1 on v0

v1 whole, which is shorter than its diff:
```python
import functools

import jax
import jax.numpy as jnp
from jax import lax
from jax.experimental import pallas as pl
from jax.experimental.pallas import tpu as pltpu
from jax.sharding import PartitionSpec as P

HEAD_DIM = 64
EXPERTS = 2
CAP = 144
EPS = 1e-06
SMALL_ROWS = 16
BF16 = jnp.bfloat16
F32 = jnp.float32
HIGHEST = lax.Precision.HIGHEST
NT = (((1,), (1,)), ((), ()))
TN = (((0,), (0,)), ((), ()))
GELU_C = 0.7978845608028654
GELU_A = 0.044715


def dot(a, b):
    return jnp.dot(a, b, preferred_element_type=F32)


def dot_nt(a, b, precision=None):
    return lax.dot_general(a, b, NT, preferred_element_type=F32, precision=precision)


def dot_tn(a, b):
    return lax.dot_general(a, b, TN, preferred_element_type=F32)


def inverse_rms(values):
    return lax.rsqrt(jnp.mean(values * values, axis=-1, keepdims=True) + EPS)


def share_of(index, rows):
    return pl.ds(pl.multiple_of(index * rows, rows), rows)


def put_shares(acc_ref, share_refs):
    me = lax.axis_index("tensor")
    for k, ref in enumerate(share_refs):
        rows = ref.shape[0]
        ref[...] = acc_ref[share_of(jnp.bitwise_xor(me, k), rows), :].astype(ref.dtype)


def assemble(full_ref, share_refs):
    me = lax.axis_index("tensor")
    for k, ref in enumerate(share_refs):
        rows = ref.shape[0]
        full_ref[share_of(jnp.bitwise_xor(me, k), rows), :] = ref[...]


def total_of(refs):
    total = refs[0][...].astype(F32)
    for ref in refs[1:]:
        total = total + ref[...].astype(F32)
    return total


def column_of(row, length):
    eye = lax.broadcasted_iota(jnp.int32, (length, length), 0) == lax.broadcasted_iota(
        jnp.int32, (length, length), 1
    )
    return jnp.sum(jnp.where(eye, row, jnp.zeros_like(row)), axis=1, keepdims=True)


def head_mask(head, width):
    lane = lax.broadcasted_iota(jnp.int32, (1, width), 1)
    return (lane >= head * HEAD_DIM) & (lane < (head + 1) * HEAD_DIM)


def masked(values, head):
    return jnp.where(head_mask(head, values.shape[1]), values, jnp.zeros_like(values))


def bucket_hot_of(buckets_ref, bucket_count):
    offsets = buckets_ref.shape[1]
    return (
        lax.broadcasted_iota(jnp.int32, (bucket_count, offsets), 0) == buckets_ref[...]
    ).astype(F32)


def attention_kernel(members, inputs, segment, buckets, gain, table, wq, wk, wv, wo, *rest):
    outs = rest[: members + 6]
    normed_o, q_o, k_o, v_o, probs_o, mixed_o = outs[members:]
    acc, offset_rows = rest[members + 6 :]
    length = inputs.shape[0]
    heads = wq.shape[1] // HEAD_DIM
    x = inputs[...].astype(F32)
    normed = (x * inverse_rms(x) * gain[...]).astype(BF16)
    normed_o[...] = normed
    q = dot(normed, wq[...]).astype(BF16)
    k = dot(normed, wk[...]).astype(BF16)
    v = dot(normed, wv[...]).astype(BF16)
    q_o[...] = q
    k_o[...] = k
    v_o[...] = v
    hot = bucket_hot_of(buckets, table.shape[0])
    seg_row = segment[...].astype(F32)
    same = column_of(seg_row, length) == seg_row
    mixed = jnp.zeros((length, wq.shape[1]), F32)
    offset_rows[...] = jnp.zeros_like(offset_rows)
    for h in range(heads):
        offset_rows[h : h + 1, 0 : hot.shape[1]] = jnp.sum(
            hot * table[:, h : h + 1], axis=0, keepdims=True
        )
    for h in range(heads):
        spread = jnp.broadcast_to(offset_rows[h : h + 1, :], (length, 2 * length))
        bias = pltpu.roll(spread, length + 1, 1, stride=1, stride_axis=0)[:, :length]
        scores = dot_nt(masked(q, h), k) + bias
        scores = jnp.where(same, scores, -1e30)
        shifted = jnp.exp(scores - jnp.max(scores, axis=-1, keepdims=True))
        probs = shifted / jnp.sum(shifted, axis=-1, keepdims=True)
        probs_o[h] = probs
        mixed = mixed + dot(probs.astype(BF16), masked(v, h))
    mixed = mixed.astype(BF16)
    mixed_o[...] = mixed
    acc[...] = dot(mixed, wo[...])
    put_shares(acc, outs[:members])


def hidden_kernel(members, inputs, gain, *rest):
    parts = rest[:members]
    hidden_o, normed_o = rest[members:]
    share = hidden_o.shape[0]
    x = inputs[share_of(lax.axis_index("tensor"), share), :].astype(F32)
    hidden = x + total_of(parts)
    hidden_o[...] = hidden
    normed_o[...] = (hidden * inverse_rms(hidden) * gain[...]).astype(BF16)


def expert_kernel(members, where_to, cotangent, router_t, up, down, *rest):
    pieces = rest[:members]
    rest = rest[members:]
    back_o, row_o = rest[:members], rest[members : 2 * members]
    buffer_o, active_o, grad_before_o, grad_expert_o, router_o = rest[2 * members : 2 * members + 5]
    normed, backs, rows, acc = rest[2 * members + 5 :]
    length = cotangent.shape[0]
    assemble(normed, pieces)
    place = (
        lax.broadcasted_iota(jnp.int32, (EXPERTS * CAP, length), 0) == where_to[...]
    ).astype(BF16)
    buffer = dot(place, normed[...]).astype(BF16)
    buffer_o[...] = buffer
    dy_buffer = dot(place, cotangent[...])
    router_rows = router_t[...].astype(F32)
    router_grad = [jnp.zeros((1, buffer.shape[1]), F32) for _ in range(EXPERTS)]
    for e in range(EXPERTS):
        slot = slice(e * CAP, (e + 1) * CAP)
        rows_in = buffer[slot]
        logits = dot_nt(rows_in, router_t[...])
        shifted = jnp.exp(logits - jnp.max(logits, axis=-1, keepdims=True))
        router_probs = shifted / jnp.sum(shifted, axis=-1, keepdims=True)
        gate = router_probs[:, e : e + 1]
        dy = dy_buffer[slot]
        grad_expert = (dy * gate).astype(BF16)
        grad_expert_o[slot, :] = grad_expert
        before = dot(rows_in, up[e])
        inner = jnp.tanh(GELU_C * (before + GELU_A * before * before * before))
        active = (0.5 * before * (1.0 + inner)).astype(BF16)
        active_o[slot, :] = active
        slope = 0.5 * (1.0 + inner) + 0.5 * before * (1.0 - inner * inner) * GELU_C * (
            1.0 + 3.0 * GELU_A * before * before
        )
        result = dot(active, down[e])
        grad_before = (dot_nt(grad_expert, down[e]) * slope).astype(BF16)
        grad_before_o[slot, :] = grad_before
        rows[slot, :] = (result * gate).astype(BF16)
        scaled = jnp.sum(dy * result, axis=-1, keepdims=True) * gate
        back = dot_nt(grad_before, up[e])
        for other in range(EXPERTS):
            own = 1.0 if other == e else 0.0
            grad_logit = scaled * (own - router_probs[:, other : other + 1])
            router_grad[other] = router_grad[other] + jnp.sum(
                grad_logit * rows_in.astype(F32), axis=0, keepdims=True
            )
            back = back + grad_logit * router_rows[other : other + 1, :]
        backs[slot, :] = back.astype(BF16)
    for other in range(EXPERTS):
        router_o[other : other + 1, :] = router_grad[other]
    acc[...] = dot_tn(place, backs[...])
    put_shares(acc, back_o)
    acc[...] = dot_tn(place, rows[...])
    put_shares(acc, row_o)


def split_rows(keep, send, chip, part):
    core = lax.rem(lax.axis_index("dp"), 2)
    return share_of(2 * chip + core, part), share_of(2 * chip + 1 - core, part)


def expert_grad_kernel(split, buffer, active, grad_before, grad_expert, *rest):
    width = buffer.shape[1]
    scratch = rest[-1]
    for e in range(EXPERTS):
        slot = slice(e * CAP, (e + 1) * CAP)
        for which in range(2):
            if which == 0:
                product = dot_tn(buffer[slot, :], grad_before[slot, :])
            else:
                product = dot_tn(grad_expert[slot, :], active[slot, :])
            hidden_units = active.shape[1]
            first = (2 * e + which) * hidden_units
            if not split:
                rest[0][:, first : first + hidden_units] = product
                continue
            keep, send = rest[0], rest[1]
            part = keep.shape[1]
            scratch[...] = product
            for chip in range(keep.shape[0]):
                mine, other = split_rows(keep, send, chip, part)
                keep[chip, :, first : first + hidden_units] = scratch[mine, :].astype(BF16)
                send[chip, :, first : first + hidden_units] = scratch[other, :].astype(BF16)


def merge_kernel(kept, came, *outs):
    chips = kept.shape[0]
    chip = lax.div(lax.axis_index("dp"), 2)
    for k in range(chips):
        there = jnp.bitwise_xor(chip, k)
        total = kept[there].astype(F32) + came[there].astype(F32)
        outs[k][...] = total.astype(outs[k].dtype)


def expert_final_kernel(chips, *refs):
    up_o, down_o = refs[chips:]
    total = total_of(refs[:chips])
    for e in range(EXPERTS):
        width = up_o.shape[2]
        first = 2 * e * width
        up_o[e] = total[:, first : first + width]
        down_o[e] = total[:, first + width : first + 2 * width].T


def output_kernel(members, hidden, *rest):
    rest[-1][...] = (hidden[...] + total_of(rest[:members])).astype(BF16)


def gather_kernel(*refs):
    assemble(refs[-1], refs[:-1])


def hidden_back_kernel(members, hidden, cotangent, gain, *rest):
    parts = rest[:members]
    grad_o, low_o, gain_o = rest[members:]
    share = hidden.shape[0]
    h = hidden[...]
    dy = cotangent[share_of(lax.axis_index("tensor"), share), :].astype(F32)
    r = inverse_rms(h)
    grad_normed = total_of(parts)
    z = grad_normed * gain[...]
    gain_o[...] = jnp.sum(grad_normed * h * r, axis=0, keepdims=True)
    grad = dy + r * z - h * (r * r * r) * jnp.mean(z * h, axis=-1, keepdims=True)
    grad_o[...] = grad
    low_o[...] = grad.astype(BF16)


def attention_back_kernel(members, inputs, probs, q, k, v, wq, wk, wv, wo, *rest):
    pieces = rest[:members]
    rest = rest[members:]
    share_o = rest[:members]
    grads_o, attended_o, scores_o, gain_o = rest[members : members + 4]
    acc = rest[members + 4]
    assemble(attended_o, pieces)
    heads = wq.shape[1] // HEAD_DIM
    grad_mixed = dot_nt(attended_o[...], wo[...]).astype(BF16)
    qv, kv, vv = q[...], k[...], v[...]
    dq = jnp.zeros(qv.shape, F32)
    dk = jnp.zeros(qv.shape, F32)
    dv = jnp.zeros(qv.shape, F32)
    for h in range(heads):
        grad_mixed_h = masked(grad_mixed, h)
        p = probs[h]
        grad_probs = dot_nt(grad_mixed_h, vv)
        inner = jnp.sum(p * grad_probs, axis=-1, keepdims=True)
        grad_scores = (p * (grad_probs - inner)).astype(BF16)
        scores_o[h] = grad_scores
        dq = dq + dot(grad_scores, masked(kv, h))
        dk = dk + dot_tn(grad_scores, masked(qv, h))
        dv = dv + dot_tn(p.astype(BF16), grad_mixed_h)
    dq, dk, dv = dq.astype(BF16), dk.astype(BF16), dv.astype(BF16)
    grads_o[0] = dq
    grads_o[1] = dk
    grads_o[2] = dv
    total = dot_nt(dq, wq[...]) + dot_nt(dk, wk[...]) + dot_nt(dv, wv[...])
    acc[...] = total
    put_shares(acc, share_o)
    x = inputs[...].astype(F32)
    gain_o[...] = jnp.sum(total * x * inverse_rms(x), axis=0, keepdims=True)


def weight_grad_kernel(
    split, normed, grads, attended, mixed, scores, buckets, gain_one, gain_two, router, *rest
):
    bucket_count = 32
    small, scratch = rest[-2:]
    length = normed.shape[0]
    cols = grads.shape[2]
    normed_v = normed[...]
    for i in range(4):
        if i < 3:
            product = dot_tn(normed_v, grads[i])
        else:
            product = dot_tn(attended[...], mixed[...])
        scratch[:, i * cols : (i + 1) * cols] = product
    small[...] = jnp.zeros_like(small)
    width = gain_one.shape[1]
    small[0:1, 0:width] = gain_one[...]
    small[1:2, 0:width] = gain_two[...]
    small[2 : 2 + EXPERTS, 0:width] = router[...]
    flip = (
        lax.broadcasted_iota(jnp.int32, (length, length), 0)
        + lax.broadcasted_iota(jnp.int32, (length, length), 1)
        == length - 1
    ).astype(BF16)
    hot = (
        lax.broadcasted_iota(jnp.int32, (bucket_count, 2 * length), 0) == buckets[...]
    ).astype(F32)
    for h in range(scores.shape[0]):
        flipped = dot(flip, scores[h])
        wide = jnp.concatenate([flipped, jnp.zeros_like(flipped)], axis=1)
        sheared = pltpu.roll(wide, 0, 1, stride=1, stride_axis=0)
        offsets = jnp.sum(sheared, axis=0, keepdims=True)
        small[2 + EXPERTS + h : 3 + EXPERTS + h, 0:bucket_count] = dot_nt(
            jnp.broadcast_to(offsets, (8, 2 * length)), hot, HIGHEST
        )[0:1]
    if not split:
        rest[0][...] = scratch[...]
        rest[1][...] = small[...]
        return
    keep, send = rest[0], rest[1]
    chips, rows, _ = keep.shape
    part = rows - SMALL_ROWS
    for chip in range(chips):
        mine, other = split_rows(keep, send, chip, part)
        keep[chip, 0:part, :] = scratch[mine, :].astype(BF16)
        send[chip, 0:part, :] = scratch[other, :].astype(BF16)
        keep[chip, part:rows, :] = small[...].astype(BF16)
        send[chip, part:rows, :] = small[...].astype(BF16)


def weight_final_kernel(chips, *refs):
    wq_o, wk_o, wv_o, wo_o, table_o, small_o = refs[chips:]
    total = total_of(refs[:chips])
    part, cols = wq_o.shape
    wq_o[...] = total[0:part, 0:cols]
    wk_o[...] = total[0:part, cols : 2 * cols]
    wv_o[...] = total[0:part, 2 * cols : 3 * cols]
    wo_o[...] = total[0:part, 3 * cols : 4 * cols].T
    small = total[part:, :]
    small_o[...] = small
    bucket_count, heads = table_o.shape
    pick = (
        lax.broadcasted_iota(jnp.int32, (bucket_count, small.shape[1]), 0)
        == lax.broadcasted_iota(jnp.int32, (bucket_count, small.shape[1]), 1)
    ).astype(F32)
    table_o[...] = dot_nt(pick, small, HIGHEST)[:, 2 + EXPERTS : 2 + EXPERTS + heads]


def small_final_kernel(members, *refs):
    one_o, two_o, router_o = refs[members:]
    total = total_of(refs[:members])
    part = router_o.shape[0]
    first = (lax.axis_index("dp") * members + lax.axis_index("tensor")) * part
    shape = (part, total.shape[1])
    pick = (
        lax.broadcasted_iota(jnp.int32, shape, 0) + first
        == lax.broadcasted_iota(jnp.int32, shape, 1)
    ).astype(F32)
    rows = dot_nt(total, pick, HIGHEST)
    one_o[...] = rows[0:1]
    two_o[...] = rows[1:2]
    router_o[...] = dot_nt(pick, total, HIGHEST)[:, 2 : 2 + EXPERTS]


def input_back_kernel(members, inputs, gain, grad_hidden, *rest):
    out = rest[-1]
    share = out.shape[0]
    x = inputs[share_of(lax.axis_index("tensor"), share), :].astype(F32)
    r = inverse_rms(x)
    z = total_of(rest[:members]) * gain[...]
    out[...] = (
        grad_hidden[...] + r * z - x * (r * r * r) * jnp.mean(z * x, axis=-1, keepdims=True)
    ).astype(BF16)


def run(kernel, outs, args, scratch=(), flops=0, name=None):
    vmem = pl.BlockSpec(memory_space=pltpu.VMEM)
    size = sum(a.size * a.dtype.itemsize for a in args)
    size += sum(o.size * o.dtype.itemsize for o in outs)
    return pl.pallas_call(
        kernel,
        out_shape=outs,
        in_specs=[vmem] * len(args),
        out_specs=[vmem] * len(outs),
        scratch_shapes=list(scratch),
        compiler_params=pltpu.CompilerParams(vmem_limit_bytes=48 * 1024 * 1024),
        cost_estimate=pl.CostEstimate(flops=flops, bytes_accessed=size, transcendentals=0),
        name=name,
    )(*args)


def sds(shape, dtype):
    return jax.ShapeDtypeStruct(tuple(shape), dtype)


def swap(values, axis, k):
    size = lax.axis_size(axis)
    return lax.ppermute(values, axis, [(i, i ^ k) for i in range(size)])


def exchange(shares):
    return [shares[0]] + [swap(s, "tensor", k) for k, s in enumerate(shares) if k > 0]


def spread(share):
    members = lax.axis_size("tensor")
    return [share] + [swap(share, "tensor", k) for k in range(1, members)]


def shards(
    inputs,
    segments,
    buckets,
    routes,
    capacity_slots,
    gain_attn,
    bias_table,
    query_weight,
    key_weight,
    value_weight,
    out_weight,
    gain_expert,
    router_weight,
    expert_up,
    expert_down,
    cotangent,
):
    length, width = inputs.shape
    members = lax.axis_size("tensor")
    dp = lax.axis_size("dp")
    share = length // members
    cols = query_weight.shape[1]
    heads = cols // HEAD_DIM
    hidden_units = expert_up.shape[2]
    bucket_count = bias_table.shape[0]
    part = width // dp
    split = dp == 8 and part % 16 == 0
    chips = dp // 2
    bind = functools.partial

    def shares_sds(dtype, own=None):
        return [sds((share, width), own or dtype)] + [
            sds((share, width), dtype) for _ in range(members - 1)
        ]

    gain_row = gain_attn.reshape(1, width)
    gain_two_row = gain_expert.reshape(1, width)
    bucket_row = buckets.reshape(1, -1)
    bucket_wide = jnp.pad(bucket_row, ((0, 0), (0, 1)), constant_values=-1)
    where_to = (routes * CAP + capacity_slots).reshape(1, length)
    router_t = router_weight.T

    outs = run(
        bind(attention_kernel, members),
        shares_sds(BF16, F32)
        + [sds((length, width), BF16)]
        + [sds((length, cols), BF16)] * 3
        + [sds((heads, length, length), F32), sds((length, cols), BF16)],
        [
            inputs,
            segments,
            bucket_row,
            gain_row,
            bias_table,
            query_weight,
            key_weight,
            value_weight,
            out_weight,
        ],
        [pltpu.VMEM((length, width), F32), pltpu.VMEM((8, 2 * length), F32)],
        name="attention",
    )
    attended = exchange(outs[:members])
    normed, q, k, v, probs, mixed = outs[members:]

    hidden, normed_two = run(
        bind(hidden_kernel, members),
        [sds((share, width), F32), sds((share, width), BF16)],
        [inputs, gain_two_row] + attended,
        name="hidden",
    )
    normed_two = spread(normed_two)

    slots = EXPERTS * CAP
    outs = run(
        bind(expert_kernel, members),
        shares_sds(BF16)
        + shares_sds(BF16)
        + [sds((slots, width), BF16)]
        + [sds((slots, hidden_units), BF16)] * 2
        + [sds((slots, width), BF16), sds((EXPERTS, width), F32)],
        [where_to, cotangent, router_t, expert_up, expert_down] + normed_two,
        [
            pltpu.VMEM((length, width), BF16),
            pltpu.VMEM((slots, width), BF16),
            pltpu.VMEM((slots, width), BF16),
            pltpu.VMEM((length, width), F32),
        ],
        name="expert",
    )
    back_rows = exchange(outs[:members])
    out_rows = outs[members : 2 * members]
    buffer, active, grad_before, grad_expert, grad_router = outs[2 * members :]

    def split_sds(rows, columns):
        return [sds((chips, rows, columns), BF16)] * 2

    expert_grads = run(
        bind(expert_grad_kernel, split),
        split_sds(part, 4 * hidden_units) if split else [sds((width, 4 * hidden_units), F32)],
        [buffer, active, grad_before, grad_expert],
        [pltpu.VMEM((width, hidden_units), F32)],
        flops=8 * CAP * width * hidden_units,
        name="expert_grads",
    )

    grad_hidden, grad_attended, grad_gain_expert = run(
        bind(hidden_back_kernel, members),
        [sds((share, width), F32), sds((share, width), BF16), sds((1, width), F32)],
        [hidden, cotangent, gain_two_row] + back_rows,
        name="hidden_back",
    )
    grad_attended = spread(grad_attended)
    out_rows = exchange(out_rows)
    (output,) = run(
        bind(output_kernel, members),
        [sds((share, width), BF16)],
        [hidden] + out_rows,
        name="output_share",
    )
    output = spread(output)
    (output,) = run(gather_kernel, [sds((length, width), BF16)], output, name="output_rows")

    outs = run(
        bind(attention_back_kernel, members),
        shares_sds(BF16, F32)
        + [
            sds((3, length, cols), BF16),
            sds((length, width), BF16),
            sds((heads, length, length), BF16),
            sds((1, width), F32),
        ],
        [inputs, probs, q, k, v, query_weight, key_weight, value_weight, out_weight]
        + grad_attended,
        [pltpu.VMEM((length, width), F32)],
        name="attention_back",
    )
    grad_normed = exchange(outs[:members])
    projections, attended_low, grad_scores, grad_gain_attn = outs[members:]

    weight_cols = 4 * cols
    weight_grads = run(
        bind(weight_grad_kernel, split),
        split_sds(part + SMALL_ROWS, weight_cols)
        if split
        else [sds((width, weight_cols), F32), sds((SMALL_ROWS, weight_cols), F32)],
        [
            normed,
            projections,
            attended_low,
            mixed,
            grad_scores,
            bucket_wide,
            grad_gain_attn,
            grad_gain_expert,
            grad_router,
        ],
        [pltpu.VMEM((SMALL_ROWS, weight_cols), F32), pltpu.VMEM((width, weight_cols), F32)],
        name="weight_grads",
    )

    (grad_inputs,) = run(
        bind(input_back_kernel, members),
        [sds((share, width), BF16)],
        [inputs, gain_row, grad_hidden] + grad_normed,
        name="input_back",
    )
    grad_inputs = spread(grad_inputs)
    (grad_inputs,) = run(
        gather_kernel, [sds((length, width), BF16)], grad_inputs, name="grad_rows"
    )

    if split:

        def over_chips(kept, sent):
            rows, columns = kept.shape[1:]
            came = swap(sent, "dp", 1)
            merged = run(
                merge_kernel,
                [sds((rows, columns), F32)] + [sds((rows, columns), BF16)] * (chips - 1),
                [kept, came],
                name="merge",
            )
            return [merged[0]] + [swap(merged[i], "dp", 2 * i) for i in range(1, chips)]

        parts = over_chips(*expert_grads)
        grad_expert_up, grad_expert_down = run(
            bind(expert_final_kernel, chips),
            [sds((EXPERTS, part, hidden_units), F32), sds((EXPERTS, hidden_units, part), F32)],
            parts,
            name="expert_final",
        )
        parts = over_chips(*weight_grads)
        (
            grad_query_weight,
            grad_key_weight,
            grad_value_weight,
            grad_out_weight,
            grad_table,
            small,
        ) = run(
            bind(weight_final_kernel, chips),
            [sds((part, cols), F32)] * 3
            + [sds((cols, part), F32), sds((bucket_count, heads), F32)]
            + [sds((SMALL_ROWS, weight_cols), F32)],
            parts,
            name="weight_final",
        )
        small = [small] + [swap(small, "tensor", i) for i in range(1, members)]
        per = part // members
        grad_gain_attn, grad_gain_expert, grad_router = run(
            bind(small_final_kernel, members),
            [sds((1, per), F32), sds((1, per), F32), sds((per, EXPERTS), F32)],
            small,
            name="small_final",
        )
        grad_gain_attn = grad_gain_attn.reshape(per)
        grad_gain_expert = grad_gain_expert.reshape(per)
    else:

        def scatter(values, axes, dimension):
            return lax.psum_scatter(values, axes, scatter_dimension=dimension, tiled=True)

        grads = expert_grads[0].reshape(width, EXPERTS, 2, hidden_units)
        grad_expert_up = scatter(grads[:, :, 0].transpose(1, 0, 2), "dp", 1)
        grad_expert_down = scatter(grads[:, :, 1].transpose(1, 2, 0), "dp", 2)
        grads, small = weight_grads
        grad_query_weight = scatter(grads[:, 0:cols], "dp", 0)
        grad_key_weight = scatter(grads[:, cols : 2 * cols], "dp", 0)
        grad_value_weight = scatter(grads[:, 2 * cols : 3 * cols], "dp", 0)
        grad_out_weight = scatter(grads[:, 3 * cols :].T, "dp", 1)
        first = 2 + EXPERTS
        grad_table = lax.psum(small[first : first + heads, :bucket_count].T, "dp")
        both = ("dp", "tensor")
        grad_gain_attn = scatter(small[0, :width], both, 0)
        grad_gain_expert = scatter(small[1, :width], both, 0)
        grad_router = scatter(small[2:first, :width].T, both, 0)
    return (
        output,
        grad_inputs,
        grad_gain_attn,
        grad_table,
        grad_query_weight,
        grad_key_weight,
        grad_value_weight,
        grad_out_weight,
        grad_gain_expert,
        grad_router,
        grad_expert_up,
        grad_expert_down,
    )


def solution(mesh):
    return jax.shard_map(
        shards,
        mesh=mesh,
        in_specs=(
            P("dp", None),
            P("dp", None),
            P(),
            P("dp"),
            P("dp"),
            P(),
            P(None, "tensor"),
            P(None, "tensor"),
            P(None, "tensor"),
            P(None, "tensor"),
            P("tensor", None),
            P(),
            P(),
            P(None, None, "tensor"),
            P(None, "tensor", None),
            P("dp", None),
        ),
        out_specs=(
            P("dp", None),
            P("dp", None),
            P(("dp", "tensor")),
            P(None, "tensor"),
            P("dp", "tensor"),
            P("dp", "tensor"),
            P("dp", "tensor"),
            P("tensor", "dp"),
            P(("dp", "tensor")),
            P(("dp", "tensor"), None),
            P(None, "dp", "tensor"),
            P(None, "tensor", "dp"),
        ),
        check_vma=False,
    )
```

time: 672 us -> 155 us (0.23)
  local copies, waits for them, and re-layouts: 258 us -> 11.7 us
  waiting for transfers between devices: 237 us -> 71.1 us
  blocking collectives: 110 us -> 0 us
  starting transfers between devices: 0.41 us -> 46.6 us
  matrix products: 31.8 us -> 0 us
  Pallas kernels: 0 us -> 23.9 us
  other arithmetic: 19.1 us -> 0.01 us
  between operations: 14.7 us -> 0.88 us
    gather x4 -> x0, local copies, waits for them, and re-layouts: 238 us -> none  [the longest x2 235 us: block_scores(): scores = scores + jnp.take(offset_bias, offset_index, axis=1)]
    reduce_scatter x9 -> x0, waiting for transfers between devices: 237 us -> none  [the longest x1 58.3 us: shards(): lax.psum_scatter(grad_expert_up, 'dp', scatter_dimension=1, tiled=True)]
    ppermute x0 -> x35, waiting for transfers between devices: none -> 71.1 us  [swap(): return lax.ppermute(values, axis, [(i, i ^ k) for i in range(size)])]
    all_gather x4 -> x0, blocking collectives: 59.5 us -> none  [the longest x1 15 us: shards(): lax.all_gather((grad_hidden + grad_input_norm).astype(jnp.bfloat16), 'ten...]
    ppermute x0 -> x35, starting transfers between devices: none -> 46.6 us  [swap(): return lax.ppermute(values, axis, [(i, i ^ k) for i in range(size)])]
    unnamed x1 -> x0, blocking collectives: 37.9 us -> none
    dot_general x28 -> x0, matrix products: 30.6 us -> none  [the longest x3 4.1 us: project(): projected = jnp.dot(normed, weight, preferred_element_type=jnp.float32)]
    pallas_call x0 -> x16, Pallas kernels: none -> 23.9 us  [run(): pl.pallas_call(kernel, out_shape=outs, in_specs=[vmem] * len(args), out_s...]
  transfers between devices with their start and end apart: 10 -> 35, of which waited for: 7 -> 18; matrix products, arithmetic and copies ran while one was open for 6% -> 1% of each run, Pallas kernels for 0% -> 7%
where the time goes in v1:
time: 155 us; the launch traced here: 154 us
  waiting for transfers between devices  71.1 us (46%)
  starting transfers between devices  46.6 us (30%)
  Pallas kernels  23.9 us (15%)
  local copies, waits for them, and re-layouts  11.7 us (8%)
    ppermute x35, waiting for transfers between devices, swap(): return lax.ppermute(values, axis, [(i, i ^ k) for i in range(size)])  71.1 us
    ppermute x35, starting transfers between devices, swap(): return lax.ppermute(values, axis, [(i, i ^ k) for i in range(size)])  46.6 us
    pallas_call x16, Pallas kernels, run(): pl.pallas_call(kernel, out_shape=outs, in_specs=[vmem] * len(args), out_s...  23.9 us
    unnamed x37, local copies, waits for them, and re-layouts  11 us
  transfers between devices with their start and end apart: 35, of which 18 were waited for; matrix products, arithmetic and copies ran while one was open for 1% of the time, Pallas kernels for 7%

profile of v1, /device:TPU:0, one launch (start us, length us, event | category | flops | bytes accessed | tf_op | source)
XLA Modules:
  0.0 154.1 jit_solution(10158680732948474987)
XLA Ops:
  0.7 0.7 reshape.44.gain
  1.4 0.8 copy.28.table
  2.2 1.2 copy.29.wq
  3.4 1.1 copy.30.wk
  4.5 1.1 copy.31.wv
  5.7 1.1 copy-done.3
  6.8 0.7 copy-done.7
  7.5 0.7 copy-done.10
  8.1 2.4 %attention.1 = (f32[64,768]{1,0:T(8,128)S(1)}, bf16[64,768]{1,0:T(8,128)(2,1)S(1)}, bf16[64,768]{1,0:T(8,128)(2,1)S(1)}, bf16[64,768]{1,0:T(8,128)(2,1)S(1)}, bf...) custom-call(bf16[256,768]{1,0:T(8,128)(2,1)S(1)} %copy-done, ...), custom_call_target="tpu_custom_call" | custom-call | bytes 3643772 | tf_op jit(solution)/shard_map/attention/pallas_call | solution.py:396
  10.5 3.1 %collective-permute-start = (bf16[64,768]{1,0:T(8,128)(2,1)S(1)}, bf16[64,768]{1,0:T(8,128)(2,1)S(1)}, u32[]{:S(2)}, u32[]{:S(2)}) collective-permute-start(bf16[64,768]{1,0:T(8,128)(2,1)S(1)} %get-tuple-element.72), channel_id=1, source_target_pairs={{0,1},{1,0},{2,3},{3,2},{4,5},{5,4},{6,7},{7,6},{8,9},{9,8},{10,11... | collective-permute-start | bytes 294920 | tf_op jit(solution)/shard_map/ppermute | solution.py:414
  13.6 2.6 %collective-permute-start.1 = (bf16[64,768]{1,0:T(8,128)(2,1)S(1)}, bf16[64,768]{1,0:T(8,128)(2,1)S(1)}, u32[]{:S(2)}, u32[]{:S(2)}) collective-permute-start(bf16[64,768]{1,0:T(8,128)(2,1)S(1)} %get-tuple-element.73), channel_id=1, source_target_pairs={{0,2},{1,3},{2,0},{3,1},{4,6},{5,7},{6,4},{7,5},{8,10},{9,11},{10,... | collective-permute-start | bytes 294920 | tf_op jit(solution)/shard_map/ppermute | solution.py:414
  16.4 7.6 %collective-permute-done.1.rest_2_ = bf16[64,768]{1,0:T(8,128)(2,1)S(1)} collective-permute-done((bf16[64,768]{1,0:T(8,128)(2,1)S(1)}, bf16[64,768]{1,0:T(8,128)(2,1)S(1)}, u32[]{:S(2)}, u32[]{:S(2)}) %collective-permute-start.1) | collective-permute-done | bytes 98336 | tf_op jit(solution)/shard_map/ppermute | solution.py:414
  24.2 2.5 %collective-permute-start.5 = (bf16[64,768]{1,0:T(8,128)(2,1)S(1)}, bf16[64,768]{1,0:T(8,128)(2,1)S(1)}, u32[]{:S(2)}, u32[]{:S(2)}) collective-permute-start(bf16[64,768]{1,0:T(8,128)(2,1)S(1)} %get-tuple-element.76.rest_0_), channel_id=1, source_target_pairs={{0,3},{1,2},{2,1},{3,0},{4,7},{5,6},{6,5},{7,4},{8,11},{9,10},{10,... | collective-permute-start | bytes 294920 | tf_op jit(solution)/shard_map/ppermute | solution.py:414
  27.3 1.3 collective-permute-start.3
  28.7 3.1 %collective-permute-done.5.rest_3_ = bf16[64,768]{1,0:T(8,128)(2,1)S(1)} collective-permute-done((bf16[64,768]{1,0:T(8,128)(2,1)S(1)}, bf16[64,768]{1,0:T(8,128)(2,1)S(1)}, u32[]{:S(2)}, u32[]{:S(2)}) %collective-permute-start.5) | collective-permute-done | bytes 98336 | tf_op jit(solution)/shard_map/ppermute | solution.py:414
  31.8 3.2 %collective-permute-done.4.rest_2_ = bf16[64,768]{1,0:T(8,128)(2,1)S(1)} collective-permute-done((bf16[64,768]{1,0:T(8,128)(2,1)S(1)}, bf16[64,768]{1,0:T(8,128)(2,1)S(1)}, u32[]{:S(2)}, u32[]{:S(2)}) %collective-permute-start.4) | collective-permute-done | bytes 98336 | tf_op jit(solution)/shard_map/ppermute | solution.py:414
  35.0 5.4 %expert.1 = (bf16[64,768]{1,0:T(8,128)(2,1)S(1)}, bf16[64,768]{1,0:T(8,128)(2,1)S(1)}, bf16[64,768]{1,0:T(8,128)(2,1)S(1)}, bf16[64,768]{1,0:T(8,128)(2,1)S(1)},...) custom-call(s32[1,256]{1,0:T(1,128)S(1)} %bitcast.7, ...), custom_call_target="tpu_custom_call" | custom-call | bytes 8071168 | tf_op jit(solution)/shard_map/expert/pallas_call | solution.py:396
  40.4 4.1 %expert_grads.1 = (bf16[4,96,3072]{2,1,0:T(8,128)(2,1)S(1)}, bf16[4,96,3072]{2,1,0:T(8,128)(2,1)}) custom-call(bf16[288,768]{1,0:T(8,128)(2,1)S(1)} %get-tuple-element.118.buffer, bf16[288,768]{1,0:T(8,128)(2,1)S(1)} %get-tuple-element.119.active, bf16[288,768]{1,0:T(8,128)(2,1)S(1)} %get-tuple-element.120.grad_before, ...), custom_call_target="tpu_custom_call" | custom-call | flops 679477248 | bytes 6488064 | tf_op jit(solution)/shard_map/expert_grads/pallas_call | solution.py:396
  44.6 2.0 %collective-permute-start.13 = (bf16[64,768]{1,0:T(8,128)(2,1)S(1)}, bf16[64,768]{1,0:T(8,128)(2,1)S(1)}, u32[]{:S(2)}, u32[]{:S(2)}) collective-permute-start(bf16[64,768]{1,0:T(8,128)(2,1)S(1)} %get-tuple-element.83), channel_id=1, source_target_pairs={{0,2},{1,3},{2,0},{3,1},{4,6},{5,7},{6,4},{7,5},{8,10},{9,11},{10,... | collective-permute-start | bytes 294920 | tf_op jit(solution)/shard_map/ppermute | solution.py:414
  46.5 2.4 %collective-permute-start.14 = (bf16[64,768]{1,0:T(8,128)(2,1)S(1)}, bf16[64,768]{1,0:T(8,128)(2,1)S(1)}, u32[]{:S(2)}, u32[]{:S(2)}) collective-permute-start(bf16[64,768]{1,0:T(8,128)(2,1)S(1)} %get-tuple-element.84), channel_id=1, source_target_pairs={{0,3},{1,2},{2,1},{3,0},{4,7},{5,6},{6,5},{7,4},{8,11},{9,10},{10,... | collective-permute-start | bytes 294920 | tf_op jit(solution)/shard_map/ppermute | solution.py:414
  48.9 2.1 %collective-permute-done.12.rest_1_ = bf16[64,768]{1,0:T(8,128)(2,1)S(1)} collective-permute-done((bf16[64,768]{1,0:T(8,128)(2,1)S(1)}, bf16[64,768]{1,0:T(8,128)(2,1)S(1)}, u32[]{:S(2)}, u32[]{:S(2)}) %collective-permute-start.12) | collective-permute-done | bytes 98336 | tf_op jit(solution)/shard_map/ppermute | solution.py:414
  51.0 4.3 %collective-permute-done.13.rest_2_ = bf16[64,768]{1,0:T(8,128)(2,1)S(1)} collective-permute-done((bf16[64,768]{1,0:T(8,128)(2,1)S(1)}, bf16[64,768]{1,0:T(8,128)(2,1)S(1)}, u32[]{:S(2)}, u32[]{:S(2)}) %collective-permute-start.13) | collective-permute-done | bytes 98336 | tf_op jit(solution)/shard_map/ppermute | solution.py:414
  55.5 1.5 collective-permute-start.17
  57.0 2.3 %collective-permute-start.16 = (bf16[64,768]{1,0:T(8,128)(2,1)S(1)}, bf16[64,768]{1,0:T(8,128)(2,1)S(1)}, u32[]{:S(2)}, u32[]{:S(2)}) collective-permute-start(bf16[64,768]{1,0:T(8,128)(2,1)S(1)} %get-tuple-element.90.rest_0_), channel_id=1, source_target_pairs={{0,2},{1,3},{2,0},{3,1},{4,6},{5,7},{6,4},{7,5},{8,10},{9,11},{10,... | collective-permute-start | bytes 294920 | tf_op jit(solution)/shard_map/ppermute | solution.py:414
  59.3 0.6 collective-permute-start.15
  59.9 3.1 %collective-permute-done.17.rest_3_ = bf16[64,768]{1,0:T(8,128)(2,1)S(1)} collective-permute-done((bf16[64,768]{1,0:T(8,128)(2,1)S(1)}, bf16[64,768]{1,0:T(8,128)(2,1)S(1)}, u32[]{:S(2)}, u32[]{:S(2)}) %collective-permute-start.17) | collective-permute-done | bytes 98336 | tf_op jit(solution)/shard_map/ppermute | solution.py:414
  63.0 4.7 %collective-permute-done.16.rest_2_ = bf16[64,768]{1,0:T(8,128)(2,1)S(1)} collective-permute-done((bf16[64,768]{1,0:T(8,128)(2,1)S(1)}, bf16[64,768]{1,0:T(8,128)(2,1)S(1)}, u32[]{:S(2)}, u32[]{:S(2)}) %collective-permute-start.16) | collective-permute-done | bytes 98336 | tf_op jit(solution)/shard_map/ppermute | solution.py:414
  67.7 1.8 %attention_back.1 = (f32[64,768]{1,0:T(8,128)S(1)}, bf16[64,768]{1,0:T(8,128)(2,1)S(1)}, bf16[64,768]{1,0:T(8,128)(2,1)S(1)}, bf16[64,768]{1,0:T(8,128)(2,1)S(1)...) custom-call(bf16[256,768]{1,0:T(8,128)(2,1)S(1)} %copy-done, ...), custom_call_target="tpu_custom_call" | custom-call | bytes 4623360 | tf_op jit(solution)/shard_map/attention_back/pallas_call | solution.py:396
  69.6 1.7 %weight_grads.1 = (bf16[4,112,768]{2,1,0:T(8,128)(2,1)S(1)}, bf16[4,112,768]{2,1,0:T(8,128)(2,1)S(1)}) custom-call(bf16[256,768]{1,0:T(8,128)(2,1)S(1)} %get-tuple-element.95.normed, bf16[3,256,192]{2,1,0:T(8,128)(2,1)S(1)} %get-tuple-element.96.grads, bf16[256,768]{1,0:T(8,128)(2,1)S(1)} %get-tuple-element.97.attended, ...), custom_call_target="tpu_custom_call" | custom-call | bytes 2963456 | tf_op jit(solution)/shard_map/weight_grads/pallas_call | solution.py:396
  71.4 1.7 %collective-permute-start.7 = (bf16[64,768]{1,0:T(8,128)(2,1)S(1)}, bf16[64,768]{1,0:T(8,128)(2,1)S(1)}, u32[]{:S(2)}, u32[]{:S(2)}) collective-permute-start(bf16[64,768]{1,0:T(8,128)(2,1)S(1)} %get-tuple-element.79), channel_id=1, source_target_pairs={{0,2},{1,3},{2,0},{3,1},{4,6},{5,7},{6,4},{7,5},{8,10},{9,11},{10,... | collective-permute-start | bytes 294920 | tf_op jit(solution)/shard_map/ppermute | solution.py:414
  73.2 2.6 %collective-permute-start.8 = (bf16[64,768]{1,0:T(8,128)(2,1)S(1)}, bf16[64,768]{1,0:T(8,128)(2,1)S(1)}, u32[]{:S(2)}, u32[]{:S(2)}) collective-permute-start(bf16[64,768]{1,0:T(8,128)(2,1)S(1)} %get-tuple-element.80), channel_id=1, source_target_pairs={{0,3},{1,2},{2,1},{3,0},{4,7},{5,6},{6,5},{7,4},{8,11},{9,10},{10,... | collective-permute-start | bytes 294920 | tf_op jit(solution)/shard_map/ppermute | solution.py:414
  75.8 2.0 %collective-permute-done.6.rest_1_ = bf16[64,768]{1,0:T(8,128)(2,1)S(1)} collective-permute-done((bf16[64,768]{1,0:T(8,128)(2,1)S(1)}, bf16[64,768]{1,0:T(8,128)(2,1)S(1)}, u32[]{:S(2)}, u32[]{:S(2)}) %collective-permute-start.6) | collective-permute-done | bytes 98336 | tf_op jit(solution)/shard_map/ppermute | solution.py:414
  77.8 4.4 %collective-permute-done.7.rest_2_ = bf16[64,768]{1,0:T(8,128)(2,1)S(1)} collective-permute-done((bf16[64,768]{1,0:T(8,128)(2,1)S(1)}, bf16[64,768]{1,0:T(8,128)(2,1)S(1)}, u32[]{:S(2)}, u32[]{:S(2)}) %collective-permute-start.7) | collective-permute-done | bytes 98336 | tf_op jit(solution)/shard_map/ppermute | solution.py:414
  82.3 1.4 collective-permute-start.11
  83.8 2.2 %collective-permute-start.10 = (bf16[64,768]{1,0:T(8,128)(2,1)S(1)}, bf16[64,768]{1,0:T(8,128)(2,1)S(1)}, u32[]{:S(2)}, u32[]{:S(2)}) collective-permute-start(bf16[64,768]{1,0:T(8,128)(2,1)S(1)} %output_share.1.refs_0_), channel_id=1, source_target_pairs={{0,2},{1,3},{2,0},{3,1},{4,6},{5,7},{6,4},{7,5},{8,10},{9,11},{10,... | collective-permute-start | bytes 294920 | tf_op jit(solution)/shard_map/ppermute | solution.py:414
  86.0 0.8 collective-permute-start.18
  86.8 3.0 %collective-permute-done.11.refs_3_ = bf16[64,768]{1,0:T(8,128)(2,1)S(1)} collective-permute-done((bf16[64,768]{1,0:T(8,128)(2,1)S(1)}, bf16[64,768]{1,0:T(8,128)(2,1)S(1)}, u32[]{:S(2)}, u32[]{:S(2)}) %collective-permute-start.11) | collective-permute-done | bytes 98336 | tf_op jit(solution)/shard_map/ppermute | solution.py:414
  89.8 3.6 %collective-permute-start.19 = (bf16[64,768]{1,0:T(8,128)(2,1)S(1)}, bf16[64,768]{1,0:T(8,128)(2,1)S(1)}, u32[]{:S(2)}, u32[]{:S(2)}) collective-permute-start(bf16[64,768]{1,0:T(8,128)(2,1)S(1)} %get-tuple-element.93), channel_id=1, source_target_pairs={{0,2},{1,3},{2,0},{3,1},{4,6},{5,7},{6,4},{7,5},{8,10},{9,11},{10,... | collective-permute-start | bytes 294920 | tf_op jit(solution)/shard_map/ppermute | solution.py:414
  93.4 2.3 %collective-permute-start.20 = (bf16[64,768]{1,0:T(8,128)(2,1)S(1)}, bf16[64,768]{1,0:T(8,128)(2,1)S(1)}, u32[]{:S(2)}, u32[]{:S(2)}) collective-permute-start(bf16[64,768]{1,0:T(8,128)(2,1)S(1)} %get-tuple-element.94), channel_id=1, source_target_pairs={{0,3},{1,2},{2,1},{3,0},{4,7},{5,6},{6,5},{7,4},{8,11},{9,10},{10,... | collective-permute-start | bytes 294920 | tf_op jit(solution)/shard_map/ppermute | solution.py:414
  95.8 3.2 %merge.3 = (f32[96,3072]{1,0:T(8,128)S(1)}, bf16[96,3072]{1,0:T(8,128)(2,1)}, bf16[96,3072]{1,0:T(8,128)(2,1)}, bf16[96,3072]{1,0:T(8,128)(2,1)}) custom-call(bf16[4,96,3072]{2,1,0:T(8,128)(2,1)S(1)} %get-tuple-element.122.kept, bf16[4,96,3072]{2,1,0:T(8,128)(2,1)} %copy-done.11), custom_call_target="tpu_custom_call" | custom-call | bytes 7667712 | tf_op jit(solution)/shard_map/merge/pallas_call | solution.py:396
  99.0 1.5 collective-permute-start.32
  100.5 1.5 collective-permute-start.33
  102.0 1.7 %collective-permute-start.34 = (bf16[96,3072]{1,0:T(8,128)(2,1)}, bf16[96,3072]{1,0:T(8,128)(2,1)S(1)}, u32[]{:S(2)}, u32[]{:S(2)}) collective-permute-start(bf16[96,3072]{1,0:T(8,128)(2,1)} %get-tuple-element.127), channel_id=1, source_target_pairs={{0,24},{4,28},{8,16},{12,20},{16,8},{20,12},{24,0},{28,4},{1,25},{... | collective-permute-start | bytes 1769480 | tf_op jit(solution)/shard_map/ppermute | solution.py:414
  103.9 0.6 collective-permute-start.25
  104.6 3.7 %collective-permute-done.9.refs_1_ = bf16[64,768]{1,0:T(8,128)(2,1)S(1)} collective-permute-done((bf16[64,768]{1,0:T(8,128)(2,1)S(1)}, bf16[64,768]{1,0:T(8,128)(2,1)S(1)}, u32[]{:S(2)}, u32[]{:S(2)}) %collective-permute-start.9) | collective-permute-done | bytes 98336 | tf_op jit(solution)/shard_map/ppermute | solution.py:414
  108.3 1.4 collective-permute-start.23
  109.7 5.0 %collective-permute-done.23.refs_3_ = bf16[64,768]{1,0:T(8,128)(2,1)S(1)} collective-permute-done((bf16[64,768]{1,0:T(8,128)(2,1)S(1)}, bf16[64,768]{1,0:T(8,128)(2,1)S(1)}, u32[]{:S(2)}, u32[]{:S(2)}) %collective-permute-start.23) | collective-permute-done | bytes 98336 | tf_op jit(solution)/shard_map/ppermute | solution.py:414
  115.3 13.1 %collective-permute-done.25.refs_1_ = bf16[112,768]{1,0:T(8,128)(2,1)S(1)} collective-permute-done((bf16[112,768]{1,0:T(8,128)(2,1)S(1)}, bf16[112,768]{1,0:T(8,128)(2,1)S(1)}, u32[]{:S(2)}, u32[]{:S(2)}) %collective-permute-start.25) | collective-permute-done | bytes 172064 | tf_op jit(solution)/shard_map/ppermute | solution.py:414
  128.4 3.1 %collective-permute-start.27 = (bf16[112,768]{1,0:T(8,128)(2,1)S(1)}, bf16[112,768]{1,0:T(8,128)(2,1)S(1)}, u32[]{:S(2)}, u32[]{:S(2)}) collective-permute-start(bf16[112,768]{1,0:T(8,128)(2,1)S(1)} %get-tuple-element.108), channel_id=1, source_target_pairs={{0,24},{4,28},{8,16},{12,20},{16,8},{20,12},{24,0},{28,4},{1,25},{... | collective-permute-start | bytes 516104 | tf_op jit(solution)/shard_map/ppermute | solution.py:414
  131.5 3.4 %collective-permute-done.27.refs_3_ = bf16[112,768]{1,0:T(8,128)(2,1)S(1)} collective-permute-done((bf16[112,768]{1,0:T(8,128)(2,1)S(1)}, bf16[112,768]{1,0:T(8,128)(2,1)S(1)}, u32[]{:S(2)}, u32[]{:S(2)}) %collective-permute-start.27) | collective-permute-done | bytes 172064 | tf_op jit(solution)/shard_map/ppermute | solution.py:414
  134.9 1.0 weight_final.1
  135.9 2.6 %collective-permute-done.22.refs_2_ = bf16[64,768]{1,0:T(8,128)(2,1)S(1)} collective-permute-done((bf16[64,768]{1,0:T(8,128)(2,1)S(1)}, bf16[64,768]{1,0:T(8,128)(2,1)S(1)}, u32[]{:S(2)}, u32[]{:S(2)}) %collective-permute-start.22) | collective-permute-done | bytes 98336 | tf_op jit(solution)/shard_map/ppermute | solution.py:414
  138.5 2.3 %collective-permute-start.30 = (f32[16,768]{1,0:T(8,128)S(1)}, f32[16,768]{1,0:T(8,128)S(1)}, u32[]{:S(2)}, u32[]{:S(2)}) collective-permute-start(f32[16,768]{1,0:T(8,128)S(1)} %get-tuple-element.109.refs_0_), channel_id=1, source_target_pairs={{0,3},{1,2},{2,1},{3,0},{4,7},{5,6},{6,5},{7,4},{8,11},{9,10},{10,... | collective-permute-start | bytes 147464 | tf_op jit(solution)/shard_map/ppermute | solution.py:414
  140.8 3.6 %collective-permute-done.30.refs_3_ = f32[16,768]{1,0:T(8,128)S(1)} collective-permute-done((f32[16,768]{1,0:T(8,128)S(1)}, f32[16,768]{1,0:T(8,128)S(1)}, u32[]{:S(2)}, u32[]{:S(2)}) %collective-permute-start.30) | collective-permute-done | bytes 49184 | tf_op jit(solution)/shard_map/ppermute | solution.py:414
  144.4 0.8 output_rows.1
  145.2 0.8 grad_rows.1
  145.9 0.7 copy.35
  146.6 1.9 %collective-permute-done.28.refs_1_ = f32[16,768]{1,0:T(8,128)S(1)} collective-permute-done((f32[16,768]{1,0:T(8,128)S(1)}, f32[16,768]{1,0:T(8,128)S(1)}, u32[]{:S(2)}, u32[]{:S(2)}) %collective-permute-start.28) | collective-permute-done | bytes 49184 | tf_op jit(solution)/shard_map/ppermute | solution.py:414
  148.5 0.8 small_final.1
  149.3 0.6 copy.36
  149.9 0.8 copy-done.5
  150.7 1.1 copy-done.6
  151.8 1.2 expert_final.1
  153.0 1.1 copy.37
  (63 shorter events, 2.3 us)
Async XLA Ops:
  0.6 5.0 %copy-start = (bf16[256,768]{1,0:T(8,128)(2,1)S(1)}, bf16[256,768]{1,0:T(8,128)(2,1)}, u32[]{:S(2)}) copy-start(bf16[256,768]{1,0:T(8,128)(2,1)} %inputs.7) | copy-start | bytes 1179652
  0.7 15.6 %copy-start.12 = (f32[768]{0:T(1024)S(1)}, f32[768]{0:T(1024)}, u32[]{:S(2)}) copy-start(f32[768]{0:T(1024)} %param.27) | copy-start | bytes 9220
  2.2 26.5 %copy-start.13 = (s32[256]{0:T(256)S(1)}, s32[256]{0:T(256)}, u32[]{:S(2)}) copy-start(s32[256]{0:T(256)} %param.20) | copy-start | bytes 3076
  2.2 26.5 %copy-start.14 = (s32[256]{0:T(256)S(1)}, s32[256]{0:T(256)}, u32[]{:S(2)}) copy-start(s32[256]{0:T(256)} %param.19) | copy-start | bytes 3076
  2.2 32.8 %copy-start.2 = (bf16[256,768]{1,0:T(8,128)(2,1)S(1)}, bf16[256,768]{1,0:T(8,128)(2,1)}, u32[]{:S(2)}) copy-start(bf16[256,768]{1,0:T(8,128)(2,1)} %cotangent.3) | copy-start | bytes 1179652
  2.2 32.8 %copy-start.9 = (bf16[768,2]{0,1:T(2,128)(2,1)S(1)}, bf16[768,2]{0,1:T(2,128)(2,1)}, u32[]{:S(2)}) copy-start(bf16[768,2]{0,1:T(2,128)(2,1)} %param.28) | copy-start | bytes 9220
  5.6 29.4 %copy-start.1 = (bf16[2,768,768]{2,1,0:T(8,128)(2,1)S(1)}, bf16[2,768,768]{2,1,0:T(8,128)(2,1)}, u32[]{:S(2)}) copy-start(bf16[2,768,768]{2,1,0:T(8,128)(2,1)} %up.1) | copy-start | bytes 7077892
  5.7 1.1 copy-start.3
  6.8 0.7 copy-start.7
  7.5 0.7 copy-start.10
  10.5 5.9 %collective-permute-start = (bf16[64,768]{1,0:T(8,128)(2,1)S(1)}, bf16[64,768]{1,0:T(8,128)(2,1)S(1)}, u32[]{:S(2)}, u32[]{:S(2)}) collective-permute-start(bf16[64,768]{1,0:T(8,128)(2,1)S(1)} %get-tuple-element.72), channel_id=1, source_target_pairs={{0,1},{1,0},{2,3},{3,2},{4,5},{5,4},{6,7},{7,6},{8,9},{9,8},{10,11... | collective-permute-start | bytes 294920 | tf_op jit(solution)/shard_map/ppermute | solution.py:414
  13.6 10.4 %collective-permute-start.1 = (bf16[64,768]{1,0:T(8,128)(2,1)S(1)}, bf16[64,768]{1,0:T(8,128)(2,1)S(1)}, u32[]{:S(2)}, u32[]{:S(2)}) collective-permute-start(bf16[64,768]{1,0:T(8,128)(2,1)S(1)} %get-tuple-element.73), channel_id=1, source_target_pairs={{0,2},{1,3},{2,0},{3,1},{4,6},{5,7},{6,4},{7,5},{8,10},{9,11},{10,... | collective-permute-start | bytes 294920 | tf_op jit(solution)/shard_map/ppermute | solution.py:414
  16.2 7.8 %collective-permute-start.2 = (bf16[64,768]{1,0:T(8,128)(2,1)S(1)}, bf16[64,768]{1,0:T(8,128)(2,1)S(1)}, u32[]{:S(2)}, u32[]{:S(2)}) collective-permute-start(bf16[64,768]{1,0:T(8,128)(2,1)S(1)} %get-tuple-element.74), channel_id=1, source_target_pairs={{0,3},{1,2},{2,1},{3,0},{4,7},{5,6},{6,5},{7,4},{8,11},{9,10},{10,... | collective-permute-start | bytes 294920 | tf_op jit(solution)/shard_map/ppermute | solution.py:414
  24.2 7.6 %collective-permute-start.5 = (bf16[64,768]{1,0:T(8,128)(2,1)S(1)}, bf16[64,768]{1,0:T(8,128)(2,1)S(1)}, u32[]{:S(2)}, u32[]{:S(2)}) collective-permute-start(bf16[64,768]{1,0:T(8,128)(2,1)S(1)} %get-tuple-element.76.rest_0_), channel_id=1, source_target_pairs={{0,3},{1,2},{2,1},{3,0},{4,7},{5,6},{6,5},{7,4},{8,11},{9,10},{10,... | collective-permute-start | bytes 294920 | tf_op jit(solution)/shard_map/ppermute | solution.py:414
  26.7 8.3 %collective-permute-start.4 = (bf16[64,768]{1,0:T(8,128)(2,1)S(1)}, bf16[64,768]{1,0:T(8,128)(2,1)S(1)}, u32[]{:S(2)}, u32[]{:S(2)}) collective-permute-start(bf16[64,768]{1,0:T(8,128)(2,1)S(1)} %get-tuple-element.76.rest_0_), channel_id=1, source_target_pairs={{0,2},{1,3},{2,0},{3,1},{4,6},{5,7},{6,4},{7,5},{8,10},{9,11},{10,... | collective-permute-start | bytes 294920 | tf_op jit(solution)/shard_map/ppermute | solution.py:414
  27.3 7.7 %collective-permute-start.3 = (bf16[64,768]{1,0:T(8,128)(2,1)S(1)}, bf16[64,768]{1,0:T(8,128)(2,1)S(1)}, u32[]{:S(2)}, u32[]{:S(2)}) collective-permute-start(bf16[64,768]{1,0:T(8,128)(2,1)S(1)} %get-tuple-element.76.rest_0_), channel_id=1, source_target_pairs={{0,1},{1,0},{2,3},{3,2},{4,5},{5,4},{6,7},{7,6},{8,9},{9,8},{10,11... | collective-permute-start | bytes 294920 | tf_op jit(solution)/shard_map/ppermute | solution.py:414
  40.4 19.5 %copy-start.8 = (s32[511]{0:T(512)S(1)}, s32[511]{0:T(512)}, u32[]{:S(2)}) copy-start(s32[511]{0:T(512)} %param.18) | copy-start | bytes 6136
  40.4 27.3 %copy-start.4 = (bf16[192,768]{1,0:T(8,128)(2,1)S(1)}, bf16[192,768]{1,0:T(8,128)(2,1)}, u32[]{:S(2)}) copy-start(bf16[192,768]{1,0:T(8,128)(2,1)} %wo.3) | copy-start | bytes 884740
  44.5 48.8 %collective-permute-start.31 = (bf16[4,96,3072]{2,1,0:T(8,128)(2,1)}, bf16[4,96,3072]{2,1,0:T(8,128)(2,1)S(1)}, u32[]{:S(2)}, u32[]{:S(2)}) collective-permute-start(bf16[4,96,3072]{2,1,0:T(8,128)(2,1)} %get-tuple-element.123), channel_id=1, source_target_pairs={{0,4},{4,0},{8,12},{12,8},{16,20},{20,16},{24,28},{28,24},{1,5},{5... | collective-permute-start | bytes 7077896 | tf_op jit(solution)/shard_map/ppermute | solution.py:414
  44.6 6.4 %collective-permute-start.12 = (bf16[64,768]{1,0:T(8,128)(2,1)S(1)}, bf16[64,768]{1,0:T(8,128)(2,1)S(1)}, u32[]{:S(2)}, u32[]{:S(2)}) collective-permute-start(bf16[64,768]{1,0:T(8,128)(2,1)S(1)} %get-tuple-element.82), channel_id=1, source_target_pairs={{0,1},{1,0},{2,3},{3,2},{4,5},{5,4},{6,7},{7,6},{8,9},{9,8},{10,11... | collective-permute-start | bytes 294920 | tf_op jit(solution)/shard_map/ppermute | solution.py:414
  44.6 10.8 %collective-permute-start.13 = (bf16[64,768]{1,0:T(8,128)(2,1)S(1)}, bf16[64,768]{1,0:T(8,128)(2,1)S(1)}, u32[]{:S(2)}, u32[]{:S(2)}) collective-permute-start(bf16[64,768]{1,0:T(8,128)(2,1)S(1)} %get-tuple-element.83), channel_id=1, source_target_pairs={{0,2},{1,3},{2,0},{3,1},{4,6},{5,7},{6,4},{7,5},{8,10},{9,11},{10,... | collective-permute-start | bytes 294920 | tf_op jit(solution)/shard_map/ppermute | solution.py:414
  46.5 8.8 %collective-permute-start.14 = (bf16[64,768]{1,0:T(8,128)(2,1)S(1)}, bf16[64,768]{1,0:T(8,128)(2,1)S(1)}, u32[]{:S(2)}, u32[]{:S(2)}) collective-permute-start(bf16[64,768]{1,0:T(8,128)(2,1)S(1)} %get-tuple-element.84), channel_id=1, source_target_pairs={{0,3},{1,2},{2,1},{3,0},{4,7},{5,6},{6,5},{7,4},{8,11},{9,10},{10,... | collective-permute-start | bytes 294920 | tf_op jit(solution)/shard_map/ppermute | solution.py:414
  55.5 7.6 %collective-permute-start.17 = (bf16[64,768]{1,0:T(8,128)(2,1)S(1)}, bf16[64,768]{1,0:T(8,128)(2,1)S(1)}, u32[]{:S(2)}, u32[]{:S(2)}) collective-permute-start(bf16[64,768]{1,0:T(8,128)(2,1)S(1)} %get-tuple-element.90.rest_0_), channel_id=1, source_target_pairs={{0,3},{1,2},{2,1},{3,0},{4,7},{5,6},{6,5},{7,4},{8,11},{9,10},{10,... | collective-permute-start | bytes 294920 | tf_op jit(solution)/shard_map/ppermute | solution.py:414
  57.0 10.7 %collective-permute-start.16 = (bf16[64,768]{1,0:T(8,128)(2,1)S(1)}, bf16[64,768]{1,0:T(8,128)(2,1)S(1)}, u32[]{:S(2)}, u32[]{:S(2)}) collective-permute-start(bf16[64,768]{1,0:T(8,128)(2,1)S(1)} %get-tuple-element.90.rest_0_), channel_id=1, source_target_pairs={{0,2},{1,3},{2,0},{3,1},{4,6},{5,7},{6,4},{7,5},{8,10},{9,11},{10,... | collective-permute-start | bytes 294920 | tf_op jit(solution)/shard_map/ppermute | solution.py:414
  59.3 8.4 %collective-permute-start.15 = (bf16[64,768]{1,0:T(8,128)(2,1)S(1)}, bf16[64,768]{1,0:T(8,128)(2,1)S(1)}, u32[]{:S(2)}, u32[]{:S(2)}) collective-permute-start(bf16[64,768]{1,0:T(8,128)(2,1)S(1)} %get-tuple-element.90.rest_0_), channel_id=1, source_target_pairs={{0,1},{1,0},{2,3},{3,2},{4,5},{5,4},{6,7},{7,6},{8,9},{9,8},{10,11... | collective-permute-start | bytes 294920 | tf_op jit(solution)/shard_map/ppermute | solution.py:414
  71.3 32.4 %collective-permute-start.24 = (bf16[4,112,768]{2,1,0:T(8,128)(2,1)S(1)}, bf16[4,112,768]{2,1,0:T(8,128)(2,1)S(1)}, u32[]{:S(2)}, u32[]{:S(2)}) collective-permute-start(bf16[4,112,768]{2,1,0:T(8,128)(2,1)S(1)} %get-tuple-element.104), channel_id=1, source_target_pairs={{0,4},{4,0},{8,12},{12,8},{16,20},{20,16},{24,28},{28,24},{1,5},{5... | collective-permute-start | bytes 2064392 | tf_op jit(solution)/shard_map/ppermute | solution.py:414
  71.4 6.5 %collective-permute-start.6 = (bf16[64,768]{1,0:T(8,128)(2,1)S(1)}, bf16[64,768]{1,0:T(8,128)(2,1)S(1)}, u32[]{:S(2)}, u32[]{:S(2)}) collective-permute-start(bf16[64,768]{1,0:T(8,128)(2,1)S(1)} %get-tuple-element.78), channel_id=1, source_target_pairs={{0,1},{1,0},{2,3},{3,2},{4,5},{5,4},{6,7},{7,6},{8,9},{9,8},{10,11... | collective-permute-start | bytes 294920 | tf_op jit(solution)/shard_map/ppermute | solution.py:414
  71.4 10.8 %collective-permute-start.7 = (bf16[64,768]{1,0:T(8,128)(2,1)S(1)}, bf16[64,768]{1,0:T(8,128)(2,1)S(1)}, u32[]{:S(2)}, u32[]{:S(2)}) collective-permute-start(bf16[64,768]{1,0:T(8,128)(2,1)S(1)} %get-tuple-element.79), channel_id=1, source_target_pairs={{0,2},{1,3},{2,0},{3,1},{4,6},{5,7},{6,4},{7,5},{8,10},{9,11},{10,... | collective-permute-start | bytes 294920 | tf_op jit(solution)/shard_map/ppermute | solution.py:414
  73.2 9.1 %collective-permute-start.8 = (bf16[64,768]{1,0:T(8,128)(2,1)S(1)}, bf16[64,768]{1,0:T(8,128)(2,1)S(1)}, u32[]{:S(2)}, u32[]{:S(2)}) collective-permute-start(bf16[64,768]{1,0:T(8,128)(2,1)S(1)} %get-tuple-element.80), channel_id=1, source_target_pairs={{0,3},{1,2},{2,1},{3,0},{4,7},{5,6},{6,5},{7,4},{8,11},{9,10},{10,... | collective-permute-start | bytes 294920 | tf_op jit(solution)/shard_map/ppermute | solution.py:414
  82.3 7.5 %collective-permute-start.11 = (bf16[64,768]{1,0:T(8,128)(2,1)S(1)}, bf16[64,768]{1,0:T(8,128)(2,1)S(1)}, u32[]{:S(2)}, u32[]{:S(2)}) collective-permute-start(bf16[64,768]{1,0:T(8,128)(2,1)S(1)} %output_share.1.refs_0_), channel_id=1, source_target_pairs={{0,3},{1,2},{2,1},{3,0},{4,7},{5,6},{6,5},{7,4},{8,11},{9,10},{10,... | collective-permute-start | bytes 294920 | tf_op jit(solution)/shard_map/ppermute | solution.py:414
  83.8 15.2 %collective-permute-start.10 = (bf16[64,768]{1,0:T(8,128)(2,1)S(1)}, bf16[64,768]{1,0:T(8,128)(2,1)S(1)}, u32[]{:S(2)}, u32[]{:S(2)}) collective-permute-start(bf16[64,768]{1,0:T(8,128)(2,1)S(1)} %output_share.1.refs_0_), channel_id=1, source_target_pairs={{0,2},{1,3},{2,0},{3,1},{4,6},{5,7},{6,4},{7,5},{8,10},{9,11},{10,... | collective-permute-start | bytes 294920 | tf_op jit(solution)/shard_map/ppermute | solution.py:414
  86.0 14.5 %collective-permute-start.18 = (bf16[64,768]{1,0:T(8,128)(2,1)S(1)}, bf16[64,768]{1,0:T(8,128)(2,1)S(1)}, u32[]{:S(2)}, u32[]{:S(2)}) collective-permute-start(bf16[64,768]{1,0:T(8,128)(2,1)S(1)} %get-tuple-element.92), channel_id=1, source_target_pairs={{0,1},{1,0},{2,3},{3,2},{4,5},{5,4},{6,7},{7,6},{8,9},{9,8},{10,11... | collective-permute-start | bytes 294920 | tf_op jit(solution)/shard_map/ppermute | solution.py:414
  89.8 12.1 %collective-permute-start.19 = (bf16[64,768]{1,0:T(8,128)(2,1)S(1)}, bf16[64,768]{1,0:T(8,128)(2,1)S(1)}, u32[]{:S(2)}, u32[]{:S(2)}) collective-permute-start(bf16[64,768]{1,0:T(8,128)(2,1)S(1)} %get-tuple-element.93), channel_id=1, source_target_pairs={{0,2},{1,3},{2,0},{3,1},{4,6},{5,7},{6,4},{7,5},{8,10},{9,11},{10,... | collective-permute-start | bytes 294920 | tf_op jit(solution)/shard_map/ppermute | solution.py:414
  93.4 2.4 %copy-start.11 = (bf16[4,96,3072]{2,1,0:T(8,128)(2,1)}, bf16[4,96,3072]{2,1,0:T(8,128)(2,1)S(1)}, u32[]{:S(2)}) copy-start(bf16[4,96,3072]{2,1,0:T(8,128)(2,1)S(1)} %collective-permute-done.31.came) | copy-start | bytes 7077892
  93.4 10.5 %collective-permute-start.20 = (bf16[64,768]{1,0:T(8,128)(2,1)S(1)}, bf16[64,768]{1,0:T(8,128)(2,1)S(1)}, u32[]{:S(2)}, u32[]{:S(2)}) collective-permute-start(bf16[64,768]{1,0:T(8,128)(2,1)S(1)} %get-tuple-element.94), channel_id=1, source_target_pairs={{0,3},{1,2},{2,1},{3,0},{4,7},{5,6},{6,5},{7,4},{8,11},{9,10},{10,... | collective-permute-start | bytes 294920 | tf_op jit(solution)/shard_map/ppermute | solution.py:414
  99.0 51.0 %collective-permute-start.32 = (bf16[96,3072]{1,0:T(8,128)(2,1)}, bf16[96,3072]{1,0:T(8,128)(2,1)S(1)}, u32[]{:S(2)}, u32[]{:S(2)}) collective-permute-start(bf16[96,3072]{1,0:T(8,128)(2,1)} %get-tuple-element.125), channel_id=1, source_target_pairs={{0,8},{4,12},{8,0},{12,4},{16,24},{20,28},{24,16},{28,20},{1,9},{5... | collective-permute-start | bytes 1769480 | tf_op jit(solution)/shard_map/ppermute | solution.py:414
  100.5 49.4 %collective-permute-start.33 = (bf16[96,3072]{1,0:T(8,128)(2,1)}, bf16[96,3072]{1,0:T(8,128)(2,1)S(1)}, u32[]{:S(2)}, u32[]{:S(2)}) collective-permute-start(bf16[96,3072]{1,0:T(8,128)(2,1)} %get-tuple-element.126), channel_id=1, source_target_pairs={{0,16},{4,20},{8,24},{12,28},{16,0},{20,4},{24,8},{28,12},{1,17},{... | collective-permute-start | bytes 1769480 | tf_op jit(solution)/shard_map/ppermute | solution.py:414
  102.0 47.9 %collective-permute-start.34 = (bf16[96,3072]{1,0:T(8,128)(2,1)}, bf16[96,3072]{1,0:T(8,128)(2,1)S(1)}, u32[]{:S(2)}, u32[]{:S(2)}) collective-permute-start(bf16[96,3072]{1,0:T(8,128)(2,1)} %get-tuple-element.127), channel_id=1, source_target_pairs={{0,24},{4,28},{8,16},{12,20},{16,8},{20,12},{24,0},{28,4},{1,25},{... | collective-permute-start | bytes 1769480 | tf_op jit(solution)/shard_map/ppermute | solution.py:414
  103.7 4.6 %collective-permute-start.9 = (bf16[64,768]{1,0:T(8,128)(2,1)S(1)}, bf16[64,768]{1,0:T(8,128)(2,1)S(1)}, u32[]{:S(2)}, u32[]{:S(2)}) collective-permute-start(bf16[64,768]{1,0:T(8,128)(2,1)S(1)} %output_share.1.refs_0_), channel_id=1, source_target_pairs={{0,1},{1,0},{2,3},{3,2},{4,5},{5,4},{6,7},{7,6},{8,9},{9,8},{10,11... | collective-permute-start | bytes 294920 | tf_op jit(solution)/shard_map/ppermute | solution.py:414
  103.9 24.5 %collective-permute-start.25 = (bf16[112,768]{1,0:T(8,128)(2,1)S(1)}, bf16[112,768]{1,0:T(8,128)(2,1)S(1)}, u32[]{:S(2)}, u32[]{:S(2)}) collective-permute-start(bf16[112,768]{1,0:T(8,128)(2,1)S(1)} %get-tuple-element.106), channel_id=1, source_target_pairs={{0,8},{4,12},{8,0},{12,4},{16,24},{20,28},{24,16},{28,20},{1,9},{5... | collective-permute-start | bytes 516104 | tf_op jit(solution)/shard_map/ppermute | solution.py:414
  108.3 6.4 %collective-permute-start.23 = (bf16[64,768]{1,0:T(8,128)(2,1)S(1)}, bf16[64,768]{1,0:T(8,128)(2,1)S(1)}, u32[]{:S(2)}, u32[]{:S(2)}) collective-permute-start(bf16[64,768]{1,0:T(8,128)(2,1)S(1)} %input_back.1.refs_0_), channel_id=1, source_target_pairs={{0,3},{1,2},{2,1},{3,0},{4,7},{5,6},{6,5},{7,4},{8,11},{9,10},{10,... | collective-permute-start | bytes 294920 | tf_op jit(solution)/shard_map/ppermute | solution.py:414
  114.7 16.8 %collective-permute-start.26 = (bf16[112,768]{1,0:T(8,128)(2,1)S(1)}, bf16[112,768]{1,0:T(8,128)(2,1)S(1)}, u32[]{:S(2)}, u32[]{:S(2)}) collective-permute-start(bf16[112,768]{1,0:T(8,128)(2,1)S(1)} %get-tuple-element.107), channel_id=1, source_target_pairs={{0,16},{4,20},{8,24},{12,28},{16,0},{20,4},{24,8},{28,12},{1,17},{... | collective-permute-start | bytes 516104 | tf_op jit(solution)/shard_map/ppermute | solution.py:414
  128.4 6.5 %collective-permute-start.27 = (bf16[112,768]{1,0:T(8,128)(2,1)S(1)}, bf16[112,768]{1,0:T(8,128)(2,1)S(1)}, u32[]{:S(2)}, u32[]{:S(2)}) collective-permute-start(bf16[112,768]{1,0:T(8,128)(2,1)S(1)} %get-tuple-element.108), channel_id=1, source_target_pairs={{0,24},{4,28},{8,16},{12,20},{16,8},{20,12},{24,0},{28,4},{1,25},{... | collective-permute-start | bytes 516104 | tf_op jit(solution)/shard_map/ppermute | solution.py:414
  131.5 7.0 %collective-permute-start.22 = (bf16[64,768]{1,0:T(8,128)(2,1)S(1)}, bf16[64,768]{1,0:T(8,128)(2,1)S(1)}, u32[]{:S(2)}, u32[]{:S(2)}) collective-permute-start(bf16[64,768]{1,0:T(8,128)(2,1)S(1)} %input_back.1.refs_0_), channel_id=1, source_target_pairs={{0,2},{1,3},{2,0},{3,1},{4,6},{5,7},{6,4},{7,5},{8,10},{9,11},{10,... | collective-permute-start | bytes 294920 | tf_op jit(solution)/shard_map/ppermute | solution.py:414
  134.9 5.9 %collective-permute-start.21 = (bf16[64,768]{1,0:T(8,128)(2,1)S(1)}, bf16[64,768]{1,0:T(8,128)(2,1)S(1)}, u32[]{:S(2)}, u32[]{:S(2)}) collective-permute-start(bf16[64,768]{1,0:T(8,128)(2,1)S(1)} %input_back.1.refs_0_), channel_id=1, source_target_pairs={{0,1},{1,0},{2,3},{3,2},{4,5},{5,4},{6,7},{7,6},{8,9},{9,8},{10,11... | collective-permute-start | bytes 294920 | tf_op jit(solution)/shard_map/ppermute | solution.py:414
  138.5 5.9 %collective-permute-start.30 = (f32[16,768]{1,0:T(8,128)S(1)}, f32[16,768]{1,0:T(8,128)S(1)}, u32[]{:S(2)}, u32[]{:S(2)}) collective-permute-start(f32[16,768]{1,0:T(8,128)S(1)} %get-tuple-element.109.refs_0_), channel_id=1, source_target_pairs={{0,3},{1,2},{2,1},{3,0},{4,7},{5,6},{6,5},{7,4},{8,11},{9,10},{10,... | collective-permute-start | bytes 147464 | tf_op jit(solution)/shard_map/ppermute | solution.py:414
  140.8 5.8 %collective-permute-start.29 = (f32[16,768]{1,0:T(8,128)S(1)}, f32[16,768]{1,0:T(8,128)S(1)}, u32[]{:S(2)}, u32[]{:S(2)}) collective-permute-start(f32[16,768]{1,0:T(8,128)S(1)} %get-tuple-element.109.refs_0_), channel_id=1, source_target_pairs={{0,2},{1,3},{2,0},{3,1},{4,6},{5,7},{6,4},{7,5},{8,10},{9,11},{10,... | collective-permute-start | bytes 147464 | tf_op jit(solution)/shard_map/ppermute | solution.py:414
  144.4 4.1 %collective-permute-start.28 = (f32[16,768]{1,0:T(8,128)S(1)}, f32[16,768]{1,0:T(8,128)S(1)}, u32[]{:S(2)}, u32[]{:S(2)}) collective-permute-start(f32[16,768]{1,0:T(8,128)S(1)} %get-tuple-element.109.refs_0_), channel_id=1, source_target_pairs={{0,1},{1,0},{2,3},{3,2},{4,5},{5,4},{6,7},{7,6},{8,9},{9,8},{10,11... | collective-permute-start | bytes 147464 | tf_op jit(solution)/shard_map/ppermute | solution.py:414
  149.9 0.8 copy-start.5
  150.7 1.1 copy-start.6

commit v2 on v1

--- a/solution.py
+++ b/solution.py
@@ -12,6 +12,18 @@
 CAP = 144
 EPS = 1e-06
 SMALL_ROWS = 16
+TABLE_ROW = 2 + EXPERTS
+WEIGHTS = {
+    "expert": 5,
+    "expert_grads": 400,
+    "hidden_back": 1000,
+    "expert_merge": 400,
+    "attention_back": 1000,
+    "weight_grads": 12,
+    "input_back": 1000,
+    "expert_final": 1,
+    "weight_final": 1,
+}
 BF16 = jnp.bfloat16
 F32 = jnp.float32
 HIGHEST = lax.Precision.HIGHEST
@@ -85,30 +97,41 @@
     ).astype(F32)
 
 
-def attention_kernel(members, inputs, segment, buckets, gain, table, wq, wk, wv, wo, *rest):
-    outs = rest[: members + 6]
+def attention_kernel(members, *refs):
+    sources, outs = refs[:9], refs[9 : members + 15]
     normed_o, q_o, k_o, v_o, probs_o, mixed_o = outs[members:]
-    acc, offset_rows = rest[members + 6 :]
+    acc, offset_rows = refs[members + 15 : members + 17]
+    local, sems = refs[members + 17 : members + 26], refs[members + 26]
+    copies = [
+        pltpu.make_async_copy(source, held, sems.at[i])
+        for i, (source, held) in enumerate(zip(sources, local))
+    ]
+    for copy in copies:
+        copy.start()
+    inputs, gain, wq, wk, wv, buckets, table, segment, wo = local
     length = inputs.shape[0]
-    heads = wq.shape[1] // HEAD_DIM
+    heads = wq.shape[0] // HEAD_DIM
+    copies[0].wait()
     x = inputs[...].astype(F32)
-    normed = (x * inverse_rms(x) * gain[...]).astype(BF16)
+    scaled = x * inverse_rms(x)
+    for copy in copies[1:8]:
+        copy.wait()
+    normed = (scaled * gain[...].reshape(1, -1)).astype(BF16)
     normed_o[...] = normed
-    q = dot(normed, wq[...]).astype(BF16)
-    k = dot(normed, wk[...]).astype(BF16)
-    v = dot(normed, wv[...]).astype(BF16)
+    q = dot_nt(normed, wq[...]).astype(BF16)
+    k = dot_nt(normed, wk[...]).astype(BF16)
+    v = dot_nt(normed, wv[...]).astype(BF16)
     q_o[...] = q
     k_o[...] = k
     v_o[...] = v
-    hot = bucket_hot_of(buckets, table.shape[0])
+    hot = bucket_hot_of(buckets, table.shape[1])
     seg_row = segment[...].astype(F32)
     same = column_of(seg_row, length) == seg_row
-    mixed = jnp.zeros((length, wq.shape[1]), F32)
+    mixed = jnp.zeros((length, wq.shape[0]), F32)
     offset_rows[...] = jnp.zeros_like(offset_rows)
-    for h in range(heads):
-        offset_rows[h : h + 1, 0 : hot.shape[1]] = jnp.sum(
-            hot * table[:, h : h + 1], axis=0, keepdims=True
-        )
+    offset_rows[0:heads, 0 : hot.shape[1]] = jnp.dot(
+        table[...], hot, preferred_element_type=F32, precision=HIGHEST
+    )
     for h in range(heads):
         spread = jnp.broadcast_to(offset_rows[h : h + 1, :], (length, 2 * length))
         bias = pltpu.roll(spread, length + 1, 1, stride=1, stride_axis=0)[:, :length]
@@ -120,6 +143,7 @@
         mixed = mixed + dot(probs.astype(BF16), masked(v, h))
     mixed = mixed.astype(BF16)
     mixed_o[...] = mixed
+    copies[8].wait()
     acc[...] = dot(mixed, wo[...])
     put_shares(acc, outs[:members])
 
@@ -137,9 +161,9 @@
 def expert_kernel(members, where_to, cotangent, router_t, up, down, *rest):
     pieces = rest[:members]
     rest = rest[members:]
-    back_o, row_o = rest[:members], rest[members : 2 * members]
-    buffer_o, active_o, grad_before_o, grad_expert_o, router_o = rest[2 * members : 2 * members + 5]
-    normed, backs, rows, acc = rest[2 * members + 5 :]
+    back_o, row_o = rest[:members], rest[members : members + 2]
+    buffer_o, active_o, grad_before_o, grad_expert_o, router_o = rest[members + 2 : members + 7]
+    normed, backs, rows, acc = rest[members + 7 :]
     length = cotangent.shape[0]
     assemble(normed, pieces)
     place = (
@@ -186,7 +210,12 @@
     acc[...] = dot_tn(place, backs[...])
     put_shares(acc, back_o)
     acc[...] = dot_tn(place, rows[...])
-    put_shares(acc, row_o)
+    me = lax.axis_index("tensor")
+    share = back_o[0].shape[0]
+    for first, ref in enumerate(row_o):
+        for k in range(2):
+            index = jnp.bitwise_xor(me, first + 2 * k)
+            ref[k * share : (k + 1) * share, :] = acc[share_of(index, share), :].astype(BF16)
 
 
 def split_rows(keep, send, chip, part):
@@ -218,27 +247,68 @@
                 send[chip, :, first : first + hidden_units] = scratch[other, :].astype(BF16)
 
 
-def merge_kernel(kept, came, *outs):
-    chips = kept.shape[0]
+def chip_bits():
+    core = lax.rem(lax.axis_index("dp"), 2)
+    return 1 + core, 2 - core
+
+
+def merge_kernel(kept, came, keep, send):
     chip = lax.div(lax.axis_index("dp"), 2)
-    for k in range(chips):
-        there = jnp.bitwise_xor(chip, k)
-        total = kept[there].astype(F32) + came[there].astype(F32)
-        outs[k][...] = total.astype(outs[k].dtype)
-
-
-def expert_final_kernel(chips, *refs):
-    up_o, down_o = refs[chips:]
-    total = total_of(refs[:chips])
+    first, second = chip_bits()
+    for ref, start in ((keep, chip), (send, jnp.bitwise_xor(chip, first))):
+        for k, there in enumerate((start, jnp.bitwise_xor(start, second))):
+            total = kept[there].astype(F32) + came[there].astype(F32)
+            ref[k] = total.astype(ref.dtype)
+
+
+def merge_small_kernel(kept, came, small, small_came, keep, send):
+    merge_kernel(kept, came, keep, send)
+    total = small[...] + small_came[...]
+    first = kept.shape[1] - SMALL_ROWS
+    rows = slice(first, first + TABLE_ROW)
+    for ref in (keep, send):
+        for k in range(2):
+            ref[k, rows, 0 : total.shape[1]] = total[0:TABLE_ROW].astype(ref.dtype)
+
+
+def merge_two_kernel(kept, came, keep, send):
+    keep[...] = kept[0] + came[0].astype(F32)
+    send[...] = (kept[1] + came[1].astype(F32)).astype(BF16)
+
+
+def expert_final_kernel(*refs):
+    up_o, down_o = refs[2:]
+    total = total_of(refs[:2])
     for e in range(EXPERTS):
         width = up_o.shape[2]
         first = 2 * e * width
         up_o[e] = total[:, first : first + width]
-        down_o[e] = total[:, first + width : first + 2 * width].T
-
-
-def output_kernel(members, hidden, *rest):
-    rest[-1][...] = (hidden[...] + total_of(rest[:members])).astype(BF16)
+        down_o[e] = total[:, first + width : first + 2 * width]
+
+
+def pair_sum_kernel(kept, came, own, other):
+    share = own.shape[0]
+    own[...] = kept[0:share, :].astype(F32) + came[0:share, :].astype(F32)
+    other[...] = (kept[share:, :].astype(F32) + came[share:, :].astype(F32)).astype(BF16)
+
+
+def output_kernel(hidden, own, came, out):
+    out[...] = (hidden[...] + own[...] + came[...].astype(F32)).astype(BF16)
+
+
+def pair_kernel(own, came, out):
+    share = own.shape[0]
+    out[0:share, :] = own[...]
+    out[share:, :] = came[...]
+
+
+def pair_rows_kernel(own, came, out):
+    me = lax.axis_index("tensor")
+    share = own.shape[0] // 2
+    for first, ref in enumerate((own, came)):
+        for k in range(2):
+            index = jnp.bitwise_xor(me, first + 2 * k)
+            out[share_of(index, share), :] = ref[k * share : (k + 1) * share, :]
 
 
 def gather_kernel(*refs):
@@ -260,14 +330,16 @@
     low_o[...] = grad.astype(BF16)
 
 
-def attention_back_kernel(members, inputs, probs, q, k, v, wq, wk, wv, wo, *rest):
+def attention_back_kernel(
+    members, inputs, probs, q, k, v, wq, wk, wv, wo, gain_two, router, *rest
+):
     pieces = rest[:members]
     rest = rest[members:]
     share_o = rest[:members]
-    grads_o, attended_o, scores_o, gain_o = rest[members : members + 4]
-    acc = rest[members + 4]
+    grads_o, attended_o, scores_o = rest[members : members + 3]
+    acc = rest[members + 3]
     assemble(attended_o, pieces)
-    heads = wq.shape[1] // HEAD_DIM
+    heads = wq.shape[0] // HEAD_DIM
     grad_mixed = dot_nt(attended_o[...], wo[...]).astype(BF16)
     qv, kv, vv = q[...], k[...], v[...]
     dq = jnp.zeros(qv.shape, F32)
@@ -287,15 +359,28 @@
     grads_o[0] = dq
     grads_o[1] = dk
     grads_o[2] = dv
-    total = dot_nt(dq, wq[...]) + dot_nt(dk, wk[...]) + dot_nt(dv, wv[...])
+    total = dot(dq, wq[...]) + dot(dk, wk[...]) + dot(dv, wv[...])
     acc[...] = total
-    put_shares(acc, share_o)
     x = inputs[...].astype(F32)
-    gain_o[...] = jnp.sum(total * x * inverse_rms(x), axis=0, keepdims=True)
+    gain_one = jnp.sum(total * x * inverse_rms(x), axis=0, keepdims=True)
+    small = jnp.concatenate(
+        [
+            gain_one,
+            gain_two[...],
+            router[...],
+            jnp.zeros((SMALL_ROWS - 2 - EXPERTS, gain_one.shape[1]), F32),
+        ],
+        axis=0,
+    )
+    me = lax.axis_index("tensor")
+    for k, ref in enumerate(share_o):
+        share = ref.shape[0] - SMALL_ROWS
+        ref[0:share, :] = acc[share_of(jnp.bitwise_xor(me, k), share), :].astype(ref.dtype)
+        ref[share:, :] = small.astype(ref.dtype)
 
 
 def weight_grad_kernel(
-    split, normed, grads, attended, mixed, scores, buckets, gain_one, gain_two, router, *rest
+    split, normed, grads, attended, mixed, scores, buckets, *rest
 ):
     bucket_count = 32
     small, scratch = rest[-2:]
@@ -309,10 +394,6 @@
             product = dot_tn(attended[...], mixed[...])
         scratch[:, i * cols : (i + 1) * cols] = product
     small[...] = jnp.zeros_like(small)
-    width = gain_one.shape[1]
-    small[0:1, 0:width] = gain_one[...]
-    small[1:2, 0:width] = gain_two[...]
-    small[2 : 2 + EXPERTS, 0:width] = router[...]
     flip = (
         lax.broadcasted_iota(jnp.int32, (length, length), 0)
         + lax.broadcasted_iota(jnp.int32, (length, length), 1)
@@ -326,7 +407,7 @@
         wide = jnp.concatenate([flipped, jnp.zeros_like(flipped)], axis=1)
         sheared = pltpu.roll(wide, 0, 1, stride=1, stride_axis=0)
         offsets = jnp.sum(sheared, axis=0, keepdims=True)
-        small[2 + EXPERTS + h : 3 + EXPERTS + h, 0:bucket_count] = dot_nt(
+        small[TABLE_ROW + h : TABLE_ROW + h + 1, 0:bucket_count] = dot_nt(
             jnp.broadcast_to(offsets, (8, 2 * length)), hot, HIGHEST
         )[0:1]
     if not split:
@@ -344,65 +425,63 @@
         send[chip, part:rows, :] = small[...].astype(BF16)
 
 
-def weight_final_kernel(chips, *refs):
-    wq_o, wk_o, wv_o, wo_o, table_o, small_o = refs[chips:]
-    total = total_of(refs[:chips])
+def weight_final_kernel(members, *refs):
+    wq_o, wk_o, wv_o, wo_o, table_o, one_o, two_o, router_o = refs[2:]
+    total = total_of(refs[:2])
     part, cols = wq_o.shape
     wq_o[...] = total[0:part, 0:cols]
     wk_o[...] = total[0:part, cols : 2 * cols]
     wv_o[...] = total[0:part, 2 * cols : 3 * cols]
     wo_o[...] = total[0:part, 3 * cols : 4 * cols].T
     small = total[part:, :]
-    small_o[...] = small
-    bucket_count, heads = table_o.shape
-    pick = (
-        lax.broadcasted_iota(jnp.int32, (bucket_count, small.shape[1]), 0)
-        == lax.broadcasted_iota(jnp.int32, (bucket_count, small.shape[1]), 1)
-    ).astype(F32)
-    table_o[...] = dot_nt(pick, small, HIGHEST)[:, 2 + EXPERTS : 2 + EXPERTS + heads]
-
-
-def small_final_kernel(members, *refs):
-    one_o, two_o, router_o = refs[members:]
-    total = total_of(refs[:members])
-    part = router_o.shape[0]
-    first = (lax.axis_index("dp") * members + lax.axis_index("tensor")) * part
-    shape = (part, total.shape[1])
+    heads, bucket_count = table_o.shape
+    table_o[...] = small[TABLE_ROW : TABLE_ROW + heads, 0:bucket_count]
+    per = one_o.shape[1]
+    first = (lax.axis_index("dp") * members + lax.axis_index("tensor")) * per
+    shape = (per, small.shape[1])
     pick = (
         lax.broadcasted_iota(jnp.int32, shape, 0) + first
         == lax.broadcasted_iota(jnp.int32, shape, 1)
     ).astype(F32)
-    rows = dot_nt(total, pick, HIGHEST)
+    rows = dot_nt(small, pick, HIGHEST)
     one_o[...] = rows[0:1]
     two_o[...] = rows[1:2]
-    router_o[...] = dot_nt(pick, total, HIGHEST)[:, 2 : 2 + EXPERTS]
+    router_o[...] = rows[2:TABLE_ROW]
 
 
 def input_back_kernel(members, inputs, gain, grad_hidden, *rest):
-    out = rest[-1]
+    out, small_o = rest[members:]
     share = out.shape[0]
     x = inputs[share_of(lax.axis_index("tensor"), share), :].astype(F32)
     r = inverse_rms(x)
-    z = total_of(rest[:members]) * gain[...]
+    total = total_of(rest[:members])
+    small_o[...] = total[share:]
+    z = total[0:share] * gain[...]
     out[...] = (
         grad_hidden[...] + r * z - x * (r * r * r) * jnp.mean(z * x, axis=-1, keepdims=True)
     ).astype(BF16)
 
 
-def run(kernel, outs, args, scratch=(), flops=0, name=None):
+def run(kernel, outs, args, scratch=(), name=None, after=(), space=pltpu.VMEM):
     vmem = pl.BlockSpec(memory_space=pltpu.VMEM)
-    size = sum(a.size * a.dtype.itemsize for a in args)
-    size += sum(o.size * o.dtype.itemsize for o in outs)
+    anywhere = pl.BlockSpec(memory_space=pl.ANY)
+    count, extra = len(args), len(after)
+
+    def body(*refs):
+        kernel(*refs[:count], *refs[count + extra :])
+
     return pl.pallas_call(
-        kernel,
+        body,
         out_shape=outs,
-        in_specs=[vmem] * len(args),
+        in_specs=[pl.BlockSpec(memory_space=space)] * count + [anywhere] * extra,
         out_specs=[vmem] * len(outs),
         scratch_shapes=list(scratch),
         compiler_params=pltpu.CompilerParams(vmem_limit_bytes=48 * 1024 * 1024),
-        cost_estimate=pl.CostEstimate(flops=flops, bytes_accessed=size, transcendentals=0),
+        cost_estimate=pl.CostEstimate(
+            flops=int(WEIGHTS.get(name, 0.2) * 1e9), bytes_accessed=0, transcendentals=0
+        ),
         name=name,
-    )(*args)
+    )(*args, *after)
 
 
 def sds(shape, dtype):
@@ -412,6 +491,12 @@
 def swap(values, axis, k):
     size = lax.axis_size(axis)
     return lax.ppermute(values, axis, [(i, i ^ k) for i in range(size)])
+
+
+def swap_chips(values, even, odd):
+    size = lax.axis_size("dp")
+    pairs = [(i, i ^ (odd if i % 2 else even)) for i in range(size)]
+    return lax.ppermute(values, "dp", pairs)
 
 
 def exchange(shares):
@@ -465,26 +550,32 @@
     bucket_wide = jnp.pad(bucket_row, ((0, 0), (0, 1)), constant_values=-1)
     where_to = (routes * CAP + capacity_slots).reshape(1, length)
     router_t = router_weight.T
-
+    query_t, key_t, value_t = query_weight.T, key_weight.T, value_weight.T
+
+    attention_args = [
+        inputs,
+        gain_attn,
+        query_t,
+        key_t,
+        value_t,
+        bucket_row,
+        bias_table.T,
+        segments,
+        out_weight,
+    ]
+    attention_args = [pltpu.with_memory_space_constraint(a, pltpu.HBM) for a in attention_args]
     outs = run(
         bind(attention_kernel, members),
         shares_sds(BF16, F32)
         + [sds((length, width), BF16)]
         + [sds((length, cols), BF16)] * 3
         + [sds((heads, length, length), F32), sds((length, cols), BF16)],
-        [
-            inputs,
-            segments,
-            bucket_row,
-            gain_row,
-            bias_table,
-            query_weight,
-            key_weight,
-            value_weight,
-            out_weight,
-        ],
-        [pltpu.VMEM((length, width), F32), pltpu.VMEM((8, 2 * length), F32)],
+        attention_args,
+        [pltpu.VMEM((length, width), F32), pltpu.VMEM((8, 2 * length), F32)]
+        + [pltpu.VMEM(a.shape, a.dtype) for a in attention_args]
+        + [pltpu.SemaphoreType.DMA((len(attention_args),))],
         name="attention",
+        space=pltpu.HBM,
     )
     attended = exchange(outs[:members])
     normed, q, k, v, probs, mixed = outs[members:]
@@ -501,7 +592,7 @@
     outs = run(
         bind(expert_kernel, members),
         shares_sds(BF16)
-        + shares_sds(BF16)
+        + [sds((2 * share, width), BF16)] * 2
         + [sds((slots, width), BF16)]
         + [sds((slots, hidden_units), BF16)] * 2
         + [sds((slots, width), BF16), sds((EXPERTS, width), F32)],
@@ -515,54 +606,85 @@
         name="expert",
     )
     back_rows = exchange(outs[:members])
-    out_rows = outs[members : 2 * members]
-    buffer, active, grad_before, grad_expert, grad_router = outs[2 * members :]
+    rows_kept, rows_sent = outs[members : members + 2]
+    buffer, active, grad_before, grad_expert, grad_router = outs[members + 2 :]
 
     def split_sds(rows, columns):
         return [sds((chips, rows, columns), BF16)] * 2
+
+    def merge_sds(rows, columns):
+        return [sds((2, rows, columns), F32), sds((2, rows, columns), BF16)]
+
+    def merge_two(merged, name, after=()):
+        rows, columns = merged[0].shape[1:]
+        return run(
+            merge_two_kernel,
+            [sds((rows, columns), F32), sds((rows, columns), BF16)],
+            [merged[0], swap_chips(merged[1], 2, 4)],
+            name=name,
+            after=after,
+        )
 
     expert_grads = run(
         bind(expert_grad_kernel, split),
         split_sds(part, 4 * hidden_units) if split else [sds((width, 4 * hidden_units), F32)],
         [buffer, active, grad_before, grad_expert],
         [pltpu.VMEM((width, hidden_units), F32)],
-        flops=8 * CAP * width * hidden_units,
         name="expert_grads",
     )
 
+    own_rows, other_rows = run(
+        pair_sum_kernel,
+        [sds((share, width), F32), sds((share, width), BF16)],
+        [rows_kept, swap(rows_sent, "tensor", 1)],
+        name="pair_sum",
+    )
     grad_hidden, grad_attended, grad_gain_expert = run(
         bind(hidden_back_kernel, members),
         [sds((share, width), F32), sds((share, width), BF16), sds((1, width), F32)],
         [hidden, cotangent, gain_two_row] + back_rows,
         name="hidden_back",
+        after=[own_rows, *expert_grads[-1:]],
     )
     grad_attended = spread(grad_attended)
-    out_rows = exchange(out_rows)
-    (output,) = run(
-        bind(output_kernel, members),
+
+    (output_share,) = run(
+        output_kernel,
         [sds((share, width), BF16)],
-        [hidden] + out_rows,
+        [hidden, own_rows, swap(other_rows, "tensor", 2)],
         name="output_share",
     )
-    output = spread(output)
-    (output,) = run(gather_kernel, [sds((length, width), BF16)], output, name="output_rows")
+    expert_merged = []
+    if split:
+        expert_merged = run(
+            merge_kernel,
+            merge_sds(part, 4 * hidden_units),
+            [expert_grads[0], swap(expert_grads[1], "dp", 1)],
+            name="expert_merge",
+        )
+    expert_halves = []
+
+    def tall_sds(dtype):
+        return sds((share + SMALL_ROWS, width), dtype)
 
     outs = run(
         bind(attention_back_kernel, members),
-        shares_sds(BF16, F32)
+        [tall_sds(F32)]
+        + [tall_sds(BF16)] * (members - 1)
         + [
             sds((3, length, cols), BF16),
             sds((length, width), BF16),
             sds((heads, length, length), BF16),
-            sds((1, width), F32),
         ],
-        [inputs, probs, q, k, v, query_weight, key_weight, value_weight, out_weight]
+        [inputs, probs, q, k, v, query_t, key_t, value_t, out_weight]
+        + [grad_gain_expert, grad_router]
         + grad_attended,
         [pltpu.VMEM((length, width), F32)],
         name="attention_back",
+        after=expert_merged[:1],
     )
     grad_normed = exchange(outs[:members])
-    projections, attended_low, grad_scores, grad_gain_attn = outs[members:]
+    projections, attended_low, grad_scores = outs[members:]
 
     weight_cols = 4 * cols
     weight_grads = run(
@@ -570,76 +692,80 @@
         split_sds(part + SMALL_ROWS, weight_cols)
         if split
         else [sds((width, weight_cols), F32), sds((SMALL_ROWS, weight_cols), F32)],
-        [
-            normed,
-            projections,
-            attended_low,
-            mixed,
-            grad_scores,
-            bucket_wide,
-            grad_gain_attn,
-            grad_gain_expert,
-            grad_router,
-        ],
+        [normed, projections, attended_low, mixed, grad_scores, bucket_wide],
         [pltpu.VMEM((SMALL_ROWS, weight_cols), F32), pltpu.VMEM((width, weight_cols), F32)],
         name="weight_grads",
     )
 
-    (grad_inputs,) = run(
+    if split:
+        expert_halves = merge_two(expert_merged, "expert_merge_two")
+    grad_inputs, small = run(
         bind(input_back_kernel, members),
-        [sds((share, width), BF16)],
+        [sds((share, width), BF16), sds((SMALL_ROWS, width), F32)],
         [inputs, gain_row, grad_hidden] + grad_normed,
         name="input_back",
-    )
-    grad_inputs = spread(grad_inputs)
+        after=[output_share, *weight_grads[-1:], *expert_halves[:1]],
+    )
+    (output_pair,) = run(
+        pair_kernel,
+        [sds((2 * share, width), BF16)],
+        [output_share, swap(output_share, "tensor", 2)],
+        name="output_pair",
+    )
+    (output,) = run(
+        pair_rows_kernel,
+        [sds((length, width), BF16)],
+        [output_pair, swap(output_pair, "tensor", 1)],
+        name="output_rows",
+    )
+
+
+    input_parts = spread(grad_inputs)
     (grad_inputs,) = run(
-        gather_kernel, [sds((length, width), BF16)], grad_inputs, name="grad_rows"
+        gather_kernel, [sds((length, width), BF16)], input_parts, name="grad_rows"
     )
 
     if split:
-
-        def over_chips(kept, sent):
-            rows, columns = kept.shape[1:]
-            came = swap(sent, "dp", 1)
-            merged = run(
-                merge_kernel,
-                [sds((rows, columns), F32)] + [sds((rows, columns), BF16)] * (chips - 1),
-                [kept, came],
-                name="merge",
-            )
-            return [merged[0]] + [swap(merged[i], "dp", 2 * i) for i in range(1, chips)]
-
-        parts = over_chips(*expert_grads)
         grad_expert_up, grad_expert_down = run(
-            bind(expert_final_kernel, chips),
-            [sds((EXPERTS, part, hidden_units), F32), sds((EXPERTS, hidden_units, part), F32)],
-            parts,
+            expert_final_kernel,
+            [sds((EXPERTS, part, hidden_units), F32), sds((EXPERTS, part, hidden_units), F32)],
+            [expert_halves[0], swap_chips(expert_halves[1], 4, 2)],
             name="expert_final",
         )
-        parts = over_chips(*weight_grads)
+        grad_expert_down = grad_expert_down.transpose(0, 2, 1)
+        merged = run(
+            merge_small_kernel,
+            merge_sds(part + SMALL_ROWS, weight_cols),
+            [
+                weight_grads[0],
+                swap(weight_grads[1], "dp", 1),
+                small,
+                swap(small, "dp", 1),
+            ],
+            name="weight_merge",
+            after=[output_pair, input_parts[1]],
+        )
+        merged = merge_two(merged, "weight_merge_two", after=input_parts[2:])
+        per = part // members
         (
             grad_query_weight,
             grad_key_weight,
             grad_value_weight,
             grad_out_weight,
             grad_table,
-            small,
+            grad_gain_attn,
+            grad_gain_expert,
+            grad_router,
         ) = run(
-            bind(weight_final_kernel, chips),
+            bind(weight_final_kernel, members),
             [sds((part, cols), F32)] * 3
-            + [sds((cols, part), F32), sds((bucket_count, heads), F32)]
-            + [sds((SMALL_ROWS, weight_cols), F32)],
-            parts,
+            + [sds((cols, part), F32), sds((heads, bucket_count), F32)]
+            + [sds((1, per), F32), sds((1, per), F32), sds((EXPERTS, per), F32)],
+            [merged[0], swap_chips(merged[1], 4, 2)],
             name="weight_final",
         )
-        small = [small] + [swap(small, "tensor", i) for i in range(1, members)]
-        per = part // members
-        grad_gain_attn, grad_gain_expert, grad_router = run(
-            bind(small_final_kernel, members),
-            [sds((1, per), F32), sds((1, per), F32), sds((per, EXPERTS), F32)],
-            small,
-            name="small_final",
-        )
+        grad_table = grad_table.T
+        grad_router = grad_router.T
         grad_gain_attn = grad_gain_attn.reshape(per)
         grad_gain_expert = grad_gain_expert.reshape(per)
     else:
@@ -647,20 +773,22 @@
         def scatter(values, axes, dimension):
             return lax.psum_scatter(values, axes, scatter_dimension=dimension, tiled=True)
 
+        def pick(values):
+            at = lax.axis_index("tensor") * (part // members)
+            return lax.dynamic_slice_in_dim(scatter(values, "dp", 0), at, part // members)
+
         grads = expert_grads[0].reshape(width, EXPERTS, 2, hidden_units)
         grad_expert_up = scatter(grads[:, :, 0].transpose(1, 0, 2), "dp", 1)
         grad_expert_down = scatter(grads[:, :, 1].transpose(1, 2, 0), "dp", 2)
-        grads, small = weight_grads
+        grads, table_rows = weight_grads
         grad_query_weight = scatter(grads[:, 0:cols], "dp", 0)
         grad_key_weight = scatter(grads[:, cols : 2 * cols], "dp", 0)
         grad_value_weight = scatter(grads[:, 2 * cols : 3 * cols], "dp", 0)
         grad_out_weight = scatter(grads[:, 3 * cols :].T, "dp", 1)
-        first = 2 + EXPERTS
-        grad_table = lax.psum(small[first : first + heads, :bucket_count].T, "dp")
-        both = ("dp", "tensor")
-        grad_gain_attn = scatter(small[0, :width], both, 0)
-        grad_gain_expert = scatter(small[1, :width], both, 0)
-        grad_router = scatter(small[2:first, :width].T, both, 0)
+        grad_table = lax.psum(table_rows[TABLE_ROW : TABLE_ROW + heads, :bucket_count].T, "dp")
+        grad_gain_attn = pick(small[0])
+        grad_gain_expert = pick(small[1])
+        grad_router = pick(small[2:TABLE_ROW].T)
     return (
         output,
         grad_inputs,

time: 155 us -> 115 us (0.74)
  waiting for transfers between devices: 71.1 us -> 33 us
  Pallas kernels: 23.9 us -> 36.8 us
  starting transfers between devices: 46.6 us -> 36.8 us
  local copies, waits for them, and re-layouts: 11.7 us -> 6.49 us
    ppermute x35 -> x25, waiting for transfers between devices: 71.1 us -> 28.2 us  [swap(): return lax.ppermute(values, axis, [(i, i ^ k) for i in range(size)])]
    ppermute x35 -> x25, starting transfers between devices: 46.6 us -> 32 us  [swap(): return lax.ppermute(values, axis, [(i, i ^ k) for i in range(size)])]
    pallas_call x16 -> x19, Pallas kernels: 23.9 us -> 36.8 us  [run(): pl.pallas_call(body, out_shape=outs, in_specs=[pl.BlockSpec(memory_space=...]
    unnamed x37 -> x36, local copies, waits for them, and re-layouts: 11 us -> 5.79 us
    ppermute x0 -> x4, starting transfers between devices: none -> 4.81 us  [swap_chips(): return lax.ppermute(values, 'dp', pairs)]
    ppermute x0 -> x4, waiting for transfers between devices: none -> 4.8 us  [swap_chips(): return lax.ppermute(values, 'dp', pairs)]
  transfers between devices with their start and end apart: 35 -> 29, of which waited for: 18 -> 11; matrix products, arithmetic and copies ran while one was open for 1% -> 1% of each run, Pallas kernels for 7% -> 23%
where the time goes in v2:
time: 115 us; the launch traced here: 114 us
  Pallas kernels  36.8 us (32%)
  starting transfers between devices  36.8 us (32%)
  waiting for transfers between devices  33 us (29%)
  local copies, waits for them, and re-layouts  6.49 us (6%)
    pallas_call x19, Pallas kernels, run(): pl.pallas_call(body, out_shape=outs, in_specs=[pl.BlockSpec(memory_space=...  36.8 us
    ppermute x25, starting transfers between devices, swap(): return lax.ppermute(values, axis, [(i, i ^ k) for i in range(size)])  32 us
    ppermute x25, waiting for transfers between devices, swap(): return lax.ppermute(values, axis, [(i, i ^ k) for i in range(size)])  28.2 us
    unnamed x36, local copies, waits for them, and re-layouts  5.79 us
    ppermute x4, starting transfers between devices, swap_chips(): return lax.ppermute(values, 'dp', pairs)  4.81 us
    ppermute x4, waiting for transfers between devices, swap_chips(): return lax.ppermute(values, 'dp', pairs)  4.8 us
  transfers between devices with their start and end apart: 29, of which 11 were waited for; matrix products, arithmetic and copies ran while one was open for 1% of the time, Pallas kernels for 23%

profile of v2, /device:TPU:0, one launch (start us, length us, event | category | flops | bytes accessed | tf_op | source)
XLA Modules:
  0.0 114.0 jit_solution(16051434834214880904)
XLA Ops:
  0.7 3.5 %attention.1 = (f32[64,768]{1,0:T(8,128)S(1)}, bf16[64,768]{1,0:T(8,128)(2,1)S(1)}, bf16[64,768]{1,0:T(8,128)(2,1)S(1)}, bf16[64,768]{1,0:T(8,128)(2,1)S(1)}, bf...) custom-call(bf16[256,768]{1,0:T(8,128)(2,1)} %refs_0_.7, ...), custom_call_target="tpu_custom_call" | custom-call | flops 200000000 | tf_op jit(solution)/shard_map/attention/pallas_call | solution.py:473
  4.2 3.1 %collective-permute-start = (bf16[64,768]{1,0:T(8,128)(2,1)S(1)}, bf16[64,768]{1,0:T(8,128)(2,1)S(1)}, u32[]{:S(2)}, u32[]{:S(2)}) collective-permute-start(bf16[64,768]{1,0:T(8,128)(2,1)S(1)} %get-tuple-element.72), channel_id=1, source_target_pairs={{0,1},{1,0},{2,3},{3,2},{4,5},{5,4},{6,7},{7,6},{8,9},{9,8},{10,11... | collective-permute-start | bytes 294920 | tf_op jit(solution)/shard_map/ppermute | solution.py:493
  7.3 2.6 %collective-permute-start.1 = (bf16[64,768]{1,0:T(8,128)(2,1)S(1)}, bf16[64,768]{1,0:T(8,128)(2,1)S(1)}, u32[]{:S(2)}, u32[]{:S(2)}) collective-permute-start(bf16[64,768]{1,0:T(8,128)(2,1)S(1)} %get-tuple-element.73), channel_id=1, source_target_pairs={{0,2},{1,3},{2,0},{3,1},{4,6},{5,7},{6,4},{7,5},{8,10},{9,11},{10,... | collective-permute-start | bytes 294920 | tf_op jit(solution)/shard_map/ppermute | solution.py:493
  9.9 0.7 reshape.42.refs_1_.refs_2_
  10.6 7.1 %collective-permute-done.1.refs_4_ = bf16[64,768]{1,0:T(8,128)(2,1)S(1)} collective-permute-done((bf16[64,768]{1,0:T(8,128)(2,1)S(1)}, bf16[64,768]{1,0:T(8,128)(2,1)S(1)}, u32[]{:S(2)}, u32[]{:S(2)}) %collective-permute-start.1) | collective-permute-done | bytes 98336 | tf_op jit(solution)/shard_map/ppermute | solution.py:493
  17.7 1.0 copy-done.2
  18.7 0.1 hidden.1
  18.9 1.7 %collective-permute-start.3 = (bf16[64,768]{1,0:T(8,128)(2,1)S(1)}, bf16[64,768]{1,0:T(8,128)(2,1)S(1)}, u32[]{:S(2)}, u32[]{:S(2)}) collective-permute-start(bf16[64,768]{1,0:T(8,128)(2,1)S(1)} %get-tuple-element.76.refs_5_), channel_id=1, source_target_pairs={{0,1},{1,0},{2,3},{3,2},{4,5},{5,4},{6,7},{7,6},{8,9},{9,8},{10,11... | collective-permute-start | bytes 294920 | tf_op jit(solution)/shard_map/ppermute | solution.py:493
  20.6 1.4 %collective-permute-start.4 = (bf16[64,768]{1,0:T(8,128)(2,1)S(1)}, bf16[64,768]{1,0:T(8,128)(2,1)S(1)}, u32[]{:S(2)}, u32[]{:S(2)}) collective-permute-start(bf16[64,768]{1,0:T(8,128)(2,1)S(1)} %get-tuple-element.76.refs_5_), channel_id=1, source_target_pairs={{0,2},{1,3},{2,0},{3,1},{4,6},{5,7},{6,4},{7,5},{8,10},{9,11},{10,... | collective-permute-start | bytes 294920 | tf_op jit(solution)/shard_map/ppermute | solution.py:493
  22.0 1.4 %collective-permute-start.5 = (bf16[64,768]{1,0:T(8,128)(2,1)S(1)}, bf16[64,768]{1,0:T(8,128)(2,1)S(1)}, u32[]{:S(2)}, u32[]{:S(2)}) collective-permute-start(bf16[64,768]{1,0:T(8,128)(2,1)S(1)} %get-tuple-element.76.refs_5_), channel_id=1, source_target_pairs={{0,3},{1,2},{2,1},{3,0},{4,7},{5,6},{6,5},{7,4},{8,11},{9,10},{10,... | collective-permute-start | bytes 294920 | tf_op jit(solution)/shard_map/ppermute | solution.py:493
  23.4 1.0 collective-permute-done.3.refs_6_
  24.4 5.4 %collective-permute-done.4.refs_7_ = bf16[64,768]{1,0:T(8,128)(2,1)S(1)} collective-permute-done((bf16[64,768]{1,0:T(8,128)(2,1)S(1)}, bf16[64,768]{1,0:T(8,128)(2,1)S(1)}, u32[]{:S(2)}, u32[]{:S(2)}) %collective-permute-start.4) | collective-permute-done | bytes 98336 | tf_op jit(solution)/shard_map/ppermute | solution.py:493
  29.8 0.0 copy-start.10
  29.8 1.7 %copy-done.10 = bf16[2,768,768]{2,1,0:T(8,128)(2,1)S(1)} copy-done((bf16[2,768,768]{2,1,0:T(8,128)(2,1)S(1)}, bf16[2,768,768]{2,1,0:T(8,128)(2,1)}, u32[]{:S(2)}) %copy-start.10) | copy-done | bytes 2359320
  31.5 6.1 %expert.1 = (bf16[64,768]{1,0:T(8,128)(2,1)S(1)}, bf16[64,768]{1,0:T(8,128)(2,1)}, bf16[64,768]{1,0:T(8,128)(2,1)}, bf16[64,768]{1,0:T(8,128)(2,1)}, bf16[128,76...) custom-call(s32[1,256]{1,0:T(1,128)S(1)} %bitcast.18, ...), custom_call_target="tpu_custom_call" | custom-call | flops 5000000000 | tf_op jit(solution)/shard_map/expert/pallas_call | solution.py:473
  37.6 1.6 %collective-permute-start.6 = (bf16[128,768]{1,0:T(8,128)(2,1)}, bf16[128,768]{1,0:T(8,128)(2,1)}, u32[]{:S(2)}, u32[]{:S(2)}) collective-permute-start(bf16[128,768]{1,0:T(8,128)(2,1)} %get-tuple-element.78), channel_id=1, source_target_pairs={{0,1},{1,0},{2,3},{3,2},{4,5},{5,4},{6,7},{7,6},{8,9},{9,8},{10,11... | collective-permute-start | bytes 589832 | tf_op jit(solution)/shard_map/ppermute | solution.py:493
  39.2 0.4 collective-permute-start.10
  39.6 2.4 %collective-permute-start.11 = (bf16[64,768]{1,0:T(8,128)(2,1)}, bf16[64,768]{1,0:T(8,128)(2,1)}, u32[]{:S(2)}, u32[]{:S(2)}) collective-permute-start(bf16[64,768]{1,0:T(8,128)(2,1)} %get-tuple-element.83), channel_id=1, source_target_pairs={{0,2},{1,3},{2,0},{3,1},{4,6},{5,7},{6,4},{7,5},{8,10},{9,11},{10,... | collective-permute-start | bytes 294920 | tf_op jit(solution)/shard_map/ppermute | solution.py:493
  42.0 1.5 %collective-permute-start.12 = (bf16[64,768]{1,0:T(8,128)(2,1)}, bf16[64,768]{1,0:T(8,128)(2,1)}, u32[]{:S(2)}, u32[]{:S(2)}) collective-permute-start(bf16[64,768]{1,0:T(8,128)(2,1)} %get-tuple-element.84), channel_id=1, source_target_pairs={{0,3},{1,2},{2,1},{3,0},{4,7},{5,6},{6,5},{7,4},{8,11},{9,10},{10,... | collective-permute-start | bytes 294920 | tf_op jit(solution)/shard_map/ppermute | solution.py:493
  43.6 4.2 %expert_grads.1 = (bf16[4,96,3072]{2,1,0:T(8,128)(2,1)S(1)}, bf16[4,96,3072]{2,1,0:T(8,128)(2,1)}) custom-call(bf16[288,768]{1,0:T(8,128)(2,1)S(1)} %get-tuple-element.85.refs_0_, bf16[288,768]{1,0:T(8,128)(2,1)S(1)} %get-tuple-element.86.refs_1_, bf16[288,768]{1,0:T(8,128)(2,1)S(1)} %get-tuple-element.87.refs_2_, bf16[288,768]{1,0:T(8,128)(2,1)S(1)} %get-tuple-element.88.refs_3_), custom_call_target="tpu_custom_call" | custom-call | flops 399999991808 | tf_op jit(solution)/shard_map/expert_grads/pallas_call | solution.py:473
  47.8 1.6 %pair_sum.1 = (f32[64,768]{1,0:T(8,128)S(1)}, bf16[64,768]{1,0:T(8,128)(2,1)}) custom-call(bf16[128,768]{1,0:T(8,128)(2,1)S(1)} %get-tuple-element.77.refs_0_, bf16[128,768]{1,0:T(8,128)(2,1)} %collective-permute-done.6.refs_1_), custom_call_target="tpu_custom_call" | custom-call | flops 200000000 | tf_op jit(solution)/shard_map/pair_sum/pallas_call | solution.py:473
  49.4 0.4 collective-permute-start.7
  49.8 2.4 %collective-permute-done.12.refs_6_ = bf16[64,768]{1,0:T(8,128)(2,1)} collective-permute-done((bf16[64,768]{1,0:T(8,128)(2,1)}, bf16[64,768]{1,0:T(8,128)(2,1)}, u32[]{:S(2)}, u32[]{:S(2)}) %collective-permute-start.12) | collective-permute-done | bytes 98336 | tf_op jit(solution)/shard_map/ppermute | solution.py:493
  52.1 1.7 %copy-done.11 = bf16[4,96,3072]{2,1,0:T(8,128)(2,1)S(1)} copy-done((bf16[4,96,3072]{2,1,0:T(8,128)(2,1)S(1)}, bf16[4,96,3072]{2,1,0:T(8,128)(2,1)}, u32[]{:S(2)}) %copy-start.11) | copy-done | bytes 2359320
  53.8 1.8 %hidden_back.1 = (f32[64,768]{1,0:T(8,128)S(1)}, bf16[64,768]{1,0:T(8,128)(2,1)}, f32[1,768]{1,0:T(1,128)S(1)}) custom-call(f32[64,768]{1,0:T(8,128)S(1)} %get-tuple-element.75.refs_0_, bf16[256,768]{1,0:T(8,128)(2,1)S(1)} %copy-done.12, f32[1,768]{1,0:T(1,128)S(1)} %copy-done.9, bf16[64,768]{1,0:T(8,128)(2,1)S(1)} %get-tuple-element.81.refs_3_, ...), custom_call_target="tpu_custom_call" | custom-call | flops 999999995904 | tf_op jit(solution)/shard_map/hidden_back/pallas_call | solution.py:473
  55.6 0.1 collective-permute-start.13
  55.7 1.4 %collective-permute-start.14 = (bf16[64,768]{1,0:T(8,128)(2,1)}, bf16[64,768]{1,0:T(8,128)(2,1)}, u32[]{:S(2)}, u32[]{:S(2)}) collective-permute-start(bf16[64,768]{1,0:T(8,128)(2,1)} %get-tuple-element.97.refs_11_), channel_id=1, source_target_pairs={{0,2},{1,3},{2,0},{3,1},{4,6},{5,7},{6,4},{7,5},{8,10},{9,11},{10,... | collective-permute-start | bytes 294920 | tf_op jit(solution)/shard_map/ppermute | solution.py:493
  57.1 2.9 %collective-permute-start.15 = (bf16[64,768]{1,0:T(8,128)(2,1)}, bf16[64,768]{1,0:T(8,128)(2,1)}, u32[]{:S(2)}, u32[]{:S(2)}) collective-permute-start(bf16[64,768]{1,0:T(8,128)(2,1)} %get-tuple-element.97.refs_11_), channel_id=1, source_target_pairs={{0,3},{1,2},{2,1},{3,0},{4,7},{5,6},{6,5},{7,4},{8,11},{9,10},{10,... | collective-permute-start | bytes 294920 | tf_op jit(solution)/shard_map/ppermute | solution.py:493
  60.0 1.6 %output_share.1.refs_0_.refs_7_ = bf16[64,768]{1,0:T(8,128)(2,1)} custom-call(f32[64,768]{1,0:T(8,128)S(1)} %get-tuple-element.75.refs_0_, f32[64,768]{1,0:T(8,128)S(1)} %get-tuple-element.79.refs_1_.refs_7_, bf16[64,768]{1,0:T(8,128)(2,1)} %collective-permute-done.7.refs_2_), custom_call_target="tpu_custom_call" | custom-call | flops 200000000 | tf_op jit(solution)/shard_map/output_share/pallas_call | solution.py:473
  61.6 0.0 copy-start.4
  61.6 0.0 copy-start.5
  61.6 0.0 copy-start.6
  61.6 0.0 copy-start.7
  61.6 3.2 %expert_merge.1 = (f32[2,96,3072]{2,1,0:T(8,128)S(1)}, bf16[2,96,3072]{2,1,0:T(8,128)(2,1)}) custom-call(bf16[4,96,3072]{2,1,0:T(8,128)(2,1)S(1)} %get-tuple-element.98.refs_0_, bf16[4,96,3072]{2,1,0:T(8,128)(2,1)} %collective-permute-done.16.refs_1_), custom_call_target="tpu_custom_call" | custom-call | flops 399999991808 | tf_op jit(solution)/shard_map/expert_merge/pallas_call | solution.py:473
  64.9 1.4 %copy-done = f32[2,96,3072]{2,1,0:T(8,128)} copy-done((f32[2,96,3072]{2,1,0:T(8,128)}, f32[2,96,3072]{2,1,0:T(8,128)S(1)}, u32[]{:S(2)}) %copy-start) | copy-done | bytes 2359320
  66.3 1.5 %collective-permute-start.20 = (bf16[2,96,3072]{2,1,0:T(8,128)(2,1)}, bf16[2,96,3072]{2,1,0:T(8,128)(2,1)}, u32[]{:S(2)}, u32[]{:S(2)}) collective-permute-start(bf16[2,96,3072]{2,1,0:T(8,128)(2,1)} %get-tuple-element.110), channel_id=1, source_target_pairs={{0,8},{4,20},{8,0},{12,28},{16,24},{20,4},{24,16},{28,12},{1,9},{5... | collective-permute-start | bytes 3538952 | tf_op jit(solution)/shard_map/ppermute | solution.py:499
  67.8 0.8 collective-permute-done.14.refs_13_
  68.6 2.9 %attention_back.1 = (f32[80,768]{1,0:T(8,128)S(1)}, bf16[80,768]{1,0:T(8,128)(2,1)S(1)}, bf16[80,768]{1,0:T(8,128)(2,1)S(1)}, bf16[80,768]{1,0:T(8,128)(2,1)S(1)...) custom-call(bf16[256,768]{1,0:T(8,128)(2,1)S(1)} %copy-done.3, ...), custom_call_target="tpu_custom_call" | custom-call | flops 999999995904 | tf_op jit(solution)/shard_map/attention_back/pallas_call | solution.py:473
  71.4 2.7 %collective-permute-start.17 = (bf16[80,768]{1,0:T(8,128)(2,1)S(1)}, bf16[80,768]{1,0:T(8,128)(2,1)S(1)}, u32[]{:S(2)}, u32[]{:S(2)}) collective-permute-start(bf16[80,768]{1,0:T(8,128)(2,1)S(1)} %get-tuple-element.101), channel_id=1, source_target_pairs={{0,1},{1,0},{2,3},{3,2},{4,5},{5,4},{6,7},{7,6},{8,9},{9,8},{10,11... | collective-permute-start | bytes 368648 | tf_op jit(solution)/shard_map/ppermute | solution.py:493
  74.2 0.5 collective-permute-start.18
  74.7 1.9 %collective-permute-start.19 = (bf16[80,768]{1,0:T(8,128)(2,1)S(1)}, bf16[80,768]{1,0:T(8,128)(2,1)S(1)}, u32[]{:S(2)}, u32[]{:S(2)}) collective-permute-start(bf16[80,768]{1,0:T(8,128)(2,1)S(1)} %get-tuple-element.103), channel_id=1, source_target_pairs={{0,3},{1,2},{2,1},{3,0},{4,7},{5,6},{6,5},{7,4},{8,11},{9,10},{10,... | collective-permute-start | bytes 368648 | tf_op jit(solution)/shard_map/ppermute | solution.py:493
  76.6 2.6 %weight_grads.1 = (bf16[4,112,768]{2,1,0:T(8,128)(2,1)S(1)}, bf16[4,112,768]{2,1,0:T(8,128)(2,1)}) custom-call(bf16[256,768]{1,0:T(8,128)(2,1)S(1)} %get-tuple-element.104.refs_0_, bf16[3,256,192]{2,1,0:T(8,128)(2,1)S(1)} %get-tuple-element.105.refs_1_, bf16[256,768]{1,0:T(8,128)(2,1)S(1)} %get-tuple-element.106.refs_2_, ...), custom_call_target="tpu_custom_call" | custom-call | flops 12000000000 | tf_op jit(solution)/shard_map/weight_grads/pallas_call | solution.py:473
  79.2 3.6 %collective-permute-done.20.refs_1_ = bf16[2,96,3072]{2,1,0:T(8,128)(2,1)} collective-permute-done((bf16[2,96,3072]{2,1,0:T(8,128)(2,1)}, bf16[2,96,3072]{2,1,0:T(8,128)(2,1)}, u32[]{:S(2)}, u32[]{:S(2)}) %collective-permute-start.20) | collective-permute-done | bytes 1179680 | tf_op jit(solution)/shard_map/ppermute | solution.py:499
  82.8 2.2 %expert_merge_two.1 = (f32[96,3072]{1,0:T(8,128)S(1)}, bf16[96,3072]{1,0:T(8,128)(2,1)}) custom-call(f32[2,96,3072]{2,1,0:T(8,128)S(1)} %copy-done.1, bf16[2,96,3072]{2,1,0:T(8,128)(2,1)} %collective-permute-done.20.refs_1_), custom_call_target="tpu_custom_call" | custom-call | flops 200000000 | tf_op jit(solution)/shard_map/expert_merge_two/pallas_call | solution.py:473
  85.0 1.5 %collective-permute-start.28 = (bf16[96,3072]{1,0:T(8,128)(2,1)}, bf16[96,3072]{1,0:T(8,128)(2,1)}, u32[]{:S(2)}, u32[]{:S(2)}) collective-permute-start(bf16[96,3072]{1,0:T(8,128)(2,1)} %get-tuple-element.127), channel_id=1, source_target_pairs={{0,16},{4,12},{8,24},{12,4},{16,0},{20,28},{24,8},{28,20},{1,17},{... | collective-permute-start | bytes 1769480 | tf_op jit(solution)/shard_map/ppermute | solution.py:499
  86.6 0.2 input_back.1
  86.8 1.5 %collective-permute-start.21 = (bf16[64,768]{1,0:T(8,128)(2,1)S(1)}, bf16[64,768]{1,0:T(8,128)(2,1)S(1)}, u32[]{:S(2)}, u32[]{:S(2)}) collective-permute-start(bf16[64,768]{1,0:T(8,128)(2,1)S(1)} %get-tuple-element.112.refs_0_), channel_id=1, source_target_pairs={{0,1},{1,0},{2,3},{3,2},{4,5},{5,4},{6,7},{7,6},{8,9},{9,8},{10,11... | collective-permute-start | bytes 294920 | tf_op jit(solution)/shard_map/ppermute | solution.py:493
  88.3 1.0 output_pair.1.refs_0_.refs_4_
  89.2 0.3 collective-permute-done.25.refs_3_
  89.5 2.2 %collective-permute-done.21.refs_1_.refs_5_ = bf16[64,768]{1,0:T(8,128)(2,1)S(1)} collective-permute-done((bf16[64,768]{1,0:T(8,128)(2,1)S(1)}, bf16[64,768]{1,0:T(8,128)(2,1)S(1)}, u32[]{:S(2)}, u32[]{:S(2)}) %collective-permute-start.21) | collective-permute-done | bytes 98336 | tf_op jit(solution)/shard_map/ppermute | solution.py:493
  91.7 1.3 %weight_merge.1 = (f32[2,112,768]{2,1,0:T(8,128)S(1)}, bf16[2,112,768]{2,1,0:T(8,128)(2,1)S(1)}) custom-call(bf16[4,112,768]{2,1,0:T(8,128)(2,1)S(1)} %get-tuple-element.113.refs_0_, bf16[4,112,768]{2,1,0:T(8,128)(2,1)} %collective-permute-done.24.refs_1_, f32[16,768]{1,0:T(8,128)S(1)} %get-tuple-element.114.refs_2_, ...), custom_call_target="tpu_custom_call" | custom-call | flops 200000000 | tf_op jit(solution)/shard_map/weight_merge/pallas_call | solution.py:473
  93.0 1.3 %collective-permute-start.26 = (bf16[2,112,768]{2,1,0:T(8,128)(2,1)S(1)}, bf16[2,112,768]{2,1,0:T(8,128)(2,1)S(1)}, u32[]{:S(2)}, u32[]{:S(2)}) collective-permute-start(bf16[2,112,768]{2,1,0:T(8,128)(2,1)S(1)} %get-tuple-element.116), channel_id=1, source_target_pairs={{0,8},{4,20},{8,0},{12,28},{16,24},{20,4},{24,16},{28,12},{1,9},{5... | collective-permute-start | bytes 1032200 | tf_op jit(solution)/shard_map/ppermute | solution.py:499
  94.2 1.5 %collective-permute-start.9 = (bf16[128,768]{1,0:T(8,128)(2,1)S(1)}, bf16[128,768]{1,0:T(8,128)(2,1)S(1)}, u32[]{:S(2)}, u32[]{:S(2)}) collective-permute-start(bf16[128,768]{1,0:T(8,128)(2,1)S(1)} %output_pair.1.refs_0_.refs_4_), channel_id=1, source_target_pairs={{0,1},{1,0},{2,3},{3,2},{4,5},{5,4},{6,7},{7,6},{8,9},{9,8},{10,11... | collective-permute-start | bytes 589832 | tf_op jit(solution)/shard_map/ppermute | solution.py:493
  95.7 1.4 %collective-permute-start.22 = (bf16[64,768]{1,0:T(8,128)(2,1)S(1)}, bf16[64,768]{1,0:T(8,128)(2,1)S(1)}, u32[]{:S(2)}, u32[]{:S(2)}) collective-permute-start(bf16[64,768]{1,0:T(8,128)(2,1)S(1)} %get-tuple-element.112.refs_0_), channel_id=1, source_target_pairs={{0,2},{1,3},{2,0},{3,1},{4,6},{5,7},{6,4},{7,5},{8,10},{9,11},{10,... | collective-permute-start | bytes 294920 | tf_op jit(solution)/shard_map/ppermute | solution.py:493
  97.2 1.5 %collective-permute-start.23 = (bf16[64,768]{1,0:T(8,128)(2,1)S(1)}, bf16[64,768]{1,0:T(8,128)(2,1)S(1)}, u32[]{:S(2)}, u32[]{:S(2)}) collective-permute-start(bf16[64,768]{1,0:T(8,128)(2,1)S(1)} %get-tuple-element.112.refs_0_), channel_id=1, source_target_pairs={{0,3},{1,2},{2,1},{3,0},{4,7},{5,6},{6,5},{7,4},{8,11},{9,10},{10,... | collective-permute-start | bytes 294920 | tf_op jit(solution)/shard_map/ppermute | solution.py:493
  98.6 4.5 %collective-permute-done.22.refs_2_ = bf16[64,768]{1,0:T(8,128)(2,1)S(1)} collective-permute-done((bf16[64,768]{1,0:T(8,128)(2,1)S(1)}, bf16[64,768]{1,0:T(8,128)(2,1)S(1)}, u32[]{:S(2)}, u32[]{:S(2)}) %collective-permute-start.22) | collective-permute-done | bytes 98336 | tf_op jit(solution)/shard_map/ppermute | solution.py:493
  103.1 4.5 %collective-permute-done.23.refs_3_ = bf16[64,768]{1,0:T(8,128)(2,1)S(1)} collective-permute-done((bf16[64,768]{1,0:T(8,128)(2,1)S(1)}, bf16[64,768]{1,0:T(8,128)(2,1)S(1)}, u32[]{:S(2)}, u32[]{:S(2)}) %collective-permute-start.23) | collective-permute-done | bytes 98336 | tf_op jit(solution)/shard_map/ppermute | solution.py:493
  107.6 0.1 weight_merge_two.1
  107.7 0.5 collective-permute-start.27
  108.2 0.8 output_rows.1
  109.0 0.8 grad_rows.1
  109.8 2.2 %expert_final.1 = (f32[2,96,768]{2,1,0:T(8,128)}, f32[2,96,768]{2,1,0:T(8,128)}) custom-call(f32[96,3072]{1,0:T(8,128)S(1)} %get-tuple-element.111.refs_9_.refs_0_, bf16[96,3072]{1,0:T(8,128)(2,1)} %collective-permute-done.28.refs_1_), custom_call_target="tpu_custom_call" | custom-call | flops 1000000000 | tf_op jit(solution)/shard_map/expert_final/pallas_call | solution.py:473
  112.0 1.2 %collective-permute-done.27.refs_1_ = bf16[112,768]{1,0:T(8,128)(2,1)S(1)} collective-permute-done((bf16[112,768]{1,0:T(8,128)(2,1)S(1)}, bf16[112,768]{1,0:T(8,128)(2,1)S(1)}, u32[]{:S(2)}, u32[]{:S(2)}) %collective-permute-start.27) | collective-permute-done | bytes 172064 | tf_op jit(solution)/shard_map/ppermute | solution.py:499
  113.2 0.9 weight_final.1
  (53 shorter events, 0.1 us)
Async XLA Ops:
  0.6 22.7 %copy-start.14 = (f32[768]{0:T(1024)S(1)}, f32[768]{0:T(1024)}, u32[]{:S(2)}) copy-start(f32[768]{0:T(1024)} %refs_1_.3) | copy-start | bytes 9220
  0.7 22.7 %copy-start.15 = (s32[511]{0:T(512)S(1)}, s32[511]{0:T(512)}, u32[]{:S(2)}) copy-start(s32[511]{0:T(512)} %param.18) | copy-start | bytes 6136
  0.7 22.7 %copy-start.16 = (s32[256]{0:T(256)S(1)}, s32[256]{0:T(256)}, u32[]{:S(2)}) copy-start(s32[256]{0:T(256)} %param.20) | copy-start | bytes 3076
  0.7 22.7 %copy-start.17 = (s32[256]{0:T(256)S(1)}, s32[256]{0:T(256)}, u32[]{:S(2)}) copy-start(s32[256]{0:T(256)} %param.19) | copy-start | bytes 3076
  0.7 29.1 %copy-start.12 = (bf16[256,768]{1,0:T(8,128)(2,1)S(1)}, bf16[256,768]{1,0:T(8,128)(2,1)}, u32[]{:S(2)}) copy-start(bf16[256,768]{1,0:T(8,128)(2,1)} %refs_1_.5) | copy-start | bytes 1179652
  0.7 29.1 %copy-start.13 = (bf16[768,2]{0,1:T(2,128)(2,1)S(1)}, bf16[768,2]{0,1:T(2,128)(2,1)}, u32[]{:S(2)}) copy-start(bf16[768,2]{0,1:T(2,128)(2,1)} %param.28) | copy-start | bytes 9220
  4.2 6.4 %collective-permute-start = (bf16[64,768]{1,0:T(8,128)(2,1)S(1)}, bf16[64,768]{1,0:T(8,128)(2,1)S(1)}, u32[]{:S(2)}, u32[]{:S(2)}) collective-permute-start(bf16[64,768]{1,0:T(8,128)(2,1)S(1)} %get-tuple-element.72), channel_id=1, source_target_pairs={{0,1},{1,0},{2,3},{3,2},{4,5},{5,4},{6,7},{7,6},{8,9},{9,8},{10,11... | collective-permute-start | bytes 294920 | tf_op jit(solution)/shard_map/ppermute | solution.py:493
  7.3 10.4 %collective-permute-start.1 = (bf16[64,768]{1,0:T(8,128)(2,1)S(1)}, bf16[64,768]{1,0:T(8,128)(2,1)S(1)}, u32[]{:S(2)}, u32[]{:S(2)}) collective-permute-start(bf16[64,768]{1,0:T(8,128)(2,1)S(1)} %get-tuple-element.73), channel_id=1, source_target_pairs={{0,2},{1,3},{2,0},{3,1},{4,6},{5,7},{6,4},{7,5},{8,10},{9,11},{10,... | collective-permute-start | bytes 294920 | tf_op jit(solution)/shard_map/ppermute | solution.py:493
  9.9 7.8 %collective-permute-start.2 = (bf16[64,768]{1,0:T(8,128)(2,1)S(1)}, bf16[64,768]{1,0:T(8,128)(2,1)S(1)}, u32[]{:S(2)}, u32[]{:S(2)}) collective-permute-start(bf16[64,768]{1,0:T(8,128)(2,1)S(1)} %get-tuple-element.74), channel_id=1, source_target_pairs={{0,3},{1,2},{2,1},{3,0},{4,7},{5,6},{6,5},{7,4},{8,11},{9,10},{10,... | collective-permute-start | bytes 294920 | tf_op jit(solution)/shard_map/ppermute | solution.py:493
  10.6 8.3 %copy-start.8 = (f32[1,768]{1,0:T(1,128)}, f32[1,768]{1,0:T(1,128)S(1)}, u32[]{:S(2)}) copy-start(f32[1,768]{1,0:T(1,128)S(1)} %reshape.42.refs_1_.refs_2_) | copy-start | bytes 9220
  17.7 1.0 copy-start.2
  18.9 5.6 %collective-permute-start.3 = (bf16[64,768]{1,0:T(8,128)(2,1)S(1)}, bf16[64,768]{1,0:T(8,128)(2,1)S(1)}, u32[]{:S(2)}, u32[]{:S(2)}) collective-permute-start(bf16[64,768]{1,0:T(8,128)(2,1)S(1)} %get-tuple-element.76.refs_5_), channel_id=1, source_target_pairs={{0,1},{1,0},{2,3},{3,2},{4,5},{5,4},{6,7},{7,6},{8,9},{9,8},{10,11... | collective-permute-start | bytes 294920 | tf_op jit(solution)/shard_map/ppermute | solution.py:493
  20.6 9.3 %collective-permute-start.4 = (bf16[64,768]{1,0:T(8,128)(2,1)S(1)}, bf16[64,768]{1,0:T(8,128)(2,1)S(1)}, u32[]{:S(2)}, u32[]{:S(2)}) collective-permute-start(bf16[64,768]{1,0:T(8,128)(2,1)S(1)} %get-tuple-element.76.refs_5_), channel_id=1, source_target_pairs={{0,2},{1,3},{2,0},{3,1},{4,6},{5,7},{6,4},{7,5},{8,10},{9,11},{10,... | collective-permute-start | bytes 294920 | tf_op jit(solution)/shard_map/ppermute | solution.py:493
  22.0 7.8 %collective-permute-start.5 = (bf16[64,768]{1,0:T(8,128)(2,1)S(1)}, bf16[64,768]{1,0:T(8,128)(2,1)S(1)}, u32[]{:S(2)}, u32[]{:S(2)}) collective-permute-start(bf16[64,768]{1,0:T(8,128)(2,1)S(1)} %get-tuple-element.76.refs_5_), channel_id=1, source_target_pairs={{0,3},{1,2},{2,1},{3,0},{4,7},{5,6},{6,5},{7,4},{8,11},{9,10},{10,... | collective-permute-start | bytes 294920 | tf_op jit(solution)/shard_map/ppermute | solution.py:493
  29.8 1.7 %copy-start.10 = (bf16[2,768,768]{2,1,0:T(8,128)(2,1)S(1)}, bf16[2,768,768]{2,1,0:T(8,128)(2,1)}, u32[]{:S(2)}) copy-start(bf16[2,768,768]{2,1,0:T(8,128)(2,1)} %refs_3_.1) | copy-start | bytes 7077892
  37.6 10.2 %collective-permute-start.6 = (bf16[128,768]{1,0:T(8,128)(2,1)}, bf16[128,768]{1,0:T(8,128)(2,1)}, u32[]{:S(2)}, u32[]{:S(2)}) collective-permute-start(bf16[128,768]{1,0:T(8,128)(2,1)} %get-tuple-element.78), channel_id=1, source_target_pairs={{0,1},{1,0},{2,3},{3,2},{4,5},{5,4},{6,7},{7,6},{8,9},{9,8},{10,11... | collective-permute-start | bytes 589832 | tf_op jit(solution)/shard_map/ppermute | solution.py:493
  39.2 10.6 %collective-permute-start.10 = (bf16[64,768]{1,0:T(8,128)(2,1)}, bf16[64,768]{1,0:T(8,128)(2,1)}, u32[]{:S(2)}, u32[]{:S(2)}) collective-permute-start(bf16[64,768]{1,0:T(8,128)(2,1)} %get-tuple-element.82), channel_id=1, source_target_pairs={{0,1},{1,0},{2,3},{3,2},{4,5},{5,4},{6,7},{7,6},{8,9},{9,8},{10,11... | collective-permute-start | bytes 294920 | tf_op jit(solution)/shard_map/ppermute | solution.py:493
  39.6 10.2 %collective-permute-start.11 = (bf16[64,768]{1,0:T(8,128)(2,1)}, bf16[64,768]{1,0:T(8,128)(2,1)}, u32[]{:S(2)}, u32[]{:S(2)}) collective-permute-start(bf16[64,768]{1,0:T(8,128)(2,1)} %get-tuple-element.83), channel_id=1, source_target_pairs={{0,2},{1,3},{2,0},{3,1},{4,6},{5,7},{6,4},{7,5},{8,10},{9,11},{10,... | collective-permute-start | bytes 294920 | tf_op jit(solution)/shard_map/ppermute | solution.py:493
  42.0 10.1 %collective-permute-start.12 = (bf16[64,768]{1,0:T(8,128)(2,1)}, bf16[64,768]{1,0:T(8,128)(2,1)}, u32[]{:S(2)}, u32[]{:S(2)}) collective-permute-start(bf16[64,768]{1,0:T(8,128)(2,1)} %get-tuple-element.84), channel_id=1, source_target_pairs={{0,3},{1,2},{2,1},{3,0},{4,7},{5,6},{6,5},{7,4},{8,11},{9,10},{10,... | collective-permute-start | bytes 294920 | tf_op jit(solution)/shard_map/ppermute | solution.py:493
  43.6 8.6 %copy-start.9 = (f32[1,768]{1,0:T(1,128)S(1)}, f32[1,768]{1,0:T(1,128)}, u32[]{:S(2)}) copy-start(f32[1,768]{1,0:T(1,128)} %copy-done.8) | copy-start | bytes 9220
  47.8 13.8 %collective-permute-start.16 = (bf16[4,96,3072]{2,1,0:T(8,128)(2,1)}, bf16[4,96,3072]{2,1,0:T(8,128)(2,1)}, u32[]{:S(2)}, u32[]{:S(2)}) collective-permute-start(bf16[4,96,3072]{2,1,0:T(8,128)(2,1)} %get-tuple-element.89.refs_8_), channel_id=1, source_target_pairs={{0,4},{4,0},{8,12},{12,8},{16,20},{20,16},{24,28},{28,24},{1,5},{5... | collective-permute-start | bytes 7077896 | tf_op jit(solution)/shard_map/ppermute | solution.py:493
  49.4 10.6 %collective-permute-start.7 = (bf16[64,768]{1,0:T(8,128)(2,1)}, bf16[64,768]{1,0:T(8,128)(2,1)}, u32[]{:S(2)}, u32[]{:S(2)}) collective-permute-start(bf16[64,768]{1,0:T(8,128)(2,1)} %get-tuple-element.80), channel_id=1, source_target_pairs={{0,2},{1,3},{2,0},{3,1},{4,6},{5,7},{6,4},{7,5},{8,10},{9,11},{10,... | collective-permute-start | bytes 294920 | tf_op jit(solution)/shard_map/ppermute | solution.py:493
  52.1 1.7 %copy-start.11 = (bf16[4,96,3072]{2,1,0:T(8,128)(2,1)S(1)}, bf16[4,96,3072]{2,1,0:T(8,128)(2,1)}, u32[]{:S(2)}) copy-start(bf16[4,96,3072]{2,1,0:T(8,128)(2,1)} %get-tuple-element.89.refs_8_) | copy-start | bytes 7077892
  55.6 12.2 %collective-permute-start.13 = (bf16[64,768]{1,0:T(8,128)(2,1)}, bf16[64,768]{1,0:T(8,128)(2,1)}, u32[]{:S(2)}, u32[]{:S(2)}) collective-permute-start(bf16[64,768]{1,0:T(8,128)(2,1)} %get-tuple-element.97.refs_11_), channel_id=1, source_target_pairs={{0,1},{1,0},{2,3},{3,2},{4,5},{5,4},{6,7},{7,6},{8,9},{9,8},{10,11... | collective-permute-start | bytes 294920 | tf_op jit(solution)/shard_map/ppermute | solution.py:493
  55.7 12.8 %collective-permute-start.14 = (bf16[64,768]{1,0:T(8,128)(2,1)}, bf16[64,768]{1,0:T(8,128)(2,1)}, u32[]{:S(2)}, u32[]{:S(2)}) collective-permute-start(bf16[64,768]{1,0:T(8,128)(2,1)} %get-tuple-element.97.refs_11_), channel_id=1, source_target_pairs={{0,2},{1,3},{2,0},{3,1},{4,6},{5,7},{6,4},{7,5},{8,10},{9,11},{10,... | collective-permute-start | bytes 294920 | tf_op jit(solution)/shard_map/ppermute | solution.py:493
  57.1 11.4 %collective-permute-start.15 = (bf16[64,768]{1,0:T(8,128)(2,1)}, bf16[64,768]{1,0:T(8,128)(2,1)}, u32[]{:S(2)}, u32[]{:S(2)}) collective-permute-start(bf16[64,768]{1,0:T(8,128)(2,1)} %get-tuple-element.97.refs_11_), channel_id=1, source_target_pairs={{0,3},{1,2},{2,1},{3,0},{4,7},{5,6},{6,5},{7,4},{8,11},{9,10},{10,... | collective-permute-start | bytes 294920 | tf_op jit(solution)/shard_map/ppermute | solution.py:493
  61.6 26.7 %collective-permute-start.8 = (bf16[64,768]{1,0:T(8,128)(2,1)}, bf16[64,768]{1,0:T(8,128)(2,1)}, u32[]{:S(2)}, u32[]{:S(2)}) collective-permute-start(bf16[64,768]{1,0:T(8,128)(2,1)} %output_share.1.refs_0_.refs_7_), channel_id=1, source_target_pairs={{0,2},{1,3},{2,0},{3,1},{4,6},{5,7},{6,4},{7,5},{8,10},{9,11},{10,... | collective-permute-start | bytes 294920 | tf_op jit(solution)/shard_map/ppermute | solution.py:493
  61.6 6.9 %copy-start.3 = (bf16[256,768]{1,0:T(8,128)(2,1)S(1)}, bf16[256,768]{1,0:T(8,128)(2,1)}, u32[]{:S(2)}) copy-start(bf16[256,768]{1,0:T(8,128)(2,1)} %refs_0_.7) | copy-start | bytes 1179652
  61.6 6.9 %copy-start.4 = (bf16[768,192]{0,1:T(8,128)(2,1)S(1)}, bf16[768,192]{0,1:T(8,128)(2,1)}, u32[]{:S(2)}) copy-start(bf16[768,192]{0,1:T(8,128)(2,1)} %param.23) | copy-start | bytes 884740
  61.6 6.9 %copy-start.5 = (bf16[768,192]{0,1:T(8,128)(2,1)S(1)}, bf16[768,192]{0,1:T(8,128)(2,1)}, u32[]{:S(2)}) copy-start(bf16[768,192]{0,1:T(8,128)(2,1)} %param.24) | copy-start | bytes 884740
  61.6 6.9 %copy-start.6 = (bf16[768,192]{0,1:T(8,128)(2,1)S(1)}, bf16[768,192]{0,1:T(8,128)(2,1)}, u32[]{:S(2)}) copy-start(bf16[768,192]{0,1:T(8,128)(2,1)} %param.25) | copy-start | bytes 884740
  61.6 6.9 %copy-start.7 = (bf16[192,768]{1,0:T(8,128)(2,1)S(1)}, bf16[192,768]{1,0:T(8,128)(2,1)}, u32[]{:S(2)}) copy-start(bf16[192,768]{1,0:T(8,128)(2,1)} %refs_8_.3) | copy-start | bytes 884740
  64.9 1.4 %copy-start = (f32[2,96,3072]{2,1,0:T(8,128)}, f32[2,96,3072]{2,1,0:T(8,128)S(1)}, u32[]{:S(2)}) copy-start(f32[2,96,3072]{2,1,0:T(8,128)S(1)} %get-tuple-element.99.refs_15_.refs_0_) | copy-start | bytes 7077892
  66.3 16.5 %collective-permute-start.20 = (bf16[2,96,3072]{2,1,0:T(8,128)(2,1)}, bf16[2,96,3072]{2,1,0:T(8,128)(2,1)}, u32[]{:S(2)}, u32[]{:S(2)}) collective-permute-start(bf16[2,96,3072]{2,1,0:T(8,128)(2,1)} %get-tuple-element.110), channel_id=1, source_target_pairs={{0,8},{4,20},{8,0},{12,28},{16,24},{20,4},{24,16},{28,12},{1,9},{5... | collective-permute-start | bytes 3538952 | tf_op jit(solution)/shard_map/ppermute | solution.py:499
  71.4 13.6 %collective-permute-start.17 = (bf16[80,768]{1,0:T(8,128)(2,1)S(1)}, bf16[80,768]{1,0:T(8,128)(2,1)S(1)}, u32[]{:S(2)}, u32[]{:S(2)}) collective-permute-start(bf16[80,768]{1,0:T(8,128)(2,1)S(1)} %get-tuple-element.101), channel_id=1, source_target_pairs={{0,1},{1,0},{2,3},{3,2},{4,5},{5,4},{6,7},{7,6},{8,9},{9,8},{10,11... | collective-permute-start | bytes 368648 | tf_op jit(solution)/shard_map/ppermute | solution.py:493
  74.2 12.4 %collective-permute-start.18 = (bf16[80,768]{1,0:T(8,128)(2,1)S(1)}, bf16[80,768]{1,0:T(8,128)(2,1)S(1)}, u32[]{:S(2)}, u32[]{:S(2)}) collective-permute-start(bf16[80,768]{1,0:T(8,128)(2,1)S(1)} %get-tuple-element.102), channel_id=1, source_target_pairs={{0,2},{1,3},{2,0},{3,1},{4,6},{5,7},{6,4},{7,5},{8,10},{9,11},{10,... | collective-permute-start | bytes 368648 | tf_op jit(solution)/shard_map/ppermute | solution.py:493
  74.7 11.9 %collective-permute-start.19 = (bf16[80,768]{1,0:T(8,128)(2,1)S(1)}, bf16[80,768]{1,0:T(8,128)(2,1)S(1)}, u32[]{:S(2)}, u32[]{:S(2)}) collective-permute-start(bf16[80,768]{1,0:T(8,128)(2,1)S(1)} %get-tuple-element.103), channel_id=1, source_target_pairs={{0,3},{1,2},{2,1},{3,0},{4,7},{5,6},{6,5},{7,4},{8,11},{9,10},{10,... | collective-permute-start | bytes 368648 | tf_op jit(solution)/shard_map/ppermute | solution.py:493
  76.6 6.2 %copy-start.1 = (f32[2,96,3072]{2,1,0:T(8,128)S(1)}, f32[2,96,3072]{2,1,0:T(8,128)}, u32[]{:S(2)}) copy-start(f32[2,96,3072]{2,1,0:T(8,128)} %copy-done) | copy-start | bytes 7077892
  82.8 6.4 %collective-permute-start.24 = (bf16[4,112,768]{2,1,0:T(8,128)(2,1)}, bf16[4,112,768]{2,1,0:T(8,128)(2,1)}, u32[]{:S(2)}, u32[]{:S(2)}) collective-permute-start(bf16[4,112,768]{2,1,0:T(8,128)(2,1)} %get-tuple-element.109.refs_8_), channel_id=1, source_target_pairs={{0,4},{4,0},{8,12},{12,8},{16,20},{20,16},{24,28},{28,24},{1,5},{5... | collective-permute-start | bytes 2064392 | tf_op jit(solution)/shard_map/ppermute | solution.py:493
  85.0 24.7 %collective-permute-start.28 = (bf16[96,3072]{1,0:T(8,128)(2,1)}, bf16[96,3072]{1,0:T(8,128)(2,1)}, u32[]{:S(2)}, u32[]{:S(2)}) collective-permute-start(bf16[96,3072]{1,0:T(8,128)(2,1)} %get-tuple-element.127), channel_id=1, source_target_pairs={{0,16},{4,12},{8,24},{12,4},{16,0},{20,28},{24,8},{28,20},{1,17},{... | collective-permute-start | bytes 1769480 | tf_op jit(solution)/shard_map/ppermute | solution.py:499
  86.8 5.0 %collective-permute-start.21 = (bf16[64,768]{1,0:T(8,128)(2,1)S(1)}, bf16[64,768]{1,0:T(8,128)(2,1)S(1)}, u32[]{:S(2)}, u32[]{:S(2)}) collective-permute-start(bf16[64,768]{1,0:T(8,128)(2,1)S(1)} %get-tuple-element.112.refs_0_), channel_id=1, source_target_pairs={{0,1},{1,0},{2,3},{3,2},{4,5},{5,4},{6,7},{7,6},{8,9},{9,8},{10,11... | collective-permute-start | bytes 294920 | tf_op jit(solution)/shard_map/ppermute | solution.py:493
  88.2 1.2 %collective-permute-start.25 = (f32[16,768]{1,0:T(8,128)S(1)}, f32[16,768]{1,0:T(8,128)S(1)}, u32[]{:S(2)}, u32[]{:S(2)}) collective-permute-start(f32[16,768]{1,0:T(8,128)S(1)} %get-tuple-element.114.refs_2_), channel_id=1, source_target_pairs={{0,4},{4,0},{8,12},{12,8},{16,20},{20,16},{24,28},{28,24},{1,5},{5... | collective-permute-start | bytes 147464 | tf_op jit(solution)/shard_map/ppermute | solution.py:493
  93.0 14.7 %collective-permute-start.26 = (bf16[2,112,768]{2,1,0:T(8,128)(2,1)S(1)}, bf16[2,112,768]{2,1,0:T(8,128)(2,1)S(1)}, u32[]{:S(2)}, u32[]{:S(2)}) collective-permute-start(bf16[2,112,768]{2,1,0:T(8,128)(2,1)S(1)} %get-tuple-element.116), channel_id=1, source_target_pairs={{0,8},{4,20},{8,0},{12,28},{16,24},{20,4},{24,16},{28,12},{1,9},{5... | collective-permute-start | bytes 1032200 | tf_op jit(solution)/shard_map/ppermute | solution.py:499
  94.2 14.0 %collective-permute-start.9 = (bf16[128,768]{1,0:T(8,128)(2,1)S(1)}, bf16[128,768]{1,0:T(8,128)(2,1)S(1)}, u32[]{:S(2)}, u32[]{:S(2)}) collective-permute-start(bf16[128,768]{1,0:T(8,128)(2,1)S(1)} %output_pair.1.refs_0_.refs_4_), channel_id=1, source_target_pairs={{0,1},{1,0},{2,3},{3,2},{4,5},{5,4},{6,7},{7,6},{8,9},{9,8},{10,11... | collective-permute-start | bytes 589832 | tf_op jit(solution)/shard_map/ppermute | solution.py:493
  95.7 7.4 %collective-permute-start.22 = (bf16[64,768]{1,0:T(8,128)(2,1)S(1)}, bf16[64,768]{1,0:T(8,128)(2,1)S(1)}, u32[]{:S(2)}, u32[]{:S(2)}) collective-permute-start(bf16[64,768]{1,0:T(8,128)(2,1)S(1)} %get-tuple-element.112.refs_0_), channel_id=1, source_target_pairs={{0,2},{1,3},{2,0},{3,1},{4,6},{5,7},{6,4},{7,5},{8,10},{9,11},{10,... | collective-permute-start | bytes 294920 | tf_op jit(solution)/shard_map/ppermute | solution.py:493
  97.2 10.5 %collective-permute-start.23 = (bf16[64,768]{1,0:T(8,128)(2,1)S(1)}, bf16[64,768]{1,0:T(8,128)(2,1)S(1)}, u32[]{:S(2)}, u32[]{:S(2)}) collective-permute-start(bf16[64,768]{1,0:T(8,128)(2,1)S(1)} %get-tuple-element.112.refs_0_), channel_id=1, source_target_pairs={{0,3},{1,2},{2,1},{3,0},{4,7},{5,6},{6,5},{7,4},{8,11},{9,10},{10,... | collective-permute-start | bytes 294920 | tf_op jit(solution)/shard_map/ppermute | solution.py:493
  107.7 5.5 %collective-permute-start.27 = (bf16[112,768]{1,0:T(8,128)(2,1)S(1)}, bf16[112,768]{1,0:T(8,128)(2,1)S(1)}, u32[]{:S(2)}, u32[]{:S(2)}) collective-permute-start(bf16[112,768]{1,0:T(8,128)(2,1)S(1)} %get-tuple-element.118), channel_id=1, source_target_pairs={{0,16},{4,12},{8,24},{12,4},{16,0},{20,28},{24,8},{28,20},{1,17},{... | collective-permute-start | bytes 516104 | tf_op jit(solution)/shard_map/ppermute | solution.py:499

commit v3 on v2

--- a/solution.py
+++ b/solution.py
@@ -1,4 +1,5 @@
 import functools
+import math
 
 import jax
 import jax.numpy as jnp
@@ -14,13 +15,15 @@
 SMALL_ROWS = 16
 TABLE_ROW = 2 + EXPERTS
 WEIGHTS = {
+    "fetch": 20,
     "expert": 5,
-    "expert_grads": 400,
-    "hidden_back": 1000,
-    "expert_merge": 400,
-    "attention_back": 1000,
-    "weight_grads": 12,
-    "input_back": 1000,
+    "expert_grads": 20,
+    "hidden_back": 60,
+    "expert_merge": 20,
+    "attention_back": 60,
+    "weight_grads": 4,
+    "output_share": 8,
+    "input_back": 60,
     "expert_final": 1,
     "weight_final": 1,
 }
@@ -146,26 +149,39 @@
     copies[8].wait()
     acc[...] = dot(mixed, wo[...])
     put_shares(acc, outs[:members])
-
-
-def hidden_kernel(members, inputs, gain, *rest):
-    parts = rest[:members]
+    own = share_of(lax.axis_index("tensor"), outs[0].shape[0])
+    outs[0][...] += inputs[own, :].astype(F32)
+
+
+def hidden_kernel(members, gain, *rest):
     hidden_o, normed_o = rest[members:]
-    share = hidden_o.shape[0]
-    x = inputs[share_of(lax.axis_index("tensor"), share), :].astype(F32)
-    hidden = x + total_of(parts)
+    hidden = total_of(rest[:members])
     hidden_o[...] = hidden
     normed_o[...] = (hidden * inverse_rms(hidden) * gain[...]).astype(BF16)
+
+
+def fetch_kernel(up, down, up_o, down_o, sems):
+    copies = [
+        pltpu.make_async_copy(up, up_o, sems.at[0]),
+        pltpu.make_async_copy(down, down_o, sems.at[1]),
+    ]
+    for copy in copies:
+        copy.start()
+    for copy in copies:
+        copy.wait()
 
 
 def expert_kernel(members, where_to, cotangent, router_t, up, down, *rest):
     pieces = rest[:members]
     rest = rest[members:]
     back_o, row_o = rest[:members], rest[members : members + 2]
-    buffer_o, active_o, grad_before_o, grad_expert_o, router_o = rest[members + 2 : members + 7]
-    normed, backs, rows, acc = rest[members + 7 :]
+    buffer_o, active_o, grad_before_o, grad_expert_o, router_o, dy_o = rest[
+        members + 2 : members + 8
+    ]
+    normed, backs, rows, acc = rest[members + 8 :]
     length = cotangent.shape[0]
     assemble(normed, pieces)
+    dy_o[...] = cotangent[share_of(lax.axis_index("tensor"), dy_o.shape[0]), :]
     place = (
         lax.broadcasted_iota(jnp.int32, (EXPERTS * CAP, length), 0) == where_to[...]
     ).astype(BF16)
@@ -261,24 +277,42 @@
             ref[k] = total.astype(ref.dtype)
 
 
-def merge_small_kernel(kept, came, small, small_came, keep, send):
-    merge_kernel(kept, came, keep, send)
-    total = small[...] + small_came[...]
-    first = kept.shape[1] - SMALL_ROWS
-    rows = slice(first, first + TABLE_ROW)
-    for ref in (keep, send):
-        for k in range(2):
-            ref[k, rows, 0 : total.shape[1]] = total[0:TABLE_ROW].astype(ref.dtype)
-
-
-def merge_two_kernel(kept, came, keep, send):
-    keep[...] = kept[0] + came[0].astype(F32)
-    send[...] = (kept[1] + came[1].astype(F32)).astype(BF16)
+def add_kernel(one, other, out):
+    out[...] = one[...] + other[...]
+
+
+def cross_kernel(kept, came, weight_kept, weight_came, own, send, weight_keep):
+    rows, columns = own.shape
+    own[...] = kept[0] + came[0].astype(F32)
+    send[0:rows, :] = (kept[1] + came[1].astype(F32)).astype(BF16)
+    chip = lax.div(lax.axis_index("dp"), 2)
+    second, first = chip_bits()
+    width = weight_keep.shape[2]
+    half = rows // 2
+    for k in range(2):
+        mine = jnp.bitwise_xor(chip, k * second)
+        weight_keep[k] = weight_kept[mine].astype(F32) + weight_came[mine].astype(F32)
+        there = jnp.bitwise_xor(mine, first)
+        total = (weight_kept[there].astype(F32) + weight_came[there].astype(F32)).astype(BF16)
+        for i in range(2):
+            at = (2 * k + i) * width
+            send[rows : rows + half, at : at + width] = total[i * half : (i + 1) * half]
+
+
+def weight_cross_kernel(kept, came, own, send):
+    rows, width = own.shape
+    half = rows // 2
+    for k, ref in enumerate((own, send)):
+        for i in range(2):
+            at = (2 * k + i) * width
+            arrived = came[rows : rows + half, at : at + width].astype(F32)
+            part = slice(i * half, (i + 1) * half)
+            ref[part, :] = (kept[k, part, :] + arrived).astype(ref.dtype)
 
 
 def expert_final_kernel(*refs):
     up_o, down_o = refs[2:]
-    total = total_of(refs[:2])
+    total = refs[0][...] + refs[1][0 : refs[0].shape[0], :].astype(F32)
     for e in range(EXPERTS):
         width = up_o.shape[2]
         first = 2 * e * width
@@ -315,12 +349,12 @@
     assemble(refs[-1], refs[:-1])
 
 
-def hidden_back_kernel(members, hidden, cotangent, gain, *rest):
+def hidden_back_kernel(members, hidden, cotangent, gain, rows, *rest):
     parts = rest[:members]
-    grad_o, low_o, gain_o = rest[members:]
-    share = hidden.shape[0]
+    grad_o, low_o, gain_o, rows_o = rest[members:]
+    rows_o[...] = rows[...]
     h = hidden[...]
-    dy = cotangent[share_of(lax.axis_index("tensor"), share), :].astype(F32)
+    dy = cotangent[...].astype(F32)
     r = inverse_rms(h)
     grad_normed = total_of(parts)
     z = grad_normed * gain[...]
@@ -412,30 +446,27 @@
         )[0:1]
     if not split:
         rest[0][...] = scratch[...]
-        rest[1][...] = small[...]
         return
     keep, send = rest[0], rest[1]
-    chips, rows, _ = keep.shape
-    part = rows - SMALL_ROWS
+    chips, part, _ = keep.shape
     for chip in range(chips):
         mine, other = split_rows(keep, send, chip, part)
-        keep[chip, 0:part, :] = scratch[mine, :].astype(BF16)
-        send[chip, 0:part, :] = scratch[other, :].astype(BF16)
-        keep[chip, part:rows, :] = small[...].astype(BF16)
-        send[chip, part:rows, :] = small[...].astype(BF16)
-
-
-def weight_final_kernel(members, *refs):
-    wq_o, wk_o, wv_o, wo_o, table_o, one_o, two_o, router_o = refs[2:]
+        keep[chip] = scratch[mine, :].astype(BF16)
+        send[chip] = scratch[other, :].astype(BF16)
+
+
+def weight_final_kernel(*refs):
+    wq_o, wk_o, wv_o, wo_o = refs[2:]
     total = total_of(refs[:2])
     part, cols = wq_o.shape
     wq_o[...] = total[0:part, 0:cols]
     wk_o[...] = total[0:part, cols : 2 * cols]
     wv_o[...] = total[0:part, 2 * cols : 3 * cols]
     wo_o[...] = total[0:part, 3 * cols : 4 * cols].T
-    small = total[part:, :]
-    heads, bucket_count = table_o.shape
-    table_o[...] = small[TABLE_ROW : TABLE_ROW + heads, 0:bucket_count]
+
+
+def small_final_kernel(members, one, other, one_o, two_o, router_o, table_o):
+    small = one[...] + other[...]
     per = one_o.shape[1]
     first = (lax.axis_index("dp") * members + lax.axis_index("tensor")) * per
     shape = (per, small.shape[1])
@@ -447,36 +478,40 @@
     one_o[...] = rows[0:1]
     two_o[...] = rows[1:2]
     router_o[...] = rows[2:TABLE_ROW]
-
-
-def input_back_kernel(members, inputs, gain, grad_hidden, *rest):
+    heads, bucket_count = table_o.shape
+    table_o[...] = small[TABLE_ROW : TABLE_ROW + heads, 0:bucket_count]
+
+
+def input_back_kernel(members, inputs, gain, grad_hidden, table, *rest):
     out, small_o = rest[members:]
     share = out.shape[0]
     x = inputs[share_of(lax.axis_index("tensor"), share), :].astype(F32)
     r = inverse_rms(x)
     total = total_of(rest[:members])
-    small_o[...] = total[share:]
+    small_o[...] = total[share : share + small_o.shape[0]] + table[...]
     z = total[0:share] * gain[...]
     out[...] = (
         grad_hidden[...] + r * z - x * (r * r * r) * jnp.mean(z * x, axis=-1, keepdims=True)
     ).astype(BF16)
 
 
-def run(kernel, outs, args, scratch=(), name=None, after=(), space=pltpu.VMEM):
+def run(kernel, outs, args, scratch=(), name=None, after=(), space=pltpu.VMEM, out=pltpu.VMEM):
     vmem = pl.BlockSpec(memory_space=pltpu.VMEM)
     anywhere = pl.BlockSpec(memory_space=pl.ANY)
     count, extra = len(args), len(after)
+    held = [*args, *outs, *(x for x in scratch if x.memory_space == pltpu.VMEM)]
+    size = sum(math.prod(x.shape) * jnp.dtype(x.dtype).itemsize for x in held)
 
     def body(*refs):
         kernel(*refs[:count], *refs[count + extra :])
 
     return pl.pallas_call(
         body,
-        out_shape=outs,
+        out_shape=[out(o.shape, o.dtype) for o in outs] if out else outs,
         in_specs=[pl.BlockSpec(memory_space=space)] * count + [anywhere] * extra,
         out_specs=[vmem] * len(outs),
         scratch_shapes=list(scratch),
-        compiler_params=pltpu.CompilerParams(vmem_limit_bytes=48 * 1024 * 1024),
+        compiler_params=pltpu.CompilerParams(vmem_limit_bytes=size + size // 4 + 4 * 1024 * 1024),
         cost_estimate=pl.CostEstimate(
             flops=int(WEIGHTS.get(name, 0.2) * 1e9), bytes_accessed=0, transcendentals=0
         ),
@@ -583,8 +618,17 @@
     hidden, normed_two = run(
         bind(hidden_kernel, members),
         [sds((share, width), F32), sds((share, width), BF16)],
-        [inputs, gain_two_row] + attended,
+        [gain_two_row] + attended,
         name="hidden",
+    )
+    up, down = run(
+        fetch_kernel,
+        [sds(expert_up.shape, BF16), sds(expert_down.shape, BF16)],
+        [pltpu.with_memory_space_constraint(a, pltpu.HBM) for a in (expert_up, expert_down)],
+        [pltpu.SemaphoreType.DMA((2,))],
+        name="fetch",
+        space=pltpu.HBM,
+        after=[normed_two],
     )
     normed_two = spread(normed_two)
 
@@ -595,8 +639,8 @@
         + [sds((2 * share, width), BF16)] * 2
         + [sds((slots, width), BF16)]
         + [sds((slots, hidden_units), BF16)] * 2
-        + [sds((slots, width), BF16), sds((EXPERTS, width), F32)],
-        [where_to, cotangent, router_t, expert_up, expert_down] + normed_two,
+        + [sds((slots, width), BF16), sds((EXPERTS, width), F32), sds((share, width), BF16)],
+        [where_to, cotangent, router_t, up, down] + normed_two,
         [
             pltpu.VMEM((length, width), BF16),
             pltpu.VMEM((slots, width), BF16),
@@ -607,23 +651,13 @@
     )
     back_rows = exchange(outs[:members])
     rows_kept, rows_sent = outs[members : members + 2]
-    buffer, active, grad_before, grad_expert, grad_router = outs[members + 2 :]
+    buffer, active, grad_before, grad_expert, grad_router, dy_share = outs[members + 2 :]
 
     def split_sds(rows, columns):
         return [sds((chips, rows, columns), BF16)] * 2
 
     def merge_sds(rows, columns):
         return [sds((2, rows, columns), F32), sds((2, rows, columns), BF16)]
-
-    def merge_two(merged, name, after=()):
-        rows, columns = merged[0].shape[1:]
-        return run(
-            merge_two_kernel,
-            [sds((rows, columns), F32), sds((rows, columns), BF16)],
-            [merged[0], swap_chips(merged[1], 2, 4)],
-            name=name,
-            after=after,
-        )
 
     expert_grads = run(
         bind(expert_grad_kernel, split),
@@ -633,26 +667,22 @@
         name="expert_grads",
     )
 
+    grad_hidden, grad_attended, grad_gain_expert, rows_sent = run(
+        bind(hidden_back_kernel, members),
+        [sds((share, width), F32), sds((share, width), BF16), sds((1, width), F32)]
+        + [sds((2 * share, width), BF16)],
+        [hidden, dy_share, gain_two_row, rows_sent] + back_rows,
+        name="hidden_back",
+        after=expert_grads[-1:],
+    )
+    grad_attended = spread(grad_attended)
+
     own_rows, other_rows = run(
         pair_sum_kernel,
         [sds((share, width), F32), sds((share, width), BF16)],
         [rows_kept, swap(rows_sent, "tensor", 1)],
         name="pair_sum",
-    )
-    grad_hidden, grad_attended, grad_gain_expert = run(
-        bind(hidden_back_kernel, members),
-        [sds((share, width), F32), sds((share, width), BF16), sds((1, width), F32)],
-        [hidden, cotangent, gain_two_row] + back_rows,
-        name="hidden_back",
-        after=[own_rows, *expert_grads[-1:]],
-    )
-    grad_attended = spread(grad_attended)
-
-    (output_share,) = run(
-        output_kernel,
-        [sds((share, width), BF16)],
-        [hidden, own_rows, swap(other_rows, "tensor", 2)],
-        name="output_share",
+        after=[grad_attended[0]],
     )
     expert_merged = []
     if split:
@@ -662,7 +692,7 @@
             [expert_grads[0], swap(expert_grads[1], "dp", 1)],
             name="expert_merge",
         )
-    expert_halves = []
+    crossed = []
 
     def tall_sds(dtype):
         return sds((share + SMALL_ROWS, width), dtype)
@@ -681,7 +711,7 @@
         + grad_attended,
         [pltpu.VMEM((length, width), F32)],
         name="attention_back",
-        after=expert_merged[:1],
+        after=[own_rows, *expert_merged[:1]],
     )
     grad_normed = exchange(outs[:members])
     projections, attended_low, grad_scores = outs[members:]
@@ -689,80 +719,103 @@
     weight_cols = 4 * cols
     weight_grads = run(
         bind(weight_grad_kernel, split),
-        split_sds(part + SMALL_ROWS, weight_cols)
-        if split
-        else [sds((width, weight_cols), F32), sds((SMALL_ROWS, weight_cols), F32)],
+        (split_sds(part, weight_cols) if split else [sds((width, weight_cols), F32)])
+        + [sds((8, width), F32)],
         [normed, projections, attended_low, mixed, grad_scores, bucket_wide],
-        [pltpu.VMEM((SMALL_ROWS, weight_cols), F32), pltpu.VMEM((width, weight_cols), F32)],
+        [pltpu.VMEM((width, weight_cols), F32)],
         name="weight_grads",
     )
 
+    (output_share,) = run(
+        output_kernel,
+        [sds((share, width), BF16)],
+        [hidden, own_rows, swap(other_rows, "tensor", 2)],
+        name="output_share",
+        after=weight_grads[-1:],
+    )
     if split:
-        expert_halves = merge_two(expert_merged, "expert_merge_two")
+        expert_own, crossing, weight_kept = run(
+            cross_kernel,
+            [
+                sds((part, 4 * hidden_units), F32),
+                sds((part + part // 2, 4 * hidden_units), BF16),
+                sds((2, part, weight_cols), F32),
+            ],
+            [
+                expert_merged[0],
+                swap_chips(expert_merged[1], 2, 4),
+                weight_grads[0],
+                swap(weight_grads[1], "dp", 1),
+            ],
+            name="cross",
+            after=[output_share],
+        )
+        crossed = [expert_own]
     grad_inputs, small = run(
         bind(input_back_kernel, members),
-        [sds((share, width), BF16), sds((SMALL_ROWS, width), F32)],
-        [inputs, gain_row, grad_hidden] + grad_normed,
+        [sds((share, width), BF16), sds((8, width), F32)],
+        [inputs, gain_row, grad_hidden, weight_grads[-1]] + grad_normed,
         name="input_back",
-        after=[output_share, *weight_grads[-1:], *expert_halves[:1]],
+        after=crossed,
     )
     (output_pair,) = run(
         pair_kernel,
         [sds((2 * share, width), BF16)],
         [output_share, swap(output_share, "tensor", 2)],
         name="output_pair",
+        after=[small],
     )
     (output,) = run(
         pair_rows_kernel,
         [sds((length, width), BF16)],
         [output_pair, swap(output_pair, "tensor", 1)],
         name="output_rows",
+        out=None,
     )
 
 
     input_parts = spread(grad_inputs)
     (grad_inputs,) = run(
-        gather_kernel, [sds((length, width), BF16)], input_parts, name="grad_rows"
+        gather_kernel, [sds((length, width), BF16)], input_parts, name="grad_rows", out=None
     )
 
     if split:
+        crossing = swap_chips(crossing, 4, 2)
         grad_expert_up, grad_expert_down = run(
             expert_final_kernel,
             [sds((EXPERTS, part, hidden_units), F32), sds((EXPERTS, part, hidden_units), F32)],
-            [expert_halves[0], swap_chips(expert_halves[1], 4, 2)],
-            name="expert_final",
+            [expert_own, crossing],
+            name="expert_final", out=None,
         )
         grad_expert_down = grad_expert_down.transpose(0, 2, 1)
-        merged = run(
-            merge_small_kernel,
-            merge_sds(part + SMALL_ROWS, weight_cols),
-            [
-                weight_grads[0],
-                swap(weight_grads[1], "dp", 1),
-                small,
-                swap(small, "dp", 1),
-            ],
-            name="weight_merge",
-            after=[output_pair, input_parts[1]],
+        weight_own, weight_sent = run(
+            weight_cross_kernel,
+            [sds((part, weight_cols), F32), sds((part, weight_cols), BF16)],
+            [weight_kept, crossing],
+            name="weight_cross",
         )
-        merged = merge_two(merged, "weight_merge_two", after=input_parts[2:])
+        (grad_query_weight, grad_key_weight, grad_value_weight, grad_out_weight) = run(
+            weight_final_kernel,
+            [sds((part, cols), F32)] * 3 + [sds((cols, part), F32)],
+            [weight_own, swap_chips(weight_sent, 2, 4)],
+            name="weight_final", out=None,
+        )
+        for step in range(2):
+            came = swap(small, "dp", 1) if step == 0 else swap_chips(small, 2, 4)
+            (small,) = run(
+                add_kernel,
+                [sds(small.shape, F32)],
+                [small, came],
+                name="small_sum",
+                after=input_parts[2:] if step == 1 else input_parts[1:2],
+            )
         per = part // members
-        (
-            grad_query_weight,
-            grad_key_weight,
-            grad_value_weight,
-            grad_out_weight,
-            grad_table,
-            grad_gain_attn,
-            grad_gain_expert,
-            grad_router,
-        ) = run(
-            bind(weight_final_kernel, members),
-            [sds((part, cols), F32)] * 3
-            + [sds((cols, part), F32), sds((heads, bucket_count), F32)]
-            + [sds((1, per), F32), sds((1, per), F32), sds((EXPERTS, per), F32)],
-            [merged[0], swap_chips(merged[1], 4, 2)],
-            name="weight_final",
+        grad_gain_attn, grad_gain_expert, grad_router, grad_table = run(
+            bind(small_final_kernel, members),
+            [sds((1, per), F32), sds((1, per), F32), sds((EXPERTS, per), F32)]
+            + [sds((heads, bucket_count), F32)],
+            [small, swap_chips(small, 4, 2)],
+            name="small_final", out=None,
         )
         grad_table = grad_table.T
         grad_router = grad_router.T
@@ -780,12 +833,12 @@
         grads = expert_grads[0].reshape(width, EXPERTS, 2, hidden_units)
         grad_expert_up = scatter(grads[:, :, 0].transpose(1, 0, 2), "dp", 1)
         grad_expert_down = scatter(grads[:, :, 1].transpose(1, 2, 0), "dp", 2)
-        grads, table_rows = weight_grads
+        grads = weight_grads[0]
         grad_query_weight = scatter(grads[:, 0:cols], "dp", 0)
         grad_key_weight = scatter(grads[:, cols : 2 * cols], "dp", 0)
         grad_value_weight = scatter(grads[:, 2 * cols : 3 * cols], "dp", 0)
         grad_out_weight = scatter(grads[:, 3 * cols :].T, "dp", 1)
-        grad_table = lax.psum(table_rows[TABLE_ROW : TABLE_ROW + heads, :bucket_count].T, "dp")
+        grad_table = lax.psum(small[TABLE_ROW : TABLE_ROW + heads, :bucket_count].T, "dp")
         grad_gain_attn = pick(small[0])
         grad_gain_expert = pick(small[1])
         grad_router = pick(small[2:TABLE_ROW].T)

time: 115 us -> 96.2 us (0.84)
  Pallas kernels: 36.8 us -> 21.7 us
  starting transfers between devices: 36.8 us -> 43.8 us
  local copies, waits for them, and re-layouts: 6.49 us -> 0.74 us
  waiting for transfers between devices: 33 us -> 28.1 us
    pallas_call x19 -> x22, Pallas kernels: 36.8 us -> 21.7 us  [run(): pl.pallas_call(body, out_shape=[out(o.shape, o.dtype) for o in outs] if o...]
    unnamed x36 -> x18, local copies, waits for them, and re-layouts: 5.79 us -> 0.04 us
    ppermute x4 -> x5, waiting for transfers between devices: 4.8 us -> 0.83 us  [swap_chips(): return lax.ppermute(values, 'dp', pairs)]
    ppermute x25, starting transfers between devices: 32 us -> 35.9 us  [swap(): return lax.ppermute(values, axis, [(i, i ^ k) for i in range(size)])]
    ppermute x4 -> x5, starting transfers between devices: 4.81 us -> 7.86 us  [swap_chips(): return lax.ppermute(values, 'dp', pairs)]
  transfers between devices with their start and end apart: 29 -> 30, of which waited for: 11 -> 11; matrix products, arithmetic and copies ran while one was open for 1% -> 1% of each run, Pallas kernels for 23% -> 14%
where the time goes in v3:
time: 96.2 us; the launch traced here: 95.9 us
  starting transfers between devices  43.8 us (46%)
  waiting for transfers between devices  28.1 us (29%)
  Pallas kernels  21.7 us (23%)
    ppermute x25, starting transfers between devices, swap(): return lax.ppermute(values, axis, [(i, i ^ k) for i in range(size)])  35.9 us
    ppermute x25, waiting for transfers between devices, swap(): return lax.ppermute(values, axis, [(i, i ^ k) for i in range(size)])  27.3 us
    pallas_call x22, Pallas kernels, run(): pl.pallas_call(body, out_shape=[out(o.shape, o.dtype) for o in outs] if o...  21.7 us
    ppermute x5, starting transfers between devices, swap_chips(): return lax.ppermute(values, 'dp', pairs)  7.86 us
  transfers between devices with their start and end apart: 30, of which 11 were waited for; matrix products, arithmetic and copies ran while one was open for 1% of the time, Pallas kernels for 14%

profile of v3, /device:TPU:0, one launch (start us, length us, event | category | flops | bytes accessed | tf_op | source)
XLA Modules:
  0.0 95.9 jit_solution(752211297409964720)
XLA Ops:
  0.6 3.4 %attention.1 = (f32[64,768]{1,0:T(8,128)S(1)}, bf16[64,768]{1,0:T(8,128)(2,1)S(1)}, bf16[64,768]{1,0:T(8,128)(2,1)S(1)}, bf16[64,768]{1,0:T(8,128)(2,1)S(1)}, bf...) custom-call(bf16[256,768]{1,0:T(8,128)(2,1)} %refs_0_.7, ...), custom_call_target="tpu_custom_call" | custom-call | flops 200000000 | tf_op jit(solution)/shard_map/attention/pallas_call | solution.py:508
  4.1 3.1 %collective-permute-start = (bf16[64,768]{1,0:T(8,128)(2,1)S(1)}, bf16[64,768]{1,0:T(8,128)(2,1)S(1)}, u32[]{:S(2)}, u32[]{:S(2)}) collective-permute-start(bf16[64,768]{1,0:T(8,128)(2,1)S(1)} %get-tuple-element.76), channel_id=1, source_target_pairs={{0,1},{1,0},{2,3},{3,2},{4,5},{5,4},{6,7},{7,6},{8,9},{9,8},{10,11... | collective-permute-start | bytes 294920 | tf_op jit(solution)/shard_map/ppermute | solution.py:528
  7.2 2.6 %collective-permute-start.1 = (bf16[64,768]{1,0:T(8,128)(2,1)S(1)}, bf16[64,768]{1,0:T(8,128)(2,1)S(1)}, u32[]{:S(2)}, u32[]{:S(2)}) collective-permute-start(bf16[64,768]{1,0:T(8,128)(2,1)S(1)} %get-tuple-element.77), channel_id=1, source_target_pairs={{0,2},{1,3},{2,0},{3,1},{4,6},{5,7},{6,4},{7,5},{8,10},{9,11},{10,... | collective-permute-start | bytes 294920 | tf_op jit(solution)/shard_map/ppermute | solution.py:528
  9.8 0.0 collective-permute-start.2
  9.8 0.7 multiply_add_fusion
  10.5 0.7 reshape.42.refs_0_.refs_2_
  11.2 6.4 %collective-permute-done.1.refs_3_ = bf16[64,768]{1,0:T(8,128)(2,1)S(1)} collective-permute-done((bf16[64,768]{1,0:T(8,128)(2,1)S(1)}, bf16[64,768]{1,0:T(8,128)(2,1)S(1)}, u32[]{:S(2)}, u32[]{:S(2)}) %collective-permute-start.1) | collective-permute-done | bytes 98336 | tf_op jit(solution)/shard_map/ppermute | solution.py:528
  17.6 0.1 hidden.1
  17.8 0.0 copy-start.5
  17.8 0.0 copy-start.6
  17.8 1.7 %collective-permute-start.3 = (bf16[64,768]{1,0:T(8,128)(2,1)S(1)}, bf16[64,768]{1,0:T(8,128)(2,1)S(1)}, u32[]{:S(2)}, u32[]{:S(2)}) collective-permute-start(bf16[64,768]{1,0:T(8,128)(2,1)S(1)} %get-tuple-element.80.refs_2_.refs_5_), channel_id=1, source_target_pairs={{0,1},{1,0},{2,3},{3,2},{4,5},{5,4},{6,7},{7,6},{8,9},{9,8},{10,11... | collective-permute-start | bytes 294920 | tf_op jit(solution)/shard_map/ppermute | solution.py:528
  19.5 1.4 %collective-permute-start.4 = (bf16[64,768]{1,0:T(8,128)(2,1)S(1)}, bf16[64,768]{1,0:T(8,128)(2,1)S(1)}, u32[]{:S(2)}, u32[]{:S(2)}) collective-permute-start(bf16[64,768]{1,0:T(8,128)(2,1)S(1)} %get-tuple-element.80.refs_2_.refs_5_), channel_id=1, source_target_pairs={{0,2},{1,3},{2,0},{3,1},{4,6},{5,7},{6,4},{7,5},{8,10},{9,11},{10,... | collective-permute-start | bytes 294920 | tf_op jit(solution)/shard_map/ppermute | solution.py:528
  20.9 1.3 %collective-permute-start.5 = (bf16[64,768]{1,0:T(8,128)(2,1)S(1)}, bf16[64,768]{1,0:T(8,128)(2,1)S(1)}, u32[]{:S(2)}, u32[]{:S(2)}) collective-permute-start(bf16[64,768]{1,0:T(8,128)(2,1)S(1)} %get-tuple-element.80.refs_2_.refs_5_), channel_id=1, source_target_pairs={{0,3},{1,2},{2,1},{3,0},{4,7},{5,6},{6,5},{7,4},{8,11},{9,10},{10,... | collective-permute-start | bytes 294920 | tf_op jit(solution)/shard_map/ppermute | solution.py:528
  22.2 2.4 %fetch.1 = (bf16[2,768,768]{2,1,0:T(8,128)(2,1)S(1)}, bf16[2,768,768]{2,1,0:T(8,128)(2,1)S(1)}) custom-call(bf16[2,768,768]{2,1,0:T(8,128)(2,1)} %refs_0_.5, bf16[2,768,768]{2,1,0:T(8,128)(2,1)} %refs_1_.4, bf16[64,768]{1,0:T(8,128)(2,1)S(1)} %get-tuple-element.80.refs_2_.refs_5_), custom_call_target="tpu_custom_call" | custom-call | flops 20000000000 | tf_op jit(solution)/shard_map/fetch/pallas_call | solution.py:508
  24.6 4.1 %collective-permute-done.4.refs_7_ = bf16[64,768]{1,0:T(8,128)(2,1)S(1)} collective-permute-done((bf16[64,768]{1,0:T(8,128)(2,1)S(1)}, bf16[64,768]{1,0:T(8,128)(2,1)S(1)}, u32[]{:S(2)}, u32[]{:S(2)}) %collective-permute-start.4) | collective-permute-done | bytes 98336 | tf_op jit(solution)/shard_map/ppermute | solution.py:528
  28.7 3.7 %expert.1 = (bf16[64,768]{1,0:T(8,128)(2,1)S(1)}, bf16[64,768]{1,0:T(8,128)(2,1)S(1)}, bf16[64,768]{1,0:T(8,128)(2,1)S(1)}, bf16[64,768]{1,0:T(8,128)(2,1)S(1)},...) custom-call(s32[1,256]{1,0:T(1,128)S(1)} %bitcast.18, ...), custom_call_target="tpu_custom_call" | custom-call | flops 5000000000 | tf_op jit(solution)/shard_map/expert/pallas_call | solution.py:508
  32.4 1.7 %collective-permute-start.6 = (bf16[64,768]{1,0:T(8,128)(2,1)S(1)}, bf16[64,768]{1,0:T(8,128)(2,1)S(1)}, u32[]{:S(2)}, u32[]{:S(2)}) collective-permute-start(bf16[64,768]{1,0:T(8,128)(2,1)S(1)} %get-tuple-element.87), channel_id=1, source_target_pairs={{0,1},{1,0},{2,3},{3,2},{4,5},{5,4},{6,7},{7,6},{8,9},{9,8},{10,11... | collective-permute-start | bytes 294920 | tf_op jit(solution)/shard_map/ppermute | solution.py:528
  34.1 1.1 %collective-permute-start.7 = (bf16[64,768]{1,0:T(8,128)(2,1)S(1)}, bf16[64,768]{1,0:T(8,128)(2,1)S(1)}, u32[]{:S(2)}, u32[]{:S(2)}) collective-permute-start(bf16[64,768]{1,0:T(8,128)(2,1)S(1)} %get-tuple-element.88), channel_id=1, source_target_pairs={{0,2},{1,3},{2,0},{3,1},{4,6},{5,7},{6,4},{7,5},{8,10},{9,11},{10,... | collective-permute-start | bytes 294920 | tf_op jit(solution)/shard_map/ppermute | solution.py:528
  35.2 1.7 %collective-permute-start.8 = (bf16[64,768]{1,0:T(8,128)(2,1)S(1)}, bf16[64,768]{1,0:T(8,128)(2,1)S(1)}, u32[]{:S(2)}, u32[]{:S(2)}) collective-permute-start(bf16[64,768]{1,0:T(8,128)(2,1)S(1)} %get-tuple-element.89), channel_id=1, source_target_pairs={{0,3},{1,2},{2,1},{3,0},{4,7},{5,6},{6,5},{7,4},{8,11},{9,10},{10,... | collective-permute-start | bytes 294920 | tf_op jit(solution)/shard_map/ppermute | solution.py:528
  36.9 2.7 %expert_grads.1 = (bf16[4,96,3072]{2,1,0:T(8,128)(2,1)S(1)}, bf16[4,96,3072]{2,1,0:T(8,128)(2,1)S(1)}) custom-call(bf16[288,768]{1,0:T(8,128)(2,1)S(1)} %get-tuple-element.90.refs_0_, bf16[288,768]{1,0:T(8,128)(2,1)S(1)} %get-tuple-element.91.refs_1_, bf16[288,768]{1,0:T(8,128)(2,1)S(1)} %get-tuple-element.92.refs_2_, ...), custom_call_target="tpu_custom_call" | custom-call | flops 20000000000 | tf_op jit(solution)/shard_map/expert_grads/pallas_call | solution.py:508
  39.6 0.1 collective-permute-start.14
  39.7 3.9 %collective-permute-done.7.refs_6_ = bf16[64,768]{1,0:T(8,128)(2,1)S(1)} collective-permute-done((bf16[64,768]{1,0:T(8,128)(2,1)S(1)}, bf16[64,768]{1,0:T(8,128)(2,1)S(1)}, u32[]{:S(2)}, u32[]{:S(2)}) %collective-permute-start.7) | collective-permute-done | bytes 98336 | tf_op jit(solution)/shard_map/ppermute | solution.py:528
  43.6 0.2 hidden_back.1
  43.8 1.7 %collective-permute-start.9 = (bf16[128,768]{1,0:T(8,128)(2,1)S(1)}, bf16[128,768]{1,0:T(8,128)(2,1)S(1)}, u32[]{:S(2)}, u32[]{:S(2)}) collective-permute-start(bf16[128,768]{1,0:T(8,128)(2,1)S(1)} %get-tuple-element.95), channel_id=1, source_target_pairs={{0,1},{1,0},{2,3},{3,2},{4,5},{5,4},{6,7},{7,6},{8,9},{9,8},{10,11... | collective-permute-start | bytes 589832 | tf_op jit(solution)/shard_map/ppermute | solution.py:528
  45.5 0.5 collective-permute-start.11
  46.0 2.6 %collective-permute-start.12 = (bf16[64,768]{1,0:T(8,128)(2,1)S(1)}, bf16[64,768]{1,0:T(8,128)(2,1)S(1)}, u32[]{:S(2)}, u32[]{:S(2)}) collective-permute-start(bf16[64,768]{1,0:T(8,128)(2,1)S(1)} %get-tuple-element.96.refs_2_.refs_11_), channel_id=1, source_target_pairs={{0,2},{1,3},{2,0},{3,1},{4,6},{5,7},{6,4},{7,5},{8,10},{9,11},{10,... | collective-permute-start | bytes 294920 | tf_op jit(solution)/shard_map/ppermute | solution.py:528
  48.5 1.4 %collective-permute-start.13 = (bf16[64,768]{1,0:T(8,128)(2,1)S(1)}, bf16[64,768]{1,0:T(8,128)(2,1)S(1)}, u32[]{:S(2)}, u32[]{:S(2)}) collective-permute-start(bf16[64,768]{1,0:T(8,128)(2,1)S(1)} %get-tuple-element.96.refs_2_.refs_11_), channel_id=1, source_target_pairs={{0,3},{1,2},{2,1},{3,0},{4,7},{5,6},{6,5},{7,4},{8,11},{9,10},{10,... | collective-permute-start | bytes 294920 | tf_op jit(solution)/shard_map/ppermute | solution.py:528
  49.9 2.5 %collective-permute-done.9.refs_1_ = bf16[128,768]{1,0:T(8,128)(2,1)S(1)} collective-permute-done((bf16[128,768]{1,0:T(8,128)(2,1)S(1)}, bf16[128,768]{1,0:T(8,128)(2,1)S(1)}, u32[]{:S(2)}, u32[]{:S(2)}) %collective-permute-start.9) | collective-permute-done | bytes 196640 | tf_op jit(solution)/shard_map/ppermute | solution.py:528
  52.4 2.3 %collective-permute-start.10 = (bf16[64,768]{1,0:T(8,128)(2,1)S(1)}, bf16[64,768]{1,0:T(8,128)(2,1)S(1)}, u32[]{:S(2)}, u32[]{:S(2)}) collective-permute-start(bf16[64,768]{1,0:T(8,128)(2,1)S(1)} %get-tuple-element.98), channel_id=1, source_target_pairs={{0,2},{1,3},{2,0},{3,1},{4,6},{5,7},{6,4},{7,5},{8,10},{9,11},{10,... | collective-permute-start | bytes 294920 | tf_op jit(solution)/shard_map/ppermute | solution.py:528
  54.8 0.0 copy-start.3
  54.8 0.0 copy-start.4
  54.8 0.5 expert_merge.1
  55.3 1.6 %collective-permute-start.19 = (bf16[2,96,3072]{2,1,0:T(8,128)(2,1)S(1)}, bf16[2,96,3072]{2,1,0:T(8,128)(2,1)S(1)}, u32[]{:S(2)}, u32[]{:S(2)}) collective-permute-start(bf16[2,96,3072]{2,1,0:T(8,128)(2,1)S(1)} %get-tuple-element.118), channel_id=1, source_target_pairs={{0,8},{4,20},{8,0},{12,28},{16,24},{20,4},{24,16},{28,12},{1,9},{5... | collective-permute-start | bytes 3538952 | tf_op jit(solution)/shard_map/ppermute | solution.py:534
  56.9 2.8 %collective-permute-done.13.refs_14_ = bf16[64,768]{1,0:T(8,128)(2,1)S(1)} collective-permute-done((bf16[64,768]{1,0:T(8,128)(2,1)S(1)}, bf16[64,768]{1,0:T(8,128)(2,1)S(1)}, u32[]{:S(2)}, u32[]{:S(2)}) %collective-permute-start.13) | collective-permute-done | bytes 98336 | tf_op jit(solution)/shard_map/ppermute | solution.py:528
  59.7 1.8 %attention_back.1 = (f32[80,768]{1,0:T(8,128)S(1)}, bf16[80,768]{1,0:T(8,128)(2,1)S(1)}, bf16[80,768]{1,0:T(8,128)(2,1)S(1)}, bf16[80,768]{1,0:T(8,128)(2,1)S(1)...) custom-call(bf16[256,768]{1,0:T(8,128)(2,1)S(1)} %copy-done, ...), custom_call_target="tpu_custom_call" | custom-call | flops 60000002048 | tf_op jit(solution)/shard_map/attention_back/pallas_call | solution.py:508
  61.6 0.1 collective-permute-start.16
  61.7 2.0 %collective-permute-start.17 = (bf16[80,768]{1,0:T(8,128)(2,1)S(1)}, bf16[80,768]{1,0:T(8,128)(2,1)S(1)}, u32[]{:S(2)}, u32[]{:S(2)}) collective-permute-start(bf16[80,768]{1,0:T(8,128)(2,1)S(1)} %get-tuple-element.116), channel_id=1, source_target_pairs={{0,2},{1,3},{2,0},{3,1},{4,6},{5,7},{6,4},{7,5},{8,10},{9,11},{10,... | collective-permute-start | bytes 368648 | tf_op jit(solution)/shard_map/ppermute | solution.py:528
  63.7 2.3 %collective-permute-start.18 = (bf16[80,768]{1,0:T(8,128)(2,1)S(1)}, bf16[80,768]{1,0:T(8,128)(2,1)S(1)}, u32[]{:S(2)}, u32[]{:S(2)}) collective-permute-start(bf16[80,768]{1,0:T(8,128)(2,1)S(1)} %get-tuple-element.117), channel_id=1, source_target_pairs={{0,3},{1,2},{2,1},{3,0},{4,7},{5,6},{6,5},{7,4},{8,11},{9,10},{10,... | collective-permute-start | bytes 368648 | tf_op jit(solution)/shard_map/ppermute | solution.py:528
  66.0 1.7 %weight_grads.1 = (bf16[4,96,768]{2,1,0:T(8,128)(2,1)S(1)}, bf16[4,96,768]{2,1,0:T(8,128)(2,1)S(1)}, f32[8,768]{1,0:T(8,128)S(1)}) custom-call(bf16[256,768]{1,0:T(8,128)(2,1)S(1)} %get-tuple-element.99.refs_0_, bf16[3,256,192]{2,1,0:T(8,128)(2,1)S(1)} %get-tuple-element.108.refs_1_, bf16[256,768]{1,0:T(8,128)(2,1)S(1)} %get-tuple-element.109.refs_2_, ...), custom_call_target="tpu_custom_call" | custom-call | flops 4000000000 | tf_op jit(solution)/shard_map/weight_grads/pallas_call | solution.py:508
  67.8 0.1 collective-permute-start.20
  67.9 2.0 %collective-permute-done.20.refs_3_ = bf16[4,96,768]{2,1,0:T(8,128)(2,1)S(1)} collective-permute-done((bf16[4,96,768]{2,1,0:T(8,128)(2,1)S(1)}, bf16[4,96,768]{2,1,0:T(8,128)(2,1)S(1)}, u32[]{:S(2)}, u32[]{:S(2)}) %collective-permute-start.20) | collective-permute-done | bytes 589856 | tf_op jit(solution)/shard_map/ppermute | solution.py:528
  69.8 1.1 %collective-permute-start.15 = (bf16[64,768]{1,0:T(8,128)(2,1)S(1)}, bf16[64,768]{1,0:T(8,128)(2,1)S(1)}, u32[]{:S(2)}, u32[]{:S(2)}) collective-permute-start(bf16[64,768]{1,0:T(8,128)(2,1)S(1)} %output_share.1.refs_4_.refs_0_), channel_id=1, source_target_pairs={{0,2},{1,3},{2,0},{3,1},{4,6},{5,7},{6,4},{7,5},{8,10},{9,11},{10,... | collective-permute-start | bytes 294920 | tf_op jit(solution)/shard_map/ppermute | solution.py:528
  70.9 0.6 collective-permute-done.19.refs_1_
  71.6 0.4 cross.1
  72.0 1.6 %collective-permute-start.28 = (bf16[144,3072]{1,0:T(8,128)(2,1)S(1)}, bf16[144,3072]{1,0:T(8,128)(2,1)S(1)}, u32[]{:S(2)}, u32[]{:S(2)}) collective-permute-start(bf16[144,3072]{1,0:T(8,128)(2,1)S(1)} %get-tuple-element.127), channel_id=1, source_target_pairs={{0,16},{4,12},{8,24},{12,4},{16,0},{20,28},{24,8},{28,20},{1,17},{... | collective-permute-start | bytes 2654216 | tf_op jit(solution)/shard_map/ppermute | solution.py:534
  73.6 0.2 input_back.1
  73.7 2.7 %collective-permute-start.22 = (bf16[64,768]{1,0:T(8,128)(2,1)S(1)}, bf16[64,768]{1,0:T(8,128)(2,1)S(1)}, u32[]{:S(2)}, u32[]{:S(2)}) collective-permute-start(bf16[64,768]{1,0:T(8,128)(2,1)S(1)} %get-tuple-element.123.refs_0_), channel_id=1, source_target_pairs={{0,1},{1,0},{2,3},{3,2},{4,5},{5,4},{6,7},{7,6},{8,9},{9,8},{10,11... | collective-permute-start | bytes 294920 | tf_op jit(solution)/shard_map/ppermute | solution.py:528
  76.5 0.4 collective-permute-done.15.refs_1_
  76.9 0.1 collective-permute-start.21
  77.0 3.0 %collective-permute-start.23 = (bf16[64,768]{1,0:T(8,128)(2,1)S(1)}, bf16[64,768]{1,0:T(8,128)(2,1)S(1)}, u32[]{:S(2)}, u32[]{:S(2)}) collective-permute-start(bf16[64,768]{1,0:T(8,128)(2,1)S(1)} %get-tuple-element.123.refs_0_), channel_id=1, source_target_pairs={{0,2},{1,3},{2,0},{3,1},{4,6},{5,7},{6,4},{7,5},{8,10},{9,11},{10,... | collective-permute-start | bytes 294920 | tf_op jit(solution)/shard_map/ppermute | solution.py:528
  80.0 1.4 %collective-permute-start.24 = (bf16[64,768]{1,0:T(8,128)(2,1)S(1)}, bf16[64,768]{1,0:T(8,128)(2,1)S(1)}, u32[]{:S(2)}, u32[]{:S(2)}) collective-permute-start(bf16[64,768]{1,0:T(8,128)(2,1)S(1)} %get-tuple-element.123.refs_0_), channel_id=1, source_target_pairs={{0,3},{1,2},{2,1},{3,0},{4,7},{5,6},{6,5},{7,4},{8,11},{9,10},{10,... | collective-permute-start | bytes 294920 | tf_op jit(solution)/shard_map/ppermute | solution.py:528
  81.4 1.6 %collective-permute-start.26 = (f32[8,768]{1,0:T(8,128)S(1)}, f32[8,768]{1,0:T(8,128)S(1)}, u32[]{:S(2)}, u32[]{:S(2)}) collective-permute-start(f32[8,768]{1,0:T(8,128)S(1)} %small_sum.2.refs_0_), channel_id=1, source_target_pairs={{0,8},{4,20},{8,0},{12,28},{16,24},{20,4},{24,16},{28,12},{1,9},{5... | collective-permute-start | bytes 73736 | tf_op jit(solution)/shard_map/ppermute | solution.py:534
  82.9 3.0 %collective-permute-done.23.refs_2_ = bf16[64,768]{1,0:T(8,128)(2,1)S(1)} collective-permute-done((bf16[64,768]{1,0:T(8,128)(2,1)S(1)}, bf16[64,768]{1,0:T(8,128)(2,1)S(1)}, u32[]{:S(2)}, u32[]{:S(2)}) %collective-permute-start.23) | collective-permute-done | bytes 98336 | tf_op jit(solution)/shard_map/ppermute | solution.py:528
  85.9 2.3 %collective-permute-done.24.refs_3_ = bf16[64,768]{1,0:T(8,128)(2,1)S(1)} collective-permute-done((bf16[64,768]{1,0:T(8,128)(2,1)S(1)}, bf16[64,768]{1,0:T(8,128)(2,1)S(1)}, u32[]{:S(2)}, u32[]{:S(2)}) %collective-permute-start.24) | collective-permute-done | bytes 98336 | tf_op jit(solution)/shard_map/ppermute | solution.py:528
  88.2 1.6 %collective-permute-start.27 = (f32[8,768]{1,0:T(8,128)S(1)}, f32[8,768]{1,0:T(8,128)S(1)}, u32[]{:S(2)}, u32[]{:S(2)}) collective-permute-start(f32[8,768]{1,0:T(8,128)S(1)} %small_sum.3.refs_0_), channel_id=1, source_target_pairs={{0,16},{4,12},{8,24},{12,4},{16,0},{20,28},{24,8},{28,20},{1,17},{... | collective-permute-start | bytes 73736 | tf_op jit(solution)/shard_map/ppermute | solution.py:534
  89.8 0.1 weight_cross.1
  89.9 1.6 %collective-permute-start.29 = (bf16[96,768]{1,0:T(8,128)(2,1)S(1)}, bf16[96,768]{1,0:T(8,128)(2,1)S(1)}, u32[]{:S(2)}, u32[]{:S(2)}) collective-permute-start(bf16[96,768]{1,0:T(8,128)(2,1)S(1)} %get-tuple-element.129), channel_id=1, source_target_pairs={{0,8},{4,20},{8,0},{12,28},{16,24},{20,4},{24,16},{28,12},{1,9},{5... | collective-permute-start | bytes 442376 | tf_op jit(solution)/shard_map/ppermute | solution.py:534
  91.4 0.8 grad_rows.1
  92.2 0.2 collective-permute-done.27.refs_1_
  92.4 0.8 small_final.1
  93.1 0.8 output_rows.1
  93.9 1.1 %expert_final.1 = (f32[2,96,768]{2,1,0:T(8,128)}, f32[2,96,768]{2,1,0:T(8,128)}) custom-call(f32[96,3072]{1,0:T(8,128)S(1)} %get-tuple-element.121.refs_8_.refs_0_, bf16[144,3072]{1,0:T(8,128)(2,1)S(1)} %collective-permute-done.28.refs_1_), custom_call_target="tpu_custom_call" | custom-call | flops 1000000000 | tf_op jit(solution)/shard_map/expert_final/pallas_call | solution.py:508
  95.1 0.0 collective-permute-done.29.refs_1_
  95.1 0.8 weight_final.1
  (40 shorter events, 0.2 us)
Async XLA Ops:
  4.1 7.1 %collective-permute-start = (bf16[64,768]{1,0:T(8,128)(2,1)S(1)}, bf16[64,768]{1,0:T(8,128)(2,1)S(1)}, u32[]{:S(2)}, u32[]{:S(2)}) collective-permute-start(bf16[64,768]{1,0:T(8,128)(2,1)S(1)} %get-tuple-element.76), channel_id=1, source_target_pairs={{0,1},{1,0},{2,3},{3,2},{4,5},{5,4},{6,7},{7,6},{8,9},{9,8},{10,11... | collective-permute-start | bytes 294920 | tf_op jit(solution)/shard_map/ppermute | solution.py:528
  7.2 10.4 %collective-permute-start.1 = (bf16[64,768]{1,0:T(8,128)(2,1)S(1)}, bf16[64,768]{1,0:T(8,128)(2,1)S(1)}, u32[]{:S(2)}, u32[]{:S(2)}) collective-permute-start(bf16[64,768]{1,0:T(8,128)(2,1)S(1)} %get-tuple-element.77), channel_id=1, source_target_pairs={{0,2},{1,3},{2,0},{3,1},{4,6},{5,7},{6,4},{7,5},{8,10},{9,11},{10,... | collective-permute-start | bytes 294920 | tf_op jit(solution)/shard_map/ppermute | solution.py:528
  9.8 7.8 %collective-permute-start.2 = (bf16[64,768]{1,0:T(8,128)(2,1)S(1)}, bf16[64,768]{1,0:T(8,128)(2,1)S(1)}, u32[]{:S(2)}, u32[]{:S(2)}) collective-permute-start(bf16[64,768]{1,0:T(8,128)(2,1)S(1)} %get-tuple-element.78), channel_id=1, source_target_pairs={{0,3},{1,2},{2,1},{3,0},{4,7},{5,6},{6,5},{7,4},{8,11},{9,10},{10,... | collective-permute-start | bytes 294920 | tf_op jit(solution)/shard_map/ppermute | solution.py:528
  17.8 11.0 %copy-start.5 = (bf16[256,768]{1,0:T(8,128)(2,1)S(1)}, bf16[256,768]{1,0:T(8,128)(2,1)}, u32[]{:S(2)}) copy-start(bf16[256,768]{1,0:T(8,128)(2,1)} %refs_1_.5) | copy-start | bytes 1179652
  17.8 10.9 %copy-start.6 = (bf16[768,2]{0,1:T(2,128)(2,1)S(1)}, bf16[768,2]{0,1:T(2,128)(2,1)}, u32[]{:S(2)}) copy-start(bf16[768,2]{0,1:T(2,128)(2,1)} %param.28) | copy-start | bytes 9220
  17.8 6.9 %collective-permute-start.3 = (bf16[64,768]{1,0:T(8,128)(2,1)S(1)}, bf16[64,768]{1,0:T(8,128)(2,1)S(1)}, u32[]{:S(2)}, u32[]{:S(2)}) collective-permute-start(bf16[64,768]{1,0:T(8,128)(2,1)S(1)} %get-tuple-element.80.refs_2_.refs_5_), channel_id=1, source_target_pairs={{0,1},{1,0},{2,3},{3,2},{4,5},{5,4},{6,7},{7,6},{8,9},{9,8},{10,11... | collective-permute-start | bytes 294920 | tf_op jit(solution)/shard_map/ppermute | solution.py:528
  19.5 9.2 %collective-permute-start.4 = (bf16[64,768]{1,0:T(8,128)(2,1)S(1)}, bf16[64,768]{1,0:T(8,128)(2,1)S(1)}, u32[]{:S(2)}, u32[]{:S(2)}) collective-permute-start(bf16[64,768]{1,0:T(8,128)(2,1)S(1)} %get-tuple-element.80.refs_2_.refs_5_), channel_id=1, source_target_pairs={{0,2},{1,3},{2,0},{3,1},{4,6},{5,7},{6,4},{7,5},{8,10},{9,11},{10,... | collective-permute-start | bytes 294920 | tf_op jit(solution)/shard_map/ppermute | solution.py:528
  20.9 7.8 %collective-permute-start.5 = (bf16[64,768]{1,0:T(8,128)(2,1)S(1)}, bf16[64,768]{1,0:T(8,128)(2,1)S(1)}, u32[]{:S(2)}, u32[]{:S(2)}) collective-permute-start(bf16[64,768]{1,0:T(8,128)(2,1)S(1)} %get-tuple-element.80.refs_2_.refs_5_), channel_id=1, source_target_pairs={{0,3},{1,2},{2,1},{3,0},{4,7},{5,6},{6,5},{7,4},{8,11},{9,10},{10,... | collective-permute-start | bytes 294920 | tf_op jit(solution)/shard_map/ppermute | solution.py:528
  32.4 7.3 %collective-permute-start.6 = (bf16[64,768]{1,0:T(8,128)(2,1)S(1)}, bf16[64,768]{1,0:T(8,128)(2,1)S(1)}, u32[]{:S(2)}, u32[]{:S(2)}) collective-permute-start(bf16[64,768]{1,0:T(8,128)(2,1)S(1)} %get-tuple-element.87), channel_id=1, source_target_pairs={{0,1},{1,0},{2,3},{3,2},{4,5},{5,4},{6,7},{7,6},{8,9},{9,8},{10,11... | collective-permute-start | bytes 294920 | tf_op jit(solution)/shard_map/ppermute | solution.py:528
  34.1 9.5 %collective-permute-start.7 = (bf16[64,768]{1,0:T(8,128)(2,1)S(1)}, bf16[64,768]{1,0:T(8,128)(2,1)S(1)}, u32[]{:S(2)}, u32[]{:S(2)}) collective-permute-start(bf16[64,768]{1,0:T(8,128)(2,1)S(1)} %get-tuple-element.88), channel_id=1, source_target_pairs={{0,2},{1,3},{2,0},{3,1},{4,6},{5,7},{6,4},{7,5},{8,10},{9,11},{10,... | collective-permute-start | bytes 294920 | tf_op jit(solution)/shard_map/ppermute | solution.py:528
  35.2 8.4 %collective-permute-start.8 = (bf16[64,768]{1,0:T(8,128)(2,1)S(1)}, bf16[64,768]{1,0:T(8,128)(2,1)S(1)}, u32[]{:S(2)}, u32[]{:S(2)}) collective-permute-start(bf16[64,768]{1,0:T(8,128)(2,1)S(1)} %get-tuple-element.89), channel_id=1, source_target_pairs={{0,3},{1,2},{2,1},{3,0},{4,7},{5,6},{6,5},{7,4},{8,11},{9,10},{10,... | collective-permute-start | bytes 294920 | tf_op jit(solution)/shard_map/ppermute | solution.py:528
  39.6 15.1 %collective-permute-start.14 = (bf16[4,96,3072]{2,1,0:T(8,128)(2,1)S(1)}, bf16[4,96,3072]{2,1,0:T(8,128)(2,1)S(1)}, u32[]{:S(2)}, u32[]{:S(2)}) collective-permute-start(bf16[4,96,3072]{2,1,0:T(8,128)(2,1)S(1)} %get-tuple-element.94.refs_8_), channel_id=1, source_target_pairs={{0,4},{4,0},{8,12},{12,8},{16,20},{20,16},{24,28},{28,24},{1,5},{5... | collective-permute-start | bytes 7077896 | tf_op jit(solution)/shard_map/ppermute | solution.py:528
  43.6 1.9 %copy-start.7 = (f32[768]{0:T(1024)S(1)}, f32[768]{0:T(1024)}, u32[]{:S(2)}) copy-start(f32[768]{0:T(1024)} %refs_1_.3) | copy-start | bytes 9220
  43.6 1.9 %copy-start.8 = (s32[511]{0:T(512)S(1)}, s32[511]{0:T(512)}, u32[]{:S(2)}) copy-start(s32[511]{0:T(512)} %param.18) | copy-start | bytes 6136
  43.8 8.6 %collective-permute-start.9 = (bf16[128,768]{1,0:T(8,128)(2,1)S(1)}, bf16[128,768]{1,0:T(8,128)(2,1)S(1)}, u32[]{:S(2)}, u32[]{:S(2)}) collective-permute-start(bf16[128,768]{1,0:T(8,128)(2,1)S(1)} %get-tuple-element.95), channel_id=1, source_target_pairs={{0,1},{1,0},{2,3},{3,2},{4,5},{5,4},{6,7},{7,6},{8,9},{9,8},{10,11... | collective-permute-start | bytes 589832 | tf_op jit(solution)/shard_map/ppermute | solution.py:528
  45.5 11.4 %collective-permute-start.11 = (bf16[64,768]{1,0:T(8,128)(2,1)S(1)}, bf16[64,768]{1,0:T(8,128)(2,1)S(1)}, u32[]{:S(2)}, u32[]{:S(2)}) collective-permute-start(bf16[64,768]{1,0:T(8,128)(2,1)S(1)} %get-tuple-element.96.refs_2_.refs_11_), channel_id=1, source_target_pairs={{0,1},{1,0},{2,3},{3,2},{4,5},{5,4},{6,7},{7,6},{8,9},{9,8},{10,11... | collective-permute-start | bytes 294920 | tf_op jit(solution)/shard_map/ppermute | solution.py:528
  46.0 10.9 %collective-permute-start.12 = (bf16[64,768]{1,0:T(8,128)(2,1)S(1)}, bf16[64,768]{1,0:T(8,128)(2,1)S(1)}, u32[]{:S(2)}, u32[]{:S(2)}) collective-permute-start(bf16[64,768]{1,0:T(8,128)(2,1)S(1)} %get-tuple-element.96.refs_2_.refs_11_), channel_id=1, source_target_pairs={{0,2},{1,3},{2,0},{3,1},{4,6},{5,7},{6,4},{7,5},{8,10},{9,11},{10,... | collective-permute-start | bytes 294920 | tf_op jit(solution)/shard_map/ppermute | solution.py:528
  48.5 11.1 %collective-permute-start.13 = (bf16[64,768]{1,0:T(8,128)(2,1)S(1)}, bf16[64,768]{1,0:T(8,128)(2,1)S(1)}, u32[]{:S(2)}, u32[]{:S(2)}) collective-permute-start(bf16[64,768]{1,0:T(8,128)(2,1)S(1)} %get-tuple-element.96.refs_2_.refs_11_), channel_id=1, source_target_pairs={{0,3},{1,2},{2,1},{3,0},{4,7},{5,6},{6,5},{7,4},{8,11},{9,10},{10,... | collective-permute-start | bytes 294920 | tf_op jit(solution)/shard_map/ppermute | solution.py:528
  52.4 15.3 %collective-permute-start.10 = (bf16[64,768]{1,0:T(8,128)(2,1)S(1)}, bf16[64,768]{1,0:T(8,128)(2,1)S(1)}, u32[]{:S(2)}, u32[]{:S(2)}) collective-permute-start(bf16[64,768]{1,0:T(8,128)(2,1)S(1)} %get-tuple-element.98), channel_id=1, source_target_pairs={{0,2},{1,3},{2,0},{3,1},{4,6},{5,7},{6,4},{7,5},{8,10},{9,11},{10,... | collective-permute-start | bytes 294920 | tf_op jit(solution)/shard_map/ppermute | solution.py:528
  54.8 4.9 %copy-start = (bf16[256,768]{1,0:T(8,128)(2,1)S(1)}, bf16[256,768]{1,0:T(8,128)(2,1)}, u32[]{:S(2)}) copy-start(bf16[256,768]{1,0:T(8,128)(2,1)} %refs_0_.7) | copy-start | bytes 1179652
  54.8 4.9 %copy-start.1 = (bf16[768,192]{0,1:T(8,128)(2,1)S(1)}, bf16[768,192]{0,1:T(8,128)(2,1)}, u32[]{:S(2)}) copy-start(bf16[768,192]{0,1:T(8,128)(2,1)} %param.23) | copy-start | bytes 884740
  54.8 4.9 %copy-start.2 = (bf16[768,192]{0,1:T(8,128)(2,1)S(1)}, bf16[768,192]{0,1:T(8,128)(2,1)}, u32[]{:S(2)}) copy-start(bf16[768,192]{0,1:T(8,128)(2,1)} %param.24) | copy-start | bytes 884740
  54.8 4.9 %copy-start.3 = (bf16[768,192]{0,1:T(8,128)(2,1)S(1)}, bf16[768,192]{0,1:T(8,128)(2,1)}, u32[]{:S(2)}) copy-start(bf16[768,192]{0,1:T(8,128)(2,1)} %param.25) | copy-start | bytes 884740
  54.8 4.9 %copy-start.4 = (bf16[192,768]{1,0:T(8,128)(2,1)S(1)}, bf16[192,768]{1,0:T(8,128)(2,1)}, u32[]{:S(2)}) copy-start(bf16[192,768]{1,0:T(8,128)(2,1)} %refs_8_.3) | copy-start | bytes 884740
  55.3 16.3 %collective-permute-start.19 = (bf16[2,96,3072]{2,1,0:T(8,128)(2,1)S(1)}, bf16[2,96,3072]{2,1,0:T(8,128)(2,1)S(1)}, u32[]{:S(2)}, u32[]{:S(2)}) collective-permute-start(bf16[2,96,3072]{2,1,0:T(8,128)(2,1)S(1)} %get-tuple-element.118), channel_id=1, source_target_pairs={{0,8},{4,20},{8,0},{12,28},{16,24},{20,4},{24,16},{28,12},{1,9},{5... | collective-permute-start | bytes 3538952 | tf_op jit(solution)/shard_map/ppermute | solution.py:534
  61.6 12.0 %collective-permute-start.16 = (bf16[80,768]{1,0:T(8,128)(2,1)S(1)}, bf16[80,768]{1,0:T(8,128)(2,1)S(1)}, u32[]{:S(2)}, u32[]{:S(2)}) collective-permute-start(bf16[80,768]{1,0:T(8,128)(2,1)S(1)} %get-tuple-element.115), channel_id=1, source_target_pairs={{0,1},{1,0},{2,3},{3,2},{4,5},{5,4},{6,7},{7,6},{8,9},{9,8},{10,11... | collective-permute-start | bytes 368648 | tf_op jit(solution)/shard_map/ppermute | solution.py:528
  61.7 11.9 %collective-permute-start.17 = (bf16[80,768]{1,0:T(8,128)(2,1)S(1)}, bf16[80,768]{1,0:T(8,128)(2,1)S(1)}, u32[]{:S(2)}, u32[]{:S(2)}) collective-permute-start(bf16[80,768]{1,0:T(8,128)(2,1)S(1)} %get-tuple-element.116), channel_id=1, source_target_pairs={{0,2},{1,3},{2,0},{3,1},{4,6},{5,7},{6,4},{7,5},{8,10},{9,11},{10,... | collective-permute-start | bytes 368648 | tf_op jit(solution)/shard_map/ppermute | solution.py:528
  63.7 9.8 %collective-permute-start.18 = (bf16[80,768]{1,0:T(8,128)(2,1)S(1)}, bf16[80,768]{1,0:T(8,128)(2,1)S(1)}, u32[]{:S(2)}, u32[]{:S(2)}) collective-permute-start(bf16[80,768]{1,0:T(8,128)(2,1)S(1)} %get-tuple-element.117), channel_id=1, source_target_pairs={{0,3},{1,2},{2,1},{3,0},{4,7},{5,6},{6,5},{7,4},{8,11},{9,10},{10,... | collective-permute-start | bytes 368648 | tf_op jit(solution)/shard_map/ppermute | solution.py:528
  67.8 2.1 %collective-permute-start.20 = (bf16[4,96,768]{2,1,0:T(8,128)(2,1)S(1)}, bf16[4,96,768]{2,1,0:T(8,128)(2,1)S(1)}, u32[]{:S(2)}, u32[]{:S(2)}) collective-permute-start(bf16[4,96,768]{2,1,0:T(8,128)(2,1)S(1)} %get-tuple-element.120), channel_id=1, source_target_pairs={{0,4},{4,0},{8,12},{12,8},{16,20},{20,16},{24,28},{28,24},{1,5},{5... | collective-permute-start | bytes 1769480 | tf_op jit(solution)/shard_map/ppermute | solution.py:528
  69.8 7.0 %collective-permute-start.15 = (bf16[64,768]{1,0:T(8,128)(2,1)S(1)}, bf16[64,768]{1,0:T(8,128)(2,1)S(1)}, u32[]{:S(2)}, u32[]{:S(2)}) collective-permute-start(bf16[64,768]{1,0:T(8,128)(2,1)S(1)} %output_share.1.refs_4_.refs_0_), channel_id=1, source_target_pairs={{0,2},{1,3},{2,0},{3,1},{4,6},{5,7},{6,4},{7,5},{8,10},{9,11},{10,... | collective-permute-start | bytes 294920 | tf_op jit(solution)/shard_map/ppermute | solution.py:528
  72.0 17.9 %collective-permute-start.28 = (bf16[144,3072]{1,0:T(8,128)(2,1)S(1)}, bf16[144,3072]{1,0:T(8,128)(2,1)S(1)}, u32[]{:S(2)}, u32[]{:S(2)}) collective-permute-start(bf16[144,3072]{1,0:T(8,128)(2,1)S(1)} %get-tuple-element.127), channel_id=1, source_target_pairs={{0,16},{4,12},{8,24},{12,4},{16,0},{20,28},{24,8},{28,20},{1,17},{... | collective-permute-start | bytes 2654216 | tf_op jit(solution)/shard_map/ppermute | solution.py:534
  73.7 7.6 %collective-permute-start.22 = (bf16[64,768]{1,0:T(8,128)(2,1)S(1)}, bf16[64,768]{1,0:T(8,128)(2,1)S(1)}, u32[]{:S(2)}, u32[]{:S(2)}) collective-permute-start(bf16[64,768]{1,0:T(8,128)(2,1)S(1)} %get-tuple-element.123.refs_0_), channel_id=1, source_target_pairs={{0,1},{1,0},{2,3},{3,2},{4,5},{5,4},{6,7},{7,6},{8,9},{9,8},{10,11... | collective-permute-start | bytes 294920 | tf_op jit(solution)/shard_map/ppermute | solution.py:528
  76.5 3.5 %collective-permute-start.25 = (f32[8,768]{1,0:T(8,128)S(1)}, f32[8,768]{1,0:T(8,128)S(1)}, u32[]{:S(2)}, u32[]{:S(2)}) collective-permute-start(f32[8,768]{1,0:T(8,128)S(1)} %get-tuple-element.122.refs_2_.refs_0_), channel_id=1, source_target_pairs={{0,4},{4,0},{8,12},{12,8},{16,20},{20,16},{24,28},{28,24},{1,5},{5... | collective-permute-start | bytes 73736 | tf_op jit(solution)/shard_map/ppermute | solution.py:528
  76.9 16.3 %collective-permute-start.21 = (bf16[128,768]{1,0:T(8,128)(2,1)S(1)}, bf16[128,768]{1,0:T(8,128)(2,1)S(1)}, u32[]{:S(2)}, u32[]{:S(2)}) collective-permute-start(bf16[128,768]{1,0:T(8,128)(2,1)S(1)} %output_pair.1.refs_0_), channel_id=1, source_target_pairs={{0,1},{1,0},{2,3},{3,2},{4,5},{5,4},{6,7},{7,6},{8,9},{9,8},{10,11... | collective-permute-start | bytes 589832 | tf_op jit(solution)/shard_map/ppermute | solution.py:528
  77.0 9.0 %collective-permute-start.23 = (bf16[64,768]{1,0:T(8,128)(2,1)S(1)}, bf16[64,768]{1,0:T(8,128)(2,1)S(1)}, u32[]{:S(2)}, u32[]{:S(2)}) collective-permute-start(bf16[64,768]{1,0:T(8,128)(2,1)S(1)} %get-tuple-element.123.refs_0_), channel_id=1, source_target_pairs={{0,2},{1,3},{2,0},{3,1},{4,6},{5,7},{6,4},{7,5},{8,10},{9,11},{10,... | collective-permute-start | bytes 294920 | tf_op jit(solution)/shard_map/ppermute | solution.py:528
  80.0 8.3 %collective-permute-start.24 = (bf16[64,768]{1,0:T(8,128)(2,1)S(1)}, bf16[64,768]{1,0:T(8,128)(2,1)S(1)}, u32[]{:S(2)}, u32[]{:S(2)}) collective-permute-start(bf16[64,768]{1,0:T(8,128)(2,1)S(1)} %get-tuple-element.123.refs_0_), channel_id=1, source_target_pairs={{0,3},{1,2},{2,1},{3,0},{4,7},{5,6},{6,5},{7,4},{8,11},{9,10},{10,... | collective-permute-start | bytes 294920 | tf_op jit(solution)/shard_map/ppermute | solution.py:528
  81.4 6.9 %collective-permute-start.26 = (f32[8,768]{1,0:T(8,128)S(1)}, f32[8,768]{1,0:T(8,128)S(1)}, u32[]{:S(2)}, u32[]{:S(2)}) collective-permute-start(f32[8,768]{1,0:T(8,128)S(1)} %small_sum.2.refs_0_), channel_id=1, source_target_pairs={{0,8},{4,20},{8,0},{12,28},{16,24},{20,4},{24,16},{28,12},{1,9},{5... | collective-permute-start | bytes 73736 | tf_op jit(solution)/shard_map/ppermute | solution.py:534
  88.2 4.1 %collective-permute-start.27 = (f32[8,768]{1,0:T(8,128)S(1)}, f32[8,768]{1,0:T(8,128)S(1)}, u32[]{:S(2)}, u32[]{:S(2)}) collective-permute-start(f32[8,768]{1,0:T(8,128)S(1)} %small_sum.3.refs_0_), channel_id=1, source_target_pairs={{0,16},{4,12},{8,24},{12,4},{16,0},{20,28},{24,8},{28,20},{1,17},{... | collective-permute-start | bytes 73736 | tf_op jit(solution)/shard_map/ppermute | solution.py:534
  89.9 5.2 %collective-permute-start.29 = (bf16[96,768]{1,0:T(8,128)(2,1)S(1)}, bf16[96,768]{1,0:T(8,128)(2,1)S(1)}, u32[]{:S(2)}, u32[]{:S(2)}) collective-permute-start(bf16[96,768]{1,0:T(8,128)(2,1)S(1)} %get-tuple-element.129), channel_id=1, source_target_pairs={{0,8},{4,20},{8,0},{12,28},{16,24},{20,4},{24,16},{28,12},{1,9},{5... | collective-permute-start | bytes 442376 | tf_op jit(solution)/shard_map/ppermute | solution.py:534

commit v4 on v3

--- a/solution.py
+++ b/solution.py
@@ -13,6 +13,7 @@
 CAP = 144
 EPS = 1e-06
 SMALL_ROWS = 16
+GAIN_ROWS = 8
 TABLE_ROW = 2 + EXPERTS
 WEIGHTS = {
     "fetch": 20,
@@ -20,12 +21,15 @@
     "expert_grads": 20,
     "hidden_back": 60,
     "expert_merge": 20,
-    "attention_back": 60,
+    "attention_back": 5,
+    "pair_sum": 8,
     "weight_grads": 4,
-    "output_share": 8,
+    "expert_cross": 8,
     "input_back": 60,
-    "expert_final": 1,
-    "weight_final": 1,
+    "expert_final": 0.001,
+    "weight_final": 0.001,
+    "small_sum": 0.001,
+    "weight_cross": 0.001,
 }
 BF16 = jnp.bfloat16
 F32 = jnp.float32
@@ -56,18 +60,23 @@
     return pl.ds(pl.multiple_of(index * rows, rows), rows)
 
 
+def distance(place, members):
+    return (members - place) % members
+
+
+def member_at(place, members):
+    return jnp.bitwise_xor(lax.axis_index("tensor"), distance(place, members))
+
+
 def put_shares(acc_ref, share_refs):
-    me = lax.axis_index("tensor")
-    for k, ref in enumerate(share_refs):
-        rows = ref.shape[0]
-        ref[...] = acc_ref[share_of(jnp.bitwise_xor(me, k), rows), :].astype(ref.dtype)
+    for i, ref in enumerate(share_refs):
+        there = share_of(member_at(i, len(share_refs)), ref.shape[0])
+        ref[...] = acc_ref[there, :].astype(ref.dtype)
 
 
 def assemble(full_ref, share_refs):
-    me = lax.axis_index("tensor")
-    for k, ref in enumerate(share_refs):
-        rows = ref.shape[0]
-        full_ref[share_of(jnp.bitwise_xor(me, k), rows), :] = ref[...]
+    for i, ref in enumerate(share_refs):
+        full_ref[share_of(member_at(i, len(share_refs)), ref.shape[0]), :] = ref[...]
 
 
 def total_of(refs):
@@ -239,9 +248,9 @@
     return share_of(2 * chip + core, part), share_of(2 * chip + 1 - core, part)
 
 
-def expert_grad_kernel(split, buffer, active, grad_before, grad_expert, *rest):
-    width = buffer.shape[1]
-    scratch = rest[-1]
+def expert_grad_kernel(split, buffer, active, grad_before, grad_expert, rows, *rest):
+    scratch, rows_o = rest[-1], rest[-2]
+    rows_o[...] = rows[...]
     for e in range(EXPERTS):
         slot = slice(e * CAP, (e + 1) * CAP)
         for which in range(2):
@@ -281,10 +290,14 @@
     out[...] = one[...] + other[...]
 
 
-def cross_kernel(kept, came, weight_kept, weight_came, own, send, weight_keep):
-    rows, columns = own.shape
+def expert_cross_kernel(kept, came, own, send):
     own[...] = kept[0] + came[0].astype(F32)
-    send[0:rows, :] = (kept[1] + came[1].astype(F32)).astype(BF16)
+    send[...] = (kept[1] + came[1].astype(F32)).astype(BF16)
+
+
+def cross_kernel(expert_send, weight_kept, weight_came, send, weight_keep):
+    rows = expert_send.shape[0]
+    send[0:rows, :] = expert_send[...]
     chip = lax.div(lax.axis_index("dp"), 2)
     second, first = chip_bits()
     width = weight_keep.shape[2]
@@ -299,15 +312,18 @@
             send[rows : rows + half, at : at + width] = total[i * half : (i + 1) * half]
 
 
-def weight_cross_kernel(kept, came, own, send):
-    rows, width = own.shape
+def weight_cross_kernel(kept, came, small, small_came, own, send):
+    width = own.shape[1]
+    rows = kept.shape[1]
     half = rows // 2
+    total = jnp.concatenate([small[...] + small_came[...], jnp.zeros_like(small)], axis=0)
     for k, ref in enumerate((own, send)):
         for i in range(2):
             at = (2 * k + i) * width
             arrived = came[rows : rows + half, at : at + width].astype(F32)
             part = slice(i * half, (i + 1) * half)
             ref[part, :] = (kept[k, part, :] + arrived).astype(ref.dtype)
+        ref[rows:, :] = total.astype(ref.dtype)
 
 
 def expert_final_kernel(*refs):
@@ -326,33 +342,18 @@
     other[...] = (kept[share:, :].astype(F32) + came[share:, :].astype(F32)).astype(BF16)
 
 
-def output_kernel(hidden, own, came, out):
-    out[...] = (hidden[...] + own[...] + came[...].astype(F32)).astype(BF16)
-
-
-def pair_kernel(own, came, out):
-    share = own.shape[0]
-    out[0:share, :] = own[...]
-    out[share:, :] = came[...]
-
-
-def pair_rows_kernel(own, came, out):
-    me = lax.axis_index("tensor")
-    share = own.shape[0] // 2
-    for first, ref in enumerate((own, came)):
-        for k in range(2):
-            index = jnp.bitwise_xor(me, first + 2 * k)
-            out[share_of(index, share), :] = ref[k * share : (k + 1) * share, :]
-
-
-def gather_kernel(*refs):
-    assemble(refs[-1], refs[:-1])
-
-
-def hidden_back_kernel(members, hidden, cotangent, gain, rows, *rest):
+def rows_kernel(*refs):
+    shares, (output, grad_inputs) = refs[:-2], refs[-2:]
+    for i, ref in enumerate(shares):
+        rows = ref.shape[0] // 2
+        there = share_of(member_at(i, len(shares)), rows)
+        grad_inputs[there, :] = ref[0:rows, :]
+        output[there, :] = ref[rows:, :]
+
+
+def hidden_back_kernel(members, hidden, cotangent, gain, *rest):
     parts = rest[:members]
-    grad_o, low_o, gain_o, rows_o = rest[members:]
-    rows_o[...] = rows[...]
+    grad_o, low_o, gain_o = rest[members:]
     h = hidden[...]
     dy = cotangent[...].astype(F32)
     r = inverse_rms(h)
@@ -402,14 +403,13 @@
             gain_one,
             gain_two[...],
             router[...],
-            jnp.zeros((SMALL_ROWS - 2 - EXPERTS, gain_one.shape[1]), F32),
+            jnp.zeros((GAIN_ROWS - TABLE_ROW, gain_one.shape[1]), F32),
         ],
         axis=0,
     )
-    me = lax.axis_index("tensor")
-    for k, ref in enumerate(share_o):
-        share = ref.shape[0] - SMALL_ROWS
-        ref[0:share, :] = acc[share_of(jnp.bitwise_xor(me, k), share), :].astype(ref.dtype)
+    for i, ref in enumerate(share_o):
+        share = ref.shape[0] - GAIN_ROWS
+        ref[0:share, :] = acc[share_of(member_at(i, members), share), :].astype(ref.dtype)
         ref[share:, :] = small.astype(ref.dtype)
 
 
@@ -455,18 +455,17 @@
         send[chip] = scratch[other, :].astype(BF16)
 
 
-def weight_final_kernel(*refs):
-    wq_o, wk_o, wv_o, wo_o = refs[2:]
-    total = total_of(refs[:2])
+def weight_final_kernel(members, own, came, *outs):
+    wq_o, wk_o, wv_o, wo_o, one_o, two_o, router_o, table_o = outs
+    total = total_of((own, came))
     part, cols = wq_o.shape
     wq_o[...] = total[0:part, 0:cols]
     wk_o[...] = total[0:part, cols : 2 * cols]
     wv_o[...] = total[0:part, 2 * cols : 3 * cols]
     wo_o[...] = total[0:part, 3 * cols : 4 * cols].T
-
-
-def small_final_kernel(members, one, other, one_o, two_o, router_o, table_o):
-    small = one[...] + other[...]
+    small = total[part:]
+    heads, bucket_count = table_o.shape
+    table_o[...] = small[TABLE_ROW : TABLE_ROW + heads, 0:bucket_count]
     per = one_o.shape[1]
     first = (lax.axis_index("dp") * members + lax.axis_index("tensor")) * per
     shape = (per, small.shape[1])
@@ -478,21 +477,24 @@
     one_o[...] = rows[0:1]
     two_o[...] = rows[1:2]
     router_o[...] = rows[2:TABLE_ROW]
-    heads, bucket_count = table_o.shape
-    table_o[...] = small[TABLE_ROW : TABLE_ROW + heads, 0:bucket_count]
-
-
-def input_back_kernel(members, inputs, gain, grad_hidden, table, *rest):
+
+
+def output_kernel(hidden, own, came, out):
+    out[...] = (hidden[...] + own[...] + came[...].astype(F32)).astype(BF16)
+
+
+def input_back_kernel(members, inputs, gain, grad_hidden, table, output, *rest):
     out, small_o = rest[members:]
-    share = out.shape[0]
+    share = output.shape[0]
     x = inputs[share_of(lax.axis_index("tensor"), share), :].astype(F32)
     r = inverse_rms(x)
     total = total_of(rest[:members])
-    small_o[...] = total[share : share + small_o.shape[0]] + table[...]
+    small_o[...] = total[share:] + table[...]
     z = total[0:share] * gain[...]
-    out[...] = (
+    out[0:share, :] = (
         grad_hidden[...] + r * z - x * (r * r * r) * jnp.mean(z * x, axis=-1, keepdims=True)
     ).astype(BF16)
+    out[share:, :] = output[...]
 
 
 def run(kernel, outs, args, scratch=(), name=None, after=(), space=pltpu.VMEM, out=pltpu.VMEM):
@@ -535,12 +537,13 @@
 
 
 def exchange(shares):
-    return [shares[0]] + [swap(s, "tensor", k) for k, s in enumerate(shares) if k > 0]
+    members = len(shares)
+    sent = [swap(s, "tensor", distance(i, members)) for i, s in enumerate(shares) if i > 0]
+    return [shares[0]] + sent
 
 
 def spread(share):
-    members = lax.axis_size("tensor")
-    return [share] + [swap(share, "tensor", k) for k in range(1, members)]
+    return exchange([share] * lax.axis_size("tensor"))
 
 
 def shards(
@@ -661,29 +664,23 @@
 
     expert_grads = run(
         bind(expert_grad_kernel, split),
-        split_sds(part, 4 * hidden_units) if split else [sds((width, 4 * hidden_units), F32)],
-        [buffer, active, grad_before, grad_expert],
+        (split_sds(part, 4 * hidden_units) if split else [sds((width, 4 * hidden_units), F32)])
+        + [sds(rows_sent.shape, BF16)],
+        [buffer, active, grad_before, grad_expert, rows_sent],
         [pltpu.VMEM((width, hidden_units), F32)],
         name="expert_grads",
     )
 
-    grad_hidden, grad_attended, grad_gain_expert, rows_sent = run(
+    rows_sent = expert_grads[-1]
+    grad_hidden, grad_attended, grad_gain_expert = run(
         bind(hidden_back_kernel, members),
-        [sds((share, width), F32), sds((share, width), BF16), sds((1, width), F32)]
-        + [sds((2 * share, width), BF16)],
-        [hidden, dy_share, gain_two_row, rows_sent] + back_rows,
+        [sds((share, width), F32), sds((share, width), BF16), sds((1, width), F32)],
+        [hidden, dy_share, gain_two_row] + back_rows,
         name="hidden_back",
         after=expert_grads[-1:],
     )
     grad_attended = spread(grad_attended)
 
-    own_rows, other_rows = run(
-        pair_sum_kernel,
-        [sds((share, width), F32), sds((share, width), BF16)],
-        [rows_kept, swap(rows_sent, "tensor", 1)],
-        name="pair_sum",
-        after=[grad_attended[0]],
-    )
     expert_merged = []
     if split:
         expert_merged = run(
@@ -692,10 +689,17 @@
             [expert_grads[0], swap(expert_grads[1], "dp", 1)],
             name="expert_merge",
         )
+    own_rows, other_rows = run(
+        pair_sum_kernel,
+        [sds((share, width), F32), sds((share, width), BF16)],
+        [rows_kept, swap(rows_sent, "tensor", 1)],
+        name="pair_sum",
+        after=grad_attended[1:] + list(expert_merged[:1]),
+    )
     crossed = []
 
     def tall_sds(dtype):
-        return sds((share + SMALL_ROWS, width), dtype)
+        return sds((share + GAIN_ROWS, width), dtype)
 
     outs = run(
         bind(attention_back_kernel, members),
@@ -716,6 +720,12 @@
     grad_normed = exchange(outs[:members])
     projections, attended_low, grad_scores = outs[members:]
 
+    (output_share,) = run(
+        output_kernel,
+        [sds((share, width), BF16)],
+        [hidden, own_rows, swap(other_rows, "tensor", 2)],
+        name="output_share",
+    )
     weight_cols = 4 * cols
     weight_grads = run(
         bind(weight_grad_kernel, split),
@@ -724,61 +734,44 @@
         [normed, projections, attended_low, mixed, grad_scores, bucket_wide],
         [pltpu.VMEM((width, weight_cols), F32)],
         name="weight_grads",
-    )
-
-    (output_share,) = run(
-        output_kernel,
-        [sds((share, width), BF16)],
-        [hidden, own_rows, swap(other_rows, "tensor", 2)],
-        name="output_share",
-        after=weight_grads[-1:],
-    )
+        after=[output_share],
+    )
+
     if split:
-        expert_own, crossing, weight_kept = run(
+        expert_own, expert_sent = run(
+            expert_cross_kernel,
+            [sds((part, 4 * hidden_units), F32), sds((part, 4 * hidden_units), BF16)],
+            [expert_merged[0], swap_chips(expert_merged[1], 2, 4)],
+            name="expert_cross",
+            after=weight_grads[-1:],
+        )
+        crossing, weight_kept = run(
             cross_kernel,
             [
-                sds((part, 4 * hidden_units), F32),
                 sds((part + part // 2, 4 * hidden_units), BF16),
                 sds((2, part, weight_cols), F32),
             ],
-            [
-                expert_merged[0],
-                swap_chips(expert_merged[1], 2, 4),
-                weight_grads[0],
-                swap(weight_grads[1], "dp", 1),
-            ],
+            [expert_sent, weight_grads[0], swap(weight_grads[1], "dp", 1)],
             name="cross",
-            after=[output_share],
         )
-        crossed = [expert_own]
-    grad_inputs, small = run(
+        crossed = [weight_kept]
+    both_rows, small = run(
         bind(input_back_kernel, members),
-        [sds((share, width), BF16), sds((8, width), F32)],
-        [inputs, gain_row, grad_hidden, weight_grads[-1]] + grad_normed,
+        [sds((2 * share, width), BF16), sds((8, width), F32)],
+        [inputs, gain_row, grad_hidden, weight_grads[-1]]
+        + [output_share]
+        + grad_normed,
         name="input_back",
         after=crossed,
     )
-    (output_pair,) = run(
-        pair_kernel,
-        [sds((2 * share, width), BF16)],
-        [output_share, swap(output_share, "tensor", 2)],
-        name="output_pair",
-        after=[small],
-    )
-    (output,) = run(
-        pair_rows_kernel,
-        [sds((length, width), BF16)],
-        [output_pair, swap(output_pair, "tensor", 1)],
-        name="output_rows",
-        out=None,
-    )
-
-
-    input_parts = spread(grad_inputs)
-    (grad_inputs,) = run(
-        gather_kernel, [sds((length, width), BF16)], input_parts, name="grad_rows", out=None
-    )
-
+    row_parts = spread(both_rows)
+    if split:
+        (small,) = run(
+            add_kernel,
+            [sds(small.shape, F32)],
+            [small, swap(small, "dp", 1)],
+            name="small_sum",
+        )
     if split:
         crossing = swap_chips(crossing, 4, 2)
         grad_expert_up, grad_expert_down = run(
@@ -790,37 +783,37 @@
         grad_expert_down = grad_expert_down.transpose(0, 2, 1)
         weight_own, weight_sent = run(
             weight_cross_kernel,
-            [sds((part, weight_cols), F32), sds((part, weight_cols), BF16)],
-            [weight_kept, crossing],
+            [
+                sds((part + SMALL_ROWS, weight_cols), F32),
+                sds((part + SMALL_ROWS, weight_cols), BF16),
+            ],
+            [weight_kept, crossing, small, swap_chips(small, 4, 2)],
             name="weight_cross",
         )
-        (grad_query_weight, grad_key_weight, grad_value_weight, grad_out_weight) = run(
-            weight_final_kernel,
-            [sds((part, cols), F32)] * 3 + [sds((cols, part), F32)],
+        per = part // members
+        (
+            grad_query_weight,
+            grad_key_weight,
+            grad_value_weight,
+            grad_out_weight,
+            grad_gain_attn,
+            grad_gain_expert,
+            grad_router,
+            grad_table,
+        ) = run(
+            bind(weight_final_kernel, members),
+            [sds((part, cols), F32)] * 3
+            + [sds((cols, part), F32), sds((1, per), F32), sds((1, per), F32)]
+            + [sds((EXPERTS, per), F32), sds((heads, bucket_count), F32)],
             [weight_own, swap_chips(weight_sent, 2, 4)],
-            name="weight_final", out=None,
-        )
-        for step in range(2):
-            came = swap(small, "dp", 1) if step == 0 else swap_chips(small, 2, 4)
-            (small,) = run(
-                add_kernel,
-                [sds(small.shape, F32)],
-                [small, came],
-                name="small_sum",
-                after=input_parts[2:] if step == 1 else input_parts[1:2],
-            )
-        per = part // members
-        grad_gain_attn, grad_gain_expert, grad_router, grad_table = run(
-            bind(small_final_kernel, members),
-            [sds((1, per), F32), sds((1, per), F32), sds((EXPERTS, per), F32)]
-            + [sds((heads, bucket_count), F32)],
-            [small, swap_chips(small, 4, 2)],
-            name="small_final", out=None,
+            name="weight_final",
+            out=None,
         )
         grad_table = grad_table.T
         grad_router = grad_router.T
         grad_gain_attn = grad_gain_attn.reshape(per)
         grad_gain_expert = grad_gain_expert.reshape(per)
+        done = [grad_expert_up]
     else:
 
         def scatter(values, axes, dimension):
@@ -842,6 +835,15 @@
         grad_gain_attn = pick(small[0])
         grad_gain_expert = pick(small[1])
         grad_router = pick(small[2:TABLE_ROW].T)
+        done = []
+    output, grad_inputs = run(
+        rows_kernel,
+        [sds((length, width), BF16), sds((length, width), BF16)],
+        row_parts,
+        name="rows",
+        out=None,
+        after=done,
+    )
     return (
         output,
         grad_inputs,

time: 96.2 us -> 92.6 us (0.963)
  starting transfers between devices: 43.8 us -> 37.1 us
  local copies, waits for them, and re-layouts: 0.74 us -> 3.17 us
  waiting for transfers between devices: 28.1 us -> 30.2 us
  Pallas kernels: 21.7 us -> 20.3 us
    ppermute x25 -> x23, starting transfers between devices: 35.9 us -> 30.8 us  [swap(): return lax.ppermute(values, axis, [(i, i ^ k) for i in range(size)])]
    ppermute x5 -> x4, waiting for transfers between devices: 0.83 us -> 5.23 us  [swap_chips(): return lax.ppermute(values, 'dp', pairs)]
    ppermute x25 -> x23, waiting for transfers between devices: 27.3 us -> 25 us  [swap(): return lax.ppermute(values, axis, [(i, i ^ k) for i in range(size)])]
    ppermute x5 -> x4, starting transfers between devices: 7.86 us -> 6.25 us  [swap_chips(): return lax.ppermute(values, 'dp', pairs)]
    pallas_call x22 -> x19, Pallas kernels: 21.7 us -> 20.3 us  [run(): pl.pallas_call(body, out_shape=[out(o.shape, o.dtype) for o in outs] if o...]
    unnamed x18 -> x16, local copies, waits for them, and re-layouts: 0.04 us -> 1.11 us
  transfers between devices with their start and end apart: 30 -> 27, of which waited for: 11 -> 13; matrix products, arithmetic and copies ran while one was open for 1% -> 3% of each run, Pallas kernels for 14% -> 13%
where the time goes in v4:
time: 92.6 us; the launch traced here: 92.3 us
  starting transfers between devices  37.1 us (40%)
  waiting for transfers between devices  30.2 us (33%)
  Pallas kernels  20.3 us (22%)
  local copies, waits for them, and re-layouts  3.17 us (3%)
    ppermute x23, starting transfers between devices, swap(): return lax.ppermute(values, axis, [(i, i ^ k) for i in range(size)])  30.8 us
    ppermute x23, waiting for transfers between devices, swap(): return lax.ppermute(values, axis, [(i, i ^ k) for i in range(size)])  25 us
    pallas_call x19, Pallas kernels, run(): pl.pallas_call(body, out_shape=[out(o.shape, o.dtype) for o in outs] if o...  20.3 us
    ppermute x4, starting transfers between devices, swap_chips(): return lax.ppermute(values, 'dp', pairs)  6.25 us
    ppermute x4, waiting for transfers between devices, swap_chips(): return lax.ppermute(values, 'dp', pairs)  5.23 us
  transfers between devices with their start and end apart: 27, of which 13 were waited for; matrix products, arithmetic and copies ran while one was open for 3% of the time, Pallas kernels for 13%

profile of v4, /device:TPU:0, one launch (start us, length us, event | category | flops | bytes accessed | tf_op | source)
XLA Modules:
  0.0 92.3 jit_solution(13205558330953155336)
XLA Ops:
  0.6 3.4 %attention.1 = (f32[64,768]{1,0:T(8,128)S(1)}, bf16[64,768]{1,0:T(8,128)(2,1)S(1)}, bf16[64,768]{1,0:T(8,128)(2,1)S(1)}, bf16[64,768]{1,0:T(8,128)(2,1)S(1)}, bf...) custom-call(bf16[256,768]{1,0:T(8,128)(2,1)} %refs_0_.7, ...), custom_call_target="tpu_custom_call" | custom-call | flops 200000000 | tf_op jit(solution)/shard_map/attention/pallas_call | solution.py:510
  4.1 5.1 %collective-permute-start = (bf16[64,768]{1,0:T(8,128)(2,1)S(1)}, bf16[64,768]{1,0:T(8,128)(2,1)S(1)}, u32[]{:S(2)}, u32[]{:S(2)}) collective-permute-start(bf16[64,768]{1,0:T(8,128)(2,1)S(1)} %get-tuple-element.79), channel_id=1, source_target_pairs={{0,3},{1,2},{2,1},{3,0},{4,7},{5,6},{6,5},{7,4},{8,11},{9,10},{10,... | collective-permute-start | bytes 294920 | tf_op jit(solution)/shard_map/ppermute | solution.py:530
  9.2 0.6 collective-permute-start.2
  9.9 0.7 multiply_add_fusion
  10.6 0.7 reshape.42.refs_1_
  11.2 0.7 reshape.43.refs_0_.refs_2_
  11.9 0.7 pad.4.refs_5_
  12.6 0.3 collective-permute-done.refs_2_
  12.9 4.5 %collective-permute-done.1.refs_3_ = bf16[64,768]{1,0:T(8,128)(2,1)S(1)} collective-permute-done((bf16[64,768]{1,0:T(8,128)(2,1)S(1)}, bf16[64,768]{1,0:T(8,128)(2,1)S(1)}, u32[]{:S(2)}, u32[]{:S(2)}) %collective-permute-start.1) | collective-permute-done | bytes 98336 | tf_op jit(solution)/shard_map/ppermute | solution.py:530
  17.5 0.1 hidden.1
  17.6 0.0 copy-start.6
  17.6 0.0 copy-start.7
  17.6 2.6 %collective-permute-start.3 = (bf16[64,768]{1,0:T(8,128)(2,1)S(1)}, bf16[64,768]{1,0:T(8,128)(2,1)S(1)}, u32[]{:S(2)}, u32[]{:S(2)}) collective-permute-start(bf16[64,768]{1,0:T(8,128)(2,1)S(1)} %get-tuple-element.83.refs_2_.refs_5_), channel_id=1, source_target_pairs={{0,3},{1,2},{2,1},{3,0},{4,7},{5,6},{6,5},{7,4},{8,11},{9,10},{10,... | collective-permute-start | bytes 294920 | tf_op jit(solution)/shard_map/ppermute | solution.py:530
  20.2 1.9 %collective-permute-start.5 = (bf16[64,768]{1,0:T(8,128)(2,1)S(1)}, bf16[64,768]{1,0:T(8,128)(2,1)S(1)}, u32[]{:S(2)}, u32[]{:S(2)}) collective-permute-start(bf16[64,768]{1,0:T(8,128)(2,1)S(1)} %get-tuple-element.83.refs_2_.refs_5_), channel_id=1, source_target_pairs={{0,1},{1,0},{2,3},{3,2},{4,5},{5,4},{6,7},{7,6},{8,9},{9,8},{10,11... | collective-permute-start | bytes 294920 | tf_op jit(solution)/shard_map/ppermute | solution.py:530
  22.1 2.4 %fetch.1 = (bf16[2,768,768]{2,1,0:T(8,128)(2,1)S(1)}, bf16[2,768,768]{2,1,0:T(8,128)(2,1)S(1)}) custom-call(bf16[2,768,768]{2,1,0:T(8,128)(2,1)} %refs_0_.5, bf16[2,768,768]{2,1,0:T(8,128)(2,1)} %refs_1_.4, bf16[64,768]{1,0:T(8,128)(2,1)S(1)} %get-tuple-element.83.refs_2_.refs_5_), custom_call_target="tpu_custom_call" | custom-call | flops 20000000000 | tf_op jit(solution)/shard_map/fetch/pallas_call | solution.py:510
  24.5 0.8 collective-permute-done.3.refs_6_
  25.3 3.4 %collective-permute-done.4.refs_7_ = bf16[64,768]{1,0:T(8,128)(2,1)S(1)} collective-permute-done((bf16[64,768]{1,0:T(8,128)(2,1)S(1)}, bf16[64,768]{1,0:T(8,128)(2,1)S(1)}, u32[]{:S(2)}, u32[]{:S(2)}) %collective-permute-start.4) | collective-permute-done | bytes 98336 | tf_op jit(solution)/shard_map/ppermute | solution.py:530
  28.6 3.7 %expert.1 = (bf16[64,768]{1,0:T(8,128)(2,1)S(1)}, bf16[64,768]{1,0:T(8,128)(2,1)S(1)}, bf16[64,768]{1,0:T(8,128)(2,1)S(1)}, bf16[64,768]{1,0:T(8,128)(2,1)S(1)},...) custom-call(s32[1,256]{1,0:T(1,128)S(1)} %bitcast.18, ...), custom_call_target="tpu_custom_call" | custom-call | flops 5000000000 | tf_op jit(solution)/shard_map/expert/pallas_call | solution.py:510
  32.3 1.6 %collective-permute-start.6 = (bf16[64,768]{1,0:T(8,128)(2,1)S(1)}, bf16[64,768]{1,0:T(8,128)(2,1)S(1)}, u32[]{:S(2)}, u32[]{:S(2)}) collective-permute-start(bf16[64,768]{1,0:T(8,128)(2,1)S(1)} %get-tuple-element.88), channel_id=1, source_target_pairs={{0,3},{1,2},{2,1},{3,0},{4,7},{5,6},{6,5},{7,4},{8,11},{9,10},{10,... | collective-permute-start | bytes 294920 | tf_op jit(solution)/shard_map/ppermute | solution.py:530
  33.9 2.9 %collective-permute-start.8 = (bf16[64,768]{1,0:T(8,128)(2,1)S(1)}, bf16[64,768]{1,0:T(8,128)(2,1)S(1)}, u32[]{:S(2)}, u32[]{:S(2)}) collective-permute-start(bf16[64,768]{1,0:T(8,128)(2,1)S(1)} %get-tuple-element.90), channel_id=1, source_target_pairs={{0,1},{1,0},{2,3},{3,2},{4,5},{5,4},{6,7},{7,6},{8,9},{9,8},{10,11... | collective-permute-start | bytes 294920 | tf_op jit(solution)/shard_map/ppermute | solution.py:530
  36.8 2.7 %expert_grads.1 = (bf16[4,96,3072]{2,1,0:T(8,128)(2,1)S(1)}, bf16[4,96,3072]{2,1,0:T(8,128)(2,1)S(1)}, bf16[128,768]{1,0:T(8,128)(2,1)S(1)}) custom-call(bf16[288,768]{1,0:T(8,128)(2,1)S(1)} %get-tuple-element.91.refs_0_, bf16[288,768]{1,0:T(8,128)(2,1)S(1)} %get-tuple-element.92.refs_1_, bf16[288,768]{1,0:T(8,128)(2,1)S(1)} %get-tuple-element.93.refs_2_, ...), custom_call_target="tpu_custom_call" | custom-call | flops 20000000000 | tf_op jit(solution)/shard_map/expert_grads/pallas_call | solution.py:510
  39.5 0.1 collective-permute-start.13
  39.6 0.1 collective-permute-start.12
  39.7 0.3 collective-permute-done.6.refs_4_
  40.0 2.3 %collective-permute-done.7.refs_5_ = bf16[64,768]{1,0:T(8,128)(2,1)S(1)} collective-permute-done((bf16[64,768]{1,0:T(8,128)(2,1)S(1)}, bf16[64,768]{1,0:T(8,128)(2,1)S(1)}, u32[]{:S(2)}, u32[]{:S(2)}) %collective-permute-start.7) | collective-permute-done | bytes 98336 | tf_op jit(solution)/shard_map/ppermute | solution.py:530
  42.3 0.2 hidden_back.1
  42.4 0.6 collective-permute-start.10
  43.1 2.2 %collective-permute-start.11 = (bf16[64,768]{1,0:T(8,128)(2,1)S(1)}, bf16[64,768]{1,0:T(8,128)(2,1)S(1)}, u32[]{:S(2)}, u32[]{:S(2)}) collective-permute-start(bf16[64,768]{1,0:T(8,128)(2,1)S(1)} %get-tuple-element.105.refs_11_), channel_id=1, source_target_pairs={{0,1},{1,0},{2,3},{3,2},{4,5},{5,4},{6,7},{7,6},{8,9},{9,8},{10,11... | collective-permute-start | bytes 294920 | tf_op jit(solution)/shard_map/ppermute | solution.py:530
  45.3 1.6 %collective-permute-start.9 = (bf16[64,768]{1,0:T(8,128)(2,1)S(1)}, bf16[64,768]{1,0:T(8,128)(2,1)S(1)}, u32[]{:S(2)}, u32[]{:S(2)}) collective-permute-start(bf16[64,768]{1,0:T(8,128)(2,1)S(1)} %get-tuple-element.105.refs_11_), channel_id=1, source_target_pairs={{0,3},{1,2},{2,1},{3,0},{4,7},{5,6},{6,5},{7,4},{8,11},{9,10},{10,... | collective-permute-start | bytes 294920 | tf_op jit(solution)/shard_map/ppermute | solution.py:530
  46.9 0.5 expert_merge.1
  47.4 1.6 %collective-permute-start.18 = (bf16[2,96,3072]{2,1,0:T(8,128)(2,1)S(1)}, bf16[2,96,3072]{2,1,0:T(8,128)(2,1)S(1)}, u32[]{:S(2)}, u32[]{:S(2)}) collective-permute-start(bf16[2,96,3072]{2,1,0:T(8,128)(2,1)S(1)} %get-tuple-element.121), channel_id=1, source_target_pairs={{0,8},{4,20},{8,0},{12,28},{16,24},{20,4},{24,16},{28,12},{1,9},{5... | collective-permute-start | bytes 3538952 | tf_op jit(solution)/shard_map/ppermute | solution.py:536
  49.0 2.2 %collective-permute-done.10.refs_3_.refs_13_ = bf16[64,768]{1,0:T(8,128)(2,1)S(1)} collective-permute-done((bf16[64,768]{1,0:T(8,128)(2,1)S(1)}, bf16[64,768]{1,0:T(8,128)(2,1)S(1)}, u32[]{:S(2)}, u32[]{:S(2)}) %collective-permute-start.10) | collective-permute-done | bytes 98336 | tf_op jit(solution)/shard_map/ppermute | solution.py:530
  51.1 2.1 %collective-permute-done.11.refs_4_.refs_14_ = bf16[64,768]{1,0:T(8,128)(2,1)S(1)} collective-permute-done((bf16[64,768]{1,0:T(8,128)(2,1)S(1)}, bf16[64,768]{1,0:T(8,128)(2,1)S(1)}, u32[]{:S(2)}, u32[]{:S(2)}) %collective-permute-start.11) | collective-permute-done | bytes 98336 | tf_op jit(solution)/shard_map/ppermute | solution.py:530
  53.3 0.0 copy-start.2
  53.3 0.0 copy-start.3
  53.3 0.0 copy-start.4
  53.3 0.0 copy-start.5
  53.3 0.1 pair_sum.1
  53.4 2.5 %collective-permute-start.14 = (bf16[64,768]{1,0:T(8,128)(2,1)S(1)}, bf16[64,768]{1,0:T(8,128)(2,1)S(1)}, u32[]{:S(2)}, u32[]{:S(2)}) collective-permute-start(bf16[64,768]{1,0:T(8,128)(2,1)S(1)} %get-tuple-element.115), channel_id=1, source_target_pairs={{0,2},{1,3},{2,0},{3,1},{4,6},{5,7},{6,4},{7,5},{8,10},{9,11},{10,... | collective-permute-start | bytes 294920 | tf_op jit(solution)/shard_map/ppermute | solution.py:530
  55.9 1.8 %attention_back.1 = (f32[72,768]{1,0:T(8,128)S(1)}, bf16[72,768]{1,0:T(8,128)(2,1)S(1)}, bf16[72,768]{1,0:T(8,128)(2,1)S(1)}, bf16[72,768]{1,0:T(8,128)(2,1)S(1)...) custom-call(bf16[256,768]{1,0:T(8,128)(2,1)S(1)} %copy-done.1, ...), custom_call_target="tpu_custom_call" | custom-call | flops 5000000000 | tf_op jit(solution)/shard_map/attention_back/pallas_call | solution.py:510
  57.8 1.7 %collective-permute-start.15 = (bf16[72,768]{1,0:T(8,128)(2,1)S(1)}, bf16[72,768]{1,0:T(8,128)(2,1)S(1)}, u32[]{:S(2)}, u32[]{:S(2)}) collective-permute-start(bf16[72,768]{1,0:T(8,128)(2,1)S(1)} %get-tuple-element.118), channel_id=1, source_target_pairs={{0,3},{1,2},{2,1},{3,0},{4,7},{5,6},{6,5},{7,4},{8,11},{9,10},{10,... | collective-permute-start | bytes 331784 | tf_op jit(solution)/shard_map/ppermute | solution.py:530
  59.5 0.3 collective-permute-start.16
  59.7 2.5 %collective-permute-start.17 = (bf16[72,768]{1,0:T(8,128)(2,1)S(1)}, bf16[72,768]{1,0:T(8,128)(2,1)S(1)}, u32[]{:S(2)}, u32[]{:S(2)}) collective-permute-start(bf16[72,768]{1,0:T(8,128)(2,1)S(1)} %get-tuple-element.120), channel_id=1, source_target_pairs={{0,1},{1,0},{2,3},{3,2},{4,5},{5,4},{6,7},{7,6},{8,9},{9,8},{10,11... | collective-permute-start | bytes 331784 | tf_op jit(solution)/shard_map/ppermute | solution.py:530
  62.2 2.2 %collective-permute-done.14.refs_2_ = bf16[64,768]{1,0:T(8,128)(2,1)S(1)} collective-permute-done((bf16[64,768]{1,0:T(8,128)(2,1)S(1)}, bf16[64,768]{1,0:T(8,128)(2,1)S(1)}, u32[]{:S(2)}, u32[]{:S(2)}) %collective-permute-start.14) | collective-permute-done | bytes 98336 | tf_op jit(solution)/shard_map/ppermute | solution.py:530
  64.5 1.7 %weight_grads.1 = (bf16[4,96,768]{2,1,0:T(8,128)(2,1)S(1)}, bf16[4,96,768]{2,1,0:T(8,128)(2,1)S(1)}, f32[8,768]{1,0:T(8,128)S(1)}) custom-call(bf16[256,768]{1,0:T(8,128)(2,1)S(1)} %get-tuple-element.98.refs_0_, bf16[3,256,192]{2,1,0:T(8,128)(2,1)S(1)} %get-tuple-element.111.refs_1_, bf16[256,768]{1,0:T(8,128)(2,1)S(1)} %get-tuple-element.112.refs_2_, ...), custom_call_target="tpu_custom_call" | custom-call | flops 4000000000 | tf_op jit(solution)/shard_map/weight_grads/pallas_call | solution.py:510
  66.2 0.1 collective-permute-start.19
  66.3 0.3 expert_cross.1
  66.6 1.7 %collective-permute-done.19.refs_2_ = bf16[4,96,768]{2,1,0:T(8,128)(2,1)S(1)} collective-permute-done((bf16[4,96,768]{2,1,0:T(8,128)(2,1)S(1)}, bf16[4,96,768]{2,1,0:T(8,128)(2,1)S(1)}, u32[]{:S(2)}, u32[]{:S(2)}) %collective-permute-start.19) | collective-permute-done | bytes 589856 | tf_op jit(solution)/shard_map/ppermute | solution.py:530
  68.3 0.2 cross.1
  68.4 1.6 %collective-permute-start.23 = (bf16[144,3072]{1,0:T(8,128)(2,1)S(1)}, bf16[144,3072]{1,0:T(8,128)(2,1)S(1)}, u32[]{:S(2)}, u32[]{:S(2)}) collective-permute-start(bf16[144,3072]{1,0:T(8,128)(2,1)S(1)} %get-tuple-element.128), channel_id=1, source_target_pairs={{0,16},{4,12},{8,24},{12,4},{16,0},{20,28},{24,8},{28,20},{1,17},{... | collective-permute-start | bytes 2654216 | tf_op jit(solution)/shard_map/ppermute | solution.py:536
  70.0 0.3 collective-permute-done.16.refs_7_
  70.3 0.2 input_back.1
  70.5 0.1 collective-permute-start.24
  70.5 2.9 %collective-permute-start.20 = (bf16[128,768]{1,0:T(8,128)(2,1)S(1)}, bf16[128,768]{1,0:T(8,128)(2,1)S(1)}, u32[]{:S(2)}, u32[]{:S(2)}) collective-permute-start(bf16[128,768]{1,0:T(8,128)(2,1)S(1)} %get-tuple-element.126.refs_0_), channel_id=1, source_target_pairs={{0,3},{1,2},{2,1},{3,0},{4,7},{5,6},{6,5},{7,4},{8,11},{9,10},{10,... | collective-permute-start | bytes 589832 | tf_op jit(solution)/shard_map/ppermute | solution.py:530
  73.4 1.6 %collective-permute-start.22 = (bf16[128,768]{1,0:T(8,128)(2,1)S(1)}, bf16[128,768]{1,0:T(8,128)(2,1)S(1)}, u32[]{:S(2)}, u32[]{:S(2)}) collective-permute-start(bf16[128,768]{1,0:T(8,128)(2,1)S(1)} %get-tuple-element.126.refs_0_), channel_id=1, source_target_pairs={{0,1},{1,0},{2,3},{3,2},{4,5},{5,4},{6,7},{7,6},{8,9},{9,8},{10,11... | collective-permute-start | bytes 589832 | tf_op jit(solution)/shard_map/ppermute | solution.py:530
  75.0 1.6 %collective-permute-start.25 = (f32[8,768]{1,0:T(8,128)S(1)}, f32[8,768]{1,0:T(8,128)S(1)}, u32[]{:S(2)}, u32[]{:S(2)}) collective-permute-start(f32[8,768]{1,0:T(8,128)S(1)} %small_sum.1.refs_2_), channel_id=1, source_target_pairs={{0,16},{4,12},{8,24},{12,4},{16,0},{20,28},{24,8},{28,20},{1,17},{... | collective-permute-start | bytes 73736 | tf_op jit(solution)/shard_map/ppermute | solution.py:536
  76.6 5.2 %collective-permute-done.25.refs_3_ = f32[8,768]{1,0:T(8,128)S(1)} collective-permute-done((f32[8,768]{1,0:T(8,128)S(1)}, f32[8,768]{1,0:T(8,128)S(1)}, u32[]{:S(2)}, u32[]{:S(2)}) %collective-permute-start.25) | collective-permute-done | bytes 24608 | tf_op jit(solution)/shard_map/ppermute | solution.py:536
  81.8 0.1 weight_cross.1
  81.9 1.6 %collective-permute-start.26 = (bf16[112,768]{1,0:T(8,128)(2,1)S(1)}, bf16[112,768]{1,0:T(8,128)(2,1)S(1)}, u32[]{:S(2)}, u32[]{:S(2)}) collective-permute-start(bf16[112,768]{1,0:T(8,128)(2,1)S(1)} %get-tuple-element.134), channel_id=1, source_target_pairs={{0,8},{4,20},{8,0},{12,28},{16,24},{20,4},{24,16},{28,12},{1,9},{5... | collective-permute-start | bytes 516104 | tf_op jit(solution)/shard_map/ppermute | solution.py:536
  83.5 1.1 %expert_final.1 = (f32[2,96,768]{2,1,0:T(8,128)}, f32[2,96,768]{2,1,0:T(8,128)}) custom-call(f32[96,3072]{1,0:T(8,128)S(1)} %get-tuple-element.127.refs_0_, bf16[144,3072]{1,0:T(8,128)(2,1)S(1)} %collective-permute-done.23.refs_1_), custom_call_target="tpu_custom_call" | custom-call | flops 1000000 | tf_op jit(solution)/shard_map/expert_final/pallas_call | solution.py:510
  84.6 4.9 %collective-permute-done.21.refs_2_ = bf16[128,768]{1,0:T(8,128)(2,1)S(1)} collective-permute-done((bf16[128,768]{1,0:T(8,128)(2,1)S(1)}, bf16[128,768]{1,0:T(8,128)(2,1)S(1)}, u32[]{:S(2)}, u32[]{:S(2)}) %collective-permute-start.21) | collective-permute-done | bytes 196640 | tf_op jit(solution)/shard_map/ppermute | solution.py:530
  89.4 1.1 %copy-done = f32[2,96,768]{2,1,0:T(8,128)S(1)} copy-done((f32[2,96,768]{2,1,0:T(8,128)S(1)}, f32[2,96,768]{2,1,0:T(8,128)}, u32[]{:S(2)}) %copy-start) | copy-done | bytes 589848
  90.5 0.9 %rows.1 = (bf16[256,768]{1,0:T(8,128)(2,1)}, bf16[256,768]{1,0:T(8,128)(2,1)}) custom-call(bf16[128,768]{1,0:T(8,128)(2,1)S(1)} %get-tuple-element.126.refs_0_, bf16[128,768]{1,0:T(8,128)(2,1)S(1)} %collective-permute-done.20.refs_1_, bf16[128,768]{1,0:T(8,128)(2,1)S(1)} %collective-permute-done.21.refs_2_, ...), custom_call_target="tpu_custom_call" | custom-call | flops 200000000 | tf_op jit(solution)/shard_map/rows/pallas_call | solution.py:510
  91.4 0.9 weight_final.1
  (29 shorter events, 0.1 us)
Async XLA Ops:
  4.1 8.8 %collective-permute-start = (bf16[64,768]{1,0:T(8,128)(2,1)S(1)}, bf16[64,768]{1,0:T(8,128)(2,1)S(1)}, u32[]{:S(2)}, u32[]{:S(2)}) collective-permute-start(bf16[64,768]{1,0:T(8,128)(2,1)S(1)} %get-tuple-element.79), channel_id=1, source_target_pairs={{0,3},{1,2},{2,1},{3,0},{4,7},{5,6},{6,5},{7,4},{8,11},{9,10},{10,... | collective-permute-start | bytes 294920 | tf_op jit(solution)/shard_map/ppermute | solution.py:530
  9.2 8.3 %collective-permute-start.1 = (bf16[64,768]{1,0:T(8,128)(2,1)S(1)}, bf16[64,768]{1,0:T(8,128)(2,1)S(1)}, u32[]{:S(2)}, u32[]{:S(2)}) collective-permute-start(bf16[64,768]{1,0:T(8,128)(2,1)S(1)} %get-tuple-element.80), channel_id=1, source_target_pairs={{0,2},{1,3},{2,0},{3,1},{4,6},{5,7},{6,4},{7,5},{8,10},{9,11},{10,... | collective-permute-start | bytes 294920 | tf_op jit(solution)/shard_map/ppermute | solution.py:530
  9.2 8.3 %collective-permute-start.2 = (bf16[64,768]{1,0:T(8,128)(2,1)S(1)}, bf16[64,768]{1,0:T(8,128)(2,1)S(1)}, u32[]{:S(2)}, u32[]{:S(2)}) collective-permute-start(bf16[64,768]{1,0:T(8,128)(2,1)S(1)} %get-tuple-element.81), channel_id=1, source_target_pairs={{0,1},{1,0},{2,3},{3,2},{4,5},{5,4},{6,7},{7,6},{8,9},{9,8},{10,11... | collective-permute-start | bytes 294920 | tf_op jit(solution)/shard_map/ppermute | solution.py:530
  17.6 11.0 %copy-start.6 = (bf16[256,768]{1,0:T(8,128)(2,1)S(1)}, bf16[256,768]{1,0:T(8,128)(2,1)}, u32[]{:S(2)}) copy-start(bf16[256,768]{1,0:T(8,128)(2,1)} %refs_1_.5) | copy-start | bytes 1179652
  17.6 11.0 %copy-start.7 = (bf16[768,2]{0,1:T(2,128)(2,1)S(1)}, bf16[768,2]{0,1:T(2,128)(2,1)}, u32[]{:S(2)}) copy-start(bf16[768,2]{0,1:T(2,128)(2,1)} %param.28) | copy-start | bytes 9220
  17.6 7.6 %collective-permute-start.3 = (bf16[64,768]{1,0:T(8,128)(2,1)S(1)}, bf16[64,768]{1,0:T(8,128)(2,1)S(1)}, u32[]{:S(2)}, u32[]{:S(2)}) collective-permute-start(bf16[64,768]{1,0:T(8,128)(2,1)S(1)} %get-tuple-element.83.refs_2_.refs_5_), channel_id=1, source_target_pairs={{0,3},{1,2},{2,1},{3,0},{4,7},{5,6},{6,5},{7,4},{8,11},{9,10},{10,... | collective-permute-start | bytes 294920 | tf_op jit(solution)/shard_map/ppermute | solution.py:530
  20.2 8.4 %collective-permute-start.4 = (bf16[64,768]{1,0:T(8,128)(2,1)S(1)}, bf16[64,768]{1,0:T(8,128)(2,1)S(1)}, u32[]{:S(2)}, u32[]{:S(2)}) collective-permute-start(bf16[64,768]{1,0:T(8,128)(2,1)S(1)} %get-tuple-element.83.refs_2_.refs_5_), channel_id=1, source_target_pairs={{0,2},{1,3},{2,0},{3,1},{4,6},{5,7},{6,4},{7,5},{8,10},{9,11},{10,... | collective-permute-start | bytes 294920 | tf_op jit(solution)/shard_map/ppermute | solution.py:530
  20.2 8.4 %collective-permute-start.5 = (bf16[64,768]{1,0:T(8,128)(2,1)S(1)}, bf16[64,768]{1,0:T(8,128)(2,1)S(1)}, u32[]{:S(2)}, u32[]{:S(2)}) collective-permute-start(bf16[64,768]{1,0:T(8,128)(2,1)S(1)} %get-tuple-element.83.refs_2_.refs_5_), channel_id=1, source_target_pairs={{0,1},{1,0},{2,3},{3,2},{4,5},{5,4},{6,7},{7,6},{8,9},{9,8},{10,11... | collective-permute-start | bytes 294920 | tf_op jit(solution)/shard_map/ppermute | solution.py:530
  32.3 7.7 %collective-permute-start.6 = (bf16[64,768]{1,0:T(8,128)(2,1)S(1)}, bf16[64,768]{1,0:T(8,128)(2,1)S(1)}, u32[]{:S(2)}, u32[]{:S(2)}) collective-permute-start(bf16[64,768]{1,0:T(8,128)(2,1)S(1)} %get-tuple-element.88), channel_id=1, source_target_pairs={{0,3},{1,2},{2,1},{3,0},{4,7},{5,6},{6,5},{7,4},{8,11},{9,10},{10,... | collective-permute-start | bytes 294920 | tf_op jit(solution)/shard_map/ppermute | solution.py:530
  33.9 8.3 %collective-permute-start.7 = (bf16[64,768]{1,0:T(8,128)(2,1)S(1)}, bf16[64,768]{1,0:T(8,128)(2,1)S(1)}, u32[]{:S(2)}, u32[]{:S(2)}) collective-permute-start(bf16[64,768]{1,0:T(8,128)(2,1)S(1)} %get-tuple-element.89), channel_id=1, source_target_pairs={{0,2},{1,3},{2,0},{3,1},{4,6},{5,7},{6,4},{7,5},{8,10},{9,11},{10,... | collective-permute-start | bytes 294920 | tf_op jit(solution)/shard_map/ppermute | solution.py:530
  33.9 8.3 %collective-permute-start.8 = (bf16[64,768]{1,0:T(8,128)(2,1)S(1)}, bf16[64,768]{1,0:T(8,128)(2,1)S(1)}, u32[]{:S(2)}, u32[]{:S(2)}) collective-permute-start(bf16[64,768]{1,0:T(8,128)(2,1)S(1)} %get-tuple-element.90), channel_id=1, source_target_pairs={{0,1},{1,0},{2,3},{3,2},{4,5},{5,4},{6,7},{7,6},{8,9},{9,8},{10,11... | collective-permute-start | bytes 294920 | tf_op jit(solution)/shard_map/ppermute | solution.py:530
  39.5 7.4 %collective-permute-start.13 = (bf16[4,96,3072]{2,1,0:T(8,128)(2,1)S(1)}, bf16[4,96,3072]{2,1,0:T(8,128)(2,1)S(1)}, u32[]{:S(2)}, u32[]{:S(2)}) collective-permute-start(bf16[4,96,3072]{2,1,0:T(8,128)(2,1)S(1)} %get-tuple-element.108), channel_id=1, source_target_pairs={{0,4},{4,0},{8,12},{12,8},{16,20},{20,16},{24,28},{28,24},{1,5},{5... | collective-permute-start | bytes 7077896 | tf_op jit(solution)/shard_map/ppermute | solution.py:530
  39.6 13.6 %collective-permute-start.12 = (bf16[128,768]{1,0:T(8,128)(2,1)S(1)}, bf16[128,768]{1,0:T(8,128)(2,1)S(1)}, u32[]{:S(2)}, u32[]{:S(2)}) collective-permute-start(bf16[128,768]{1,0:T(8,128)(2,1)S(1)} %get-tuple-element.96.refs_7_), channel_id=1, source_target_pairs={{0,1},{1,0},{2,3},{3,2},{4,5},{5,4},{6,7},{7,6},{8,9},{9,8},{10,11... | collective-permute-start | bytes 589832 | tf_op jit(solution)/shard_map/ppermute | solution.py:530
  42.4 8.7 %collective-permute-start.10 = (bf16[64,768]{1,0:T(8,128)(2,1)S(1)}, bf16[64,768]{1,0:T(8,128)(2,1)S(1)}, u32[]{:S(2)}, u32[]{:S(2)}) collective-permute-start(bf16[64,768]{1,0:T(8,128)(2,1)S(1)} %get-tuple-element.105.refs_11_), channel_id=1, source_target_pairs={{0,2},{1,3},{2,0},{3,1},{4,6},{5,7},{6,4},{7,5},{8,10},{9,11},{10,... | collective-permute-start | bytes 294920 | tf_op jit(solution)/shard_map/ppermute | solution.py:530
  43.1 10.2 %collective-permute-start.11 = (bf16[64,768]{1,0:T(8,128)(2,1)S(1)}, bf16[64,768]{1,0:T(8,128)(2,1)S(1)}, u32[]{:S(2)}, u32[]{:S(2)}) collective-permute-start(bf16[64,768]{1,0:T(8,128)(2,1)S(1)} %get-tuple-element.105.refs_11_), channel_id=1, source_target_pairs={{0,1},{1,0},{2,3},{3,2},{4,5},{5,4},{6,7},{7,6},{8,9},{9,8},{10,11... | collective-permute-start | bytes 294920 | tf_op jit(solution)/shard_map/ppermute | solution.py:530
  45.3 8.0 %collective-permute-start.9 = (bf16[64,768]{1,0:T(8,128)(2,1)S(1)}, bf16[64,768]{1,0:T(8,128)(2,1)S(1)}, u32[]{:S(2)}, u32[]{:S(2)}) collective-permute-start(bf16[64,768]{1,0:T(8,128)(2,1)S(1)} %get-tuple-element.105.refs_11_), channel_id=1, source_target_pairs={{0,3},{1,2},{2,1},{3,0},{4,7},{5,6},{6,5},{7,4},{8,11},{9,10},{10,... | collective-permute-start | bytes 294920 | tf_op jit(solution)/shard_map/ppermute | solution.py:530
  47.4 18.9 %collective-permute-start.18 = (bf16[2,96,3072]{2,1,0:T(8,128)(2,1)S(1)}, bf16[2,96,3072]{2,1,0:T(8,128)(2,1)S(1)}, u32[]{:S(2)}, u32[]{:S(2)}) collective-permute-start(bf16[2,96,3072]{2,1,0:T(8,128)(2,1)S(1)} %get-tuple-element.121), channel_id=1, source_target_pairs={{0,8},{4,20},{8,0},{12,28},{16,24},{20,4},{24,16},{28,12},{1,9},{5... | collective-permute-start | bytes 3538952 | tf_op jit(solution)/shard_map/ppermute | solution.py:536
  53.3 2.6 %copy-start.1 = (bf16[256,768]{1,0:T(8,128)(2,1)S(1)}, bf16[256,768]{1,0:T(8,128)(2,1)}, u32[]{:S(2)}) copy-start(bf16[256,768]{1,0:T(8,128)(2,1)} %refs_0_.7) | copy-start | bytes 1179652
  53.3 2.6 %copy-start.2 = (bf16[768,192]{0,1:T(8,128)(2,1)S(1)}, bf16[768,192]{0,1:T(8,128)(2,1)}, u32[]{:S(2)}) copy-start(bf16[768,192]{0,1:T(8,128)(2,1)} %param.23) | copy-start | bytes 884740
  53.3 2.6 %copy-start.3 = (bf16[768,192]{0,1:T(8,128)(2,1)S(1)}, bf16[768,192]{0,1:T(8,128)(2,1)}, u32[]{:S(2)}) copy-start(bf16[768,192]{0,1:T(8,128)(2,1)} %param.24) | copy-start | bytes 884740
  53.3 2.6 %copy-start.4 = (bf16[768,192]{0,1:T(8,128)(2,1)S(1)}, bf16[768,192]{0,1:T(8,128)(2,1)}, u32[]{:S(2)}) copy-start(bf16[768,192]{0,1:T(8,128)(2,1)} %param.25) | copy-start | bytes 884740
  53.3 2.6 %copy-start.5 = (bf16[192,768]{1,0:T(8,128)(2,1)S(1)}, bf16[192,768]{1,0:T(8,128)(2,1)}, u32[]{:S(2)}) copy-start(bf16[192,768]{1,0:T(8,128)(2,1)} %refs_8_.3) | copy-start | bytes 884740
  53.4 11.1 %collective-permute-start.14 = (bf16[64,768]{1,0:T(8,128)(2,1)S(1)}, bf16[64,768]{1,0:T(8,128)(2,1)S(1)}, u32[]{:S(2)}, u32[]{:S(2)}) collective-permute-start(bf16[64,768]{1,0:T(8,128)(2,1)S(1)} %get-tuple-element.115), channel_id=1, source_target_pairs={{0,2},{1,3},{2,0},{3,1},{4,6},{5,7},{6,4},{7,5},{8,10},{9,11},{10,... | collective-permute-start | bytes 294920 | tf_op jit(solution)/shard_map/ppermute | solution.py:530
  57.8 12.3 %collective-permute-start.15 = (bf16[72,768]{1,0:T(8,128)(2,1)S(1)}, bf16[72,768]{1,0:T(8,128)(2,1)S(1)}, u32[]{:S(2)}, u32[]{:S(2)}) collective-permute-start(bf16[72,768]{1,0:T(8,128)(2,1)S(1)} %get-tuple-element.118), channel_id=1, source_target_pairs={{0,3},{1,2},{2,1},{3,0},{4,7},{5,6},{6,5},{7,4},{8,11},{9,10},{10,... | collective-permute-start | bytes 331784 | tf_op jit(solution)/shard_map/ppermute | solution.py:530
  59.5 10.8 %collective-permute-start.16 = (bf16[72,768]{1,0:T(8,128)(2,1)S(1)}, bf16[72,768]{1,0:T(8,128)(2,1)S(1)}, u32[]{:S(2)}, u32[]{:S(2)}) collective-permute-start(bf16[72,768]{1,0:T(8,128)(2,1)S(1)} %get-tuple-element.119), channel_id=1, source_target_pairs={{0,2},{1,3},{2,0},{3,1},{4,6},{5,7},{6,4},{7,5},{8,10},{9,11},{10,... | collective-permute-start | bytes 331784 | tf_op jit(solution)/shard_map/ppermute | solution.py:530
  59.7 10.6 %collective-permute-start.17 = (bf16[72,768]{1,0:T(8,128)(2,1)S(1)}, bf16[72,768]{1,0:T(8,128)(2,1)S(1)}, u32[]{:S(2)}, u32[]{:S(2)}) collective-permute-start(bf16[72,768]{1,0:T(8,128)(2,1)S(1)} %get-tuple-element.120), channel_id=1, source_target_pairs={{0,1},{1,0},{2,3},{3,2},{4,5},{5,4},{6,7},{7,6},{8,9},{9,8},{10,11... | collective-permute-start | bytes 331784 | tf_op jit(solution)/shard_map/ppermute | solution.py:530
  66.2 2.1 %collective-permute-start.19 = (bf16[4,96,768]{2,1,0:T(8,128)(2,1)S(1)}, bf16[4,96,768]{2,1,0:T(8,128)(2,1)S(1)}, u32[]{:S(2)}, u32[]{:S(2)}) collective-permute-start(bf16[4,96,768]{2,1,0:T(8,128)(2,1)S(1)} %get-tuple-element.124), channel_id=1, source_target_pairs={{0,4},{4,0},{8,12},{12,8},{16,20},{20,16},{24,28},{28,24},{1,5},{5... | collective-permute-start | bytes 1769480 | tf_op jit(solution)/shard_map/ppermute | solution.py:530
  68.4 13.4 %collective-permute-start.23 = (bf16[144,3072]{1,0:T(8,128)(2,1)S(1)}, bf16[144,3072]{1,0:T(8,128)(2,1)S(1)}, u32[]{:S(2)}, u32[]{:S(2)}) collective-permute-start(bf16[144,3072]{1,0:T(8,128)(2,1)S(1)} %get-tuple-element.128), channel_id=1, source_target_pairs={{0,16},{4,12},{8,24},{12,4},{16,0},{20,28},{24,8},{28,20},{1,17},{... | collective-permute-start | bytes 2654216 | tf_op jit(solution)/shard_map/ppermute | solution.py:536
  70.5 4.5 %collective-permute-start.24 = (f32[8,768]{1,0:T(8,128)S(1)}, f32[8,768]{1,0:T(8,128)S(1)}, u32[]{:S(2)}, u32[]{:S(2)}) collective-permute-start(f32[8,768]{1,0:T(8,128)S(1)} %get-tuple-element.132.refs_0_), channel_id=1, source_target_pairs={{0,4},{4,0},{8,12},{12,8},{16,20},{20,16},{24,28},{28,24},{1,5},{5... | collective-permute-start | bytes 73736 | tf_op jit(solution)/shard_map/ppermute | solution.py:530
  70.5 14.0 %collective-permute-start.20 = (bf16[128,768]{1,0:T(8,128)(2,1)S(1)}, bf16[128,768]{1,0:T(8,128)(2,1)S(1)}, u32[]{:S(2)}, u32[]{:S(2)}) collective-permute-start(bf16[128,768]{1,0:T(8,128)(2,1)S(1)} %get-tuple-element.126.refs_0_), channel_id=1, source_target_pairs={{0,3},{1,2},{2,1},{3,0},{4,7},{5,6},{6,5},{7,4},{8,11},{9,10},{10,... | collective-permute-start | bytes 589832 | tf_op jit(solution)/shard_map/ppermute | solution.py:530
  73.4 16.0 %collective-permute-start.21 = (bf16[128,768]{1,0:T(8,128)(2,1)S(1)}, bf16[128,768]{1,0:T(8,128)(2,1)S(1)}, u32[]{:S(2)}, u32[]{:S(2)}) collective-permute-start(bf16[128,768]{1,0:T(8,128)(2,1)S(1)} %get-tuple-element.126.refs_0_), channel_id=1, source_target_pairs={{0,2},{1,3},{2,0},{3,1},{4,6},{5,7},{6,4},{7,5},{8,10},{9,11},{10,... | collective-permute-start | bytes 589832 | tf_op jit(solution)/shard_map/ppermute | solution.py:530
  73.4 16.0 %collective-permute-start.22 = (bf16[128,768]{1,0:T(8,128)(2,1)S(1)}, bf16[128,768]{1,0:T(8,128)(2,1)S(1)}, u32[]{:S(2)}, u32[]{:S(2)}) collective-permute-start(bf16[128,768]{1,0:T(8,128)(2,1)S(1)} %get-tuple-element.126.refs_0_), channel_id=1, source_target_pairs={{0,1},{1,0},{2,3},{3,2},{4,5},{5,4},{6,7},{7,6},{8,9},{9,8},{10,11... | collective-permute-start | bytes 589832 | tf_op jit(solution)/shard_map/ppermute | solution.py:530
  75.0 6.8 %collective-permute-start.25 = (f32[8,768]{1,0:T(8,128)S(1)}, f32[8,768]{1,0:T(8,128)S(1)}, u32[]{:S(2)}, u32[]{:S(2)}) collective-permute-start(f32[8,768]{1,0:T(8,128)S(1)} %small_sum.1.refs_2_), channel_id=1, source_target_pairs={{0,16},{4,12},{8,24},{12,4},{16,0},{20,28},{24,8},{28,20},{1,17},{... | collective-permute-start | bytes 73736 | tf_op jit(solution)/shard_map/ppermute | solution.py:536
  81.9 9.5 %collective-permute-start.26 = (bf16[112,768]{1,0:T(8,128)(2,1)S(1)}, bf16[112,768]{1,0:T(8,128)(2,1)S(1)}, u32[]{:S(2)}, u32[]{:S(2)}) collective-permute-start(bf16[112,768]{1,0:T(8,128)(2,1)S(1)} %get-tuple-element.134), channel_id=1, source_target_pairs={{0,8},{4,20},{8,0},{12,28},{16,24},{20,4},{24,16},{28,12},{1,9},{5... | collective-permute-start | bytes 516104 | tf_op jit(solution)/shard_map/ppermute | solution.py:536
  89.4 1.1 %copy-start = (f32[2,96,768]{2,1,0:T(8,128)S(1)}, f32[2,96,768]{2,1,0:T(8,128)}, u32[]{:S(2)}) copy-start(f32[2,96,768]{2,1,0:T(8,128)} %get-tuple-element.76.refs_4_) | copy-start | bytes 1769476

commit v5 on v4

--- a/solution.py
+++ b/solution.py
@@ -27,7 +27,7 @@
     "expert_cross": 8,
     "input_back": 60,
     "expert_final": 0.001,
-    "weight_final": 0.001,
+    "finish": 0.001,
     "small_sum": 0.001,
     "weight_cross": 0.001,
 }
@@ -120,13 +120,26 @@
     ]
     for copy in copies:
         copy.start()
-    inputs, gain, wq, wk, wv, buckets, table, segment, wo = local
+    buckets, table, segment, inputs, gain, wq, wk, wv, wo = local
     length = inputs.shape[0]
     heads = wq.shape[0] // HEAD_DIM
-    copies[0].wait()
+    for copy in copies[:3]:
+        copy.wait()
+    hot = bucket_hot_of(buckets, table.shape[1])
+    seg_row = segment[...].astype(F32)
+    same = column_of(seg_row, length) == seg_row
+    offset_rows[...] = jnp.zeros_like(offset_rows)
+    offset_rows[0:heads, 0 : hot.shape[1]] = jnp.dot(
+        table[...], hot, preferred_element_type=F32, precision=HIGHEST
+    )
+    for h in range(heads):
+        spread = jnp.broadcast_to(offset_rows[h : h + 1, :], (length, 2 * length))
+        bias = pltpu.roll(spread, length + 1, 1, stride=1, stride_axis=0)[:, :length]
+        probs_o[h] = jnp.where(same, bias, -1e30)
+    copies[3].wait()
     x = inputs[...].astype(F32)
     scaled = x * inverse_rms(x)
-    for copy in copies[1:8]:
+    for copy in copies[4:8]:
         copy.wait()
     normed = (scaled * gain[...].reshape(1, -1)).astype(BF16)
     normed_o[...] = normed
@@ -136,19 +149,9 @@
     q_o[...] = q
     k_o[...] = k
     v_o[...] = v
-    hot = bucket_hot_of(buckets, table.shape[1])
-    seg_row = segment[...].astype(F32)
-    same = column_of(seg_row, length) == seg_row
     mixed = jnp.zeros((length, wq.shape[0]), F32)
-    offset_rows[...] = jnp.zeros_like(offset_rows)
-    offset_rows[0:heads, 0 : hot.shape[1]] = jnp.dot(
-        table[...], hot, preferred_element_type=F32, precision=HIGHEST
-    )
     for h in range(heads):
-        spread = jnp.broadcast_to(offset_rows[h : h + 1, :], (length, 2 * length))
-        bias = pltpu.roll(spread, length + 1, 1, stride=1, stride_axis=0)[:, :length]
-        scores = dot_nt(masked(q, h), k) + bias
-        scores = jnp.where(same, scores, -1e30)
+        scores = dot_nt(masked(q, h), k) + probs_o[h]
         shifted = jnp.exp(scores - jnp.max(scores, axis=-1, keepdims=True))
         probs = shifted / jnp.sum(shifted, axis=-1, keepdims=True)
         probs_o[h] = probs
@@ -169,6 +172,11 @@
     normed_o[...] = (hidden * inverse_rms(hidden) * gain[...]).astype(BF16)
 
 
+def place_of(where_to):
+    slots = lax.broadcasted_iota(jnp.int32, (EXPERTS * CAP, where_to.shape[1]), 0)
+    return (slots == where_to[...]).astype(BF16)
+
+
 def fetch_kernel(up, down, up_o, down_o, sems):
     copies = [
         pltpu.make_async_copy(up, up_o, sems.at[0]),
@@ -183,17 +191,15 @@
 def expert_kernel(members, where_to, cotangent, router_t, up, down, *rest):
     pieces = rest[:members]
     rest = rest[members:]
-    back_o, row_o = rest[:members], rest[members : members + 2]
+    back_o, rows = rest[:members], rest[members]
     buffer_o, active_o, grad_before_o, grad_expert_o, router_o, dy_o = rest[
-        members + 2 : members + 8
+        members + 1 : members + 7
     ]
-    normed, backs, rows, acc = rest[members + 8 :]
+    normed, backs, acc = rest[members + 7 :]
     length = cotangent.shape[0]
     assemble(normed, pieces)
     dy_o[...] = cotangent[share_of(lax.axis_index("tensor"), dy_o.shape[0]), :]
-    place = (
-        lax.broadcasted_iota(jnp.int32, (EXPERTS * CAP, length), 0) == where_to[...]
-    ).astype(BF16)
+    place = place_of(where_to)
     buffer = dot(place, normed[...]).astype(BF16)
     buffer_o[...] = buffer
     dy_buffer = dot(place, cotangent[...])
@@ -234,23 +240,23 @@
         router_o[other : other + 1, :] = router_grad[other]
     acc[...] = dot_tn(place, backs[...])
     put_shares(acc, back_o)
+
+
+def split_rows(keep, send, chip, part):
+    core = lax.rem(lax.axis_index("dp"), 2)
+    return share_of(2 * chip + core, part), share_of(2 * chip + 1 - core, part)
+
+
+def expert_grad_kernel(split, where_to, buffer, active, grad_before, grad_expert, rows, *rest):
+    row_o, scratch, acc = rest[-4:-2], rest[-2], rest[-1]
+    place = place_of(where_to)
     acc[...] = dot_tn(place, rows[...])
     me = lax.axis_index("tensor")
-    share = back_o[0].shape[0]
+    share = row_o[0].shape[0] // 2
     for first, ref in enumerate(row_o):
         for k in range(2):
             index = jnp.bitwise_xor(me, first + 2 * k)
             ref[k * share : (k + 1) * share, :] = acc[share_of(index, share), :].astype(BF16)
-
-
-def split_rows(keep, send, chip, part):
-    core = lax.rem(lax.axis_index("dp"), 2)
-    return share_of(2 * chip + core, part), share_of(2 * chip + 1 - core, part)
-
-
-def expert_grad_kernel(split, buffer, active, grad_before, grad_expert, rows, *rest):
-    scratch, rows_o = rest[-1], rest[-2]
-    rows_o[...] = rows[...]
     for e in range(EXPERTS):
         slot = slice(e * CAP, (e + 1) * CAP)
         for which in range(2):
@@ -342,13 +348,21 @@
     other[...] = (kept[share:, :].astype(F32) + came[share:, :].astype(F32)).astype(BF16)
 
 
+def pair_kernel(own, came, out):
+    share = own.shape[0]
+    out[0:share, :] = own[...]
+    out[share:, :] = came[...]
+
+
 def rows_kernel(*refs):
-    shares, (output, grad_inputs) = refs[:-2], refs[-2:]
-    for i, ref in enumerate(shares):
-        rows = ref.shape[0] // 2
-        there = share_of(member_at(i, len(shares)), rows)
-        grad_inputs[there, :] = ref[0:rows, :]
-        output[there, :] = ref[rows:, :]
+    shares, pairs, (output, grad_inputs) = refs[:-4], refs[-4:-2], refs[-2:]
+    assemble(grad_inputs, shares)
+    me = lax.axis_index("tensor")
+    rows = output.shape[0] // len(shares)
+    for near, ref in enumerate(pairs):
+        for k in range(2):
+            there = jnp.bitwise_xor(me, near + 2 * k)
+            output[share_of(there, rows), :] = ref[k * rows : (k + 1) * rows, :]
 
 
 def hidden_back_kernel(members, hidden, cotangent, gain, *rest):
@@ -483,18 +497,23 @@
     out[...] = (hidden[...] + own[...] + came[...].astype(F32)).astype(BF16)
 
 
-def input_back_kernel(members, inputs, gain, grad_hidden, table, output, *rest):
+def finish_kernel(members, *refs):
+    weight_in, row_in, outs = refs[:2], refs[2 : members + 4], refs[members + 4 :]
+    weight_final_kernel(members, *weight_in, *outs[2:])
+    rows_kernel(*row_in, *outs[:2])
+
+
+def input_back_kernel(members, inputs, gain, grad_hidden, table, *rest):
     out, small_o = rest[members:]
-    share = output.shape[0]
+    share = out.shape[0]
     x = inputs[share_of(lax.axis_index("tensor"), share), :].astype(F32)
     r = inverse_rms(x)
     total = total_of(rest[:members])
     small_o[...] = total[share:] + table[...]
     z = total[0:share] * gain[...]
-    out[0:share, :] = (
+    out[...] = (
         grad_hidden[...] + r * z - x * (r * r * r) * jnp.mean(z * x, axis=-1, keepdims=True)
     ).astype(BF16)
-    out[share:, :] = output[...]
 
 
 def run(kernel, outs, args, scratch=(), name=None, after=(), space=pltpu.VMEM, out=pltpu.VMEM):
@@ -591,14 +610,14 @@
     query_t, key_t, value_t = query_weight.T, key_weight.T, value_weight.T
 
     attention_args = [
+        bucket_row,
+        bias_table.T,
+        segments,
         inputs,
         gain_attn,
         query_t,
         key_t,
         value_t,
-        bucket_row,
-        bias_table.T,
-        segments,
         out_weight,
     ]
     attention_args = [pltpu.with_memory_space_constraint(a, pltpu.HBM) for a in attention_args]
@@ -639,22 +658,19 @@
     outs = run(
         bind(expert_kernel, members),
         shares_sds(BF16)
-        + [sds((2 * share, width), BF16)] * 2
-        + [sds((slots, width), BF16)]
+        + [sds((slots, width), BF16)] * 2
         + [sds((slots, hidden_units), BF16)] * 2
         + [sds((slots, width), BF16), sds((EXPERTS, width), F32), sds((share, width), BF16)],
         [where_to, cotangent, router_t, up, down] + normed_two,
         [
             pltpu.VMEM((length, width), BF16),
             pltpu.VMEM((slots, width), BF16),
-            pltpu.VMEM((slots, width), BF16),
             pltpu.VMEM((length, width), F32),
         ],
         name="expert",
     )
     back_rows = exchange(outs[:members])
-    rows_kept, rows_sent = outs[members : members + 2]
-    buffer, active, grad_before, grad_expert, grad_router, dy_share = outs[members + 2 :]
+    slot_rows, buffer, active, grad_before, grad_expert, grad_router, dy_share = outs[members:]
 
     def split_sds(rows, columns):
         return [sds((chips, rows, columns), BF16)] * 2
@@ -665,13 +681,13 @@
     expert_grads = run(
         bind(expert_grad_kernel, split),
         (split_sds(part, 4 * hidden_units) if split else [sds((width, 4 * hidden_units), F32)])
-        + [sds(rows_sent.shape, BF16)],
-        [buffer, active, grad_before, grad_expert, rows_sent],
-        [pltpu.VMEM((width, hidden_units), F32)],
+        + [sds((2 * share, width), BF16)] * 2,
+        [where_to, buffer, active, grad_before, grad_expert, slot_rows],
+        [pltpu.VMEM((width, hidden_units), F32), pltpu.VMEM((length, width), F32)],
         name="expert_grads",
     )
 
-    rows_sent = expert_grads[-1]
+    rows_kept, rows_sent = expert_grads[-2:]
     grad_hidden, grad_attended, grad_gain_expert = run(
         bind(hidden_back_kernel, members),
         [sds((share, width), F32), sds((share, width), BF16), sds((1, width), F32)],
@@ -755,16 +771,23 @@
             name="cross",
         )
         crossed = [weight_kept]
-    both_rows, small = run(
+    grad_share, small = run(
         bind(input_back_kernel, members),
-        [sds((2 * share, width), BF16), sds((8, width), F32)],
+        [sds((share, width), BF16), sds((8, width), F32)],
         [inputs, gain_row, grad_hidden, weight_grads[-1]]
-        + [output_share]
         + grad_normed,
         name="input_back",
         after=crossed,
     )
-    row_parts = spread(both_rows)
+    row_parts = spread(grad_share)
+    (output_pair,) = run(
+        pair_kernel,
+        [sds((2 * share, width), BF16)],
+        [output_share, swap(output_share, "tensor", 2)],
+        name="output_pair",
+        after=[small],
+    )
+    row_parts += [output_pair, swap(output_pair, "tensor", 1)]
     if split:
         (small,) = run(
             add_kernel,
@@ -789,9 +812,13 @@
             ],
             [weight_kept, crossing, small, swap_chips(small, 4, 2)],
             name="weight_cross",
+            after=row_parts[1:members],
         )
         per = part // members
+        done = [pltpu.with_memory_space_constraint(grad_expert_up, pltpu.HBM)]
         (
+            output,
+            grad_inputs,
             grad_query_weight,
             grad_key_weight,
             grad_value_weight,
@@ -801,19 +828,20 @@
             grad_router,
             grad_table,
         ) = run(
-            bind(weight_final_kernel, members),
-            [sds((part, cols), F32)] * 3
+            bind(finish_kernel, members),
+            [sds((length, width), BF16)] * 2
+            + [sds((part, cols), F32)] * 3
             + [sds((cols, part), F32), sds((1, per), F32), sds((1, per), F32)]
             + [sds((EXPERTS, per), F32), sds((heads, bucket_count), F32)],
-            [weight_own, swap_chips(weight_sent, 2, 4)],
-            name="weight_final",
+            [weight_own, swap_chips(weight_sent, 2, 4)] + row_parts,
+            name="finish",
             out=None,
+            after=done,
         )
         grad_table = grad_table.T
         grad_router = grad_router.T
         grad_gain_attn = grad_gain_attn.reshape(per)
         grad_gain_expert = grad_gain_expert.reshape(per)
-        done = [grad_expert_up]
     else:
 
         def scatter(values, axes, dimension):
@@ -835,15 +863,9 @@
         grad_gain_attn = pick(small[0])
         grad_gain_expert = pick(small[1])
         grad_router = pick(small[2:TABLE_ROW].T)
-        done = []
-    output, grad_inputs = run(
-        rows_kernel,
-        [sds((length, width), BF16), sds((length, width), BF16)],
-        row_parts,
-        name="rows",
-        out=None,
-        after=done,
-    )
+        output, grad_inputs = run(
+            rows_kernel, [sds((length, width), BF16)] * 2, row_parts, name="rows", out=None
+        )
     return (
         output,
         grad_inputs,

time: 92.6 us -> 91.2 us (0.985)
  starting transfers between devices: 37.1 us -> 36.1 us
    ppermute x23 -> x25, waiting for transfers between devices: 25 us -> 26.9 us  [swap(): return lax.ppermute(values, axis, [(i, i ^ k) for i in range(size)])]
    ppermute x4, waiting for transfers between devices: 5.23 us -> 3.72 us  [swap_chips(): return lax.ppermute(values, 'dp', pairs)]
    ppermute x23 -> x25, starting transfers between devices: 30.8 us -> 29.7 us  [swap(): return lax.ppermute(values, axis, [(i, i ^ k) for i in range(size)])]
  transfers between devices with their start and end apart: 27 -> 29, of which waited for: 13 -> 14; matrix products, arithmetic and copies ran while one was open for 3% -> 3% of each run, Pallas kernels for 13% -> 13%
where the time goes in v5:
time: 91.2 us; the launch traced here: 90.9 us
  starting transfers between devices  36.1 us (40%)
  waiting for transfers between devices  30.6 us (34%)
  Pallas kernels  19.9 us (22%)
  local copies, waits for them, and re-layouts  2.86 us (3%)
    ppermute x25, starting transfers between devices, swap(): return lax.ppermute(values, axis, [(i, i ^ k) for i in range(size)])  29.7 us
    ppermute x25, waiting for transfers between devices, swap(): return lax.ppermute(values, axis, [(i, i ^ k) for i in range(size)])  26.9 us
    pallas_call x19, Pallas kernels, run(): pl.pallas_call(body, out_shape=[out(o.shape, o.dtype) for o in outs] if o...  19.9 us
    ppermute x4, starting transfers between devices, swap_chips(): return lax.ppermute(values, 'dp', pairs)  6.31 us
    ppermute x4, waiting for transfers between devices, swap_chips(): return lax.ppermute(values, 'dp', pairs)  3.72 us
  transfers between devices with their start and end apart: 29, of which 14 were waited for; matrix products, arithmetic and copies ran while one was open for 3% of the time, Pallas kernels for 13%

profile of v5, /device:TPU:0, one launch (start us, length us, event | category | flops | bytes accessed | tf_op | source)
XLA Modules:
  0.0 90.9 jit_solution(5462551657998307066)
XLA Ops:
  0.6 2.9 %attention.1 = (f32[64,768]{1,0:T(8,128)S(1)}, bf16[64,768]{1,0:T(8,128)(2,1)S(1)}, bf16[64,768]{1,0:T(8,128)(2,1)S(1)}, bf16[64,768]{1,0:T(8,128)(2,1)S(1)}, bf...) custom-call(s32[1,511]{1,0:T(1,128)} %bitcast.21, ...), custom_call_target="tpu_custom_call" | custom-call | flops 200000000 | tf_op jit(solution)/shard_map/attention/pallas_call | solution.py:529
  3.6 5.1 %collective-permute-start = (bf16[64,768]{1,0:T(8,128)(2,1)S(1)}, bf16[64,768]{1,0:T(8,128)(2,1)S(1)}, u32[]{:S(2)}, u32[]{:S(2)}) collective-permute-start(bf16[64,768]{1,0:T(8,128)(2,1)S(1)} %get-tuple-element.79), channel_id=1, source_target_pairs={{0,3},{1,2},{2,1},{3,0},{4,7},{5,6},{6,5},{7,4},{8,11},{9,10},{10,... | collective-permute-start | bytes 294920 | tf_op jit(solution)/shard_map/ppermute | solution.py:549
  8.7 0.6 collective-permute-start.2
  9.4 0.7 multiply_add_fusion
  10.1 0.7 reshape.45.refs_1_
  10.8 0.7 reshape.43.refs_0_.refs_2_
  11.4 0.7 pad.4.refs_5_
  12.1 0.3 collective-permute-done.refs_2_
  12.4 4.5 %collective-permute-done.1.refs_3_ = bf16[64,768]{1,0:T(8,128)(2,1)S(1)} collective-permute-done((bf16[64,768]{1,0:T(8,128)(2,1)S(1)}, bf16[64,768]{1,0:T(8,128)(2,1)S(1)}, u32[]{:S(2)}, u32[]{:S(2)}) %collective-permute-start.1) | collective-permute-done | bytes 98336 | tf_op jit(solution)/shard_map/ppermute | solution.py:549
  17.0 0.1 hidden.1
  17.1 0.0 copy-start.5
  17.2 2.6 %collective-permute-start.3 = (bf16[64,768]{1,0:T(8,128)(2,1)S(1)}, bf16[64,768]{1,0:T(8,128)(2,1)S(1)}, u32[]{:S(2)}, u32[]{:S(2)}) collective-permute-start(bf16[64,768]{1,0:T(8,128)(2,1)S(1)} %get-tuple-element.82.refs_2_.refs_5_), channel_id=1, source_target_pairs={{0,3},{1,2},{2,1},{3,0},{4,7},{5,6},{6,5},{7,4},{8,11},{9,10},{10,... | collective-permute-start | bytes 294920 | tf_op jit(solution)/shard_map/ppermute | solution.py:549
  19.8 1.9 %collective-permute-start.5 = (bf16[64,768]{1,0:T(8,128)(2,1)S(1)}, bf16[64,768]{1,0:T(8,128)(2,1)S(1)}, u32[]{:S(2)}, u32[]{:S(2)}) collective-permute-start(bf16[64,768]{1,0:T(8,128)(2,1)S(1)} %get-tuple-element.82.refs_2_.refs_5_), channel_id=1, source_target_pairs={{0,1},{1,0},{2,3},{3,2},{4,5},{5,4},{6,7},{7,6},{8,9},{9,8},{10,11... | collective-permute-start | bytes 294920 | tf_op jit(solution)/shard_map/ppermute | solution.py:549
  21.6 2.4 %fetch.1 = (bf16[2,768,768]{2,1,0:T(8,128)(2,1)S(1)}, bf16[2,768,768]{2,1,0:T(8,128)(2,1)S(1)}) custom-call(bf16[2,768,768]{2,1,0:T(8,128)(2,1)} %refs_0_.3, bf16[2,768,768]{2,1,0:T(8,128)(2,1)} %refs_1_.2, bf16[64,768]{1,0:T(8,128)(2,1)S(1)} %get-tuple-element.82.refs_2_.refs_5_), custom_call_target="tpu_custom_call" | custom-call | flops 20000000000 | tf_op jit(solution)/shard_map/fetch/pallas_call | solution.py:529
  24.0 0.8 collective-permute-done.3.refs_6_
  24.8 3.4 %collective-permute-done.4.refs_7_ = bf16[64,768]{1,0:T(8,128)(2,1)S(1)} collective-permute-done((bf16[64,768]{1,0:T(8,128)(2,1)S(1)}, bf16[64,768]{1,0:T(8,128)(2,1)S(1)}, u32[]{:S(2)}, u32[]{:S(2)}) %collective-permute-start.4) | collective-permute-done | bytes 98336 | tf_op jit(solution)/shard_map/ppermute | solution.py:549
  28.1 3.5 %expert.1 = (bf16[64,768]{1,0:T(8,128)(2,1)S(1)}, bf16[64,768]{1,0:T(8,128)(2,1)S(1)}, bf16[64,768]{1,0:T(8,128)(2,1)S(1)}, bf16[64,768]{1,0:T(8,128)(2,1)S(1)},...) custom-call(s32[1,256]{1,0:T(1,128)S(1)} %bitcast.18, ...), custom_call_target="tpu_custom_call" | custom-call | flops 5000000000 | tf_op jit(solution)/shard_map/expert/pallas_call | solution.py:529
  31.6 1.6 %collective-permute-start.8 = (bf16[64,768]{1,0:T(8,128)(2,1)S(1)}, bf16[64,768]{1,0:T(8,128)(2,1)S(1)}, u32[]{:S(2)}, u32[]{:S(2)}) collective-permute-start(bf16[64,768]{1,0:T(8,128)(2,1)S(1)} %get-tuple-element.102), channel_id=1, source_target_pairs={{0,3},{1,2},{2,1},{3,0},{4,7},{5,6},{6,5},{7,4},{8,11},{9,10},{10,... | collective-permute-start | bytes 294920 | tf_op jit(solution)/shard_map/ppermute | solution.py:549
  33.2 2.9 %collective-permute-start.10 = (bf16[64,768]{1,0:T(8,128)(2,1)S(1)}, bf16[64,768]{1,0:T(8,128)(2,1)S(1)}, u32[]{:S(2)}, u32[]{:S(2)}) collective-permute-start(bf16[64,768]{1,0:T(8,128)(2,1)S(1)} %get-tuple-element.104), channel_id=1, source_target_pairs={{0,1},{1,0},{2,3},{3,2},{4,5},{5,4},{6,7},{7,6},{8,9},{9,8},{10,11... | collective-permute-start | bytes 294920 | tf_op jit(solution)/shard_map/ppermute | solution.py:549
  36.1 3.6 %expert_grads.1 = (bf16[4,96,3072]{2,1,0:T(8,128)(2,1)S(1)}, bf16[4,96,3072]{2,1,0:T(8,128)(2,1)S(1)}, bf16[128,768]{1,0:T(8,128)(2,1)S(1)}, bf16[128,768]{1,0:T(8,128)(2,1)S(1)}) custom-call(s32[1,256]{1,0:T(1,128)S(1)} %bitcast.19, bf16[288,768]{1,0:T(8,128)(2,1)S(1)} %get-tuple-element.85.refs_1_, bf16[288,768]{1,0:T(8,128)(2,1)S(1)} %get-tuple-element.86.refs_2_, ...), custom_call_target="tpu_custom_call" | custom-call | flops 20000000000 | tf_op jit(solution)/shard_map/expert_grads/pallas_call | solution.py:529
  39.7 0.1 collective-permute-start.6
  39.8 0.1 collective-permute-start.14
  39.9 1.7 %collective-permute-done.9.refs_5_ = bf16[64,768]{1,0:T(8,128)(2,1)S(1)} collective-permute-done((bf16[64,768]{1,0:T(8,128)(2,1)S(1)}, bf16[64,768]{1,0:T(8,128)(2,1)S(1)}, u32[]{:S(2)}, u32[]{:S(2)}) %collective-permute-start.9) | collective-permute-done | bytes 98336 | tf_op jit(solution)/shard_map/ppermute | solution.py:549
  41.6 0.2 hidden_back.1
  41.7 2.2 %collective-permute-start.11 = (bf16[64,768]{1,0:T(8,128)(2,1)S(1)}, bf16[64,768]{1,0:T(8,128)(2,1)S(1)}, u32[]{:S(2)}, u32[]{:S(2)}) collective-permute-start(bf16[64,768]{1,0:T(8,128)(2,1)S(1)} %get-tuple-element.108.refs_11_), channel_id=1, source_target_pairs={{0,3},{1,2},{2,1},{3,0},{4,7},{5,6},{6,5},{7,4},{8,11},{9,10},{10,... | collective-permute-start | bytes 294920 | tf_op jit(solution)/shard_map/ppermute | solution.py:549
  44.0 2.2 %collective-permute-start.13 = (bf16[64,768]{1,0:T(8,128)(2,1)S(1)}, bf16[64,768]{1,0:T(8,128)(2,1)S(1)}, u32[]{:S(2)}, u32[]{:S(2)}) collective-permute-start(bf16[64,768]{1,0:T(8,128)(2,1)S(1)} %get-tuple-element.108.refs_11_), channel_id=1, source_target_pairs={{0,1},{1,0},{2,3},{3,2},{4,5},{5,4},{6,7},{7,6},{8,9},{9,8},{10,11... | collective-permute-start | bytes 294920 | tf_op jit(solution)/shard_map/ppermute | solution.py:549
  46.2 0.5 expert_merge.1
  46.7 1.6 %collective-permute-start.7 = (bf16[2,96,3072]{2,1,0:T(8,128)(2,1)S(1)}, bf16[2,96,3072]{2,1,0:T(8,128)(2,1)S(1)}, u32[]{:S(2)}, u32[]{:S(2)}) collective-permute-start(bf16[2,96,3072]{2,1,0:T(8,128)(2,1)S(1)} %get-tuple-element.93), channel_id=1, source_target_pairs={{0,8},{4,20},{8,0},{12,28},{16,24},{20,4},{24,16},{28,12},{1,9},{5... | collective-permute-start | bytes 3538952 | tf_op jit(solution)/shard_map/ppermute | solution.py:555
  48.3 1.2 %collective-permute-done.11.refs_2_.refs_12_ = bf16[64,768]{1,0:T(8,128)(2,1)S(1)} collective-permute-done((bf16[64,768]{1,0:T(8,128)(2,1)S(1)}, bf16[64,768]{1,0:T(8,128)(2,1)S(1)}, u32[]{:S(2)}, u32[]{:S(2)}) %collective-permute-start.11) | collective-permute-done | bytes 98336 | tf_op jit(solution)/shard_map/ppermute | solution.py:549
  49.5 3.9 %collective-permute-done.12.refs_3_.refs_13_ = bf16[64,768]{1,0:T(8,128)(2,1)S(1)} collective-permute-done((bf16[64,768]{1,0:T(8,128)(2,1)S(1)}, bf16[64,768]{1,0:T(8,128)(2,1)S(1)}, u32[]{:S(2)}, u32[]{:S(2)}) %collective-permute-start.12) | collective-permute-done | bytes 98336 | tf_op jit(solution)/shard_map/ppermute | solution.py:549
  53.4 0.1 collective-permute-done.13.refs_4_.refs_14_
  53.5 0.1 pair_sum.1
  53.5 0.5 collective-permute-start.15
  54.0 0.4 copy-done
  54.5 0.1 copy-done.1
  54.5 0.1 copy-done.2
  54.6 0.1 copy-done.3
  54.7 0.1 copy-done.4
  54.8 1.8 %attention_back.1 = (f32[72,768]{1,0:T(8,128)S(1)}, bf16[72,768]{1,0:T(8,128)(2,1)S(1)}, bf16[72,768]{1,0:T(8,128)(2,1)S(1)}, bf16[72,768]{1,0:T(8,128)(2,1)S(1)...) custom-call(bf16[256,768]{1,0:T(8,128)(2,1)S(1)} %copy-done, ...), custom_call_target="tpu_custom_call" | custom-call | flops 5000000000 | tf_op jit(solution)/shard_map/attention_back/pallas_call | solution.py:529
  56.6 1.9 %collective-permute-start.18 = (bf16[72,768]{1,0:T(8,128)(2,1)S(1)}, bf16[72,768]{1,0:T(8,128)(2,1)S(1)}, u32[]{:S(2)}, u32[]{:S(2)}) collective-permute-start(bf16[72,768]{1,0:T(8,128)(2,1)S(1)} %get-tuple-element.124), channel_id=1, source_target_pairs={{0,3},{1,2},{2,1},{3,0},{4,7},{5,6},{6,5},{7,4},{8,11},{9,10},{10,... | collective-permute-start | bytes 331784 | tf_op jit(solution)/shard_map/ppermute | solution.py:549
  58.5 0.9 collective-permute-start.19
  59.4 1.7 %collective-permute-start.20 = (bf16[72,768]{1,0:T(8,128)(2,1)S(1)}, bf16[72,768]{1,0:T(8,128)(2,1)S(1)}, u32[]{:S(2)}, u32[]{:S(2)}) collective-permute-start(bf16[72,768]{1,0:T(8,128)(2,1)S(1)} %get-tuple-element.126), channel_id=1, source_target_pairs={{0,1},{1,0},{2,3},{3,2},{4,5},{5,4},{6,7},{7,6},{8,9},{9,8},{10,11... | collective-permute-start | bytes 331784 | tf_op jit(solution)/shard_map/ppermute | solution.py:549
  61.1 0.9 %collective-permute-start.27 = (bf16[64,768]{1,0:T(8,128)(2,1)S(1)}, bf16[64,768]{1,0:T(8,128)(2,1)S(1)}, u32[]{:S(2)}, u32[]{:S(2)}) collective-permute-start(bf16[64,768]{1,0:T(8,128)(2,1)S(1)} %output_share.1.refs_6_.refs_0_), channel_id=1, source_target_pairs={{0,2},{1,3},{2,0},{3,1},{4,6},{5,7},{6,4},{7,5},{8,10},{9,11},{10,... | collective-permute-start | bytes 294920 | tf_op jit(solution)/shard_map/ppermute | solution.py:549
  62.1 1.8 %weight_grads.1 = (bf16[4,96,768]{2,1,0:T(8,128)(2,1)S(1)}, bf16[4,96,768]{2,1,0:T(8,128)(2,1)S(1)}, f32[8,768]{1,0:T(8,128)S(1)}) custom-call(bf16[256,768]{1,0:T(8,128)(2,1)S(1)} %get-tuple-element.94.refs_0_, bf16[3,256,192]{2,1,0:T(8,128)(2,1)S(1)} %get-tuple-element.111.refs_1_, bf16[256,768]{1,0:T(8,128)(2,1)S(1)} %get-tuple-element.112.refs_2_, ...), custom_call_target="tpu_custom_call" | custom-call | flops 4000000000 | tf_op jit(solution)/shard_map/weight_grads/pallas_call | solution.py:529
  63.9 0.1 collective-permute-start.16
  63.9 0.3 expert_cross.1
  64.2 1.7 %collective-permute-done.16.refs_2_ = bf16[4,96,768]{2,1,0:T(8,128)(2,1)S(1)} collective-permute-done((bf16[4,96,768]{2,1,0:T(8,128)(2,1)S(1)}, bf16[4,96,768]{2,1,0:T(8,128)(2,1)S(1)}, u32[]{:S(2)}, u32[]{:S(2)}) %collective-permute-start.16) | collective-permute-done | bytes 589856 | tf_op jit(solution)/shard_map/ppermute | solution.py:549
  65.9 0.2 cross.1
  66.1 1.6 %collective-permute-start.17 = (bf16[144,3072]{1,0:T(8,128)(2,1)S(1)}, bf16[144,3072]{1,0:T(8,128)(2,1)S(1)}, u32[]{:S(2)}, u32[]{:S(2)}) collective-permute-start(bf16[144,3072]{1,0:T(8,128)(2,1)S(1)} %get-tuple-element.121), channel_id=1, source_target_pairs={{0,16},{4,12},{8,24},{12,4},{16,0},{20,28},{24,8},{28,20},{1,17},{... | collective-permute-start | bytes 2654216 | tf_op jit(solution)/shard_map/ppermute | solution.py:555
  67.7 5.0 %collective-permute-done.19.refs_6_ = bf16[72,768]{1,0:T(8,128)(2,1)S(1)} collective-permute-done((bf16[72,768]{1,0:T(8,128)(2,1)S(1)}, bf16[72,768]{1,0:T(8,128)(2,1)S(1)}, u32[]{:S(2)}, u32[]{:S(2)}) %collective-permute-start.19) | collective-permute-done | bytes 110624 | tf_op jit(solution)/shard_map/ppermute | solution.py:549
  72.7 0.2 input_back.1
  72.8 0.1 collective-permute-start.21
  72.9 1.7 %collective-permute-start.23 = (bf16[64,768]{1,0:T(8,128)(2,1)S(1)}, bf16[64,768]{1,0:T(8,128)(2,1)S(1)}, u32[]{:S(2)}, u32[]{:S(2)}) collective-permute-start(bf16[64,768]{1,0:T(8,128)(2,1)S(1)} %get-tuple-element.128.refs_2_), channel_id=1, source_target_pairs={{0,3},{1,2},{2,1},{3,0},{4,7},{5,6},{6,5},{7,4},{8,11},{9,10},{10,... | collective-permute-start | bytes 294920 | tf_op jit(solution)/shard_map/ppermute | solution.py:549
  74.6 2.7 %collective-permute-start.25 = (bf16[64,768]{1,0:T(8,128)(2,1)S(1)}, bf16[64,768]{1,0:T(8,128)(2,1)S(1)}, u32[]{:S(2)}, u32[]{:S(2)}) collective-permute-start(bf16[64,768]{1,0:T(8,128)(2,1)S(1)} %get-tuple-element.128.refs_2_), channel_id=1, source_target_pairs={{0,1},{1,0},{2,3},{3,2},{4,5},{5,4},{6,7},{7,6},{8,9},{9,8},{10,11... | collective-permute-start | bytes 294920 | tf_op jit(solution)/shard_map/ppermute | solution.py:549
  77.4 1.6 %collective-permute-start.22 = (f32[8,768]{1,0:T(8,128)S(1)}, f32[8,768]{1,0:T(8,128)S(1)}, u32[]{:S(2)}, u32[]{:S(2)}) collective-permute-start(f32[8,768]{1,0:T(8,128)S(1)} %small_sum.1.refs_2_), channel_id=1, source_target_pairs={{0,16},{4,12},{8,24},{12,4},{16,0},{20,28},{24,8},{28,20},{1,17},{... | collective-permute-start | bytes 73736 | tf_op jit(solution)/shard_map/ppermute | solution.py:555
  79.0 2.3 %collective-permute-done.22.refs_3_ = f32[8,768]{1,0:T(8,128)S(1)} collective-permute-done((f32[8,768]{1,0:T(8,128)S(1)}, f32[8,768]{1,0:T(8,128)S(1)}, u32[]{:S(2)}, u32[]{:S(2)}) %collective-permute-start.22) | collective-permute-done | bytes 24608 | tf_op jit(solution)/shard_map/ppermute | solution.py:555
  81.3 0.0 collective-permute-start.28
  81.3 3.0 %collective-permute-done.24.refs_5_.refs_4_ = bf16[64,768]{1,0:T(8,128)(2,1)S(1)} collective-permute-done((bf16[64,768]{1,0:T(8,128)(2,1)S(1)}, bf16[64,768]{1,0:T(8,128)(2,1)S(1)}, u32[]{:S(2)}, u32[]{:S(2)}) %collective-permute-start.24) | collective-permute-done | bytes 98336 | tf_op jit(solution)/shard_map/ppermute | solution.py:549
  84.2 0.1 weight_cross.1
  84.3 1.6 %collective-permute-start.26 = (bf16[112,768]{1,0:T(8,128)(2,1)S(1)}, bf16[112,768]{1,0:T(8,128)(2,1)S(1)}, u32[]{:S(2)}, u32[]{:S(2)}) collective-permute-start(bf16[112,768]{1,0:T(8,128)(2,1)S(1)} %get-tuple-element.130), channel_id=1, source_target_pairs={{0,8},{4,20},{8,0},{12,28},{16,24},{20,4},{24,16},{28,12},{1,9},{5... | collective-permute-start | bytes 516104 | tf_op jit(solution)/shard_map/ppermute | solution.py:555
  85.9 1.1 %expert_final.1 = (f32[2,96,768]{2,1,0:T(8,128)}, f32[2,96,768]{2,1,0:T(8,128)}) custom-call(f32[96,3072]{1,0:T(8,128)S(1)} %get-tuple-element.131.refs_0_, bf16[144,3072]{1,0:T(8,128)(2,1)S(1)} %collective-permute-done.17.refs_1_), custom_call_target="tpu_custom_call" | custom-call | flops 1000000 | tf_op jit(solution)/shard_map/expert_final/pallas_call | solution.py:529
  87.0 1.4 %collective-permute-done.28.refs_7_ = bf16[128,768]{1,0:T(8,128)(2,1)S(1)} collective-permute-done((bf16[128,768]{1,0:T(8,128)(2,1)S(1)}, bf16[128,768]{1,0:T(8,128)(2,1)S(1)}, u32[]{:S(2)}, u32[]{:S(2)}) %collective-permute-start.28) | collective-permute-done | bytes 196640 | tf_op jit(solution)/shard_map/ppermute | solution.py:549
  88.3 1.4 %collective-permute-done.26.refs_1_ = bf16[112,768]{1,0:T(8,128)(2,1)S(1)} collective-permute-done((bf16[112,768]{1,0:T(8,128)(2,1)S(1)}, bf16[112,768]{1,0:T(8,128)(2,1)S(1)}, u32[]{:S(2)}, u32[]{:S(2)}) %collective-permute-start.26) | collective-permute-done | bytes 172064 | tf_op jit(solution)/shard_map/ppermute | solution.py:555
  89.8 1.1 %finish.1 = (bf16[256,768]{1,0:T(8,128)(2,1)}, bf16[256,768]{1,0:T(8,128)(2,1)}, f32[96,192]{1,0:T(8,128)}, f32[96,192]{1,0:T(8,128)}, f32[96,192]{1,0:T(8,128)}...) custom-call(f32[112,768]{1,0:T(8,128)S(1)} %get-tuple-element.129.refs_0_, ...), custom_call_target="tpu_custom_call" | custom-call | flops 1000000 | tf_op jit(solution)/shard_map/finish/pallas_call | solution.py:529
  (31 shorter events, 0.1 us)
Async XLA Ops:
  3.6 8.8 %collective-permute-start = (bf16[64,768]{1,0:T(8,128)(2,1)S(1)}, bf16[64,768]{1,0:T(8,128)(2,1)S(1)}, u32[]{:S(2)}, u32[]{:S(2)}) collective-permute-start(bf16[64,768]{1,0:T(8,128)(2,1)S(1)} %get-tuple-element.79), channel_id=1, source_target_pairs={{0,3},{1,2},{2,1},{3,0},{4,7},{5,6},{6,5},{7,4},{8,11},{9,10},{10,... | collective-permute-start | bytes 294920 | tf_op jit(solution)/shard_map/ppermute | solution.py:549
  8.7 8.3 %collective-permute-start.1 = (bf16[64,768]{1,0:T(8,128)(2,1)S(1)}, bf16[64,768]{1,0:T(8,128)(2,1)S(1)}, u32[]{:S(2)}, u32[]{:S(2)}) collective-permute-start(bf16[64,768]{1,0:T(8,128)(2,1)S(1)} %get-tuple-element.80), channel_id=1, source_target_pairs={{0,2},{1,3},{2,0},{3,1},{4,6},{5,7},{6,4},{7,5},{8,10},{9,11},{10,... | collective-permute-start | bytes 294920 | tf_op jit(solution)/shard_map/ppermute | solution.py:549
  8.7 8.3 %collective-permute-start.2 = (bf16[64,768]{1,0:T(8,128)(2,1)S(1)}, bf16[64,768]{1,0:T(8,128)(2,1)S(1)}, u32[]{:S(2)}, u32[]{:S(2)}) collective-permute-start(bf16[64,768]{1,0:T(8,128)(2,1)S(1)} %get-tuple-element.81), channel_id=1, source_target_pairs={{0,1},{1,0},{2,3},{3,2},{4,5},{5,4},{6,7},{7,6},{8,9},{9,8},{10,11... | collective-permute-start | bytes 294920 | tf_op jit(solution)/shard_map/ppermute | solution.py:549
  17.1 11.0 %copy-start.5 = (bf16[256,768]{1,0:T(8,128)(2,1)S(1)}, bf16[256,768]{1,0:T(8,128)(2,1)}, u32[]{:S(2)}) copy-start(bf16[256,768]{1,0:T(8,128)(2,1)} %refs_1_.3) | copy-start | bytes 1179652
  17.1 11.0 %copy-start.6 = (bf16[768,2]{0,1:T(2,128)(2,1)S(1)}, bf16[768,2]{0,1:T(2,128)(2,1)}, u32[]{:S(2)}) copy-start(bf16[768,2]{0,1:T(2,128)(2,1)} %param.28) | copy-start | bytes 9220
  17.2 7.6 %collective-permute-start.3 = (bf16[64,768]{1,0:T(8,128)(2,1)S(1)}, bf16[64,768]{1,0:T(8,128)(2,1)S(1)}, u32[]{:S(2)}, u32[]{:S(2)}) collective-permute-start(bf16[64,768]{1,0:T(8,128)(2,1)S(1)} %get-tuple-element.82.refs_2_.refs_5_), channel_id=1, source_target_pairs={{0,3},{1,2},{2,1},{3,0},{4,7},{5,6},{6,5},{7,4},{8,11},{9,10},{10,... | collective-permute-start | bytes 294920 | tf_op jit(solution)/shard_map/ppermute | solution.py:549
  19.7 8.4 %collective-permute-start.4 = (bf16[64,768]{1,0:T(8,128)(2,1)S(1)}, bf16[64,768]{1,0:T(8,128)(2,1)S(1)}, u32[]{:S(2)}, u32[]{:S(2)}) collective-permute-start(bf16[64,768]{1,0:T(8,128)(2,1)S(1)} %get-tuple-element.82.refs_2_.refs_5_), channel_id=1, source_target_pairs={{0,2},{1,3},{2,0},{3,1},{4,6},{5,7},{6,4},{7,5},{8,10},{9,11},{10,... | collective-permute-start | bytes 294920 | tf_op jit(solution)/shard_map/ppermute | solution.py:549
  19.8 8.4 %collective-permute-start.5 = (bf16[64,768]{1,0:T(8,128)(2,1)S(1)}, bf16[64,768]{1,0:T(8,128)(2,1)S(1)}, u32[]{:S(2)}, u32[]{:S(2)}) collective-permute-start(bf16[64,768]{1,0:T(8,128)(2,1)S(1)} %get-tuple-element.82.refs_2_.refs_5_), channel_id=1, source_target_pairs={{0,1},{1,0},{2,3},{3,2},{4,5},{5,4},{6,7},{7,6},{8,9},{9,8},{10,11... | collective-permute-start | bytes 294920 | tf_op jit(solution)/shard_map/ppermute | solution.py:549
  31.6 8.2 %collective-permute-start.8 = (bf16[64,768]{1,0:T(8,128)(2,1)S(1)}, bf16[64,768]{1,0:T(8,128)(2,1)S(1)}, u32[]{:S(2)}, u32[]{:S(2)}) collective-permute-start(bf16[64,768]{1,0:T(8,128)(2,1)S(1)} %get-tuple-element.102), channel_id=1, source_target_pairs={{0,3},{1,2},{2,1},{3,0},{4,7},{5,6},{6,5},{7,4},{8,11},{9,10},{10,... | collective-permute-start | bytes 294920 | tf_op jit(solution)/shard_map/ppermute | solution.py:549
  33.2 8.3 %collective-permute-start.9 = (bf16[64,768]{1,0:T(8,128)(2,1)S(1)}, bf16[64,768]{1,0:T(8,128)(2,1)S(1)}, u32[]{:S(2)}, u32[]{:S(2)}) collective-permute-start(bf16[64,768]{1,0:T(8,128)(2,1)S(1)} %get-tuple-element.103), channel_id=1, source_target_pairs={{0,2},{1,3},{2,0},{3,1},{4,6},{5,7},{6,4},{7,5},{8,10},{9,11},{10,... | collective-permute-start | bytes 294920 | tf_op jit(solution)/shard_map/ppermute | solution.py:549
  33.2 8.3 %collective-permute-start.10 = (bf16[64,768]{1,0:T(8,128)(2,1)S(1)}, bf16[64,768]{1,0:T(8,128)(2,1)S(1)}, u32[]{:S(2)}, u32[]{:S(2)}) collective-permute-start(bf16[64,768]{1,0:T(8,128)(2,1)S(1)} %get-tuple-element.104), channel_id=1, source_target_pairs={{0,1},{1,0},{2,3},{3,2},{4,5},{5,4},{6,7},{7,6},{8,9},{9,8},{10,11... | collective-permute-start | bytes 294920 | tf_op jit(solution)/shard_map/ppermute | solution.py:549
  39.7 6.5 %collective-permute-start.6 = (bf16[4,96,3072]{2,1,0:T(8,128)(2,1)S(1)}, bf16[4,96,3072]{2,1,0:T(8,128)(2,1)S(1)}, u32[]{:S(2)}, u32[]{:S(2)}) collective-permute-start(bf16[4,96,3072]{2,1,0:T(8,128)(2,1)S(1)} %get-tuple-element.91), channel_id=1, source_target_pairs={{0,4},{4,0},{8,12},{12,8},{16,20},{20,16},{24,28},{28,24},{1,5},{5... | collective-permute-start | bytes 7077896 | tf_op jit(solution)/shard_map/ppermute | solution.py:549
  39.8 13.6 %collective-permute-start.14 = (bf16[128,768]{1,0:T(8,128)(2,1)S(1)}, bf16[128,768]{1,0:T(8,128)(2,1)S(1)}, u32[]{:S(2)}, u32[]{:S(2)}) collective-permute-start(bf16[128,768]{1,0:T(8,128)(2,1)S(1)} %get-tuple-element.105.refs_7_), channel_id=1, source_target_pairs={{0,1},{1,0},{2,3},{3,2},{4,5},{5,4},{6,7},{7,6},{8,9},{9,8},{10,11... | collective-permute-start | bytes 589832 | tf_op jit(solution)/shard_map/ppermute | solution.py:549
  41.7 7.7 %collective-permute-start.11 = (bf16[64,768]{1,0:T(8,128)(2,1)S(1)}, bf16[64,768]{1,0:T(8,128)(2,1)S(1)}, u32[]{:S(2)}, u32[]{:S(2)}) collective-permute-start(bf16[64,768]{1,0:T(8,128)(2,1)S(1)} %get-tuple-element.108.refs_11_), channel_id=1, source_target_pairs={{0,3},{1,2},{2,1},{3,0},{4,7},{5,6},{6,5},{7,4},{8,11},{9,10},{10,... | collective-permute-start | bytes 294920 | tf_op jit(solution)/shard_map/ppermute | solution.py:549
  44.0 9.4 %collective-permute-start.12 = (bf16[64,768]{1,0:T(8,128)(2,1)S(1)}, bf16[64,768]{1,0:T(8,128)(2,1)S(1)}, u32[]{:S(2)}, u32[]{:S(2)}) collective-permute-start(bf16[64,768]{1,0:T(8,128)(2,1)S(1)} %get-tuple-element.108.refs_11_), channel_id=1, source_target_pairs={{0,2},{1,3},{2,0},{3,1},{4,6},{5,7},{6,4},{7,5},{8,10},{9,11},{10,... | collective-permute-start | bytes 294920 | tf_op jit(solution)/shard_map/ppermute | solution.py:549
  44.0 9.5 %collective-permute-start.13 = (bf16[64,768]{1,0:T(8,128)(2,1)S(1)}, bf16[64,768]{1,0:T(8,128)(2,1)S(1)}, u32[]{:S(2)}, u32[]{:S(2)}) collective-permute-start(bf16[64,768]{1,0:T(8,128)(2,1)S(1)} %get-tuple-element.108.refs_11_), channel_id=1, source_target_pairs={{0,1},{1,0},{2,3},{3,2},{4,5},{5,4},{6,7},{7,6},{8,9},{9,8},{10,11... | collective-permute-start | bytes 294920 | tf_op jit(solution)/shard_map/ppermute | solution.py:549
  46.7 17.2 %collective-permute-start.7 = (bf16[2,96,3072]{2,1,0:T(8,128)(2,1)S(1)}, bf16[2,96,3072]{2,1,0:T(8,128)(2,1)S(1)}, u32[]{:S(2)}, u32[]{:S(2)}) collective-permute-start(bf16[2,96,3072]{2,1,0:T(8,128)(2,1)S(1)} %get-tuple-element.93), channel_id=1, source_target_pairs={{0,8},{4,20},{8,0},{12,28},{16,24},{20,4},{24,16},{28,12},{1,9},{5... | collective-permute-start | bytes 3538952 | tf_op jit(solution)/shard_map/ppermute | solution.py:555
  53.5 1.0 %copy-start = (bf16[256,768]{1,0:T(8,128)(2,1)S(1)}, bf16[256,768]{1,0:T(8,128)(2,1)}, u32[]{:S(2)}) copy-start(bf16[256,768]{1,0:T(8,128)(2,1)} %refs_0_.5) | copy-start | bytes 1179652
  53.5 1.1 %copy-start.1 = (bf16[768,192]{0,1:T(8,128)(2,1)S(1)}, bf16[768,192]{0,1:T(8,128)(2,1)}, u32[]{:S(2)}) copy-start(bf16[768,192]{0,1:T(8,128)(2,1)} %param.23) | copy-start | bytes 884740
  53.5 1.2 %copy-start.2 = (bf16[768,192]{0,1:T(8,128)(2,1)S(1)}, bf16[768,192]{0,1:T(8,128)(2,1)}, u32[]{:S(2)}) copy-start(bf16[768,192]{0,1:T(8,128)(2,1)} %param.24) | copy-start | bytes 884740
  53.5 1.2 %copy-start.3 = (bf16[768,192]{0,1:T(8,128)(2,1)S(1)}, bf16[768,192]{0,1:T(8,128)(2,1)}, u32[]{:S(2)}) copy-start(bf16[768,192]{0,1:T(8,128)(2,1)} %param.25) | copy-start | bytes 884740
  53.5 1.3 %copy-start.4 = (bf16[192,768]{1,0:T(8,128)(2,1)S(1)}, bf16[192,768]{1,0:T(8,128)(2,1)}, u32[]{:S(2)}) copy-start(bf16[192,768]{1,0:T(8,128)(2,1)} %refs_8_.3) | copy-start | bytes 884740
  53.5 7.6 %collective-permute-start.15 = (bf16[64,768]{1,0:T(8,128)(2,1)S(1)}, bf16[64,768]{1,0:T(8,128)(2,1)S(1)}, u32[]{:S(2)}, u32[]{:S(2)}) collective-permute-start(bf16[64,768]{1,0:T(8,128)(2,1)S(1)} %get-tuple-element.115), channel_id=1, source_target_pairs={{0,2},{1,3},{2,0},{3,1},{4,6},{5,7},{6,4},{7,5},{8,10},{9,11},{10,... | collective-permute-start | bytes 294920 | tf_op jit(solution)/shard_map/ppermute | solution.py:549
  56.6 11.0 %collective-permute-start.18 = (bf16[72,768]{1,0:T(8,128)(2,1)S(1)}, bf16[72,768]{1,0:T(8,128)(2,1)S(1)}, u32[]{:S(2)}, u32[]{:S(2)}) collective-permute-start(bf16[72,768]{1,0:T(8,128)(2,1)S(1)} %get-tuple-element.124), channel_id=1, source_target_pairs={{0,3},{1,2},{2,1},{3,0},{4,7},{5,6},{6,5},{7,4},{8,11},{9,10},{10,... | collective-permute-start | bytes 331784 | tf_op jit(solution)/shard_map/ppermute | solution.py:549
  58.5 14.1 %collective-permute-start.19 = (bf16[72,768]{1,0:T(8,128)(2,1)S(1)}, bf16[72,768]{1,0:T(8,128)(2,1)S(1)}, u32[]{:S(2)}, u32[]{:S(2)}) collective-permute-start(bf16[72,768]{1,0:T(8,128)(2,1)S(1)} %get-tuple-element.125), channel_id=1, source_target_pairs={{0,2},{1,3},{2,0},{3,1},{4,6},{5,7},{6,4},{7,5},{8,10},{9,11},{10,... | collective-permute-start | bytes 331784 | tf_op jit(solution)/shard_map/ppermute | solution.py:549
  59.4 13.3 %collective-permute-start.20 = (bf16[72,768]{1,0:T(8,128)(2,1)S(1)}, bf16[72,768]{1,0:T(8,128)(2,1)S(1)}, u32[]{:S(2)}, u32[]{:S(2)}) collective-permute-start(bf16[72,768]{1,0:T(8,128)(2,1)S(1)} %get-tuple-element.126), channel_id=1, source_target_pairs={{0,1},{1,0},{2,3},{3,2},{4,5},{5,4},{6,7},{7,6},{8,9},{9,8},{10,11... | collective-permute-start | bytes 331784 | tf_op jit(solution)/shard_map/ppermute | solution.py:549
  61.1 16.2 %collective-permute-start.27 = (bf16[64,768]{1,0:T(8,128)(2,1)S(1)}, bf16[64,768]{1,0:T(8,128)(2,1)S(1)}, u32[]{:S(2)}, u32[]{:S(2)}) collective-permute-start(bf16[64,768]{1,0:T(8,128)(2,1)S(1)} %output_share.1.refs_6_.refs_0_), channel_id=1, source_target_pairs={{0,2},{1,3},{2,0},{3,1},{4,6},{5,7},{6,4},{7,5},{8,10},{9,11},{10,... | collective-permute-start | bytes 294920 | tf_op jit(solution)/shard_map/ppermute | solution.py:549
  63.9 2.1 %collective-permute-start.16 = (bf16[4,96,768]{2,1,0:T(8,128)(2,1)S(1)}, bf16[4,96,768]{2,1,0:T(8,128)(2,1)S(1)}, u32[]{:S(2)}, u32[]{:S(2)}) collective-permute-start(bf16[4,96,768]{2,1,0:T(8,128)(2,1)S(1)} %get-tuple-element.119), channel_id=1, source_target_pairs={{0,4},{4,0},{8,12},{12,8},{16,20},{20,16},{24,28},{28,24},{1,5},{5... | collective-permute-start | bytes 1769480 | tf_op jit(solution)/shard_map/ppermute | solution.py:549
  66.1 18.1 %collective-permute-start.17 = (bf16[144,3072]{1,0:T(8,128)(2,1)S(1)}, bf16[144,3072]{1,0:T(8,128)(2,1)S(1)}, u32[]{:S(2)}, u32[]{:S(2)}) collective-permute-start(bf16[144,3072]{1,0:T(8,128)(2,1)S(1)} %get-tuple-element.121), channel_id=1, source_target_pairs={{0,16},{4,12},{8,24},{12,4},{16,0},{20,28},{24,8},{28,20},{1,17},{... | collective-permute-start | bytes 2654216 | tf_op jit(solution)/shard_map/ppermute | solution.py:555
  72.8 1.8 %collective-permute-start.21 = (f32[8,768]{1,0:T(8,128)S(1)}, f32[8,768]{1,0:T(8,128)S(1)}, u32[]{:S(2)}, u32[]{:S(2)}) collective-permute-start(f32[8,768]{1,0:T(8,128)S(1)} %get-tuple-element.127.refs_0_.refs_2_), channel_id=1, source_target_pairs={{0,4},{4,0},{8,12},{12,8},{16,20},{20,16},{24,28},{28,24},{1,5},{5... | collective-permute-start | bytes 73736 | tf_op jit(solution)/shard_map/ppermute | solution.py:549
  72.9 8.4 %collective-permute-start.23 = (bf16[64,768]{1,0:T(8,128)(2,1)S(1)}, bf16[64,768]{1,0:T(8,128)(2,1)S(1)}, u32[]{:S(2)}, u32[]{:S(2)}) collective-permute-start(bf16[64,768]{1,0:T(8,128)(2,1)S(1)} %get-tuple-element.128.refs_2_), channel_id=1, source_target_pairs={{0,3},{1,2},{2,1},{3,0},{4,7},{5,6},{6,5},{7,4},{8,11},{9,10},{10,... | collective-permute-start | bytes 294920 | tf_op jit(solution)/shard_map/ppermute | solution.py:549
  74.6 9.6 %collective-permute-start.24 = (bf16[64,768]{1,0:T(8,128)(2,1)S(1)}, bf16[64,768]{1,0:T(8,128)(2,1)S(1)}, u32[]{:S(2)}, u32[]{:S(2)}) collective-permute-start(bf16[64,768]{1,0:T(8,128)(2,1)S(1)} %get-tuple-element.128.refs_2_), channel_id=1, source_target_pairs={{0,2},{1,3},{2,0},{3,1},{4,6},{5,7},{6,4},{7,5},{8,10},{9,11},{10,... | collective-permute-start | bytes 294920 | tf_op jit(solution)/shard_map/ppermute | solution.py:549
  74.6 9.6 %collective-permute-start.25 = (bf16[64,768]{1,0:T(8,128)(2,1)S(1)}, bf16[64,768]{1,0:T(8,128)(2,1)S(1)}, u32[]{:S(2)}, u32[]{:S(2)}) collective-permute-start(bf16[64,768]{1,0:T(8,128)(2,1)S(1)} %get-tuple-element.128.refs_2_), channel_id=1, source_target_pairs={{0,1},{1,0},{2,3},{3,2},{4,5},{5,4},{6,7},{7,6},{8,9},{9,8},{10,11... | collective-permute-start | bytes 294920 | tf_op jit(solution)/shard_map/ppermute | solution.py:549
  77.4 3.9 %collective-permute-start.22 = (f32[8,768]{1,0:T(8,128)S(1)}, f32[8,768]{1,0:T(8,128)S(1)}, u32[]{:S(2)}, u32[]{:S(2)}) collective-permute-start(f32[8,768]{1,0:T(8,128)S(1)} %small_sum.1.refs_2_), channel_id=1, source_target_pairs={{0,16},{4,12},{8,24},{12,4},{16,0},{20,28},{24,8},{28,20},{1,17},{... | collective-permute-start | bytes 73736 | tf_op jit(solution)/shard_map/ppermute | solution.py:555
  81.3 7.1 %collective-permute-start.28 = (bf16[128,768]{1,0:T(8,128)(2,1)S(1)}, bf16[128,768]{1,0:T(8,128)(2,1)S(1)}, u32[]{:S(2)}, u32[]{:S(2)}) collective-permute-start(bf16[128,768]{1,0:T(8,128)(2,1)S(1)} %output_pair.1.refs_6_), channel_id=1, source_target_pairs={{0,1},{1,0},{2,3},{3,2},{4,5},{5,4},{6,7},{7,6},{8,9},{9,8},{10,11... | collective-permute-start | bytes 589832 | tf_op jit(solution)/shard_map/ppermute | solution.py:549
  84.3 5.5 %collective-permute-start.26 = (bf16[112,768]{1,0:T(8,128)(2,1)S(1)}, bf16[112,768]{1,0:T(8,128)(2,1)S(1)}, u32[]{:S(2)}, u32[]{:S(2)}) collective-permute-start(bf16[112,768]{1,0:T(8,128)(2,1)S(1)} %get-tuple-element.130), channel_id=1, source_target_pairs={{0,8},{4,20},{8,0},{12,28},{16,24},{20,4},{24,16},{28,12},{1,9},{5... | collective-permute-start | bytes 516104 | tf_op jit(solution)/shard_map/ppermute | solution.py:555

commit v6 on v5

--- a/solution.py
+++ b/solution.py
@@ -710,7 +710,7 @@
         [sds((share, width), F32), sds((share, width), BF16)],
         [rows_kept, swap(rows_sent, "tensor", 1)],
         name="pair_sum",
-        after=grad_attended[1:] + list(expert_merged[:1]),
+        after=expert_merged[:1],
     )
     crossed = []
 

time: 91.2 us -> 89.1 us (0.977)
  waiting for transfers between devices: 30.6 us -> 27.7 us
  starting transfers between devices: 36.1 us -> 37.6 us
    ppermute x25, waiting for transfers between devices: 26.9 us -> 23 us  [swap(): return lax.ppermute(values, axis, [(i, i ^ k) for i in range(size)])]
    ppermute x25, starting transfers between devices: 29.7 us -> 31.3 us  [swap(): return lax.ppermute(values, axis, [(i, i ^ k) for i in range(size)])]
    ppermute x4, waiting for transfers between devices: 3.72 us -> 4.68 us  [swap_chips(): return lax.ppermute(values, 'dp', pairs)]
  transfers between devices with their start and end apart: 29 -> 29, of which waited for: 14 -> 13; matrix products, arithmetic and copies ran while one was open for 3% -> 3% of each run, Pallas kernels for 13% -> 14%
where the time goes in v6:
time: 89.1 us; the launch traced here: 88.8 us
  starting transfers between devices  37.6 us (42%)
  waiting for transfers between devices  27.7 us (31%)
  Pallas kernels  19.9 us (22%)
  local copies, waits for them, and re-layouts  2.1 us (2%)
    ppermute x25, starting transfers between devices, swap(): return lax.ppermute(values, axis, [(i, i ^ k) for i in range(size)])  31.3 us
    ppermute x25, waiting for transfers between devices, swap(): return lax.ppermute(values, axis, [(i, i ^ k) for i in range(size)])  23 us
    pallas_call x19, Pallas kernels, run(): pl.pallas_call(body, out_shape=[out(o.shape, o.dtype) for o in outs] if o...  19.9 us
    ppermute x4, starting transfers between devices, swap_chips(): return lax.ppermute(values, 'dp', pairs)  6.28 us
    ppermute x4, waiting for transfers between devices, swap_chips(): return lax.ppermute(values, 'dp', pairs)  4.68 us
  transfers between devices with their start and end apart: 29, of which 13 were waited for; matrix products, arithmetic and copies ran while one was open for 3% of the time, Pallas kernels for 14%

profile of v6, /device:TPU:0, one launch (start us, length us, event | category | flops | bytes accessed | tf_op | source)
XLA Modules:
  0.0 88.8 jit_solution(10011830249887308583)
XLA Ops:
  0.6 2.9 %attention.1 = (f32[64,768]{1,0:T(8,128)S(1)}, bf16[64,768]{1,0:T(8,128)(2,1)S(1)}, bf16[64,768]{1,0:T(8,128)(2,1)S(1)}, bf16[64,768]{1,0:T(8,128)(2,1)S(1)}, bf...) custom-call(s32[1,511]{1,0:T(1,128)} %bitcast.21, ...), custom_call_target="tpu_custom_call" | custom-call | flops 200000000 | tf_op jit(solution)/shard_map/attention/pallas_call | solution.py:529
  3.6 5.1 %collective-permute-start = (bf16[64,768]{1,0:T(8,128)(2,1)S(1)}, bf16[64,768]{1,0:T(8,128)(2,1)S(1)}, u32[]{:S(2)}, u32[]{:S(2)}) collective-permute-start(bf16[64,768]{1,0:T(8,128)(2,1)S(1)} %get-tuple-element.79), channel_id=1, source_target_pairs={{0,3},{1,2},{2,1},{3,0},{4,7},{5,6},{6,5},{7,4},{8,11},{9,10},{10,... | collective-permute-start | bytes 294920 | tf_op jit(solution)/shard_map/ppermute | solution.py:549
  8.7 0.6 collective-permute-start.2
  9.4 0.7 multiply_add_fusion
  10.1 0.7 reshape.45.refs_1_
  10.8 0.7 reshape.43.refs_0_.refs_2_
  11.4 0.7 pad.4.refs_5_
  12.1 0.3 collective-permute-done.refs_2_
  12.4 4.5 %collective-permute-done.1.refs_3_ = bf16[64,768]{1,0:T(8,128)(2,1)S(1)} collective-permute-done((bf16[64,768]{1,0:T(8,128)(2,1)S(1)}, bf16[64,768]{1,0:T(8,128)(2,1)S(1)}, u32[]{:S(2)}, u32[]{:S(2)}) %collective-permute-start.1) | collective-permute-done | bytes 98336 | tf_op jit(solution)/shard_map/ppermute | solution.py:549
  17.0 0.1 hidden.1
  17.1 0.0 copy-start.5
  17.1 0.0 copy-start.6
  17.2 2.6 %collective-permute-start.3 = (bf16[64,768]{1,0:T(8,128)(2,1)S(1)}, bf16[64,768]{1,0:T(8,128)(2,1)S(1)}, u32[]{:S(2)}, u32[]{:S(2)}) collective-permute-start(bf16[64,768]{1,0:T(8,128)(2,1)S(1)} %get-tuple-element.82.refs_2_.refs_5_), channel_id=1, source_target_pairs={{0,3},{1,2},{2,1},{3,0},{4,7},{5,6},{6,5},{7,4},{8,11},{9,10},{10,... | collective-permute-start | bytes 294920 | tf_op jit(solution)/shard_map/ppermute | solution.py:549
  19.8 1.9 %collective-permute-start.5 = (bf16[64,768]{1,0:T(8,128)(2,1)S(1)}, bf16[64,768]{1,0:T(8,128)(2,1)S(1)}, u32[]{:S(2)}, u32[]{:S(2)}) collective-permute-start(bf16[64,768]{1,0:T(8,128)(2,1)S(1)} %get-tuple-element.82.refs_2_.refs_5_), channel_id=1, source_target_pairs={{0,1},{1,0},{2,3},{3,2},{4,5},{5,4},{6,7},{7,6},{8,9},{9,8},{10,11... | collective-permute-start | bytes 294920 | tf_op jit(solution)/shard_map/ppermute | solution.py:549
  21.6 2.4 %fetch.1 = (bf16[2,768,768]{2,1,0:T(8,128)(2,1)S(1)}, bf16[2,768,768]{2,1,0:T(8,128)(2,1)S(1)}) custom-call(bf16[2,768,768]{2,1,0:T(8,128)(2,1)} %refs_0_.3, bf16[2,768,768]{2,1,0:T(8,128)(2,1)} %refs_1_.2, bf16[64,768]{1,0:T(8,128)(2,1)S(1)} %get-tuple-element.82.refs_2_.refs_5_), custom_call_target="tpu_custom_call" | custom-call | flops 20000000000 | tf_op jit(solution)/shard_map/fetch/pallas_call | solution.py:529
  24.0 0.8 collective-permute-done.3.refs_6_
  24.8 3.4 %collective-permute-done.4.refs_7_ = bf16[64,768]{1,0:T(8,128)(2,1)S(1)} collective-permute-done((bf16[64,768]{1,0:T(8,128)(2,1)S(1)}, bf16[64,768]{1,0:T(8,128)(2,1)S(1)}, u32[]{:S(2)}, u32[]{:S(2)}) %collective-permute-start.4) | collective-permute-done | bytes 98336 | tf_op jit(solution)/shard_map/ppermute | solution.py:549
  28.1 0.0 collective-permute-done.5.refs_8_
  28.1 3.5 %expert.1 = (bf16[64,768]{1,0:T(8,128)(2,1)S(1)}, bf16[64,768]{1,0:T(8,128)(2,1)S(1)}, bf16[64,768]{1,0:T(8,128)(2,1)S(1)}, bf16[64,768]{1,0:T(8,128)(2,1)S(1)},...) custom-call(s32[1,256]{1,0:T(1,128)S(1)} %bitcast.18, ...), custom_call_target="tpu_custom_call" | custom-call | flops 5000000000 | tf_op jit(solution)/shard_map/expert/pallas_call | solution.py:529
  31.6 0.1 collective-permute-start.10
  31.7 1.6 %collective-permute-start.8 = (bf16[64,768]{1,0:T(8,128)(2,1)S(1)}, bf16[64,768]{1,0:T(8,128)(2,1)S(1)}, u32[]{:S(2)}, u32[]{:S(2)}) collective-permute-start(bf16[64,768]{1,0:T(8,128)(2,1)S(1)} %get-tuple-element.102), channel_id=1, source_target_pairs={{0,3},{1,2},{2,1},{3,0},{4,7},{5,6},{6,5},{7,4},{8,11},{9,10},{10,... | collective-permute-start | bytes 294920 | tf_op jit(solution)/shard_map/ppermute | solution.py:549
  33.3 1.9 %collective-permute-start.9 = (bf16[64,768]{1,0:T(8,128)(2,1)S(1)}, bf16[64,768]{1,0:T(8,128)(2,1)S(1)}, u32[]{:S(2)}, u32[]{:S(2)}) collective-permute-start(bf16[64,768]{1,0:T(8,128)(2,1)S(1)} %get-tuple-element.103), channel_id=1, source_target_pairs={{0,2},{1,3},{2,0},{3,1},{4,6},{5,7},{6,4},{7,5},{8,10},{9,11},{10,... | collective-permute-start | bytes 294920 | tf_op jit(solution)/shard_map/ppermute | solution.py:549
  35.2 3.6 %expert_grads.1 = (bf16[4,96,3072]{2,1,0:T(8,128)(2,1)S(1)}, bf16[4,96,3072]{2,1,0:T(8,128)(2,1)S(1)}, bf16[128,768]{1,0:T(8,128)(2,1)S(1)}, bf16[128,768]{1,0:T(8,128)(2,1)S(1)}) custom-call(s32[1,256]{1,0:T(1,128)S(1)} %bitcast.19, bf16[288,768]{1,0:T(8,128)(2,1)S(1)} %get-tuple-element.85.refs_1_, bf16[288,768]{1,0:T(8,128)(2,1)S(1)} %get-tuple-element.86.refs_2_, ...), custom_call_target="tpu_custom_call" | custom-call | flops 20000000000 | tf_op jit(solution)/shard_map/expert_grads/pallas_call | solution.py:529
  38.8 0.1 collective-permute-start.6
  38.9 1.0 %collective-permute-start.14 = (bf16[128,768]{1,0:T(8,128)(2,1)S(1)}, bf16[128,768]{1,0:T(8,128)(2,1)S(1)}, u32[]{:S(2)}, u32[]{:S(2)}) collective-permute-start(bf16[128,768]{1,0:T(8,128)(2,1)S(1)} %get-tuple-element.105.refs_7_), channel_id=1, source_target_pairs={{0,1},{1,0},{2,3},{3,2},{4,5},{5,4},{6,7},{7,6},{8,9},{9,8},{10,11... | collective-permute-start | bytes 589832 | tf_op jit(solution)/shard_map/ppermute | solution.py:549
  40.0 0.0 collective-permute-done.10.refs_6_
  40.0 0.0 collective-permute-done.8.refs_4_
  40.0 3.3 %collective-permute-done.9.refs_5_ = bf16[64,768]{1,0:T(8,128)(2,1)S(1)} collective-permute-done((bf16[64,768]{1,0:T(8,128)(2,1)S(1)}, bf16[64,768]{1,0:T(8,128)(2,1)S(1)}, u32[]{:S(2)}, u32[]{:S(2)}) %collective-permute-start.9) | collective-permute-done | bytes 98336 | tf_op jit(solution)/shard_map/ppermute | solution.py:549
  43.3 0.2 hidden_back.1
  43.4 2.1 %collective-permute-start.11 = (bf16[64,768]{1,0:T(8,128)(2,1)S(1)}, bf16[64,768]{1,0:T(8,128)(2,1)S(1)}, u32[]{:S(2)}, u32[]{:S(2)}) collective-permute-start(bf16[64,768]{1,0:T(8,128)(2,1)S(1)} %get-tuple-element.108.refs_11_), channel_id=1, source_target_pairs={{0,3},{1,2},{2,1},{3,0},{4,7},{5,6},{6,5},{7,4},{8,11},{9,10},{10,... | collective-permute-start | bytes 294920 | tf_op jit(solution)/shard_map/ppermute | solution.py:549
  45.6 0.0 collective-permute-start.12
  45.6 2.3 %collective-permute-start.13 = (bf16[64,768]{1,0:T(8,128)(2,1)S(1)}, bf16[64,768]{1,0:T(8,128)(2,1)S(1)}, u32[]{:S(2)}, u32[]{:S(2)}) collective-permute-start(bf16[64,768]{1,0:T(8,128)(2,1)S(1)} %get-tuple-element.108.refs_11_), channel_id=1, source_target_pairs={{0,1},{1,0},{2,3},{3,2},{4,5},{5,4},{6,7},{7,6},{8,9},{9,8},{10,11... | collective-permute-start | bytes 294920 | tf_op jit(solution)/shard_map/ppermute | solution.py:549
  47.9 0.5 expert_merge.1
  48.4 1.6 %collective-permute-start.7 = (bf16[2,96,3072]{2,1,0:T(8,128)(2,1)S(1)}, bf16[2,96,3072]{2,1,0:T(8,128)(2,1)S(1)}, u32[]{:S(2)}, u32[]{:S(2)}) collective-permute-start(bf16[2,96,3072]{2,1,0:T(8,128)(2,1)S(1)} %get-tuple-element.93), channel_id=1, source_target_pairs={{0,8},{4,20},{8,0},{12,28},{16,24},{20,4},{24,16},{28,12},{1,9},{5... | collective-permute-start | bytes 3538952 | tf_op jit(solution)/shard_map/ppermute | solution.py:555
  50.0 0.0 copy-start.3
  50.0 0.0 copy-start.4
  50.0 0.1 pair_sum.1
  50.0 0.7 collective-permute-start.15
  50.7 0.3 collective-permute-done.11.refs_12_
  51.0 4.8 %collective-permute-done.12.refs_13_ = bf16[64,768]{1,0:T(8,128)(2,1)S(1)} collective-permute-done((bf16[64,768]{1,0:T(8,128)(2,1)S(1)}, bf16[64,768]{1,0:T(8,128)(2,1)S(1)}, u32[]{:S(2)}, u32[]{:S(2)}) %collective-permute-start.12) | collective-permute-done | bytes 98336 | tf_op jit(solution)/shard_map/ppermute | solution.py:549
  55.9 1.8 %attention_back.1 = (f32[72,768]{1,0:T(8,128)S(1)}, bf16[72,768]{1,0:T(8,128)(2,1)S(1)}, bf16[72,768]{1,0:T(8,128)(2,1)S(1)}, bf16[72,768]{1,0:T(8,128)(2,1)S(1)...) custom-call(bf16[256,768]{1,0:T(8,128)(2,1)S(1)} %copy-done, ...), custom_call_target="tpu_custom_call" | custom-call | flops 5000000000 | tf_op jit(solution)/shard_map/attention_back/pallas_call | solution.py:529
  57.8 1.9 %collective-permute-start.18 = (bf16[72,768]{1,0:T(8,128)(2,1)S(1)}, bf16[72,768]{1,0:T(8,128)(2,1)S(1)}, u32[]{:S(2)}, u32[]{:S(2)}) collective-permute-start(bf16[72,768]{1,0:T(8,128)(2,1)S(1)} %get-tuple-element.124), channel_id=1, source_target_pairs={{0,3},{1,2},{2,1},{3,0},{4,7},{5,6},{6,5},{7,4},{8,11},{9,10},{10,... | collective-permute-start | bytes 331784 | tf_op jit(solution)/shard_map/ppermute | solution.py:549
  59.7 2.5 %collective-permute-start.20 = (bf16[72,768]{1,0:T(8,128)(2,1)S(1)}, bf16[72,768]{1,0:T(8,128)(2,1)S(1)}, u32[]{:S(2)}, u32[]{:S(2)}) collective-permute-start(bf16[72,768]{1,0:T(8,128)(2,1)S(1)} %get-tuple-element.126), channel_id=1, source_target_pairs={{0,1},{1,0},{2,3},{3,2},{4,5},{5,4},{6,7},{7,6},{8,9},{9,8},{10,11... | collective-permute-start | bytes 331784 | tf_op jit(solution)/shard_map/ppermute | solution.py:549
  62.3 0.4 collective-permute-start.27
  62.7 1.8 %weight_grads.1 = (bf16[4,96,768]{2,1,0:T(8,128)(2,1)S(1)}, bf16[4,96,768]{2,1,0:T(8,128)(2,1)S(1)}, f32[8,768]{1,0:T(8,128)S(1)}) custom-call(bf16[256,768]{1,0:T(8,128)(2,1)S(1)} %get-tuple-element.94.refs_0_, bf16[3,256,192]{2,1,0:T(8,128)(2,1)S(1)} %get-tuple-element.111.refs_1_, bf16[256,768]{1,0:T(8,128)(2,1)S(1)} %get-tuple-element.112.refs_2_, ...), custom_call_target="tpu_custom_call" | custom-call | flops 4000000000 | tf_op jit(solution)/shard_map/weight_grads/pallas_call | solution.py:529
  64.5 0.2 collective-permute-done.7.refs_1_
  64.7 0.3 expert_cross.1
  64.9 1.7 %collective-permute-done.16.refs_2_ = bf16[4,96,768]{2,1,0:T(8,128)(2,1)S(1)} collective-permute-done((bf16[4,96,768]{2,1,0:T(8,128)(2,1)S(1)}, bf16[4,96,768]{2,1,0:T(8,128)(2,1)S(1)}, u32[]{:S(2)}, u32[]{:S(2)}) %collective-permute-start.16) | collective-permute-done | bytes 589856 | tf_op jit(solution)/shard_map/ppermute | solution.py:549
  66.7 0.2 cross.1
  66.8 1.6 %collective-permute-start.17 = (bf16[144,3072]{1,0:T(8,128)(2,1)S(1)}, bf16[144,3072]{1,0:T(8,128)(2,1)S(1)}, u32[]{:S(2)}, u32[]{:S(2)}) collective-permute-start(bf16[144,3072]{1,0:T(8,128)(2,1)S(1)} %get-tuple-element.121), channel_id=1, source_target_pairs={{0,16},{4,12},{8,24},{12,4},{16,0},{20,28},{24,8},{28,20},{1,17},{... | collective-permute-start | bytes 2654216 | tf_op jit(solution)/shard_map/ppermute | solution.py:555
  68.4 2.2 %collective-permute-done.19.refs_6_ = bf16[72,768]{1,0:T(8,128)(2,1)S(1)} collective-permute-done((bf16[72,768]{1,0:T(8,128)(2,1)S(1)}, bf16[72,768]{1,0:T(8,128)(2,1)S(1)}, u32[]{:S(2)}, u32[]{:S(2)}) %collective-permute-start.19) | collective-permute-done | bytes 110624 | tf_op jit(solution)/shard_map/ppermute | solution.py:549
  70.6 0.2 input_back.1
  70.8 0.1 collective-permute-start.21
  70.9 2.0 %collective-permute-start.23 = (bf16[64,768]{1,0:T(8,128)(2,1)S(1)}, bf16[64,768]{1,0:T(8,128)(2,1)S(1)}, u32[]{:S(2)}, u32[]{:S(2)}) collective-permute-start(bf16[64,768]{1,0:T(8,128)(2,1)S(1)} %get-tuple-element.128.refs_2_), channel_id=1, source_target_pairs={{0,3},{1,2},{2,1},{3,0},{4,7},{5,6},{6,5},{7,4},{8,11},{9,10},{10,... | collective-permute-start | bytes 294920 | tf_op jit(solution)/shard_map/ppermute | solution.py:549
  72.9 2.4 %collective-permute-start.25 = (bf16[64,768]{1,0:T(8,128)(2,1)S(1)}, bf16[64,768]{1,0:T(8,128)(2,1)S(1)}, u32[]{:S(2)}, u32[]{:S(2)}) collective-permute-start(bf16[64,768]{1,0:T(8,128)(2,1)S(1)} %get-tuple-element.128.refs_2_), channel_id=1, source_target_pairs={{0,1},{1,0},{2,3},{3,2},{4,5},{5,4},{6,7},{7,6},{8,9},{9,8},{10,11... | collective-permute-start | bytes 294920 | tf_op jit(solution)/shard_map/ppermute | solution.py:549
  75.3 1.6 %collective-permute-start.22 = (f32[8,768]{1,0:T(8,128)S(1)}, f32[8,768]{1,0:T(8,128)S(1)}, u32[]{:S(2)}, u32[]{:S(2)}) collective-permute-start(f32[8,768]{1,0:T(8,128)S(1)} %small_sum.1.refs_2_), channel_id=1, source_target_pairs={{0,16},{4,12},{8,24},{12,4},{16,0},{20,28},{24,8},{28,20},{1,17},{... | collective-permute-start | bytes 73736 | tf_op jit(solution)/shard_map/ppermute | solution.py:555
  76.9 3.3 %collective-permute-done.22.refs_3_ = f32[8,768]{1,0:T(8,128)S(1)} collective-permute-done((f32[8,768]{1,0:T(8,128)S(1)}, f32[8,768]{1,0:T(8,128)S(1)}, u32[]{:S(2)}, u32[]{:S(2)}) %collective-permute-start.22) | collective-permute-done | bytes 24608 | tf_op jit(solution)/shard_map/ppermute | solution.py:555
  80.2 1.9 %collective-permute-start.28 = (bf16[128,768]{1,0:T(8,128)(2,1)S(1)}, bf16[128,768]{1,0:T(8,128)(2,1)S(1)}, u32[]{:S(2)}, u32[]{:S(2)}) collective-permute-start(bf16[128,768]{1,0:T(8,128)(2,1)S(1)} %output_pair.1.refs_6_), channel_id=1, source_target_pairs={{0,1},{1,0},{2,3},{3,2},{4,5},{5,4},{6,7},{7,6},{8,9},{9,8},{10,11... | collective-permute-start | bytes 589832 | tf_op jit(solution)/shard_map/ppermute | solution.py:549
  82.1 0.1 weight_cross.1
  82.2 1.6 %collective-permute-start.26 = (bf16[112,768]{1,0:T(8,128)(2,1)S(1)}, bf16[112,768]{1,0:T(8,128)(2,1)S(1)}, u32[]{:S(2)}, u32[]{:S(2)}) collective-permute-start(bf16[112,768]{1,0:T(8,128)(2,1)S(1)} %get-tuple-element.130), channel_id=1, source_target_pairs={{0,8},{4,20},{8,0},{12,28},{16,24},{20,4},{24,16},{28,12},{1,9},{5... | collective-permute-start | bytes 516104 | tf_op jit(solution)/shard_map/ppermute | solution.py:555
  83.8 1.1 %expert_final.1 = (f32[2,96,768]{2,1,0:T(8,128)}, f32[2,96,768]{2,1,0:T(8,128)}) custom-call(f32[96,3072]{1,0:T(8,128)S(1)} %get-tuple-element.131.refs_0_, bf16[144,3072]{1,0:T(8,128)(2,1)S(1)} %collective-permute-done.17.refs_1_), custom_call_target="tpu_custom_call" | custom-call | flops 1000000 | tf_op jit(solution)/shard_map/expert_final/pallas_call | solution.py:529
  84.9 1.6 %collective-permute-done.28.refs_7_ = bf16[128,768]{1,0:T(8,128)(2,1)S(1)} collective-permute-done((bf16[128,768]{1,0:T(8,128)(2,1)S(1)}, bf16[128,768]{1,0:T(8,128)(2,1)S(1)}, u32[]{:S(2)}, u32[]{:S(2)}) %collective-permute-start.28) | collective-permute-done | bytes 196640 | tf_op jit(solution)/shard_map/ppermute | solution.py:549
  86.5 1.2 %collective-permute-done.26.refs_1_ = bf16[112,768]{1,0:T(8,128)(2,1)S(1)} collective-permute-done((bf16[112,768]{1,0:T(8,128)(2,1)S(1)}, bf16[112,768]{1,0:T(8,128)(2,1)S(1)}, u32[]{:S(2)}, u32[]{:S(2)}) %collective-permute-start.26) | collective-permute-done | bytes 172064 | tf_op jit(solution)/shard_map/ppermute | solution.py:555
  87.7 1.1 %finish.1 = (bf16[256,768]{1,0:T(8,128)(2,1)}, bf16[256,768]{1,0:T(8,128)(2,1)}, f32[96,192]{1,0:T(8,128)}, f32[96,192]{1,0:T(8,128)}, f32[96,192]{1,0:T(8,128)}...) custom-call(f32[112,768]{1,0:T(8,128)S(1)} %get-tuple-element.129.refs_0_, ...), custom_call_target="tpu_custom_call" | custom-call | flops 1000000 | tf_op jit(solution)/shard_map/finish/pallas_call | solution.py:529
  (31 shorter events, 0.1 us)
Async XLA Ops:
  3.6 8.8 %collective-permute-start = (bf16[64,768]{1,0:T(8,128)(2,1)S(1)}, bf16[64,768]{1,0:T(8,128)(2,1)S(1)}, u32[]{:S(2)}, u32[]{:S(2)}) collective-permute-start(bf16[64,768]{1,0:T(8,128)(2,1)S(1)} %get-tuple-element.79), channel_id=1, source_target_pairs={{0,3},{1,2},{2,1},{3,0},{4,7},{5,6},{6,5},{7,4},{8,11},{9,10},{10,... | collective-permute-start | bytes 294920 | tf_op jit(solution)/shard_map/ppermute | solution.py:549
  8.7 8.3 %collective-permute-start.1 = (bf16[64,768]{1,0:T(8,128)(2,1)S(1)}, bf16[64,768]{1,0:T(8,128)(2,1)S(1)}, u32[]{:S(2)}, u32[]{:S(2)}) collective-permute-start(bf16[64,768]{1,0:T(8,128)(2,1)S(1)} %get-tuple-element.80), channel_id=1, source_target_pairs={{0,2},{1,3},{2,0},{3,1},{4,6},{5,7},{6,4},{7,5},{8,10},{9,11},{10,... | collective-permute-start | bytes 294920 | tf_op jit(solution)/shard_map/ppermute | solution.py:549
  8.7 8.3 %collective-permute-start.2 = (bf16[64,768]{1,0:T(8,128)(2,1)S(1)}, bf16[64,768]{1,0:T(8,128)(2,1)S(1)}, u32[]{:S(2)}, u32[]{:S(2)}) collective-permute-start(bf16[64,768]{1,0:T(8,128)(2,1)S(1)} %get-tuple-element.81), channel_id=1, source_target_pairs={{0,1},{1,0},{2,3},{3,2},{4,5},{5,4},{6,7},{7,6},{8,9},{9,8},{10,11... | collective-permute-start | bytes 294920 | tf_op jit(solution)/shard_map/ppermute | solution.py:549
  17.1 11.0 %copy-start.5 = (bf16[256,768]{1,0:T(8,128)(2,1)S(1)}, bf16[256,768]{1,0:T(8,128)(2,1)}, u32[]{:S(2)}) copy-start(bf16[256,768]{1,0:T(8,128)(2,1)} %refs_1_.3) | copy-start | bytes 1179652
  17.1 11.0 %copy-start.6 = (bf16[768,2]{0,1:T(2,128)(2,1)S(1)}, bf16[768,2]{0,1:T(2,128)(2,1)}, u32[]{:S(2)}) copy-start(bf16[768,2]{0,1:T(2,128)(2,1)} %param.28) | copy-start | bytes 9220
  17.2 7.6 %collective-permute-start.3 = (bf16[64,768]{1,0:T(8,128)(2,1)S(1)}, bf16[64,768]{1,0:T(8,128)(2,1)S(1)}, u32[]{:S(2)}, u32[]{:S(2)}) collective-permute-start(bf16[64,768]{1,0:T(8,128)(2,1)S(1)} %get-tuple-element.82.refs_2_.refs_5_), channel_id=1, source_target_pairs={{0,3},{1,2},{2,1},{3,0},{4,7},{5,6},{6,5},{7,4},{8,11},{9,10},{10,... | collective-permute-start | bytes 294920 | tf_op jit(solution)/shard_map/ppermute | solution.py:549
  19.7 8.4 %collective-permute-start.4 = (bf16[64,768]{1,0:T(8,128)(2,1)S(1)}, bf16[64,768]{1,0:T(8,128)(2,1)S(1)}, u32[]{:S(2)}, u32[]{:S(2)}) collective-permute-start(bf16[64,768]{1,0:T(8,128)(2,1)S(1)} %get-tuple-element.82.refs_2_.refs_5_), channel_id=1, source_target_pairs={{0,2},{1,3},{2,0},{3,1},{4,6},{5,7},{6,4},{7,5},{8,10},{9,11},{10,... | collective-permute-start | bytes 294920 | tf_op jit(solution)/shard_map/ppermute | solution.py:549
  19.8 8.4 %collective-permute-start.5 = (bf16[64,768]{1,0:T(8,128)(2,1)S(1)}, bf16[64,768]{1,0:T(8,128)(2,1)S(1)}, u32[]{:S(2)}, u32[]{:S(2)}) collective-permute-start(bf16[64,768]{1,0:T(8,128)(2,1)S(1)} %get-tuple-element.82.refs_2_.refs_5_), channel_id=1, source_target_pairs={{0,1},{1,0},{2,3},{3,2},{4,5},{5,4},{6,7},{7,6},{8,9},{9,8},{10,11... | collective-permute-start | bytes 294920 | tf_op jit(solution)/shard_map/ppermute | solution.py:549
  31.6 8.3 %collective-permute-start.10 = (bf16[64,768]{1,0:T(8,128)(2,1)S(1)}, bf16[64,768]{1,0:T(8,128)(2,1)S(1)}, u32[]{:S(2)}, u32[]{:S(2)}) collective-permute-start(bf16[64,768]{1,0:T(8,128)(2,1)S(1)} %get-tuple-element.104), channel_id=1, source_target_pairs={{0,1},{1,0},{2,3},{3,2},{4,5},{5,4},{6,7},{7,6},{8,9},{9,8},{10,11... | collective-permute-start | bytes 294920 | tf_op jit(solution)/shard_map/ppermute | solution.py:549
  31.7 8.2 %collective-permute-start.8 = (bf16[64,768]{1,0:T(8,128)(2,1)S(1)}, bf16[64,768]{1,0:T(8,128)(2,1)S(1)}, u32[]{:S(2)}, u32[]{:S(2)}) collective-permute-start(bf16[64,768]{1,0:T(8,128)(2,1)S(1)} %get-tuple-element.102), channel_id=1, source_target_pairs={{0,3},{1,2},{2,1},{3,0},{4,7},{5,6},{6,5},{7,4},{8,11},{9,10},{10,... | collective-permute-start | bytes 294920 | tf_op jit(solution)/shard_map/ppermute | solution.py:549
  33.3 10.0 %collective-permute-start.9 = (bf16[64,768]{1,0:T(8,128)(2,1)S(1)}, bf16[64,768]{1,0:T(8,128)(2,1)S(1)}, u32[]{:S(2)}, u32[]{:S(2)}) collective-permute-start(bf16[64,768]{1,0:T(8,128)(2,1)S(1)} %get-tuple-element.103), channel_id=1, source_target_pairs={{0,2},{1,3},{2,0},{3,1},{4,6},{5,7},{6,4},{7,5},{8,10},{9,11},{10,... | collective-permute-start | bytes 294920 | tf_op jit(solution)/shard_map/ppermute | solution.py:549
  38.8 9.1 %collective-permute-start.6 = (bf16[4,96,3072]{2,1,0:T(8,128)(2,1)S(1)}, bf16[4,96,3072]{2,1,0:T(8,128)(2,1)S(1)}, u32[]{:S(2)}, u32[]{:S(2)}) collective-permute-start(bf16[4,96,3072]{2,1,0:T(8,128)(2,1)S(1)} %get-tuple-element.91), channel_id=1, source_target_pairs={{0,4},{4,0},{8,12},{12,8},{16,20},{20,16},{24,28},{28,24},{1,5},{5... | collective-permute-start | bytes 7077896 | tf_op jit(solution)/shard_map/ppermute | solution.py:549
  38.9 11.0 %collective-permute-start.14 = (bf16[128,768]{1,0:T(8,128)(2,1)S(1)}, bf16[128,768]{1,0:T(8,128)(2,1)S(1)}, u32[]{:S(2)}, u32[]{:S(2)}) collective-permute-start(bf16[128,768]{1,0:T(8,128)(2,1)S(1)} %get-tuple-element.105.refs_7_), channel_id=1, source_target_pairs={{0,1},{1,0},{2,3},{3,2},{4,5},{5,4},{6,7},{7,6},{8,9},{9,8},{10,11... | collective-permute-start | bytes 589832 | tf_op jit(solution)/shard_map/ppermute | solution.py:549
  43.4 7.6 %collective-permute-start.11 = (bf16[64,768]{1,0:T(8,128)(2,1)S(1)}, bf16[64,768]{1,0:T(8,128)(2,1)S(1)}, u32[]{:S(2)}, u32[]{:S(2)}) collective-permute-start(bf16[64,768]{1,0:T(8,128)(2,1)S(1)} %get-tuple-element.108.refs_11_), channel_id=1, source_target_pairs={{0,3},{1,2},{2,1},{3,0},{4,7},{5,6},{6,5},{7,4},{8,11},{9,10},{10,... | collective-permute-start | bytes 294920 | tf_op jit(solution)/shard_map/ppermute | solution.py:549
  45.6 10.3 %collective-permute-start.12 = (bf16[64,768]{1,0:T(8,128)(2,1)S(1)}, bf16[64,768]{1,0:T(8,128)(2,1)S(1)}, u32[]{:S(2)}, u32[]{:S(2)}) collective-permute-start(bf16[64,768]{1,0:T(8,128)(2,1)S(1)} %get-tuple-element.108.refs_11_), channel_id=1, source_target_pairs={{0,2},{1,3},{2,0},{3,1},{4,6},{5,7},{6,4},{7,5},{8,10},{9,11},{10,... | collective-permute-start | bytes 294920 | tf_op jit(solution)/shard_map/ppermute | solution.py:549
  45.6 10.3 %collective-permute-start.13 = (bf16[64,768]{1,0:T(8,128)(2,1)S(1)}, bf16[64,768]{1,0:T(8,128)(2,1)S(1)}, u32[]{:S(2)}, u32[]{:S(2)}) collective-permute-start(bf16[64,768]{1,0:T(8,128)(2,1)S(1)} %get-tuple-element.108.refs_11_), channel_id=1, source_target_pairs={{0,1},{1,0},{2,3},{3,2},{4,5},{5,4},{6,7},{7,6},{8,9},{9,8},{10,11... | collective-permute-start | bytes 294920 | tf_op jit(solution)/shard_map/ppermute | solution.py:549
  48.4 16.3 %collective-permute-start.7 = (bf16[2,96,3072]{2,1,0:T(8,128)(2,1)S(1)}, bf16[2,96,3072]{2,1,0:T(8,128)(2,1)S(1)}, u32[]{:S(2)}, u32[]{:S(2)}) collective-permute-start(bf16[2,96,3072]{2,1,0:T(8,128)(2,1)S(1)} %get-tuple-element.93), channel_id=1, source_target_pairs={{0,8},{4,20},{8,0},{12,28},{16,24},{20,4},{24,16},{28,12},{1,9},{5... | collective-permute-start | bytes 3538952 | tf_op jit(solution)/shard_map/ppermute | solution.py:555
  49.9 5.9 %copy-start = (bf16[256,768]{1,0:T(8,128)(2,1)S(1)}, bf16[256,768]{1,0:T(8,128)(2,1)}, u32[]{:S(2)}) copy-start(bf16[256,768]{1,0:T(8,128)(2,1)} %refs_0_.5) | copy-start | bytes 1179652
  50.0 5.9 %copy-start.1 = (bf16[768,192]{0,1:T(8,128)(2,1)S(1)}, bf16[768,192]{0,1:T(8,128)(2,1)}, u32[]{:S(2)}) copy-start(bf16[768,192]{0,1:T(8,128)(2,1)} %param.23) | copy-start | bytes 884740
  50.0 5.9 %copy-start.2 = (bf16[768,192]{0,1:T(8,128)(2,1)S(1)}, bf16[768,192]{0,1:T(8,128)(2,1)}, u32[]{:S(2)}) copy-start(bf16[768,192]{0,1:T(8,128)(2,1)} %param.24) | copy-start | bytes 884740
  50.0 5.9 %copy-start.3 = (bf16[768,192]{0,1:T(8,128)(2,1)S(1)}, bf16[768,192]{0,1:T(8,128)(2,1)}, u32[]{:S(2)}) copy-start(bf16[768,192]{0,1:T(8,128)(2,1)} %param.25) | copy-start | bytes 884740
  50.0 5.9 %copy-start.4 = (bf16[192,768]{1,0:T(8,128)(2,1)S(1)}, bf16[192,768]{1,0:T(8,128)(2,1)}, u32[]{:S(2)}) copy-start(bf16[192,768]{1,0:T(8,128)(2,1)} %refs_8_.3) | copy-start | bytes 884740
  50.0 12.2 %collective-permute-start.15 = (bf16[64,768]{1,0:T(8,128)(2,1)S(1)}, bf16[64,768]{1,0:T(8,128)(2,1)S(1)}, u32[]{:S(2)}, u32[]{:S(2)}) collective-permute-start(bf16[64,768]{1,0:T(8,128)(2,1)S(1)} %get-tuple-element.115), channel_id=1, source_target_pairs={{0,2},{1,3},{2,0},{3,1},{4,6},{5,7},{6,4},{7,5},{8,10},{9,11},{10,... | collective-permute-start | bytes 294920 | tf_op jit(solution)/shard_map/ppermute | solution.py:549
  57.8 10.7 %collective-permute-start.18 = (bf16[72,768]{1,0:T(8,128)(2,1)S(1)}, bf16[72,768]{1,0:T(8,128)(2,1)S(1)}, u32[]{:S(2)}, u32[]{:S(2)}) collective-permute-start(bf16[72,768]{1,0:T(8,128)(2,1)S(1)} %get-tuple-element.124), channel_id=1, source_target_pairs={{0,3},{1,2},{2,1},{3,0},{4,7},{5,6},{6,5},{7,4},{8,11},{9,10},{10,... | collective-permute-start | bytes 331784 | tf_op jit(solution)/shard_map/ppermute | solution.py:549
  59.7 10.9 %collective-permute-start.19 = (bf16[72,768]{1,0:T(8,128)(2,1)S(1)}, bf16[72,768]{1,0:T(8,128)(2,1)S(1)}, u32[]{:S(2)}, u32[]{:S(2)}) collective-permute-start(bf16[72,768]{1,0:T(8,128)(2,1)S(1)} %get-tuple-element.125), channel_id=1, source_target_pairs={{0,2},{1,3},{2,0},{3,1},{4,6},{5,7},{6,4},{7,5},{8,10},{9,11},{10,... | collective-permute-start | bytes 331784 | tf_op jit(solution)/shard_map/ppermute | solution.py:549
  59.7 10.9 %collective-permute-start.20 = (bf16[72,768]{1,0:T(8,128)(2,1)S(1)}, bf16[72,768]{1,0:T(8,128)(2,1)S(1)}, u32[]{:S(2)}, u32[]{:S(2)}) collective-permute-start(bf16[72,768]{1,0:T(8,128)(2,1)S(1)} %get-tuple-element.126), channel_id=1, source_target_pairs={{0,1},{1,0},{2,3},{3,2},{4,5},{5,4},{6,7},{7,6},{8,9},{9,8},{10,11... | collective-permute-start | bytes 331784 | tf_op jit(solution)/shard_map/ppermute | solution.py:549
  62.3 13.1 %collective-permute-start.27 = (bf16[64,768]{1,0:T(8,128)(2,1)S(1)}, bf16[64,768]{1,0:T(8,128)(2,1)S(1)}, u32[]{:S(2)}, u32[]{:S(2)}) collective-permute-start(bf16[64,768]{1,0:T(8,128)(2,1)S(1)} %output_share.1.refs_6_.refs_0_), channel_id=1, source_target_pairs={{0,2},{1,3},{2,0},{3,1},{4,6},{5,7},{6,4},{7,5},{8,10},{9,11},{10,... | collective-permute-start | bytes 294920 | tf_op jit(solution)/shard_map/ppermute | solution.py:549
  64.7 2.0 %collective-permute-start.16 = (bf16[4,96,768]{2,1,0:T(8,128)(2,1)S(1)}, bf16[4,96,768]{2,1,0:T(8,128)(2,1)S(1)}, u32[]{:S(2)}, u32[]{:S(2)}) collective-permute-start(bf16[4,96,768]{2,1,0:T(8,128)(2,1)S(1)} %get-tuple-element.119), channel_id=1, source_target_pairs={{0,4},{4,0},{8,12},{12,8},{16,20},{20,16},{24,28},{28,24},{1,5},{5... | collective-permute-start | bytes 1769480 | tf_op jit(solution)/shard_map/ppermute | solution.py:549
  66.8 15.3 %collective-permute-start.17 = (bf16[144,3072]{1,0:T(8,128)(2,1)S(1)}, bf16[144,3072]{1,0:T(8,128)(2,1)S(1)}, u32[]{:S(2)}, u32[]{:S(2)}) collective-permute-start(bf16[144,3072]{1,0:T(8,128)(2,1)S(1)} %get-tuple-element.121), channel_id=1, source_target_pairs={{0,16},{4,12},{8,24},{12,4},{16,0},{20,28},{24,8},{28,20},{1,17},{... | collective-permute-start | bytes 2654216 | tf_op jit(solution)/shard_map/ppermute | solution.py:555
  70.8 2.1 %collective-permute-start.21 = (f32[8,768]{1,0:T(8,128)S(1)}, f32[8,768]{1,0:T(8,128)S(1)}, u32[]{:S(2)}, u32[]{:S(2)}) collective-permute-start(f32[8,768]{1,0:T(8,128)S(1)} %get-tuple-element.127.refs_0_.refs_2_), channel_id=1, source_target_pairs={{0,4},{4,0},{8,12},{12,8},{16,20},{20,16},{24,28},{28,24},{1,5},{5... | collective-permute-start | bytes 73736 | tf_op jit(solution)/shard_map/ppermute | solution.py:549
  70.9 11.3 %collective-permute-start.23 = (bf16[64,768]{1,0:T(8,128)(2,1)S(1)}, bf16[64,768]{1,0:T(8,128)(2,1)S(1)}, u32[]{:S(2)}, u32[]{:S(2)}) collective-permute-start(bf16[64,768]{1,0:T(8,128)(2,1)S(1)} %get-tuple-element.128.refs_2_), channel_id=1, source_target_pairs={{0,3},{1,2},{2,1},{3,0},{4,7},{5,6},{6,5},{7,4},{8,11},{9,10},{10,... | collective-permute-start | bytes 294920 | tf_op jit(solution)/shard_map/ppermute | solution.py:549
  72.9 9.3 %collective-permute-start.24 = (bf16[64,768]{1,0:T(8,128)(2,1)S(1)}, bf16[64,768]{1,0:T(8,128)(2,1)S(1)}, u32[]{:S(2)}, u32[]{:S(2)}) collective-permute-start(bf16[64,768]{1,0:T(8,128)(2,1)S(1)} %get-tuple-element.128.refs_2_), channel_id=1, source_target_pairs={{0,2},{1,3},{2,0},{3,1},{4,6},{5,7},{6,4},{7,5},{8,10},{9,11},{10,... | collective-permute-start | bytes 294920 | tf_op jit(solution)/shard_map/ppermute | solution.py:549
  72.9 9.3 %collective-permute-start.25 = (bf16[64,768]{1,0:T(8,128)(2,1)S(1)}, bf16[64,768]{1,0:T(8,128)(2,1)S(1)}, u32[]{:S(2)}, u32[]{:S(2)}) collective-permute-start(bf16[64,768]{1,0:T(8,128)(2,1)S(1)} %get-tuple-element.128.refs_2_), channel_id=1, source_target_pairs={{0,1},{1,0},{2,3},{3,2},{4,5},{5,4},{6,7},{7,6},{8,9},{9,8},{10,11... | collective-permute-start | bytes 294920 | tf_op jit(solution)/shard_map/ppermute | solution.py:549
  75.3 4.9 %collective-permute-start.22 = (f32[8,768]{1,0:T(8,128)S(1)}, f32[8,768]{1,0:T(8,128)S(1)}, u32[]{:S(2)}, u32[]{:S(2)}) collective-permute-start(f32[8,768]{1,0:T(8,128)S(1)} %small_sum.1.refs_2_), channel_id=1, source_target_pairs={{0,16},{4,12},{8,24},{12,4},{16,0},{20,28},{24,8},{28,20},{1,17},{... | collective-permute-start | bytes 73736 | tf_op jit(solution)/shard_map/ppermute | solution.py:555
  80.2 6.3 %collective-permute-start.28 = (bf16[128,768]{1,0:T(8,128)(2,1)S(1)}, bf16[128,768]{1,0:T(8,128)(2,1)S(1)}, u32[]{:S(2)}, u32[]{:S(2)}) collective-permute-start(bf16[128,768]{1,0:T(8,128)(2,1)S(1)} %output_pair.1.refs_6_), channel_id=1, source_target_pairs={{0,1},{1,0},{2,3},{3,2},{4,5},{5,4},{6,7},{7,6},{8,9},{9,8},{10,11... | collective-permute-start | bytes 589832 | tf_op jit(solution)/shard_map/ppermute | solution.py:549
  82.2 5.5 %collective-permute-start.26 = (bf16[112,768]{1,0:T(8,128)(2,1)S(1)}, bf16[112,768]{1,0:T(8,128)(2,1)S(1)}, u32[]{:S(2)}, u32[]{:S(2)}) collective-permute-start(bf16[112,768]{1,0:T(8,128)(2,1)S(1)} %get-tuple-element.130), channel_id=1, source_target_pairs={{0,8},{4,20},{8,0},{12,28},{16,24},{20,4},{24,16},{28,12},{1,9},{5... | collective-permute-start | bytes 516104 | tf_op jit(solution)/shard_map/ppermute | solution.py:555
